TPU v7x, 256 devices: a whole 4x4x8 slice. The times are simulated.
256 devices in a mesh: ctx: 32 (over z, x_lo, core), tp: 8 (over x_hi, y).
Axes of the slice: x: 4 (x_hi: 2, x_lo: 2; x = x_hi * 2 + x_lo), y: 4, z: 8, core: 2. Of those that a mesh axis runs over, the one named last changes fastest.
Arguments:
- tokens: bfloat16 [16384, 4608], P('ctx'), may hold values from -6 to 6
- norm_gain: float32 [4608], replicated, may hold values from 0.1 to 1.9
- q_weight: bfloat16 [4608, 2048], P(None, 'tp'), may hold values from -0.09375 to 0.09375
- k_weight: bfloat16 [4608, 1024], P(None, 'tp'), may hold values from -0.09375 to 0.09375
- v_weight: bfloat16 [4608, 1024], P(None, 'tp'), may hold values from -0.09375 to 0.09375
- o_weight: bfloat16 [2048, 4608], P('tp'), may hold values from -5.634757 to 5.634757
- post_gain: float32 [4608], P('tp'), may hold values from 0.1 to 1.9
- doc_ids: int32 [128], replicated, may hold values from 0 to 31, never falling along the last dimension, each value on 1 to 32 neighbouring positions
- plan: int32 [128], replicated, may hold values from 0 to 31, as said below
Outputs:
- attended: bfloat16 [16384, 4608], P('ctx', 'tp')
Inputs may be any that keep to these rules, and one draw needn't show every extreme that they name: `plan`: every one of the 32 shards is named by exactly 4 blocks, and never by two of the 4 blocks that one index of ctx holds.
All inputs are finite; a program needn't handle non-finite values.
Results may differ from a plain program's by a relative error of at most 0.019.
Values may be sent and summed in bfloat16 or wider, within the bound.
No kernel may reach another device: no remote copies, remote signals or barrier semaphores. Data moves between devices by JAX's collectives and lax.ppermute only.
A program may use at most 128 MiB of HBM per device.

v0:
```python
import math

import jax
import jax.numpy as jnp
from jax import lax
from jax.sharding import PartitionSpec as P

HD = 128
BLK = 128


query_scale = 144.0 ** (-0.5)
soft_cap = 50.0
norm_eps = 1e-06


def local(tokens, norm_gain, q_weight, k_weight, v_weight, o_weight, post_gain, doc_ids, plan):
    tok_rows, feature_width = tokens.shape
    head_size = HD
    block_len = BLK
    query_heads = q_weight.shape[1] // head_size
    kv_heads = k_weight.shape[1] // head_size
    group_size = query_heads // kv_heads
    local_blocks = tok_rows // block_len
    total_blocks = doc_ids.shape[0]
    shard_index = lax.axis_index("ctx")
    floated = tokens.astype(jnp.float32)
    normed = (
        floated
        * lax.rsqrt(jnp.mean(floated * floated, axis=1, keepdims=True) + norm_eps)
        * norm_gain
    ).astype(jnp.bfloat16)
    queries = (jnp.dot(normed, q_weight, preferred_element_type=jnp.float32) * query_scale).astype(
        jnp.bfloat16
    )
    key_rows = jnp.dot(normed, k_weight, preferred_element_type=jnp.float32).astype(jnp.bfloat16)
    value_rows = jnp.dot(normed, v_weight, preferred_element_type=jnp.float32).astype(jnp.bfloat16)
    block_ids = jnp.arange(total_blocks, dtype=jnp.int32)
    assigned = (plan == shard_index).astype(jnp.int32)
    slot_rank = jnp.cumsum(assigned) - 1
    slot_ids = jnp.arange(local_blocks, dtype=jnp.int32)
    chosen = ((assigned[None, :] == 1) & (slot_rank[None, :] == slot_ids[:, None])).astype(
        jnp.int32
    )
    query_block = jnp.sum(chosen * block_ids[None, :], axis=1)
    query_doc = jnp.sum(chosen * doc_ids[None, :], axis=1)
    row_doc = jnp.repeat(query_doc, block_len)
    row_pos = jnp.repeat(query_block, block_len) * block_len + jnp.tile(
        jnp.arange(block_len, dtype=jnp.int32), local_blocks
    )
    columns = queries.shape[1]
    shard_rows = lax.all_gather(queries, "ctx", axis=0, tiled=True)
    piece_blocks = shard_rows.shape[0] // block_len
    picker = (query_block[:, None] == jnp.arange(piece_blocks, dtype=jnp.int32)[None, :]).astype(
        jnp.bfloat16
    )
    placed = jnp.einsum(
        "jb,bkc->jkc",
        picker,
        shard_rows.reshape(piece_blocks, block_len, columns),
        preferred_element_type=jnp.float32,
    )
    local_queries = (
        placed.reshape(tok_rows, columns)
        .astype(jnp.bfloat16)
        .reshape(tok_rows, kv_heads, group_size, head_size)
    )
    initial = (
        jnp.zeros((tok_rows, query_heads * head_size), jnp.float32),
        jnp.zeros((kv_heads, group_size, tok_rows), jnp.float32),
    )
    key_piece = lax.all_gather(key_rows, "ctx", axis=0, tiled=True)
    value_piece = lax.all_gather(value_rows, "ctx", axis=0, tiled=True)
    piece_rows = key_piece.shape[0]
    step_rows = math.gcd(piece_rows, max(512, tok_rows))
    step_count = piece_rows // step_rows
    key_steps = key_piece.reshape(step_count, step_rows, kv_heads, head_size)
    value_steps = value_piece.reshape(step_count, step_rows, kv_heads, head_size)

    def one_step(running_sum, inputs):
        key_tile, value_tile, step_index = inputs
        first_row = step_index * step_rows
        key_pos = first_row + jnp.arange(step_rows, dtype=jnp.int32)
        key_doc = jnp.repeat(
            lax.dynamic_slice_in_dim(doc_ids, first_row // block_len, step_rows // block_len, 0),
            block_len,
        )
        allowed = (row_doc[:, None] == key_doc[None, :]) & (key_pos[None, :] <= row_pos[:, None])
        numerator, denominator = running_sum
        scores = jnp.einsum(
            "rngd,knd->ngrk", local_queries, key_tile, preferred_element_type=jnp.float32
        )
        capped = soft_cap * jnp.tanh(scores / soft_cap)
        weights = jnp.where(allowed[None, None], jnp.exp(capped), 0.0)
        denominator = denominator + jnp.sum(weights, axis=-1)
        weighted = jnp.einsum(
            "ngrk,knd->rngd",
            weights.astype(jnp.bfloat16),
            value_tile,
            preferred_element_type=jnp.float32,
        )
        updated = (numerator + weighted.reshape(tok_rows, -1), denominator)
        return (updated, None)

    finished, ignored = lax.scan(
        one_step, initial, (key_steps, value_steps, jnp.arange(step_count, dtype=jnp.int32))
    )
    numerator, denominator = finished
    heads_out = (
        (
            numerator.reshape(tok_rows, kv_heads, group_size, head_size)
            / jnp.transpose(denominator, (2, 0, 1))[..., None]
        )
        .reshape(tok_rows, -1)
        .astype(jnp.bfloat16)
    )
    partial_value = jnp.dot(heads_out, o_weight, preferred_element_type=jnp.float32).astype(
        jnp.bfloat16
    )
    own_cols = lax.psum_scatter(partial_value, "tp", scatter_dimension=1, tiled=True).astype(
        jnp.float32
    )
    squares = lax.psum(jnp.sum(own_cols * own_cols, axis=1, keepdims=True), "tp")
    return (own_cols * lax.rsqrt(squares / feature_width + norm_eps) * post_gain).astype(
        jnp.bfloat16
    )


def solution(mesh):
    placed = (
        P("ctx", None),
        P(),
        P(None, "tp"),
        P(None, "tp"),
        P(None, "tp"),
        P("tp", None),
        P("tp"),
        P(),
        P(),
    )
    return jax.shard_map(
        local, mesh=mesh, in_specs=placed, out_specs=P("ctx", "tp"), check_vma=False
    )
```

profile of v0, /device:TPU:2, one launch (start us, length us, event | category | flops | bytes accessed | tf_op | source)
XLA Modules:
  0.0 515.4 jit_solution(9400283920734509932)
XLA Ops:
  6.5 3.5 fusion.14
  10.4 4.0 fusion.19
  14.5 4.4 convolution_convert_fusion.2
  19.0 4.8 convolution_convert_fusion.1
  24.7 65.1 %all-gather.8.cloned.1.call-done = bf16[16384,256]{1,0:T(8,128)(2,1)} async-done(((bf16[512,256]{1,0:T(8,128)(2,1)}), bf16[16384,256]{1,0:T(8,128)(2,1)}) %all-gather.8.cloned.1.call-update) | async-done | bytes 8388624 | tf_op jit(solution)/shard_map/all_gather | solution.py:52
  89.8 7.9 %fusion.20 = bf16[4,128,256]{2,0,1:T(4,128)(2,1)S(1)} fusion(bf16[128,128,256]{2,1,0:T(8,128)(2,1)} %bitcast.82, s32[4]{0:T(128)S(1)} %get-tuple-element.204), kind=kOutput, calls=%fused_computation.32 | convolution fusion | flops 33686016 | bytes 8650768 | tf_op jit(solution)/shard_map/jb,bkc->jkc/dot_general | solution.py:57
  98.5 59.3 %all-gather.4.cloned.1.call-done = bf16[16384,128]{1,0:T(8,128)(2,1)} async-done(((bf16[512,128]{1,0:T(8,128)(2,1)}), bf16[16384,128]{1,0:T(8,128)(2,1)}) %all-gather.4.cloned.1.call-update) | async-done | bytes 4194320 | tf_op jit(solution)/shard_map/all_gather | solution.py:73
  157.8 68.4 %all-gather.6.cloned.1.call-done = bf16[16384,128]{1,0:T(8,128)(2,1)} async-done(((bf16[512,128]{1,0:T(8,128)(2,1)}), bf16[16384,128]{1,0:T(8,128)(2,1)}) %all-gather.6.cloned.1.call-update) | async-done | bytes 4194320 | tf_op jit(solution)/shard_map/all_gather | solution.py:72
  226.2 161.0 %while.15 = (s32[]{:T(128)}, f32[512,256]{0,1:T(8,128)S(1)}, f32[1,2,512]{2,1,0:T(2,128)S(1)}, bf16[32,512,1,128]{3,1,0,2:T(8,128)(2,1)}, s32[32]{0:T(128)S(1)},...) while((s32[]{:T(128)}, f32[512,256]{0,1:T(8,128)S(1)}, ...), condition=%wide.region_6.7_spmd.clone, body=%wide.region_4.6_spmd.clone.sunk | while | flops 272107520 | bytes 5277136 | solution.py:105
  227.9 1.9 fusion.48
  232.9 1.9 fusion.48
  243.0 1.9 fusion.48
  248.0 1.9 fusion.48
  258.1 1.9 fusion.48
  263.1 1.9 fusion.48
  273.1 1.9 fusion.48
  278.2 1.9 fusion.48
  288.2 1.9 fusion.48
  293.3 1.9 fusion.48
  303.3 1.9 fusion.48
  308.4 1.9 fusion.48
  318.4 1.9 fusion.48
  323.4 1.9 fusion.48
  333.5 1.9 fusion.48
  338.5 1.9 fusion.48
  353.6 1.9 fusion.48
  378.8 1.9 fusion.48
  383.8 1.9 fusion.48
  387.2 3.6 convolution_convert_fusion
  390.8 92.6 %reduce-scatter.2.cloned.1.call-done = bf16[512,576]{0,1:T(8,128)(2,1)} async-done(((bf16[512,4608]{0,1:T(8,128)(2,1)}), bf16[512,576]{0,1:T(8,128)(2,1)}) %reduce-scatter.2.cloned.1.call-update) | async-done | bytes 589840 | tf_op jit(solution)/shard_map/reduce_scatter | solution.py:120
  484.7 22.1 %psum.7 = f32[512,1]{0,1:T(1,128)S(1)} all-reduce(f32[512,1]{0,1:T(1,128)S(1)} %bitcast.86), channel_id=1, replica_groups=mesh['ctx'=32,'tp'=8] {'tp'}, use_global_device_ids=true, to_apply=%region_9.10 | all-reduce | flops 512 | bytes 4096 | tf_op jit(solution)/shard_map/psum | solution.py:123
  506.8 2.0 fusion.25
  (337 shorter events, 107.6 us)
Async XLA Ops:
  6.5 380.7 %copy-start = (bf16[256,4608]{1,0:T(8,128)(2,1)S(1)}, bf16[256,4608]{1,0:T(8,128)(2,1)}, u32[]{:S(2)}) copy-start(bf16[256,4608]{1,0:T(8,128)(2,1)} %param.16) | copy-start | bytes 7077892
  6.5 83.3 %all-gather.8.cloned.1.call-start = ((), (), s32[]{:S(2)}) async-start(), calls=%async_computation.3 | async-start | bytes 8650752 | tf_op jit(solution)/shard_map/all_gather | solution.py:52
  6.5 3.9 copy-start.1
  10.4 4.0 copy-start.5
  14.4 143.4 %all-gather.4.cloned.1.call-start = ((), (), s32[]{:S(2)}) async-start(), calls=%async_computation.1 | async-start | bytes 4325376 | tf_op jit(solution)/shard_map/all_gather | solution.py:73
  18.9 5.2 %copy-start.4 = (s32[128]{0:T(128)S(1)}, s32[128]{0:T(128)}, u32[]{:S(2)}) copy-start(s32[128]{0:T(128)} %param.19) | copy-start | bytes 1540
  19.0 5.6 %copy-start.3 = (s32[128]{0:T(128)S(1)}, s32[128]{0:T(128)}, u32[]{:S(2)}) copy-start(s32[128]{0:T(128)} %param.18) | copy-start | bytes 1540
  19.0 207.2 %all-gather.6.cloned.1.call-start = ((), (), s32[]{:S(2)}) async-start(), calls=%async_computation.2 | async-start | bytes 4325376 | tf_op jit(solution)/shard_map/all_gather | solution.py:72
  23.8 459.6 %reduce-scatter.2.cloned.1.call-start = ((), (), s32[]{:S(2)}) async-start(), calls=%async_computation.4 | async-start | bytes 5308416 | tf_op jit(solution)/shard_map/reduce_scatter | solution.py:120
  387.2 119.6 %copy-start.2 = (f32[576]{0:T(1024)S(1)}, f32[576]{0:T(1024)}, u32[]{:S(2)}) copy-start(f32[576]{0:T(1024)} %param.17) | copy-start | bytes 6916
Sparse Core Ops, SparseCore 0:
  14.6 75.1 all-gather.7
  91.6 66.1 all-gather.3
  159.7 66.4 all-gather.5
  390.9 92.4 reduce-scatter.1
where the time goes:
time: 517 us; the launch traced here: 515 us
  waiting for transfers between devices  285 us (55%)
  matrix products  125 us (24%)
  local copies, waits for them, and re-layouts  24.8 us (5%)
  other arithmetic  24 us (5%)
  blocking collectives  22.1 us (4%)
  loops' own time  20.8 us (4%)
  between operations  13.3 us (3%)
    reduce_scatter x1, waiting for transfers between devices, local(): lax.psum_scatter(partial_value, 'tp', scatter_dimension=1, tiled=True)  92.6 us
    all_gather x1, waiting for transfers between devices, local(): key_piece = lax.all_gather(key_rows, 'ctx', axis=0, tiled=True)  68.4 us
    all_gather x1, waiting for transfers between devices, local(): shard_rows = lax.all_gather(queries, 'ctx', axis=0, tiled=True)  65.1 us
    dot_general x32, matrix products, one_step(): jnp.einsum('rngd,knd->ngrk', local_queries, key_tile, preferred_element_t...  60.7 us
    all_gather x1, waiting for transfers between devices, local(): value_piece = lax.all_gather(value_rows, 'ctx', axis=0, tiled=True)  59.3 us
    dot_general x32, matrix products, one_step(): jnp.einsum('ngrk,knd->rngd', weights.astype(jnp.bfloat16), value_tile, pr...  39.4 us
    psum x1, blocking collectives, local(): lax.psum(jnp.sum(own_cols * own_cols, axis=1, keepdims=True), 'tp')  22.1 us
    another operation x1, loops' own time, local(): lax.scan(one_step, initial, (key_steps, value_steps, jnp.arange(step_coun...  20.8 us
  transfers between devices with their start and end apart: 4, of which 4 were waited for; matrix products, arithmetic and copies ran while one was open for 4% of the time, Pallas kernels for 0%

commit v1 on v0

v1 whole, which is shorter than its diff:
```python
import functools
import math

import jax
import jax.numpy as jnp
from jax import lax
from jax.experimental import pallas as pl
from jax.experimental.pallas import tpu as pltpu
from jax.sharding import PartitionSpec as P

HD = 128
BLK = 128
PLANE = 4
BACK = 2

query_scale = 144.0 ** (-0.5)
soft_cap = 50.0
norm_eps = 1e-06
LOG2E = math.log2(math.e)


def qkv_kernel(x_ref, g_ref, wq_ref, wk_ref, wv_ref, q_ref, kv_ref):
    x = x_ref[...].astype(jnp.float32)
    r = lax.rsqrt(jnp.mean(x * x, axis=1, keepdims=True) + norm_eps)
    normed = (x * r * g_ref[...]).astype(jnp.bfloat16)
    kv_ref[:, :HD] = jnp.dot(
        normed, wk_ref[...], preferred_element_type=jnp.float32
    ).astype(jnp.bfloat16)
    kv_ref[:, HD:] = jnp.dot(
        normed, wv_ref[...], preferred_element_type=jnp.float32
    ).astype(jnp.bfloat16)
    q_ref[...] = (
        jnp.dot(normed, wq_ref[...], preferred_element_type=jnp.float32) * query_scale
    ).astype(jnp.bfloat16)


def project(tokens, gain, wq, wk, wv):
    rows, d = tokens.shape
    tile = 128

    def whole(a):
        return pl.BlockSpec(a.shape, lambda i: (0, 0), pipeline_mode=pl.Buffered(1))

    return pl.pallas_call(
        qkv_kernel,
        grid=(rows // tile,),
        in_specs=[
            pl.BlockSpec((tile, d), lambda i: (i, 0)),
            whole(gain),
            whole(wq),
            whole(wk),
            whole(wv),
        ],
        out_specs=[
            pl.BlockSpec((tile, wq.shape[1]), lambda i: (i, 0)),
            pl.BlockSpec((tile, 2 * HD), lambda i: (i, 0)),
        ],
        out_shape=[
            jax.ShapeDtypeStruct((rows, wq.shape[1]), jnp.bfloat16),
            jax.ShapeDtypeStruct((rows, 2 * HD), jnp.bfloat16),
        ],
        compiler_params=pltpu.CompilerParams(vmem_limit_bytes=40 * 2**20),
        cost_estimate=pl.CostEstimate(
            flops=2 * rows * d * 4 * HD, bytes_accessed=2 * d * (rows + 4 * HD), transcendentals=0
        ),
        name="project",
    )(tokens, gain, wq, wk, wv)


def attend_kernel(parts, rows, info_ref, q_ref, *refs):
    kv_refs, out_ref, held, sems = refs[:parts], refs[parts], refs[parts + 1], refs[parts + 2]
    place = info_ref[0]
    copies = []
    for i in range(parts):
        slot = (i // PLANE) * PLANE + (place ^ (i % PLANE))
        copies.append(pltpu.make_async_copy(kv_refs[i], held.at[slot], sems.at[i]))
    for copy in copies:
        copy.start()
    for copy in copies:
        copy.wait()
    blocks = rows // BLK
    last = place + BACK * PLANE
    heads = q_ref.shape[1] // HD
    for b in range(blocks):
        span = slice(b * BLK, (b + 1) * BLK)
        q = jnp.concatenate([q_ref[span, h * HD : (h + 1) * HD] for h in range(heads)], axis=0)
        start = info_ref[1 + b]
        query_at = (
            last * rows + b * BLK + lax.broadcasted_iota(jnp.int32, (heads * BLK, rows), 0) % BLK
        )
        offset = lax.broadcasted_iota(jnp.int32, (heads * BLK, rows), 1)

        def step(s, carry):
            total, weight_sum = carry
            scores = lax.dot_general(
                q, held[s, :, :HD], (((1,), (1,)), ((), ())), preferred_element_type=jnp.float32
            )
            key_at = s * rows + offset
            allowed = (key_at >= start) & (key_at <= query_at)
            capped = jnp.tanh(scores * (1.0 / soft_cap)) * (soft_cap * LOG2E)
            weights = jnp.where(allowed, jnp.exp2(capped), 0.0)
            for j in range(rows // HD):
                weight_sum = weight_sum + weights[:, j * HD : (j + 1) * HD]
            total = total + jnp.dot(
                weights.astype(jnp.bfloat16), held[s, :, HD:], preferred_element_type=jnp.float32
            )
            return total, weight_sum

        zero = jnp.zeros((heads * BLK, HD), jnp.float32)
        total, weight_sum = lax.fori_loop(start // rows, last + 1, step, (zero, zero))
        done = (total / jnp.sum(weight_sum, axis=1, keepdims=True)).astype(jnp.bfloat16)
        for h in range(heads):
            out_ref[span, h * HD : (h + 1) * HD] = done[h * BLK : (h + 1) * BLK]


def attend(info, q, kvs):
    rows = q.shape[0]
    parts = len(kvs)
    return pl.pallas_call(
        functools.partial(attend_kernel, parts, rows),
        grid_spec=pltpu.PrefetchScalarGridSpec(
            num_scalar_prefetch=1,
            grid=(1,),
            in_specs=[pl.BlockSpec(q.shape, lambda i, s: (0, 0))]
            + [pl.BlockSpec(memory_space=pl.ANY)] * parts,
            out_specs=pl.BlockSpec(q.shape, lambda i, s: (0, 0)),
            scratch_shapes=[
                pltpu.VMEM((parts, rows, 2 * HD), jnp.bfloat16),
                pltpu.SemaphoreType.DMA((parts,)),
            ],
        ),
        out_shape=jax.ShapeDtypeStruct(q.shape, jnp.bfloat16),
        compiler_params=pltpu.CompilerParams(vmem_limit_bytes=32 * 2**20),
        cost_estimate=pl.CostEstimate(
            flops=2 * 10**9, bytes_accessed=4 * 10**6, transcendentals=8 * 10**6
        ),
        name="attend",
    )(info, q, *kvs)


def out_kernel(parts, *refs):
    total = jnp.dot(refs[0][...], refs[parts][...], preferred_element_type=jnp.float32)
    for i in range(1, parts):
        total = total + jnp.dot(
            refs[i][...], refs[parts + i][...], preferred_element_type=jnp.float32
        )
    refs[2 * parts][...] = total
    refs[2 * parts + 1][...] = jnp.sum(total * total, axis=1, keepdims=True)


def out_project(heads, weights):
    rows, inner = heads[0].shape
    cols = weights[0].shape[1]
    parts = len(heads)
    tile = 256
    return pl.pallas_call(
        functools.partial(out_kernel, parts),
        grid=(rows // tile,),
        in_specs=[pl.BlockSpec((tile, inner), lambda i: (i, 0))] * parts
        + [pl.BlockSpec((inner, cols), lambda i: (0, 0), pipeline_mode=pl.Buffered(1))] * parts,
        out_specs=[
            pl.BlockSpec((tile, cols), lambda i: (i, 0)),
            pl.BlockSpec((tile, 1), lambda i: (i, 0)),
        ],
        out_shape=[
            jax.ShapeDtypeStruct((rows, cols), jnp.float32),
            jax.ShapeDtypeStruct((rows, 1), jnp.float32),
        ],
        compiler_params=pltpu.CompilerParams(vmem_limit_bytes=32 * 2**20),
        cost_estimate=pl.CostEstimate(
            flops=2 * rows * inner * parts * cols, bytes_accessed=6 * 10**6, transcendentals=0
        ),
        name="out_project",
    )(*heads, *weights)


def local(n_ctx, n_tp, tokens, norm_gain, q_weight, k_weight, v_weight, o_weight, post_gain, doc_ids, plan):
    rows, features = tokens.shape
    blocks = rows // BLK
    total_blocks = doc_ids.shape[0]
    shard = lax.axis_index("ctx")
    group = lax.axis_index("tp")
    planes = n_ctx // PLANE
    cols = o_weight.shape[1] // n_tp

    def ctx_xor(a, m):
        return lax.ppermute(a, "ctx", [(i, i ^ m) for i in range(n_ctx)])

    def ctx_z(a, d):
        return lax.ppermute(a, "ctx", [(i, (i + d * PLANE) % n_ctx) for i in range(n_ctx)])

    def tp_xor(a, m):
        return lax.ppermute(a, "tp", [(i, i ^ m) for i in range(n_tp)])

    out_weights = [
        lax.dynamic_slice_in_dim(o_weight, (group ^ m) * cols, cols, axis=1) for m in range(n_tp)
    ]
    out_weights = [w if m == 0 else tp_xor(w, m) for m, w in enumerate(out_weights)]

    queries, own_kv = project(tokens, norm_gain.reshape(1, -1), q_weight, k_weight, v_weight)

    kvs = []
    for back in range(BACK, -1, -1):
        near = own_kv if back == 0 else ctx_z(own_kv, back)
        across = ctx_xor(near, 2)
        kvs += [near, ctx_xor(near, 1), across, ctx_xor(across, 1)]

    first_block = jnp.sum(
        (doc_ids[None, :] < doc_ids[:, None]).astype(jnp.int32), axis=1
    )
    own_first = lax.dynamic_slice_in_dim(first_block, shard * blocks, blocks, 0)
    plane_first = (shard // PLANE - BACK) * PLANE * blocks
    info = jnp.concatenate(
        [(shard % PLANE).reshape(1), (own_first - plane_first) * BLK]
    ).astype(jnp.int32)
    natural = attend(info, queries, kvs)

    width = natural.shape[1]
    piece = BLK // n_ctx
    same = (plan[None, :] == plan[:, None]).astype(jnp.int32)
    block_ids = jnp.arange(total_blocks, dtype=jnp.int32)
    rank = jnp.sum(same * (block_ids[None, :] < block_ids[:, None]), axis=1)
    target = plan * blocks + rank
    picker = (target[None, :] == block_ids[:, None]).astype(jnp.bfloat16)
    striped = natural.reshape(blocks, n_ctx, piece, width).transpose(1, 0, 2, 3)
    striped = striped.reshape(n_ctx, blocks, piece * width)
    gathered = lax.all_to_all(striped, "ctx", 0, 0, tiled=True)
    ordered = jnp.dot(
        picker,
        gathered.reshape(total_blocks, piece * width),
        preferred_element_type=jnp.float32,
    ).astype(jnp.bfloat16)
    placed = lax.all_to_all(
        ordered.reshape(n_ctx, blocks, piece * width), "ctx", 0, 0, tiled=True
    )
    placed = (
        placed.reshape(n_ctx, blocks, piece, width).transpose(1, 0, 2, 3).reshape(rows, width)
    )

    heads = [placed if m == 0 else tp_xor(placed, m) for m in range(n_tp)]
    summed, squares = out_project(heads, out_weights)
    squares = squares.reshape(rows)
    m = 1
    while m < n_tp:
        squares = squares + tp_xor(squares, m)
        m *= 2
    scale = lax.rsqrt(squares / features + norm_eps)
    return (summed * scale[:, None] * post_gain).astype(jnp.bfloat16)


def solution(mesh):
    placed = (
        P("ctx", None),
        P(),
        P(None, "tp"),
        P(None, "tp"),
        P(None, "tp"),
        P("tp", None),
        P("tp"),
        P(),
        P(),
    )
    return jax.shard_map(
        functools.partial(local, mesh.shape["ctx"], mesh.shape["tp"]),
        mesh=mesh,
        in_specs=placed,
        out_specs=P("ctx", "tp"),
        check_vma=False,
    )
```

time: 517 us -> 175 us (0.34)
  waiting for transfers between devices: 285 us -> 79 us
  matrix products: 125 us -> 0.22 us
  starting transfers between devices: 0.31 us -> 63 us
  other arithmetic: 24 us -> 1.79 us
  blocking collectives: 22.1 us -> 0 us
  loops' own time: 20.8 us -> 0 us
  between operations: 13.3 us -> 0.29 us
  Pallas kernels: 0 us -> 11 us
  local copies, waits for them, and re-layouts: 24.8 us -> 18.8 us
    all_gather x3 -> x0, waiting for transfers between devices: 193 us -> none  [the longest x1 68.4 us: local(): key_piece = lax.all_gather(key_rows, 'ctx', axis=0, tiled=True)]
    dot_general x69 -> x1, matrix products: 125 us -> 0.22 us  [local(): jnp.dot(picker, gathered.reshape(total_blocks, piece * width), preferred_...]
    reduce_scatter x1 -> x0, waiting for transfers between devices: 92.6 us -> none  [local(): lax.psum_scatter(partial_value, 'tp', scatter_dimension=1, tiled=True)]
    ppermute x0 -> x28, waiting for transfers between devices: none -> 67.2 us  [the longest x17 46.8 us: tp_xor(): return lax.ppermute(a, 'tp', [(i, i ^ m) for i in range(n_tp)])]
    ppermute x0 -> x28, starting transfers between devices: none -> 39 us  [the longest x17 31.1 us: tp_xor(): return lax.ppermute(a, 'tp', [(i, i ^ m) for i in range(n_tp)])]
    all_to_all x0 -> x2, starting transfers between devices: none -> 24 us  [the longest x1 20.1 us: local(): gathered = lax.all_to_all(striped, 'ctx', 0, 0, tiled=True)]
    psum x1 -> x0, blocking collectives: 22.1 us -> none  [local(): lax.psum(jnp.sum(own_cols * own_cols, axis=1, keepdims=True), 'tp')]
    another operation x1 -> x0, loops' own time: 20.8 us -> none  [local(): lax.scan(one_step, initial, (key_steps, value_steps, jnp.arange(step_coun...]
  transfers between devices with their start and end apart: 4 -> 30, of which waited for: 4 -> 17; matrix products, arithmetic and copies ran while one was open for 4% -> 2% of each run, Pallas kernels for 0% -> 0%
where the time goes in v1:
time: 175 us; the launch traced here: 174 us
  waiting for transfers between devices  79 us (45%)
  starting transfers between devices  63 us (36%)
  local copies, waits for them, and re-layouts  18.8 us (11%)
  Pallas kernels  11 us (6%)
  other arithmetic  1.79 us (1%)
    ppermute x17, waiting for transfers between devices, tp_xor(): return lax.ppermute(a, 'tp', [(i, i ^ m) for i in range(n_tp)])  46.8 us
    ppermute x17, starting transfers between devices, tp_xor(): return lax.ppermute(a, 'tp', [(i, i ^ m) for i in range(n_tp)])  31.1 us
    all_to_all x1, starting transfers between devices, local(): gathered = lax.all_to_all(striped, 'ctx', 0, 0, tiled=True)  20.1 us
    ppermute x2, waiting for transfers between devices, ctx_z(): lax.ppermute(a, 'ctx', [(i, (i + d * PLANE) % n_ctx) for i in range(n_ctx)])  13.8 us
    unnamed x30, local copies, waits for them, and re-layouts  12.3 us
    all_to_all x1, waiting for transfers between devices, local(): gathered = lax.all_to_all(striped, 'ctx', 0, 0, tiled=True)  11.9 us
    ppermute x9, waiting for transfers between devices, ctx_xor(): return lax.ppermute(a, 'ctx', [(i, i ^ m) for i in range(n_ctx)])  6.63 us
    pallas_call x1, Pallas kernels, project(): pl.pallas_call(qkv_kernel, grid=(rows // tile,), in_specs=[pl.BlockSpec((...  5.57 us
  transfers between devices with their start and end apart: 30, of which 17 were waited for; matrix products, arithmetic and copies ran while one was open for 2% of the time, Pallas kernels for 0%

profile of v1, /device:TPU:2, one launch (start us, length us, event | category | flops | bytes accessed | tf_op | source)
XLA Modules:
  0.0 174.0 jit_solution(2093714750381402517)
XLA Ops:
  0.8 2.3 %copy-done = bf16[512,4608]{1,0:T(8,128)(2,1)S(1)} copy-done((bf16[512,4608]{1,0:T(8,128)(2,1)S(1)}, bf16[512,4608]{1,0:T(8,128)(2,1)}, u32[]{:S(2)}) %copy-start) | copy-done | bytes 4718616
  7.3 5.6 %project.1 = (bf16[512,256]{1,0:T(8,128)(2,1)S(1)}, bf16[512,256]{1,0:T(8,128)(2,1)S(1)}) custom-call(bf16[512,4608]{1,0:T(8,128)(2,1)S(1)} %copy-done, f32[1,4608]{1,0:T(1,128)S(1)} %reshape.35.g_ref, bf16[4608,256]{1,0:T(8,128)(2,1)S(1)} %copy-done.1, bf16[4608,128]{1,0:T(8,128)(2,1)S(1)} %copy-done.2, bf16[4608,128]{1,0:T(8,128)(2,1)S(1)} %copy-done.3), custom_call_target="tpu_custom_call" | custom-call | flops 2415919104 | bytes 9437184 | tf_op jit(solution)/shard_map/project/pallas_call | solution.py:44
  14.9 3.3 %collective-permute-start = (bf16[512,256]{1,0:T(8,128)(2,1)S(1)}, bf16[512,256]{1,0:T(8,128)(2,1)S(1)}, u32[]{:S(2)}, u32[]{:S(2)}) collective-permute-start(bf16[512,256]{1,0:T(8,128)(2,1)S(1)} %get-tuple-element.10.refs_8_), channel_id=1, source_target_pairs={{0,64},{8,72},{16,80},{24,88},{32,96},{40,104},{48,112},{56,120},{... | collective-permute-start | bytes 786440 | tf_op jit(solution)/shard_map/ppermute | solution.py:190
  18.7 7.7 %collective-permute-done.4.refs_4_ = bf16[512,256]{1,0:T(8,128)(2,1)S(1)} collective-permute-done((bf16[512,256]{1,0:T(8,128)(2,1)S(1)}, bf16[512,256]{1,0:T(8,128)(2,1)S(1)}, u32[]{:S(2)}, u32[]{:S(2)}) %collective-permute-start.4) | collective-permute-done | bytes 262176 | tf_op jit(solution)/shard_map/ppermute | solution.py:190
  27.0 6.0 %collective-permute-done.refs_0_ = bf16[512,256]{1,0:T(8,128)(2,1)S(1)} collective-permute-done((bf16[512,256]{1,0:T(8,128)(2,1)S(1)}, bf16[512,256]{1,0:T(8,128)(2,1)S(1)}, u32[]{:S(2)}, u32[]{:S(2)}) %collective-permute-start) | collective-permute-done | bytes 262176 | tf_op jit(solution)/shard_map/ppermute | solution.py:190
  34.5 5.5 %collective-permute-done.2.refs_2_ = bf16[512,256]{1,0:T(8,128)(2,1)S(1)} collective-permute-done((bf16[512,256]{1,0:T(8,128)(2,1)S(1)}, bf16[512,256]{1,0:T(8,128)(2,1)S(1)}, u32[]{:S(2)}, u32[]{:S(2)}) %collective-permute-start.2) | collective-permute-done | bytes 262176 | tf_op jit(solution)/shard_map/ppermute | solution.py:187
  43.2 3.3 %attend.1 = bf16[512,256]{1,0:T(8,128)(2,1)S(1)} custom-call(s32[5]{0:T(128)S(1)} %pad_add_fusion.info_ref, bf16[512,256]{1,0:T(8,128)(2,1)S(1)} %get-tuple-element.9.q_ref, bf16[512,256]{1,0:T(8,128)(2,1)S(1)} %collective-permute-done.refs_0_, bf16[512,256]{1,0:T(8,128)(2,1)S(1)} %collective-permute-done.1.refs_1_, ...), custom_call_target="tpu_custom_call" | custom-call | flops 2000000000 | bytes 4000000 | tf_op jit(solution)/shard_map/attend/pallas_call | solution.py:119
  47.6 20.1 %all-to-all-start = ((bf16[32,4,1024]{2,1,0:T(4,128)(2,1)}), bf16[32,4,1024]{2,1,0:T(4,128)(2,1)S(1)}, u32[]{:S(2)}, u32[]{:S(2)}) async-start(bf16[32,4,1024]{2,1,0:T(4,128)(2,1)} %copy.18), calls=%async_computation | async-start | bytes 524288 | tf_op jit(solution)/shard_map/all_to_all | solution.py:227
  67.9 11.9 %all-to-all-done = bf16[32,4,1024]{2,1,0:T(4,128)(2,1)S(1)} async-done(((bf16[32,4,1024]{2,1,0:T(4,128)(2,1)}), bf16[32,4,1024]{2,1,0:T(4,128)(2,1)S(1)}, u32[]{:S(2)}, u32[]{:S(2)}) %all-to-all-start) | async-done | bytes 262176 | tf_op jit(solution)/shard_map/all_to_all | solution.py:227
  80.9 3.9 %all-to-all-start.1 = ((bf16[32,4,1024]{2,1,0:T(4,128)(2,1)}), bf16[32,4,1024]{2,1,0:T(4,128)(2,1)S(1)}, u32[]{:S(2)}, u32[]{:S(2)}) async-start(bf16[32,4,1024]{2,1,0:T(4,128)(2,1)} %reshape.39), calls=%async_computation.1 | async-start | bytes 524288 | tf_op jit(solution)/shard_map/all_to_all | solution.py:233
  84.8 2.4 %constant_dynamic-slice_fusion = (bf16[256,576]{1,0:T(8,128)(2,1)S(1)}, bf16[256,576]{1,0:T(8,128)(2,1)S(1)}, bf16[256,576]{1,0:T(8,128)(2,1)}, bf16[256,576]{1,...) fusion(bf16[256,4608]{1,0:T(8,128)(2,1)S(1)} %copy-done.11, ...), kind=kLoop, calls=%fused_computation.9 | loop fusion | bytes 4718624 | tf_op jit(solution)/shard_map/dynamic_slice | solution.py:196
  87.2 4.6 %collective-permute-start.24 = (bf16[256,576]{1,0:T(8,128)(2,1)S(1)}, bf16[256,576]{1,0:T(8,128)(2,1)S(1)}, u32[]{:S(2)}, u32[]{:S(2)}) collective-permute-start(bf16[256,576]{1,0:T(8,128)(2,1)S(1)} %get-tuple-element.13), channel_id=1, source_target_pairs={{0,7},{1,6},{2,5},{3,4},{4,3},{5,2},{6,1},{7,0},{8,15},{9,14},{10,... | collective-permute-start | bytes 884744 | tf_op jit(solution)/shard_map/ppermute | solution.py:193
  92.8 2.1 %collective-permute-start.21 = (bf16[256,576]{1,0:T(8,128)(2,1)}, bf16[256,576]{1,0:T(8,128)(2,1)S(1)}, u32[]{:S(2)}, u32[]{:S(2)}) collective-permute-start(bf16[256,576]{1,0:T(8,128)(2,1)} %get-tuple-element.15), channel_id=1, source_target_pairs={{0,4},{1,5},{2,6},{3,7},{4,0},{5,1},{6,2},{7,3},{8,12},{9,13},{10,... | collective-permute-start | bytes 884744 | tf_op jit(solution)/shard_map/ppermute | solution.py:193
  96.0 2.9 %collective-permute-start.19 = (bf16[256,576]{1,0:T(8,128)(2,1)}, bf16[256,576]{1,0:T(8,128)(2,1)S(1)}, u32[]{:S(2)}, u32[]{:S(2)}) collective-permute-start(bf16[256,576]{1,0:T(8,128)(2,1)} %get-tuple-element.17), channel_id=1, source_target_pairs={{0,2},{1,3},{2,0},{3,1},{4,6},{5,7},{6,4},{7,5},{8,10},{9,11},{10,... | collective-permute-start | bytes 884744 | tf_op jit(solution)/shard_map/ppermute | solution.py:193
  98.9 6.7 %collective-permute-done.24.refs_15_ = bf16[256,576]{1,0:T(8,128)(2,1)S(1)} collective-permute-done((bf16[256,576]{1,0:T(8,128)(2,1)S(1)}, bf16[256,576]{1,0:T(8,128)(2,1)S(1)}, u32[]{:S(2)}, u32[]{:S(2)}) %collective-permute-start.24) | collective-permute-done | bytes 294944 | tf_op jit(solution)/shard_map/ppermute | solution.py:193
  105.6 4.2 %collective-permute-done.22.refs_13_ = bf16[256,576]{1,0:T(8,128)(2,1)S(1)} collective-permute-done((bf16[256,576]{1,0:T(8,128)(2,1)S(1)}, bf16[256,576]{1,0:T(8,128)(2,1)S(1)}, u32[]{:S(2)}, u32[]{:S(2)}) %collective-permute-start.22) | collective-permute-done | bytes 294944 | tf_op jit(solution)/shard_map/ppermute | solution.py:193
  109.8 4.0 %collective-permute-start.23 = (bf16[256,576]{1,0:T(8,128)(2,1)S(1)}, bf16[256,576]{1,0:T(8,128)(2,1)S(1)}, u32[]{:S(2)}, u32[]{:S(2)}) collective-permute-start(bf16[256,576]{1,0:T(8,128)(2,1)S(1)} %get-tuple-element.20), channel_id=1, source_target_pairs={{0,6},{1,7},{2,4},{3,5},{4,2},{5,3},{6,0},{7,1},{8,14},{9,15},{10,... | collective-permute-start | bytes 884744 | tf_op jit(solution)/shard_map/ppermute | solution.py:193
  114.1 3.3 %collective-permute-done.21.refs_12_ = bf16[256,576]{1,0:T(8,128)(2,1)S(1)} collective-permute-done((bf16[256,576]{1,0:T(8,128)(2,1)}, bf16[256,576]{1,0:T(8,128)(2,1)S(1)}, u32[]{:S(2)}, u32[]{:S(2)}) %collective-permute-start.21) | collective-permute-done | bytes 294944 | tf_op jit(solution)/shard_map/ppermute | solution.py:193
  117.4 2.5 %collective-permute-start.17 = (bf16[512,256]{1,0:T(8,128)(2,1)S(1)}, bf16[512,256]{1,0:T(8,128)(2,1)S(1)}, u32[]{:S(2)}, u32[]{:S(2)}) collective-permute-start(bf16[512,256]{1,0:T(8,128)(2,1)S(1)} %reshape.41.refs_0_), channel_id=1, source_target_pairs={{0,7},{1,6},{2,5},{3,4},{4,3},{5,2},{6,1},{7,0},{8,15},{9,14},{10,... | collective-permute-start | bytes 786440 | tf_op jit(solution)/shard_map/ppermute | solution.py:193
  121.8 2.1 %collective-permute-start.15 = (bf16[512,256]{1,0:T(8,128)(2,1)S(1)}, bf16[512,256]{1,0:T(8,128)(2,1)S(1)}, u32[]{:S(2)}, u32[]{:S(2)}) collective-permute-start(bf16[512,256]{1,0:T(8,128)(2,1)S(1)} %reshape.41.refs_0_), channel_id=1, source_target_pairs={{0,5},{1,4},{2,7},{3,6},{4,1},{5,0},{6,3},{7,2},{8,13},{9,12},{10,... | collective-permute-start | bytes 786440 | tf_op jit(solution)/shard_map/ppermute | solution.py:193
  123.9 4.2 %collective-permute-done.18.refs_9_ = bf16[256,576]{1,0:T(8,128)(2,1)S(1)} collective-permute-done((bf16[256,576]{1,0:T(8,128)(2,1)}, bf16[256,576]{1,0:T(8,128)(2,1)S(1)}, u32[]{:S(2)}, u32[]{:S(2)}) %collective-permute-start.18) | collective-permute-done | bytes 294944 | tf_op jit(solution)/shard_map/ppermute | solution.py:193
  132.6 2.3 %collective-permute-start.12 = (bf16[512,256]{1,0:T(8,128)(2,1)S(1)}, bf16[512,256]{1,0:T(8,128)(2,1)S(1)}, u32[]{:S(2)}, u32[]{:S(2)}) collective-permute-start(bf16[512,256]{1,0:T(8,128)(2,1)S(1)} %reshape.41.refs_0_), channel_id=1, source_target_pairs={{0,2},{1,3},{2,0},{3,1},{4,6},{5,7},{6,4},{7,5},{8,10},{9,11},{10,... | collective-permute-start | bytes 786440 | tf_op jit(solution)/shard_map/ppermute | solution.py:193
  134.9 3.3 %collective-permute-done.16.refs_6_ = bf16[512,256]{1,0:T(8,128)(2,1)S(1)} collective-permute-done((bf16[512,256]{1,0:T(8,128)(2,1)S(1)}, bf16[512,256]{1,0:T(8,128)(2,1)S(1)}, u32[]{:S(2)}, u32[]{:S(2)}) %collective-permute-start.16) | collective-permute-done | bytes 262176 | tf_op jit(solution)/shard_map/ppermute | solution.py:193
  138.2 4.2 %collective-permute-done.15.refs_5_ = bf16[512,256]{1,0:T(8,128)(2,1)S(1)} collective-permute-done((bf16[512,256]{1,0:T(8,128)(2,1)S(1)}, bf16[512,256]{1,0:T(8,128)(2,1)S(1)}, u32[]{:S(2)}, u32[]{:S(2)}) %collective-permute-start.15) | collective-permute-done | bytes 262176 | tf_op jit(solution)/shard_map/ppermute | solution.py:193
  142.4 4.2 %collective-permute-done.14.refs_4_ = bf16[512,256]{1,0:T(8,128)(2,1)S(1)} collective-permute-done((bf16[512,256]{1,0:T(8,128)(2,1)S(1)}, bf16[512,256]{1,0:T(8,128)(2,1)S(1)}, u32[]{:S(2)}, u32[]{:S(2)}) %collective-permute-start.14) | collective-permute-done | bytes 262176 | tf_op jit(solution)/shard_map/ppermute | solution.py:193
  146.7 2.3 %collective-permute-done.12.refs_2_ = bf16[512,256]{1,0:T(8,128)(2,1)S(1)} collective-permute-done((bf16[512,256]{1,0:T(8,128)(2,1)S(1)}, bf16[512,256]{1,0:T(8,128)(2,1)S(1)}, u32[]{:S(2)}, u32[]{:S(2)}) %collective-permute-start.12) | collective-permute-done | bytes 262176 | tf_op jit(solution)/shard_map/ppermute | solution.py:193
  149.0 4.1 %collective-permute-done.11.refs_1_ = bf16[512,256]{1,0:T(8,128)(2,1)S(1)} collective-permute-done((bf16[512,256]{1,0:T(8,128)(2,1)S(1)}, bf16[512,256]{1,0:T(8,128)(2,1)S(1)}, u32[]{:S(2)}, u32[]{:S(2)}) %collective-permute-start.11) | collective-permute-done | bytes 262176 | tf_op jit(solution)/shard_map/ppermute | solution.py:193
  155.0 2.1 %out_project.1 = (f32[512,576]{1,0:T(8,128)S(1)}, f32[512,1]{1,0:T(8,128)S(1)}) custom-call(bf16[512,256]{1,0:T(8,128)(2,1)S(1)} %reshape.41.refs_0_, bf16[512,256]{1,0:T(8,128)(2,1)S(1)} %collective-permute-done.11.refs_1_, bf16[512,256]{1,0:T(8,128)(2,1)S(1)} %collective-permute-done.12.refs_2_, bf16[512,256]{1,0:T(8,128)(2,1)S(1)} %collective-permute-done.13.refs_3_, ...), custom_call_target="tpu_custom_call" | custom-call | flops 1207959552 | bytes 6000000 | tf_op jit(solution)/shard_map/out_project/pallas_call | solution.py:156
  159.7 2.9 %collective-permute-done.25 = f32[512]{0:T(512)S(1)} collective-permute-done((f32[512]{0:T(512)S(1)}, f32[512]{0:T(512)S(1)}, u32[]{:S(2)}, u32[]{:S(2)}) %collective-permute-start.25) | collective-permute-done | bytes 2080 | tf_op jit(solution)/shard_map/ppermute | solution.py:193
  162.6 2.1 %collective-permute-start.26 = (f32[512]{0:T(512)S(1)}, f32[512]{0:T(512)S(1)}, u32[]{:S(2)}, u32[]{:S(2)}) collective-permute-start(f32[512]{0:T(512)S(1)} %add.62), channel_id=1, source_target_pairs={{0,2},{1,3},{2,0},{3,1},{4,6},{5,7},{6,4},{7,5},{8,10},{9,11},{10,... | collective-permute-start | bytes 6152 | tf_op jit(solution)/shard_map/ppermute | solution.py:193
  164.7 3.0 %collective-permute-done.26 = f32[512]{0:T(512)S(1)} collective-permute-done((f32[512]{0:T(512)S(1)}, f32[512]{0:T(512)S(1)}, u32[]{:S(2)}, u32[]{:S(2)}) %collective-permute-start.26) | collective-permute-done | bytes 2080 | tf_op jit(solution)/shard_map/ppermute | solution.py:193
  168.4 4.4 %collective-permute-done.27 = f32[512]{0:T(512)S(1)} collective-permute-done((f32[512]{0:T(512)S(1)}, f32[512]{0:T(512)S(1)}, u32[]{:S(2)}, u32[]{:S(2)}) %collective-permute-start.27) | collective-permute-done | bytes 2080 | tf_op jit(solution)/shard_map/ppermute | solution.py:193
  (83 shorter events, 30.3 us)
Async XLA Ops:
  7.3 32.7 %copy-start.13 = (s32[128]{0:T(128)S(1)}, s32[128]{0:T(128)}, u32[]{:S(2)}) copy-start(s32[128]{0:T(128)} %param.16) | copy-start | bytes 1540
  12.9 13.5 %collective-permute-start.4 = (bf16[512,256]{1,0:T(8,128)(2,1)S(1)}, bf16[512,256]{1,0:T(8,128)(2,1)S(1)}, u32[]{:S(2)}, u32[]{:S(2)}) collective-permute-start(bf16[512,256]{1,0:T(8,128)(2,1)S(1)} %get-tuple-element.10.refs_8_), channel_id=1, source_target_pairs={{0,32},{8,40},{16,48},{24,56},{32,64},{40,72},{48,80},{56,88},{64,... | collective-permute-start | bytes 786440 | tf_op jit(solution)/shard_map/ppermute | solution.py:190
  14.9 18.1 %collective-permute-start = (bf16[512,256]{1,0:T(8,128)(2,1)S(1)}, bf16[512,256]{1,0:T(8,128)(2,1)S(1)}, u32[]{:S(2)}, u32[]{:S(2)}) collective-permute-start(bf16[512,256]{1,0:T(8,128)(2,1)S(1)} %get-tuple-element.10.refs_8_), channel_id=1, source_target_pairs={{0,64},{8,72},{16,80},{24,88},{32,96},{40,104},{48,112},{56,120},{... | collective-permute-start | bytes 786440 | tf_op jit(solution)/shard_map/ppermute | solution.py:190
  18.1 15.4 %collective-permute-start.9 = (bf16[512,256]{1,0:T(8,128)(2,1)S(1)}, bf16[512,256]{1,0:T(8,128)(2,1)S(1)}, u32[]{:S(2)}, u32[]{:S(2)}) collective-permute-start(bf16[512,256]{1,0:T(8,128)(2,1)S(1)} %get-tuple-element.10.refs_8_), channel_id=1, source_target_pairs={{0,16},{8,24},{16,0},{24,8},{32,48},{40,56},{48,32},{56,40},{64,80... | collective-permute-start | bytes 786440 | tf_op jit(solution)/shard_map/ppermute | solution.py:187
  18.7 15.4 %collective-permute-start.8 = (bf16[512,256]{1,0:T(8,128)(2,1)S(1)}, bf16[512,256]{1,0:T(8,128)(2,1)S(1)}, u32[]{:S(2)}, u32[]{:S(2)}) collective-permute-start(bf16[512,256]{1,0:T(8,128)(2,1)S(1)} %get-tuple-element.10.refs_8_), channel_id=1, source_target_pairs={{0,8},{8,0},{16,24},{24,16},{32,40},{40,32},{48,56},{56,48},{64,72... | collective-permute-start | bytes 786440 | tf_op jit(solution)/shard_map/ppermute | solution.py:187
  26.4 7.7 %collective-permute-start.6 = (bf16[512,256]{1,0:T(8,128)(2,1)S(1)}, bf16[512,256]{1,0:T(8,128)(2,1)S(1)}, u32[]{:S(2)}, u32[]{:S(2)}) collective-permute-start(bf16[512,256]{1,0:T(8,128)(2,1)S(1)} %collective-permute-done.4.refs_4_), channel_id=1, source_target_pairs={{0,16},{8,24},{16,0},{24,8},{32,48},{40,56},{48,32},{56,40},{64,80... | collective-permute-start | bytes 786440 | tf_op jit(solution)/shard_map/ppermute | solution.py:187
  33.0 7.0 %collective-permute-start.2 = (bf16[512,256]{1,0:T(8,128)(2,1)S(1)}, bf16[512,256]{1,0:T(8,128)(2,1)S(1)}, u32[]{:S(2)}, u32[]{:S(2)}) collective-permute-start(bf16[512,256]{1,0:T(8,128)(2,1)S(1)} %collective-permute-done.refs_0_), channel_id=1, source_target_pairs={{0,16},{8,24},{16,0},{24,8},{32,48},{40,56},{48,32},{56,40},{64,80... | collective-permute-start | bytes 786440 | tf_op jit(solution)/shard_map/ppermute | solution.py:187
  33.5 6.9 %collective-permute-start.5 = (bf16[512,256]{1,0:T(8,128)(2,1)S(1)}, bf16[512,256]{1,0:T(8,128)(2,1)S(1)}, u32[]{:S(2)}, u32[]{:S(2)}) collective-permute-start(bf16[512,256]{1,0:T(8,128)(2,1)S(1)} %collective-permute-done.4.refs_4_), channel_id=1, source_target_pairs={{0,8},{8,0},{16,24},{24,16},{32,40},{40,32},{48,56},{56,48},{64,72... | collective-permute-start | bytes 786440 | tf_op jit(solution)/shard_map/ppermute | solution.py:187
  33.5 6.9 %collective-permute-start.1 = (bf16[512,256]{1,0:T(8,128)(2,1)S(1)}, bf16[512,256]{1,0:T(8,128)(2,1)S(1)}, u32[]{:S(2)}, u32[]{:S(2)}) collective-permute-start(bf16[512,256]{1,0:T(8,128)(2,1)S(1)} %collective-permute-done.refs_0_), channel_id=1, source_target_pairs={{0,8},{8,0},{16,24},{24,16},{32,40},{40,32},{48,56},{56,48},{64,72... | collective-permute-start | bytes 786440 | tf_op jit(solution)/shard_map/ppermute | solution.py:187
  34.0 6.3 %collective-permute-start.10 = (bf16[512,256]{1,0:T(8,128)(2,1)S(1)}, bf16[512,256]{1,0:T(8,128)(2,1)S(1)}, u32[]{:S(2)}, u32[]{:S(2)}) collective-permute-start(bf16[512,256]{1,0:T(8,128)(2,1)S(1)} %collective-permute-done.9.refs_10_), channel_id=1, source_target_pairs={{0,8},{8,0},{16,24},{24,16},{32,40},{40,32},{48,56},{56,48},{64,72... | collective-permute-start | bytes 786440 | tf_op jit(solution)/shard_map/ppermute | solution.py:187
  34.1 6.3 %collective-permute-start.7 = (bf16[512,256]{1,0:T(8,128)(2,1)S(1)}, bf16[512,256]{1,0:T(8,128)(2,1)S(1)}, u32[]{:S(2)}, u32[]{:S(2)}) collective-permute-start(bf16[512,256]{1,0:T(8,128)(2,1)S(1)} %collective-permute-done.6.refs_6_), channel_id=1, source_target_pairs={{0,8},{8,0},{16,24},{24,16},{32,40},{40,32},{48,56},{56,48},{64,72... | collective-permute-start | bytes 786440 | tf_op jit(solution)/shard_map/ppermute | solution.py:187
  40.0 1.5 collective-permute-start.3
  47.6 37.2 %copy-start.11 = (bf16[256,4608]{1,0:T(8,128)(2,1)S(1)}, bf16[256,4608]{1,0:T(8,128)(2,1)}, u32[]{:S(2)}) copy-start(bf16[256,4608]{1,0:T(8,128)(2,1)} %param.14) | copy-start | bytes 7077892
  47.6 32.2 %all-to-all-start = ((bf16[32,4,1024]{2,1,0:T(4,128)(2,1)}), bf16[32,4,1024]{2,1,0:T(4,128)(2,1)S(1)}, u32[]{:S(2)}, u32[]{:S(2)}) async-start(bf16[32,4,1024]{2,1,0:T(4,128)(2,1)} %copy.18), calls=%async_computation | async-start | bytes 524288 | tf_op jit(solution)/shard_map/all_to_all | solution.py:227
  80.9 32.9 %all-to-all-start.1 = ((bf16[32,4,1024]{2,1,0:T(4,128)(2,1)}), bf16[32,4,1024]{2,1,0:T(4,128)(2,1)S(1)}, u32[]{:S(2)}, u32[]{:S(2)}) async-start(bf16[32,4,1024]{2,1,0:T(4,128)(2,1)} %reshape.39), calls=%async_computation.1 | async-start | bytes 524288 | tf_op jit(solution)/shard_map/all_to_all | solution.py:233
  87.2 18.4 %collective-permute-start.24 = (bf16[256,576]{1,0:T(8,128)(2,1)S(1)}, bf16[256,576]{1,0:T(8,128)(2,1)S(1)}, u32[]{:S(2)}, u32[]{:S(2)}) collective-permute-start(bf16[256,576]{1,0:T(8,128)(2,1)S(1)} %get-tuple-element.13), channel_id=1, source_target_pairs={{0,7},{1,6},{2,5},{3,4},{4,3},{5,2},{6,1},{7,0},{8,15},{9,14},{10,... | collective-permute-start | bytes 884744 | tf_op jit(solution)/shard_map/ppermute | solution.py:193
  91.8 17.9 %collective-permute-start.22 = (bf16[256,576]{1,0:T(8,128)(2,1)S(1)}, bf16[256,576]{1,0:T(8,128)(2,1)S(1)}, u32[]{:S(2)}, u32[]{:S(2)}) collective-permute-start(bf16[256,576]{1,0:T(8,128)(2,1)S(1)} %get-tuple-element.14), channel_id=1, source_target_pairs={{0,5},{1,4},{2,7},{3,6},{4,1},{5,0},{6,3},{7,2},{8,13},{9,12},{10,... | collective-permute-start | bytes 884744 | tf_op jit(solution)/shard_map/ppermute | solution.py:193
  92.8 24.6 %collective-permute-start.21 = (bf16[256,576]{1,0:T(8,128)(2,1)}, bf16[256,576]{1,0:T(8,128)(2,1)S(1)}, u32[]{:S(2)}, u32[]{:S(2)}) collective-permute-start(bf16[256,576]{1,0:T(8,128)(2,1)} %get-tuple-element.15), channel_id=1, source_target_pairs={{0,4},{1,5},{2,6},{3,7},{4,0},{5,1},{6,2},{7,3},{8,12},{9,13},{10,... | collective-permute-start | bytes 884744 | tf_op jit(solution)/shard_map/ppermute | solution.py:193
  94.9 25.0 %collective-permute-start.20 = (bf16[256,576]{1,0:T(8,128)(2,1)}, bf16[256,576]{1,0:T(8,128)(2,1)S(1)}, u32[]{:S(2)}, u32[]{:S(2)}) collective-permute-start(bf16[256,576]{1,0:T(8,128)(2,1)} %get-tuple-element.16), channel_id=1, source_target_pairs={{0,3},{1,2},{2,1},{3,0},{4,7},{5,6},{6,5},{7,4},{8,11},{9,10},{10,... | collective-permute-start | bytes 884744 | tf_op jit(solution)/shard_map/ppermute | solution.py:193
  96.0 25.8 %collective-permute-start.19 = (bf16[256,576]{1,0:T(8,128)(2,1)}, bf16[256,576]{1,0:T(8,128)(2,1)S(1)}, u32[]{:S(2)}, u32[]{:S(2)}) collective-permute-start(bf16[256,576]{1,0:T(8,128)(2,1)} %get-tuple-element.17), channel_id=1, source_target_pairs={{0,2},{1,3},{2,0},{3,1},{4,6},{5,7},{6,4},{7,5},{8,10},{9,11},{10,... | collective-permute-start | bytes 884744 | tf_op jit(solution)/shard_map/ppermute | solution.py:193
  105.6 22.5 %collective-permute-start.18 = (bf16[256,576]{1,0:T(8,128)(2,1)}, bf16[256,576]{1,0:T(8,128)(2,1)S(1)}, u32[]{:S(2)}, u32[]{:S(2)}) collective-permute-start(bf16[256,576]{1,0:T(8,128)(2,1)} %get-tuple-element.18), channel_id=1, source_target_pairs={{0,1},{1,0},{2,3},{3,2},{4,5},{5,4},{6,7},{7,6},{8,9},{9,8},{10,11... | collective-permute-start | bytes 884744 | tf_op jit(solution)/shard_map/ppermute | solution.py:193
  109.8 20.6 %collective-permute-start.23 = (bf16[256,576]{1,0:T(8,128)(2,1)S(1)}, bf16[256,576]{1,0:T(8,128)(2,1)S(1)}, u32[]{:S(2)}, u32[]{:S(2)}) collective-permute-start(bf16[256,576]{1,0:T(8,128)(2,1)S(1)} %get-tuple-element.20), channel_id=1, source_target_pairs={{0,6},{1,7},{2,4},{3,5},{4,2},{5,3},{6,0},{7,1},{8,14},{9,15},{10,... | collective-permute-start | bytes 884744 | tf_op jit(solution)/shard_map/ppermute | solution.py:193
  117.4 15.2 %collective-permute-start.17 = (bf16[512,256]{1,0:T(8,128)(2,1)S(1)}, bf16[512,256]{1,0:T(8,128)(2,1)S(1)}, u32[]{:S(2)}, u32[]{:S(2)}) collective-permute-start(bf16[512,256]{1,0:T(8,128)(2,1)S(1)} %reshape.41.refs_0_), channel_id=1, source_target_pairs={{0,7},{1,6},{2,5},{3,4},{4,3},{5,2},{6,1},{7,0},{8,15},{9,14},{10,... | collective-permute-start | bytes 786440 | tf_op jit(solution)/shard_map/ppermute | solution.py:193
  119.9 18.3 %collective-permute-start.16 = (bf16[512,256]{1,0:T(8,128)(2,1)S(1)}, bf16[512,256]{1,0:T(8,128)(2,1)S(1)}, u32[]{:S(2)}, u32[]{:S(2)}) collective-permute-start(bf16[512,256]{1,0:T(8,128)(2,1)S(1)} %reshape.41.refs_0_), channel_id=1, source_target_pairs={{0,6},{1,7},{2,4},{3,5},{4,2},{5,3},{6,0},{7,1},{8,14},{9,15},{10,... | collective-permute-start | bytes 786440 | tf_op jit(solution)/shard_map/ppermute | solution.py:193
  121.8 20.6 %collective-permute-start.15 = (bf16[512,256]{1,0:T(8,128)(2,1)S(1)}, bf16[512,256]{1,0:T(8,128)(2,1)S(1)}, u32[]{:S(2)}, u32[]{:S(2)}) collective-permute-start(bf16[512,256]{1,0:T(8,128)(2,1)S(1)} %reshape.41.refs_0_), channel_id=1, source_target_pairs={{0,5},{1,4},{2,7},{3,6},{4,1},{5,0},{6,3},{7,2},{8,13},{9,12},{10,... | collective-permute-start | bytes 786440 | tf_op jit(solution)/shard_map/ppermute | solution.py:193
  128.8 17.8 %collective-permute-start.14 = (bf16[512,256]{1,0:T(8,128)(2,1)S(1)}, bf16[512,256]{1,0:T(8,128)(2,1)S(1)}, u32[]{:S(2)}, u32[]{:S(2)}) collective-permute-start(bf16[512,256]{1,0:T(8,128)(2,1)S(1)} %reshape.41.refs_0_), channel_id=1, source_target_pairs={{0,4},{1,5},{2,6},{3,7},{4,0},{5,1},{6,2},{7,3},{8,12},{9,13},{10,... | collective-permute-start | bytes 786440 | tf_op jit(solution)/shard_map/ppermute | solution.py:193
  131.1 15.5 %collective-permute-start.13 = (bf16[512,256]{1,0:T(8,128)(2,1)S(1)}, bf16[512,256]{1,0:T(8,128)(2,1)S(1)}, u32[]{:S(2)}, u32[]{:S(2)}) collective-permute-start(bf16[512,256]{1,0:T(8,128)(2,1)S(1)} %reshape.41.refs_0_), channel_id=1, source_target_pairs={{0,3},{1,2},{2,1},{3,0},{4,7},{5,6},{6,5},{7,4},{8,11},{9,10},{10,... | collective-permute-start | bytes 786440 | tf_op jit(solution)/shard_map/ppermute | solution.py:193
  132.6 16.4 %collective-permute-start.12 = (bf16[512,256]{1,0:T(8,128)(2,1)S(1)}, bf16[512,256]{1,0:T(8,128)(2,1)S(1)}, u32[]{:S(2)}, u32[]{:S(2)}) collective-permute-start(bf16[512,256]{1,0:T(8,128)(2,1)S(1)} %reshape.41.refs_0_), channel_id=1, source_target_pairs={{0,2},{1,3},{2,0},{3,1},{4,6},{5,7},{6,4},{7,5},{8,10},{9,11},{10,... | collective-permute-start | bytes 786440 | tf_op jit(solution)/shard_map/ppermute | solution.py:193
  138.2 14.8 %collective-permute-start.11 = (bf16[512,256]{1,0:T(8,128)(2,1)S(1)}, bf16[512,256]{1,0:T(8,128)(2,1)S(1)}, u32[]{:S(2)}, u32[]{:S(2)}) collective-permute-start(bf16[512,256]{1,0:T(8,128)(2,1)S(1)} %reshape.41.refs_0_), channel_id=1, source_target_pairs={{0,1},{1,0},{2,3},{3,2},{4,5},{5,4},{6,7},{7,6},{8,9},{9,8},{10,11... | collective-permute-start | bytes 786440 | tf_op jit(solution)/shard_map/ppermute | solution.py:193
  158.9 3.7 %collective-permute-start.25 = (f32[512]{0:T(512)S(1)}, f32[512]{0:T(512)S(1)}, u32[]{:S(2)}, u32[]{:S(2)}) collective-permute-start(f32[512]{0:T(512)S(1)} %reduce), channel_id=1, source_target_pairs={{0,1},{1,0},{2,3},{3,2},{4,5},{5,4},{6,7},{7,6},{8,9},{9,8},{10,11... | collective-permute-start | bytes 6152 | tf_op jit(solution)/shard_map/ppermute | solution.py:193
  162.6 5.1 %collective-permute-start.26 = (f32[512]{0:T(512)S(1)}, f32[512]{0:T(512)S(1)}, u32[]{:S(2)}, u32[]{:S(2)}) collective-permute-start(f32[512]{0:T(512)S(1)} %add.62), channel_id=1, source_target_pairs={{0,2},{1,3},{2,0},{3,1},{4,6},{5,7},{6,4},{7,5},{8,10},{9,11},{10,... | collective-permute-start | bytes 6152 | tf_op jit(solution)/shard_map/ppermute | solution.py:193
  167.7 5.1 %collective-permute-start.27 = (f32[512]{0:T(512)S(1)}, f32[512]{0:T(512)S(1)}, u32[]{:S(2)}, u32[]{:S(2)}) collective-permute-start(f32[512]{0:T(512)S(1)} %add.63), channel_id=1, source_target_pairs={{0,4},{1,5},{2,6},{3,7},{4,0},{5,1},{6,2},{7,3},{8,12},{9,13},{10,... | collective-permute-start | bytes 6152 | tf_op jit(solution)/shard_map/ppermute | solution.py:193
  (13 other events, 51.4 us)

commit v2 on v1

v2 whole, which is shorter than its diff:
```python
import functools
import math

import jax
import jax.numpy as jnp
from jax import lax
from jax.experimental import pallas as pl
from jax.experimental.pallas import tpu as pltpu
from jax.sharding import PartitionSpec as P

HD = 128
BLK = 128
PLANE = 4
BACK = 2

query_scale = 144.0 ** (-0.5)
soft_cap = 50.0
norm_eps = 1e-06
LOG2E = math.log2(math.e)


def project_kernel(scale, tile, count, x_hbm, g_ref, *refs):
    w_hbms, out_ref, x_buf, w_buf, x_sems, w_sems = (
        refs[:count],
        refs[count],
        refs[count + 1],
        refs[count + 2],
        refs[count + 3],
        refs[count + 4],
    )
    tiles = x_buf.shape[0]

    def x_copy(i):
        return pltpu.make_async_copy(
            x_hbm.at[pl.ds(pl.multiple_of(i * tile, tile), tile)], x_buf.at[i], x_sems.at[i]
        )

    width = w_buf.shape[1] // count
    w_copies = [
        pltpu.make_async_copy(
            w_hbms[j], w_buf.at[:, j * width : (j + 1) * width], w_sems.at[j]
        )
        for j in range(count)
    ]
    x_copy(0).start()
    for copy in w_copies:
        copy.start()
    for i in range(1, tiles):
        x_copy(i).start()

    @pl.loop(0, tiles)
    def _(i):
        x_copy(i).wait()
        x = x_buf[i].astype(jnp.float32)
        r = lax.rsqrt(jnp.mean(x * x, axis=1, keepdims=True) + norm_eps)
        normed = (x * r * g_ref[...]).astype(jnp.bfloat16)

        @pl.when(i == 0)
        def _():
            for copy in w_copies:
                copy.wait()

        done = jnp.dot(normed, w_buf[...], preferred_element_type=jnp.float32)
        if scale is not None:
            done = done * scale
        out_ref[pl.ds(pl.multiple_of(i * tile, tile), tile), :] = done.astype(jnp.bfloat16)


def project(tokens, gain, weights, scale, name, vmem):
    rows, d = tokens.shape
    tile = 128
    count = len(weights)
    width = sum(w.shape[1] for w in weights)
    return pl.pallas_call(
        functools.partial(project_kernel, scale, tile, count),
        in_specs=[pl.BlockSpec(memory_space=pl.ANY), pl.BlockSpec(memory_space=pltpu.VMEM)]
        + [pl.BlockSpec(memory_space=pl.ANY)] * count,
        out_specs=pl.BlockSpec(memory_space=pltpu.VMEM),
        out_shape=jax.ShapeDtypeStruct((rows, width), jnp.bfloat16),
        scratch_shapes=[
            pltpu.VMEM((rows // tile, tile, d), jnp.bfloat16),
            pltpu.VMEM((d, width), jnp.bfloat16),
            pltpu.SemaphoreType.DMA((rows // tile,)),
            pltpu.SemaphoreType.DMA((count,)),
        ],
        compiler_params=pltpu.CompilerParams(vmem_limit_bytes=vmem * 2**20),
        cost_estimate=pl.CostEstimate(
            flops=2 * rows * d * width, bytes_accessed=2 * d * (rows + width), transcendentals=0
        ),
        name=name,
    )(tokens, gain, *weights)


def attend_kernel(rows, stage, info_ref, q_ref, *refs):
    kv_refs, refs = refs[:PLANE], refs[PLANE:]
    if stage == 0:
        num_ref, den_ref, held, sems = refs
    elif stage < BACK:
        num_in, den_in, num_ref, den_ref, held, sems = refs
    else:
        num_in, den_in, out_ref, num_ref, den_ref, held, sems = refs
    place = info_ref[0]
    copies = [
        pltpu.make_async_copy(kv_refs[i], held.at[place ^ i], sems.at[i]) for i in range(PLANE)
    ]
    for copy in copies:
        copy.start()
    if stage == 0:
        num_ref[...] = jnp.zeros_like(num_ref)
        den_ref[...] = jnp.zeros_like(den_ref)
    else:
        num_ref[...] = num_in[...]
        den_ref[...] = den_in[...]
    blocks = rows // BLK
    heads = num_ref.shape[0]
    base = (BACK - stage) * PLANE
    starts = [info_ref[1 + b] - base * rows for b in range(blocks)]
    row = lax.broadcasted_iota(jnp.int32, (rows, 1), 0)
    start_row = jnp.full((rows, 1), starts[0], jnp.int32)
    for b in range(1, blocks):
        start_row = jnp.where(row >= b * BLK, starts[b], start_row)

    def tile(s, lower, causal):
        for h in range(heads):
            scores = lax.dot_general(
                q_ref[:, h * HD : (h + 1) * HD],
                held[s, :, :HD],
                (((1,), (1,)), ((), ())),
                preferred_element_type=jnp.float32,
            )
            capped = jnp.tanh(scores * (1.0 / soft_cap)) * (soft_cap * LOG2E)
            weights = jnp.exp2(capped)
            if lower or causal:
                offset = lax.broadcasted_iota(jnp.int32, (rows, rows), 1)
                allowed = offset >= start_row - s * rows
                if causal:
                    allowed = allowed & (offset <= row)
                weights = jnp.where(allowed, weights, 0.0)
            weight_sum = weights[:, :HD]
            for j in range(1, rows // HD):
                weight_sum = weight_sum + weights[:, j * HD : (j + 1) * HD]
            den_ref[h] += weight_sum
            num_ref[h] += jnp.dot(
                weights.astype(jnp.bfloat16), held[s, :, HD:], preferred_element_type=jnp.float32
            )

    end = place if stage == 0 else PLANE
    lo = jnp.clip(lax.div(jnp.maximum(starts[0], 0), rows), 0, end)
    clear = jnp.clip(lax.div(jnp.maximum(starts[-1], 0) + rows - 1, rows), lo, end)
    for copy in copies:
        copy.wait()

    @pl.loop(lo, clear)
    def _(s):
        tile(s, True, False)

    @pl.loop(clear, end)
    def _(s):
        tile(s, False, False)

    if stage == 0:
        tile(place, True, True)
    if stage == BACK:
        for h in range(heads):
            total = jnp.sum(den_ref[h], axis=1, keepdims=True)
            out_ref[:, h * HD : (h + 1) * HD] = (num_ref[h] / total).astype(jnp.bfloat16)


def attend(stage, info, q, kvs, carry):
    rows = q.shape[0]
    heads = q.shape[1] // HD
    sums = jax.ShapeDtypeStruct((heads, rows, HD), jnp.float32)
    last = stage == BACK
    whole = pl.BlockSpec(memory_space=pltpu.VMEM)
    return pl.pallas_call(
        functools.partial(attend_kernel, rows, stage),
        in_specs=[pl.BlockSpec(memory_space=pltpu.SMEM), whole]
        + [pl.BlockSpec(memory_space=pl.ANY)] * PLANE
        + [whole] * len(carry),
        out_specs=whole if last else [whole] * 2,
        out_shape=jax.ShapeDtypeStruct(q.shape, jnp.bfloat16) if last else [sums] * 2,
        scratch_shapes=([pltpu.VMEM(sums.shape, jnp.float32)] * 2 if last else [])
        + [
            pltpu.VMEM((PLANE, rows, 2 * HD), jnp.bfloat16),
            pltpu.SemaphoreType.DMA((PLANE,)),
        ],
        compiler_params=pltpu.CompilerParams(vmem_limit_bytes=32 * 2**20),
        cost_estimate=pl.CostEstimate(
            flops=2 * 10**9, bytes_accessed=4 * 10**6, transcendentals=4 * 10**6
        ),
        name="attend",
    )(info, q, *kvs, *carry)


def out_kernel(parts, *refs):
    w_ref, sum_ref, square_ref = refs[parts:]
    total = jnp.dot(refs[0][...], w_ref[0], preferred_element_type=jnp.float32)
    for i in range(1, parts):
        total = total + jnp.dot(refs[i][...], w_ref[i], preferred_element_type=jnp.float32)
    sum_ref[...] = total
    square_ref[...] = jnp.sum(total * total, axis=1, keepdims=True)


def out_project(heads, weights):
    rows, inner = heads[0].shape
    parts, _, cols = weights.shape
    tile = 256
    return pl.pallas_call(
        functools.partial(out_kernel, parts),
        grid=(rows // tile,),
        in_specs=[pl.BlockSpec((tile, inner), lambda i: (i, 0))] * parts
        + [pl.BlockSpec(weights.shape, lambda i: (0, 0, 0), pipeline_mode=pl.Buffered(1))],
        out_specs=[
            pl.BlockSpec((tile, cols), lambda i: (i, 0)),
            pl.BlockSpec((tile, 1), lambda i: (i, 0)),
        ],
        out_shape=[
            jax.ShapeDtypeStruct((rows, cols), jnp.float32),
            jax.ShapeDtypeStruct((rows, 1), jnp.float32),
        ],
        compiler_params=pltpu.CompilerParams(vmem_limit_bytes=32 * 2**20),
        cost_estimate=pl.CostEstimate(
            flops=2 * rows * inner * parts * cols, bytes_accessed=6 * 10**6, transcendentals=0
        ),
        name="out_project",
    )(*heads, weights)


def local(n_ctx, n_tp, tokens, norm_gain, q_weight, k_weight, v_weight, o_weight, post_gain, doc_ids, plan):
    rows, features = tokens.shape
    blocks = rows // BLK
    total_blocks = doc_ids.shape[0]
    shard = lax.axis_index("ctx")
    group = lax.axis_index("tp")
    cols = o_weight.shape[1] // n_tp
    inner = o_weight.shape[0]
    half = inner // 2
    core = shard % 2

    def ctx_xor(a, m):
        return lax.ppermute(a, "ctx", [(i, i ^ m) for i in range(n_ctx)])

    def ctx_z(a, d):
        return lax.ppermute(a, "ctx", [(i, (i + d * PLANE) % n_ctx) for i in range(n_ctx)])

    def tp_xor(a, m):
        return lax.ppermute(a, "tp", [(i, i ^ m) for i in range(n_tp)])

    gain = norm_gain.reshape(1, -1)
    own_kv = project(tokens, gain, [k_weight, v_weight], None, "project_kv", 56)

    own_weight = lax.dynamic_slice_in_dim(o_weight, group * cols, cols, axis=1)
    slices = [
        lax.dynamic_slice(o_weight, (core * half, (group ^ m) * cols), (half, cols))
        for m in range(1, n_tp)
    ]
    own_kv, slices = lax.optimization_barrier((own_kv, slices))

    kvs = []
    near = own_kv
    for back in range(BACK + 1):
        near = near if back == 0 else ctx_z(near, 1)
        across = ctx_xor(near, 2)
        kvs.append([near, ctx_xor(near, 1), across, ctx_xor(across, 1)])
    mine = jnp.stack([tp_xor(w, m + 1) for m, w in enumerate(slices)])
    theirs = ctx_xor(mine, 1)
    even = core == 0
    out_weights = jnp.concatenate(
        [jnp.where(even, mine, theirs), jnp.where(even, theirs, mine)], axis=1
    )
    out_weights = jnp.concatenate([own_weight[None], out_weights], axis=0)

    queries = project(tokens, gain, [q_weight], query_scale, "project_q", 40)

    first_block = jnp.sum((doc_ids[None, :] < doc_ids[:, None]).astype(jnp.int32), axis=1)
    own_first = lax.dynamic_slice_in_dim(first_block, shard * blocks, blocks, 0)
    plane_first = (shard // PLANE - BACK) * PLANE * blocks
    info = jnp.concatenate(
        [(shard % PLANE).reshape(1), (own_first - plane_first) * BLK]
    ).astype(jnp.int32)

    same = (plan[None, :] == plan[:, None]).astype(jnp.int32)
    block_ids = jnp.arange(total_blocks, dtype=jnp.int32)
    rank = jnp.sum(same * (block_ids[None, :] < block_ids[:, None]), axis=1)
    target = plan * blocks + rank
    picker = (target[None, :] == block_ids[:, None]).astype(jnp.bfloat16)

    carry = []
    for stage in range(BACK):
        carry = attend(stage, info, queries, kvs[stage], carry)
    carry, out_weights, picker = lax.optimization_barrier((carry, out_weights, picker))
    natural = attend(BACK, info, queries, kvs[BACK], carry)

    width = natural.shape[1]
    piece = BLK // n_ctx
    striped = natural.reshape(blocks, n_ctx, piece, width).transpose(1, 0, 2, 3)
    striped = striped.reshape(n_ctx, blocks, piece * width)
    gathered = lax.all_to_all(striped, "ctx", 0, 0, tiled=True)
    ordered = jnp.dot(
        picker,
        gathered.reshape(total_blocks, piece * width),
        preferred_element_type=jnp.float32,
    ).astype(jnp.bfloat16)
    placed = lax.all_to_all(
        ordered.reshape(n_ctx, blocks, piece * width), "ctx", 0, 0, tiled=True
    )
    placed = (
        placed.reshape(n_ctx, blocks, piece, width).transpose(1, 0, 2, 3).reshape(rows, width)
    )

    heads = [placed] + [None] * (n_tp - 1)
    for m in (4, 1, 3, 2):
        heads[m] = tp_xor(placed, m)
    heads[5] = tp_xor(heads[4], 1)
    heads[7] = tp_xor(heads[4], 3)
    heads[6] = tp_xor(heads[2], 4)
    summed, squares = out_project(heads, out_weights)
    squares = squares.reshape(rows)
    squares = squares + tp_xor(squares, 4)
    squares = squares + tp_xor(squares, 1) + tp_xor(squares, 3) + tp_xor(squares, 2)
    scale = lax.rsqrt(squares / features + norm_eps)
    return (summed * scale[:, None] * post_gain).astype(jnp.bfloat16)


def solution(mesh):
    placed = (
        P("ctx", None),
        P(),
        P(None, "tp"),
        P(None, "tp"),
        P(None, "tp"),
        P("tp", None),
        P("tp"),
        P(),
        P(),
    )
    return jax.shard_map(
        functools.partial(local, mesh.shape["ctx"], mesh.shape["tp"]),
        mesh=mesh,
        in_specs=placed,
        out_specs=P("ctx", "tp"),
        check_vma=False,
    )
```

time: 175 us -> 164 us (0.937)
  blocking collectives: 0 us -> 39.8 us
  waiting for transfers between devices: 79 us -> 40 us
  starting transfers between devices: 63 us -> 36.7 us
  Pallas kernels: 11 us -> 21.2 us
  local copies, waits for them, and re-layouts: 18.8 us -> 22 us
  other arithmetic: 1.79 us -> 3.92 us
    all_to_all x0 -> x2, blocking collectives: none -> 39.8 us  [the longest x1 24.4 us: local(): gathered = lax.all_to_all(striped, 'ctx', 0, 0, tiled=True)]
    all_to_all x2 -> x0, starting transfers between devices: 24 us -> none  [the longest x1 20.1 us: local(): gathered = lax.all_to_all(striped, 'ctx', 0, 0, tiled=True)]
    ppermute x2, waiting for transfers between devices: 13.8 us -> 0.01 us  [ctx_z(): lax.ppermute(a, 'ctx', [(i, (i + d * PLANE) % n_ctx) for i in range(n_ctx)])]
    ppermute x17 -> x18, waiting for transfers between devices: 46.8 us -> 34.2 us  [tp_xor(): return lax.ppermute(a, 'tp', [(i, i ^ m) for i in range(n_tp)])]
    all_to_all x2 -> x0, waiting for transfers between devices: 11.9 us -> none  [the longest x1 11.9 us: local(): gathered = lax.all_to_all(striped, 'ctx', 0, 0, tiled=True)]
    pallas_call x2 -> x5, Pallas kernels: 8.82 us -> 19.1 us  [the longest x2 13.2 us: project(): pl.pallas_call(functools.partial(project_kernel, scale, tile, count), in_...]
    ppermute x2, starting transfers between devices: 5.26 us -> 2.07 us  [ctx_z(): lax.ppermute(a, 'ctx', [(i, (i + d * PLANE) % n_ctx) for i in range(n_ctx)])]
    another operation x0 -> x2, local copies, waits for them, and re-layouts: none -> 3.15 us  [local(): mine = jnp.stack([tp_xor(w, m + 1) for m, w in enumerate(slices)])]
  transfers between devices with their start and end apart: 30 -> 30, of which waited for: 17 -> 18; matrix products, arithmetic and copies ran while one was open for 2% -> 8% of each run, Pallas kernels for 0% -> 6%
where the time goes in v2:
time: 164 us
  waiting for transfers between devices  40 us (24%)
  blocking collectives  39.8 us (24%)
  starting transfers between devices  36.7 us (22%)
  local copies, waits for them, and re-layouts  22 us (13%)
  Pallas kernels  21.2 us (13%)
  other arithmetic  3.92 us (2%)
    ppermute x18, waiting for transfers between devices, tp_xor(): return lax.ppermute(a, 'tp', [(i, i ^ m) for i in range(n_tp)])  34.2 us
    ppermute x18, starting transfers between devices, tp_xor(): return lax.ppermute(a, 'tp', [(i, i ^ m) for i in range(n_tp)])  29.3 us
    all_to_all x1, blocking collectives, local(): gathered = lax.all_to_all(striped, 'ctx', 0, 0, tiled=True)  24.4 us
    all_to_all x1, blocking collectives, local(): lax.all_to_all(ordered.reshape(n_ctx, blocks, piece * width), 'ctx', 0, 0...  15.4 us
    pallas_call x2, Pallas kernels, project(): pl.pallas_call(functools.partial(project_kernel, scale, tile, count), in_...  13.2 us
    unnamed x32, local copies, waits for them, and re-layouts  9.22 us
    pallas_call x3, Pallas kernels, attend(): pl.pallas_call(functools.partial(attend_kernel, rows, stage), in_specs=[p...  5.85 us
    ppermute x10, waiting for transfers between devices, ctx_xor(): return lax.ppermute(a, 'ctx', [(i, i ^ m) for i in range(n_ctx)])  5.82 us
  transfers between devices with their start and end apart: 30, of which 18 were waited for; matrix products, arithmetic and copies ran while one was open for 8% of the time, Pallas kernels for 6%

profile of v2, /device:TPU:2, one launch (start us, length us, event | category | flops | bytes accessed | tf_op | source)
XLA Modules:
  0.0 164.2 jit_solution(13158856230120028483)
XLA Ops:
  1.3 7.8 %project_kv.1.refs_0_ = bf16[512,256]{1,0:T(8,128)(2,1)} custom-call(bf16[512,4608]{1,0:T(8,128)(2,1)} %x_hbm.3, f32[1,4608]{1,0:T(1,128)} %reshape.35.g_ref, bf16[4608,128]{1,0:T(8,128)(2,1)} %refs_0_.3, bf16[4608,128]{1,0:T(8,128)(2,1)} %refs_1_.1), custom_call_target="tpu_custom_call" | custom-call | flops 1207959552 | bytes 7077888 | tf_op jit(solution)/shard_map/project_kv/pallas_call | solution.py:74
  9.2 2.2 %fusion.1 = (bf16[128,576]{1,0:T(8,128)(2,1)S(1)}, bf16[128,576]{1,0:T(8,128)(2,1)S(1)}, bf16[128,576]{1,0:T(8,128)(2,1)S(1)}, bf16[128,576]{1,0:T(8,128)(2,1)S(...) fusion(bf16[256,4608]{1,0:T(8,128)(2,1)} %param.14, ...), kind=kLoop, calls=%fused_computation.23 | loop fusion | bytes 2064416 | tf_op jit(solution)/shard_map/dynamic_slice | solution.py:254
  11.5 2.4 %collective-permute-start.5 = (bf16[512,256]{1,0:T(8,128)(2,1)S(1)}, bf16[512,256]{1,0:T(8,128)(2,1)S(1)}, u32[]{:S(2)}, u32[]{:S(2)}) collective-permute-start(bf16[512,256]{1,0:T(8,128)(2,1)S(1)} %copy-done.3), channel_id=1, source_target_pairs={{0,16},{8,24},{16,0},{24,8},{32,48},{40,56},{48,32},{56,40},{64,80... | collective-permute-start | bytes 786440 | tf_op jit(solution)/shard_map/ppermute | solution.py:241
  15.6 2.9 %collective-permute-start.8 = (bf16[128,576]{1,0:T(8,128)(2,1)S(1)}, bf16[128,576]{1,0:T(8,128)(2,1)S(1)}, u32[]{:S(2)}, u32[]{:S(2)}) collective-permute-start(bf16[128,576]{1,0:T(8,128)(2,1)S(1)} %get-tuple-element.29), channel_id=1, source_target_pairs={{0,2},{1,3},{2,0},{3,1},{4,6},{5,7},{6,4},{7,5},{8,10},{9,11},{10,... | collective-permute-start | bytes 442376 | tf_op jit(solution)/shard_map/ppermute | solution.py:247
  18.7 2.3 %collective-permute-done.7 = bf16[128,576]{1,0:T(8,128)(2,1)S(1)} collective-permute-done((bf16[128,576]{1,0:T(8,128)(2,1)S(1)}, bf16[128,576]{1,0:T(8,128)(2,1)S(1)}, u32[]{:S(2)}, u32[]{:S(2)}) %collective-permute-start.7) | collective-permute-done | bytes 147488 | tf_op jit(solution)/shard_map/ppermute | solution.py:247
  21.0 3.1 %collective-permute-start.9 = (bf16[128,576]{1,0:T(8,128)(2,1)S(1)}, bf16[128,576]{1,0:T(8,128)(2,1)S(1)}, u32[]{:S(2)}, u32[]{:S(2)}) collective-permute-start(bf16[128,576]{1,0:T(8,128)(2,1)S(1)} %get-tuple-element.30), channel_id=1, source_target_pairs={{0,3},{1,2},{2,1},{3,0},{4,7},{5,6},{6,5},{7,4},{8,11},{9,10},{10,... | collective-permute-start | bytes 442376 | tf_op jit(solution)/shard_map/ppermute | solution.py:247
  26.4 2.4 %collective-permute-start.10 = (bf16[128,576]{1,0:T(8,128)(2,1)S(1)}, bf16[128,576]{1,0:T(8,128)(2,1)S(1)}, u32[]{:S(2)}, u32[]{:S(2)}) collective-permute-start(bf16[128,576]{1,0:T(8,128)(2,1)S(1)} %get-tuple-element.31), channel_id=1, source_target_pairs={{0,4},{1,5},{2,6},{3,7},{4,0},{5,1},{6,2},{7,3},{8,12},{9,13},{10,... | collective-permute-start | bytes 442376 | tf_op jit(solution)/shard_map/ppermute | solution.py:247
  29.8 2.0 %collective-permute-start.11 = (bf16[128,576]{1,0:T(8,128)(2,1)S(1)}, bf16[128,576]{1,0:T(8,128)(2,1)S(1)}, u32[]{:S(2)}, u32[]{:S(2)}) collective-permute-start(bf16[128,576]{1,0:T(8,128)(2,1)S(1)} %get-tuple-element.32), channel_id=1, source_target_pairs={{0,5},{1,4},{2,7},{3,6},{4,1},{5,0},{6,3},{7,2},{8,13},{9,12},{10,... | collective-permute-start | bytes 442376 | tf_op jit(solution)/shard_map/ppermute | solution.py:247
  33.4 2.4 %collective-permute-start.12 = (bf16[128,576]{1,0:T(8,128)(2,1)S(1)}, bf16[128,576]{1,0:T(8,128)(2,1)S(1)}, u32[]{:S(2)}, u32[]{:S(2)}) collective-permute-start(bf16[128,576]{1,0:T(8,128)(2,1)S(1)} %get-tuple-element.33), channel_id=1, source_target_pairs={{0,6},{1,7},{2,4},{3,5},{4,2},{5,3},{6,0},{7,1},{8,14},{9,15},{10,... | collective-permute-start | bytes 442376 | tf_op jit(solution)/shard_map/ppermute | solution.py:247
  36.5 2.8 %collective-permute-done.11 = bf16[128,576]{1,0:T(8,128)(2,1)S(1)} collective-permute-done((bf16[128,576]{1,0:T(8,128)(2,1)S(1)}, bf16[128,576]{1,0:T(8,128)(2,1)S(1)}, u32[]{:S(2)}, u32[]{:S(2)}) %collective-permute-start.11) | collective-permute-done | bytes 147488 | tf_op jit(solution)/shard_map/ppermute | solution.py:247
  40.8 1.7 %collective-permute-done.12 = bf16[128,576]{1,0:T(8,128)(2,1)S(1)} collective-permute-done((bf16[128,576]{1,0:T(8,128)(2,1)S(1)}, bf16[128,576]{1,0:T(8,128)(2,1)S(1)}, u32[]{:S(2)}, u32[]{:S(2)}) %collective-permute-start.12) | collective-permute-done | bytes 147488 | tf_op jit(solution)/shard_map/ppermute | solution.py:247
  43.3 4.9 %collective-permute-done.13 = bf16[128,576]{1,0:T(8,128)(2,1)S(1)} collective-permute-done((bf16[128,576]{1,0:T(8,128)(2,1)S(1)}, bf16[128,576]{1,0:T(8,128)(2,1)S(1)}, u32[]{:S(2)}, u32[]{:S(2)}) %collective-permute-start.13) | collective-permute-done | bytes 147488 | tf_op jit(solution)/shard_map/ppermute | solution.py:247
  48.9 2.5 %copy.21 = bf16[7,128,576]{1,2,0:T(8,128)(2,1)} copy(bf16[7,128,576]{2,1,0:T(8,128)(2,1)} %bitcast_dynamic-update-slice_fusion) | data formatting | bytes 2064384 | tf_op jit(solution)/shard_map/stack | solution.py:265
  53.2 1.9 %collective-permute-start.15 = (bf16[512,256]{1,0:T(8,128)(2,1)S(1)}, bf16[512,256]{1,0:T(8,128)(2,1)}, u32[]{:S(2)}, u32[]{:S(2)}) collective-permute-start(bf16[512,256]{1,0:T(8,128)(2,1)S(1)} %collective-permute-done.refs_0_), channel_id=1, source_target_pairs={{0,32},{8,40},{16,48},{24,56},{32,64},{40,72},{48,80},{56,88},{64,... | collective-permute-start | bytes 786440 | tf_op jit(solution)/shard_map/ppermute | solution.py:244
  55.1 2.3 %copy-done = bf16[512,4608]{1,0:T(8,128)(2,1)S(1)} copy-done((bf16[512,4608]{1,0:T(8,128)(2,1)S(1)}, bf16[512,4608]{1,0:T(8,128)(2,1)}, u32[]{:S(2)}) %copy-start) | copy-done | bytes 4718616
  57.4 5.4 %project_q.1.q_ref = bf16[512,256]{1,0:T(8,128)(2,1)S(1)} custom-call(bf16[512,4608]{1,0:T(8,128)(2,1)S(1)} %copy-done, f32[1,4608]{1,0:T(1,128)S(1)} %copy-done.4, bf16[4608,256]{1,0:T(8,128)(2,1)S(1)} %copy-done.1), custom_call_target="tpu_custom_call" | custom-call | flops 1207959552 | bytes 7077888 | tf_op jit(solution)/shard_map/project_q/pallas_call | solution.py:74
  63.1 1.9 %dynamic-slice_bitcast_fusion = bf16[1,256,576]{2,1,0:T(8,128)(2,1)} fusion(bf16[256,4608]{1,0:T(8,128)(2,1)} %param.14, s32[]{:T(128)S(6)} %select_n.75), kind=kLoop, calls=%fused_computation.5 | loop fusion | bytes 589828 | tf_op jit(solution)/shard_map/broadcast_in_dim | solution.py:271
  66.3 2.4 %attend.3 = (f32[2,512,128]{2,1,0:T(8,128)S(1)}, f32[2,512,128]{2,1,0:T(8,128)S(1)}) custom-call(s32[5]{0:T(128)S(1)} %pad_add_fusion.info_ref, bf16[512,256]{1,0:T(8,128)(2,1)S(1)} %project_q.1.q_ref, bf16[512,256]{1,0:T(8,128)(2,1)S(1)} %copy-done.3, bf16[512,256]{1,0:T(8,128)(2,1)} %collective-permute-done.4.refs_1_, ...), custom_call_target="tpu_custom_call" | custom-call | flops 2000000000 | bytes 4000000 | tf_op jit(solution)/shard_map/attend/pallas_call | solution.py:175
  68.7 5.8 %collective-permute-done.17.refs_2_ = bf16[512,256]{1,0:T(8,128)(2,1)} collective-permute-done((bf16[512,256]{1,0:T(8,128)(2,1)}, bf16[512,256]{1,0:T(8,128)(2,1)}, u32[]{:S(2)}, u32[]{:S(2)}) %collective-permute-start.17) | collective-permute-done | bytes 262176 | tf_op jit(solution)/shard_map/ppermute | solution.py:241
  76.9 2.2 %copy.22 = bf16[7,128,576]{2,1,0:T(8,128)(2,1)S(1)} copy(bf16[7,128,576]{1,2,0:T(8,128)(2,1)} %collective-permute-done.14) | data formatting | bytes 2064384 | tf_op jit(solution)/shard_map/ppermute | solution.py:241
  81.9 1.9 %attend.5 = bf16[512,256]{1,0:T(8,128)(2,1)S(1)} custom-call(s32[5]{0:T(128)S(1)} %pad_add_fusion.info_ref, bf16[512,256]{1,0:T(8,128)(2,1)S(1)} %project_q.1.q_ref, bf16[512,256]{1,0:T(8,128)(2,1)} %collective-permute-done.15.refs_0_, bf16[512,256]{1,0:T(8,128)(2,1)} %collective-permute-done.16.refs_1_, bf16[512,256]{1,0:T(8,128)(2,1)} %collective-permute-done.17.refs_2_, ...), custom_call_target="tpu_custom_call" | custom-call | flops 2000000000 | bytes 4000000 | tf_op jit(solution)/shard_map/attend/pallas_call | solution.py:175
  84.2 24.4 %all_to_all.10 = bf16[32,4,1024]{2,1,0:T(4,128)(2,1)S(1)} all-to-all(bf16[32,4,1024]{2,1,0:T(4,128)(2,1)S(1)} %copy.27), channel_id=1, replica_groups=mesh['ctx'=32,'tp'=8] {'ctx'}, dimensions={0} | all-to-all | bytes 524288 | tf_op jit(solution)/shard_map/all_to_all | solution.py:298
  109.0 15.4 %all_to_all.11 = bf16[32,4,1024]{2,1,0:T(4,128)(2,1)S(1)} all-to-all(bf16[32,4,1024]{2,1,0:T(4,128)(2,1)S(1)} %reshape.39), channel_id=1, replica_groups=mesh['ctx'=32,'tp'=8] {'ctx'}, dimensions={0} | all-to-all | bytes 524288 | tf_op jit(solution)/shard_map/all_to_all | solution.py:304
  124.7 2.4 %collective-permute-start.22 = (bf16[512,256]{1,0:T(8,128)(2,1)S(1)}, bf16[512,256]{1,0:T(8,128)(2,1)S(1)}, u32[]{:S(2)}, u32[]{:S(2)}) collective-permute-start(bf16[512,256]{1,0:T(8,128)(2,1)S(1)} %reshape.41.refs_0_), channel_id=1, source_target_pairs={{0,4},{1,5},{2,6},{3,7},{4,0},{5,1},{6,2},{7,3},{8,12},{9,13},{10,... | collective-permute-start | bytes 786440 | tf_op jit(solution)/shard_map/ppermute | solution.py:247
  128.0 3.3 %collective-permute-start.21 = (bf16[512,256]{1,0:T(8,128)(2,1)S(1)}, bf16[512,256]{1,0:T(8,128)(2,1)S(1)}, u32[]{:S(2)}, u32[]{:S(2)}) collective-permute-start(bf16[512,256]{1,0:T(8,128)(2,1)S(1)} %reshape.41.refs_0_), channel_id=1, source_target_pairs={{0,3},{1,2},{2,1},{3,0},{4,7},{5,6},{6,5},{7,4},{8,11},{9,10},{10,... | collective-permute-start | bytes 786440 | tf_op jit(solution)/shard_map/ppermute | solution.py:247
  131.2 2.8 %collective-permute-done.22.refs_4_ = bf16[512,256]{1,0:T(8,128)(2,1)S(1)} collective-permute-done((bf16[512,256]{1,0:T(8,128)(2,1)S(1)}, bf16[512,256]{1,0:T(8,128)(2,1)S(1)}, u32[]{:S(2)}, u32[]{:S(2)}) %collective-permute-start.22) | collective-permute-done | bytes 262176 | tf_op jit(solution)/shard_map/ppermute | solution.py:247
  134.0 3.8 %collective-permute-done.20.refs_2_ = bf16[512,256]{1,0:T(8,128)(2,1)S(1)} collective-permute-done((bf16[512,256]{1,0:T(8,128)(2,1)S(1)}, bf16[512,256]{1,0:T(8,128)(2,1)S(1)}, u32[]{:S(2)}, u32[]{:S(2)}) %collective-permute-start.20) | collective-permute-done | bytes 262176 | tf_op jit(solution)/shard_map/ppermute | solution.py:247
  141.6 2.8 %collective-permute-done.23.refs_5_ = bf16[512,256]{1,0:T(8,128)(2,1)S(1)} collective-permute-done((bf16[512,256]{1,0:T(8,128)(2,1)S(1)}, bf16[512,256]{1,0:T(8,128)(2,1)S(1)}, u32[]{:S(2)}, u32[]{:S(2)}) %collective-permute-start.23) | collective-permute-done | bytes 262176 | tf_op jit(solution)/shard_map/ppermute | solution.py:247
  147.1 2.1 %out_project.1 = (f32[512,576]{1,0:T(8,128)S(1)}, f32[512,1]{1,0:T(8,128)S(1)}) custom-call(bf16[512,256]{1,0:T(8,128)(2,1)S(1)} %reshape.41.refs_0_, bf16[512,256]{1,0:T(8,128)(2,1)S(1)} %collective-permute-done.19.refs_1_, bf16[512,256]{1,0:T(8,128)(2,1)S(1)} %collective-permute-done.20.refs_2_, bf16[512,256]{1,0:T(8,128)(2,1)S(1)} %collective-permute-done.21.refs_3_, ...), custom_call_target="tpu_custom_call" | custom-call | flops 1207959552 | bytes 6000000 | tf_op jit(solution)/shard_map/out_project/pallas_call | solution.py:208
  150.5 2.0 %collective-permute-start.26 = (f32[512]{0:T(512)S(1)}, f32[512]{0:T(512)S(1)}, u32[]{:S(2)}, u32[]{:S(2)}) collective-permute-start(f32[512]{0:T(512)S(1)} %reduce), channel_id=1, source_target_pairs={{0,4},{1,5},{2,6},{3,7},{4,0},{5,1},{6,2},{7,3},{8,12},{9,13},{10,... | collective-permute-start | bytes 6152 | tf_op jit(solution)/shard_map/ppermute | solution.py:247
  152.5 3.2 %collective-permute-done.26 = f32[512]{0:T(512)S(1)} collective-permute-done((f32[512]{0:T(512)S(1)}, f32[512]{0:T(512)S(1)}, u32[]{:S(2)}, u32[]{:S(2)}) %collective-permute-start.26) | collective-permute-done | bytes 2080 | tf_op jit(solution)/shard_map/ppermute | solution.py:247
  156.5 3.2 %collective-permute-start.29 = (f32[512]{0:T(512)S(1)}, f32[512]{0:T(512)S(1)}, u32[]{:S(2)}, u32[]{:S(2)}) collective-permute-start(f32[512]{0:T(512)S(1)} %add.79), channel_id=1, source_target_pairs={{0,2},{1,3},{2,0},{3,1},{4,6},{5,7},{6,4},{7,5},{8,10},{9,11},{10,... | collective-permute-start | bytes 6152 | tf_op jit(solution)/shard_map/ppermute | solution.py:247
  (96 shorter events, 35.0 us)
Async XLA Ops:
  9.2 9.3 %copy-start.11 = (s32[128]{0:T(128)S(1)}, s32[128]{0:T(128)}, u32[]{:S(2)}) copy-start(s32[128]{0:T(128)} %param.17) | copy-start | bytes 1540
  11.5 51.4 %collective-permute-start.5 = (bf16[512,256]{1,0:T(8,128)(2,1)S(1)}, bf16[512,256]{1,0:T(8,128)(2,1)S(1)}, u32[]{:S(2)}, u32[]{:S(2)}) collective-permute-start(bf16[512,256]{1,0:T(8,128)(2,1)S(1)} %copy-done.3), channel_id=1, source_target_pairs={{0,16},{8,24},{16,0},{24,8},{32,48},{40,56},{48,32},{56,40},{64,80... | collective-permute-start | bytes 786440 | tf_op jit(solution)/shard_map/ppermute | solution.py:241
  13.8 51.1 %collective-permute-start.4 = (bf16[512,256]{1,0:T(8,128)(2,1)S(1)}, bf16[512,256]{1,0:T(8,128)(2,1)}, u32[]{:S(2)}, u32[]{:S(2)}) collective-permute-start(bf16[512,256]{1,0:T(8,128)(2,1)S(1)} %copy-done.3), channel_id=1, source_target_pairs={{0,8},{8,0},{16,24},{24,16},{32,40},{40,32},{48,56},{56,48},{64,72... | collective-permute-start | bytes 786440 | tf_op jit(solution)/shard_map/ppermute | solution.py:241
  13.8 37.8 %collective-permute-start = (bf16[512,256]{1,0:T(8,128)(2,1)S(1)}, bf16[512,256]{1,0:T(8,128)(2,1)S(1)}, u32[]{:S(2)}, u32[]{:S(2)}) collective-permute-start(bf16[512,256]{1,0:T(8,128)(2,1)S(1)} %copy-done.3), channel_id=1, source_target_pairs={{0,32},{8,40},{16,48},{24,56},{32,64},{40,72},{48,80},{56,88},{64,... | collective-permute-start | bytes 786440 | tf_op jit(solution)/shard_map/ppermute | solution.py:244
  14.0 7.0 %collective-permute-start.7 = (bf16[128,576]{1,0:T(8,128)(2,1)S(1)}, bf16[128,576]{1,0:T(8,128)(2,1)S(1)}, u32[]{:S(2)}, u32[]{:S(2)}) collective-permute-start(bf16[128,576]{1,0:T(8,128)(2,1)S(1)} %get-tuple-element.28), channel_id=1, source_target_pairs={{0,1},{1,0},{2,3},{3,2},{4,5},{5,4},{6,7},{7,6},{8,9},{9,8},{10,11... | collective-permute-start | bytes 442376 | tf_op jit(solution)/shard_map/ppermute | solution.py:247
  15.6 10.8 %collective-permute-start.8 = (bf16[128,576]{1,0:T(8,128)(2,1)S(1)}, bf16[128,576]{1,0:T(8,128)(2,1)S(1)}, u32[]{:S(2)}, u32[]{:S(2)}) collective-permute-start(bf16[128,576]{1,0:T(8,128)(2,1)S(1)} %get-tuple-element.29), channel_id=1, source_target_pairs={{0,2},{1,3},{2,0},{3,1},{4,6},{5,7},{6,4},{7,5},{8,10},{9,11},{10,... | collective-permute-start | bytes 442376 | tf_op jit(solution)/shard_map/ppermute | solution.py:247
  21.0 8.8 %collective-permute-start.9 = (bf16[128,576]{1,0:T(8,128)(2,1)S(1)}, bf16[128,576]{1,0:T(8,128)(2,1)S(1)}, u32[]{:S(2)}, u32[]{:S(2)}) collective-permute-start(bf16[128,576]{1,0:T(8,128)(2,1)S(1)} %get-tuple-element.30), channel_id=1, source_target_pairs={{0,3},{1,2},{2,1},{3,0},{4,7},{5,6},{6,5},{7,4},{8,11},{9,10},{10,... | collective-permute-start | bytes 442376 | tf_op jit(solution)/shard_map/ppermute | solution.py:247
  26.4 6.9 %collective-permute-start.10 = (bf16[128,576]{1,0:T(8,128)(2,1)S(1)}, bf16[128,576]{1,0:T(8,128)(2,1)S(1)}, u32[]{:S(2)}, u32[]{:S(2)}) collective-permute-start(bf16[128,576]{1,0:T(8,128)(2,1)S(1)} %get-tuple-element.31), channel_id=1, source_target_pairs={{0,4},{1,5},{2,6},{3,7},{4,0},{5,1},{6,2},{7,3},{8,12},{9,13},{10,... | collective-permute-start | bytes 442376 | tf_op jit(solution)/shard_map/ppermute | solution.py:247
  29.8 9.5 %collective-permute-start.11 = (bf16[128,576]{1,0:T(8,128)(2,1)S(1)}, bf16[128,576]{1,0:T(8,128)(2,1)S(1)}, u32[]{:S(2)}, u32[]{:S(2)}) collective-permute-start(bf16[128,576]{1,0:T(8,128)(2,1)S(1)} %get-tuple-element.32), channel_id=1, source_target_pairs={{0,5},{1,4},{2,7},{3,6},{4,1},{5,0},{6,3},{7,2},{8,13},{9,12},{10,... | collective-permute-start | bytes 442376 | tf_op jit(solution)/shard_map/ppermute | solution.py:247
  33.4 9.2 %collective-permute-start.12 = (bf16[128,576]{1,0:T(8,128)(2,1)S(1)}, bf16[128,576]{1,0:T(8,128)(2,1)S(1)}, u32[]{:S(2)}, u32[]{:S(2)}) collective-permute-start(bf16[128,576]{1,0:T(8,128)(2,1)S(1)} %get-tuple-element.33), channel_id=1, source_target_pairs={{0,6},{1,7},{2,4},{3,5},{4,2},{5,3},{6,0},{7,1},{8,14},{9,15},{10,... | collective-permute-start | bytes 442376 | tf_op jit(solution)/shard_map/ppermute | solution.py:247
  39.3 8.9 %collective-permute-start.13 = (bf16[128,576]{1,0:T(8,128)(2,1)S(1)}, bf16[128,576]{1,0:T(8,128)(2,1)S(1)}, u32[]{:S(2)}, u32[]{:S(2)}) collective-permute-start(bf16[128,576]{1,0:T(8,128)(2,1)S(1)} %get-tuple-element.34), channel_id=1, source_target_pairs={{0,7},{1,6},{2,5},{3,4},{4,3},{5,2},{6,1},{7,0},{8,15},{9,14},{10,... | collective-permute-start | bytes 442376 | tf_op jit(solution)/shard_map/ppermute | solution.py:247
  51.4 25.5 %collective-permute-start.14 = (bf16[7,128,576]{1,2,0:T(8,128)(2,1)}, bf16[7,128,576]{1,2,0:T(8,128)(2,1)}, u32[]{:S(2)}, u32[]{:S(2)}) collective-permute-start(bf16[7,128,576]{1,2,0:T(8,128)(2,1)} %copy.21), channel_id=1, source_target_pairs={{0,8},{8,0},{16,24},{24,16},{32,40},{40,32},{48,56},{56,48},{64,72... | collective-permute-start | bytes 3096584 | tf_op jit(solution)/shard_map/ppermute | solution.py:241
  51.6 13.8 %collective-permute-start.2 = (bf16[512,256]{1,0:T(8,128)(2,1)S(1)}, bf16[512,256]{1,0:T(8,128)(2,1)}, u32[]{:S(2)}, u32[]{:S(2)}) collective-permute-start(bf16[512,256]{1,0:T(8,128)(2,1)S(1)} %collective-permute-done.refs_0_), channel_id=1, source_target_pairs={{0,16},{8,24},{16,0},{24,8},{32,48},{40,56},{48,32},{56,40},{64,80... | collective-permute-start | bytes 786440 | tf_op jit(solution)/shard_map/ppermute | solution.py:241
  53.2 12.3 %collective-permute-start.15 = (bf16[512,256]{1,0:T(8,128)(2,1)S(1)}, bf16[512,256]{1,0:T(8,128)(2,1)}, u32[]{:S(2)}, u32[]{:S(2)}) collective-permute-start(bf16[512,256]{1,0:T(8,128)(2,1)S(1)} %collective-permute-done.refs_0_), channel_id=1, source_target_pairs={{0,32},{8,40},{16,48},{24,56},{32,64},{40,72},{48,80},{56,88},{64,... | collective-permute-start | bytes 786440 | tf_op jit(solution)/shard_map/ppermute | solution.py:244
  62.9 3.3 %collective-permute-start.6 = (bf16[512,256]{1,0:T(8,128)(2,1)S(1)}, bf16[512,256]{1,0:T(8,128)(2,1)S(1)}, u32[]{:S(2)}, u32[]{:S(2)}) collective-permute-start(bf16[512,256]{1,0:T(8,128)(2,1)S(1)} %collective-permute-done.5.refs_2_), channel_id=1, source_target_pairs={{0,8},{8,0},{16,24},{24,16},{32,40},{40,32},{48,56},{56,48},{64,72... | collective-permute-start | bytes 786440 | tf_op jit(solution)/shard_map/ppermute | solution.py:241
  64.9 9.6 %collective-permute-start.1 = (bf16[512,256]{1,0:T(8,128)(2,1)S(1)}, bf16[512,256]{1,0:T(8,128)(2,1)S(1)}, u32[]{:S(2)}, u32[]{:S(2)}) collective-permute-start(bf16[512,256]{1,0:T(8,128)(2,1)S(1)} %collective-permute-done.refs_0_), channel_id=1, source_target_pairs={{0,8},{8,0},{16,24},{24,16},{32,40},{40,32},{48,56},{56,48},{64,72... | collective-permute-start | bytes 786440 | tf_op jit(solution)/shard_map/ppermute | solution.py:241
  65.4 9.1 %collective-permute-start.3 = (bf16[512,256]{1,0:T(8,128)(2,1)}, bf16[512,256]{1,0:T(8,128)(2,1)S(1)}, u32[]{:S(2)}, u32[]{:S(2)}) collective-permute-start(bf16[512,256]{1,0:T(8,128)(2,1)} %collective-permute-done.2.refs_2_), channel_id=1, source_target_pairs={{0,8},{8,0},{16,24},{24,16},{32,40},{40,32},{48,56},{56,48},{64,72... | collective-permute-start | bytes 786440 | tf_op jit(solution)/shard_map/ppermute | solution.py:241
  65.5 9.0 %collective-permute-start.17 = (bf16[512,256]{1,0:T(8,128)(2,1)}, bf16[512,256]{1,0:T(8,128)(2,1)}, u32[]{:S(2)}, u32[]{:S(2)}) collective-permute-start(bf16[512,256]{1,0:T(8,128)(2,1)} %collective-permute-done.15.refs_0_), channel_id=1, source_target_pairs={{0,16},{8,24},{16,0},{24,8},{32,48},{40,56},{48,32},{56,40},{64,80... | collective-permute-start | bytes 786440 | tf_op jit(solution)/shard_map/ppermute | solution.py:241
  66.1 14.8 %collective-permute-start.16 = (bf16[512,256]{1,0:T(8,128)(2,1)}, bf16[512,256]{1,0:T(8,128)(2,1)}, u32[]{:S(2)}, u32[]{:S(2)}) collective-permute-start(bf16[512,256]{1,0:T(8,128)(2,1)} %collective-permute-done.15.refs_0_), channel_id=1, source_target_pairs={{0,8},{8,0},{16,24},{24,16},{32,40},{40,32},{48,56},{56,48},{64,72... | collective-permute-start | bytes 786440 | tf_op jit(solution)/shard_map/ppermute | solution.py:241
  74.5 6.5 %collective-permute-start.18 = (bf16[512,256]{1,0:T(8,128)(2,1)}, bf16[512,256]{1,0:T(8,128)(2,1)S(1)}, u32[]{:S(2)}, u32[]{:S(2)}) collective-permute-start(bf16[512,256]{1,0:T(8,128)(2,1)} %collective-permute-done.17.refs_2_), channel_id=1, source_target_pairs={{0,8},{8,0},{16,24},{24,16},{32,40},{40,32},{48,56},{56,48},{64,72... | collective-permute-start | bytes 786440 | tf_op jit(solution)/shard_map/ppermute | solution.py:241
  124.7 36.9 %copy-start.10 = (f32[576]{0:T(1024)S(1)}, f32[576]{0:T(1024)}, u32[]{:S(2)}) copy-start(f32[576]{0:T(1024)} %param.15) | copy-start | bytes 6916
  124.7 9.3 %collective-permute-start.22 = (bf16[512,256]{1,0:T(8,128)(2,1)S(1)}, bf16[512,256]{1,0:T(8,128)(2,1)S(1)}, u32[]{:S(2)}, u32[]{:S(2)}) collective-permute-start(bf16[512,256]{1,0:T(8,128)(2,1)S(1)} %reshape.41.refs_0_), channel_id=1, source_target_pairs={{0,4},{1,5},{2,6},{3,7},{4,0},{5,1},{6,2},{7,3},{8,12},{9,13},{10,... | collective-permute-start | bytes 786440 | tf_op jit(solution)/shard_map/ppermute | solution.py:247
  127.1 10.8 %collective-permute-start.20 = (bf16[512,256]{1,0:T(8,128)(2,1)S(1)}, bf16[512,256]{1,0:T(8,128)(2,1)S(1)}, u32[]{:S(2)}, u32[]{:S(2)}) collective-permute-start(bf16[512,256]{1,0:T(8,128)(2,1)S(1)} %reshape.41.refs_0_), channel_id=1, source_target_pairs={{0,2},{1,3},{2,0},{3,1},{4,6},{5,7},{6,4},{7,5},{8,10},{9,11},{10,... | collective-permute-start | bytes 786440 | tf_op jit(solution)/shard_map/ppermute | solution.py:247
  127.1 13.7 %collective-permute-start.19 = (bf16[512,256]{1,0:T(8,128)(2,1)S(1)}, bf16[512,256]{1,0:T(8,128)(2,1)S(1)}, u32[]{:S(2)}, u32[]{:S(2)}) collective-permute-start(bf16[512,256]{1,0:T(8,128)(2,1)S(1)} %reshape.41.refs_0_), channel_id=1, source_target_pairs={{0,1},{1,0},{2,3},{3,2},{4,5},{5,4},{6,7},{7,6},{8,9},{9,8},{10,11... | collective-permute-start | bytes 786440 | tf_op jit(solution)/shard_map/ppermute | solution.py:247
  128.0 13.6 %collective-permute-start.21 = (bf16[512,256]{1,0:T(8,128)(2,1)S(1)}, bf16[512,256]{1,0:T(8,128)(2,1)S(1)}, u32[]{:S(2)}, u32[]{:S(2)}) collective-permute-start(bf16[512,256]{1,0:T(8,128)(2,1)S(1)} %reshape.41.refs_0_), channel_id=1, source_target_pairs={{0,3},{1,2},{2,1},{3,0},{4,7},{5,6},{6,5},{7,4},{8,11},{9,10},{10,... | collective-permute-start | bytes 786440 | tf_op jit(solution)/shard_map/ppermute | solution.py:247
  134.0 10.4 %collective-permute-start.23 = (bf16[512,256]{1,0:T(8,128)(2,1)S(1)}, bf16[512,256]{1,0:T(8,128)(2,1)S(1)}, u32[]{:S(2)}, u32[]{:S(2)}) collective-permute-start(bf16[512,256]{1,0:T(8,128)(2,1)S(1)} %collective-permute-done.22.refs_4_), channel_id=1, source_target_pairs={{0,1},{1,0},{2,3},{3,2},{4,5},{5,4},{6,7},{7,6},{8,9},{9,8},{10,11... | collective-permute-start | bytes 786440 | tf_op jit(solution)/shard_map/ppermute | solution.py:247
  137.9 7.9 %collective-permute-start.24 = (bf16[512,256]{1,0:T(8,128)(2,1)S(1)}, bf16[512,256]{1,0:T(8,128)(2,1)S(1)}, u32[]{:S(2)}, u32[]{:S(2)}) collective-permute-start(bf16[512,256]{1,0:T(8,128)(2,1)S(1)} %collective-permute-done.20.refs_2_), channel_id=1, source_target_pairs={{0,4},{1,5},{2,6},{3,7},{4,0},{5,1},{6,2},{7,3},{8,12},{9,13},{10,... | collective-permute-start | bytes 786440 | tf_op jit(solution)/shard_map/ppermute | solution.py:247
  139.3 7.8 %collective-permute-start.25 = (bf16[512,256]{1,0:T(8,128)(2,1)S(1)}, bf16[512,256]{1,0:T(8,128)(2,1)S(1)}, u32[]{:S(2)}, u32[]{:S(2)}) collective-permute-start(bf16[512,256]{1,0:T(8,128)(2,1)S(1)} %collective-permute-done.22.refs_4_), channel_id=1, source_target_pairs={{0,3},{1,2},{2,1},{3,0},{4,7},{5,6},{6,5},{7,4},{8,11},{9,10},{10,... | collective-permute-start | bytes 786440 | tf_op jit(solution)/shard_map/ppermute | solution.py:247
  150.5 5.2 %collective-permute-start.26 = (f32[512]{0:T(512)S(1)}, f32[512]{0:T(512)S(1)}, u32[]{:S(2)}, u32[]{:S(2)}) collective-permute-start(f32[512]{0:T(512)S(1)} %reduce), channel_id=1, source_target_pairs={{0,4},{1,5},{2,6},{3,7},{4,0},{5,1},{6,2},{7,3},{8,12},{9,13},{10,... | collective-permute-start | bytes 6152 | tf_op jit(solution)/shard_map/ppermute | solution.py:247
  155.7 4.1 %collective-permute-start.27 = (f32[512]{0:T(512)S(1)}, f32[512]{0:T(512)S(1)}, u32[]{:S(2)}, u32[]{:S(2)}) collective-permute-start(f32[512]{0:T(512)S(1)} %add.79), channel_id=1, source_target_pairs={{0,1},{1,0},{2,3},{3,2},{4,5},{5,4},{6,7},{7,6},{8,9},{9,8},{10,11... | collective-permute-start | bytes 6152 | tf_op jit(solution)/shard_map/ppermute | solution.py:247
  155.7 4.8 %collective-permute-start.28 = (f32[512]{0:T(512)S(1)}, f32[512]{0:T(512)S(1)}, u32[]{:S(2)}, u32[]{:S(2)}) collective-permute-start(f32[512]{0:T(512)S(1)} %add.79), channel_id=1, source_target_pairs={{0,3},{1,2},{2,1},{3,0},{4,7},{5,6},{6,5},{7,4},{8,11},{9,10},{10,... | collective-permute-start | bytes 6152 | tf_op jit(solution)/shard_map/ppermute | solution.py:247
  156.5 5.1 %collective-permute-start.29 = (f32[512]{0:T(512)S(1)}, f32[512]{0:T(512)S(1)}, u32[]{:S(2)}, u32[]{:S(2)}) collective-permute-start(f32[512]{0:T(512)S(1)} %add.79), channel_id=1, source_target_pairs={{0,2},{1,3},{2,0},{3,1},{4,6},{5,7},{6,4},{7,5},{8,10},{9,11},{10,... | collective-permute-start | bytes 6152 | tf_op jit(solution)/shard_map/ppermute | solution.py:247
  (11 other events, 29.6 us)

commit v3 on v2

--- a/solution.py
+++ b/solution.py
@@ -20,20 +20,15 @@
 
 
 def project_kernel(scale, tile, count, x_hbm, g_ref, *refs):
-    w_hbms, out_ref, x_buf, w_buf, x_sems, w_sems = (
-        refs[:count],
-        refs[count],
-        refs[count + 1],
-        refs[count + 2],
-        refs[count + 3],
-        refs[count + 4],
-    )
-    tiles = x_buf.shape[0]
+    w_hbms, refs = refs[:count], refs[count:]
+    out_ref, x_buf, normed_buf, w_buf, x_sems, w_sems = refs
+    tiles = x_buf.shape[0] // tile
+
+    def span(i):
+        return pl.ds(pl.multiple_of(i * tile, tile), tile)
 
     def x_copy(i):
-        return pltpu.make_async_copy(
-            x_hbm.at[pl.ds(pl.multiple_of(i * tile, tile), tile)], x_buf.at[i], x_sems.at[i]
-        )
+        return pltpu.make_async_copy(x_hbm.at[span(i)], x_buf.at[span(i)], x_sems.at[i])
 
     width = w_buf.shape[1] // count
     w_copies = [
@@ -42,33 +37,30 @@
         )
         for j in range(count)
     ]
-    x_copy(0).start()
+    for i in range(tiles):
+        x_copy(i).start()
     for copy in w_copies:
         copy.start()
-    for i in range(1, tiles):
-        x_copy(i).start()
+    gain = g_ref[...].reshape(1, -1)
 
     @pl.loop(0, tiles)
     def _(i):
         x_copy(i).wait()
-        x = x_buf[i].astype(jnp.float32)
+        x = x_buf[span(i)].astype(jnp.float32)
         r = lax.rsqrt(jnp.mean(x * x, axis=1, keepdims=True) + norm_eps)
-        normed = (x * r * g_ref[...]).astype(jnp.bfloat16)
-
-        @pl.when(i == 0)
-        def _():
-            for copy in w_copies:
-                copy.wait()
-
-        done = jnp.dot(normed, w_buf[...], preferred_element_type=jnp.float32)
-        if scale is not None:
-            done = done * scale
-        out_ref[pl.ds(pl.multiple_of(i * tile, tile), tile), :] = done.astype(jnp.bfloat16)
+        normed_buf[span(i)] = (x * r * gain).astype(jnp.bfloat16)
+
+    for copy in w_copies:
+        copy.wait()
+    done = jnp.dot(normed_buf[...], w_buf[...], preferred_element_type=jnp.float32)
+    if scale is not None:
+        done = done * scale
+    out_ref[...] = done.astype(jnp.bfloat16)
 
 
 def project(tokens, gain, weights, scale, name, vmem):
     rows, d = tokens.shape
-    tile = 128
+    tile = 64
     count = len(weights)
     width = sum(w.shape[1] for w in weights)
     return pl.pallas_call(
@@ -78,7 +70,8 @@
         out_specs=pl.BlockSpec(memory_space=pltpu.VMEM),
         out_shape=jax.ShapeDtypeStruct((rows, width), jnp.bfloat16),
         scratch_shapes=[
-            pltpu.VMEM((rows // tile, tile, d), jnp.bfloat16),
+            pltpu.VMEM((rows, d), jnp.bfloat16),
+            pltpu.VMEM((rows, d), jnp.bfloat16),
             pltpu.VMEM((d, width), jnp.bfloat16),
             pltpu.SemaphoreType.DMA((rows // tile,)),
             pltpu.SemaphoreType.DMA((count,)),
@@ -193,23 +186,25 @@
 
 
 def out_kernel(parts, *refs):
-    w_ref, sum_ref, square_ref = refs[parts:]
-    total = jnp.dot(refs[0][...], w_ref[0], preferred_element_type=jnp.float32)
+    total = jnp.dot(refs[0][...], refs[parts][...], preferred_element_type=jnp.float32)
     for i in range(1, parts):
-        total = total + jnp.dot(refs[i][...], w_ref[i], preferred_element_type=jnp.float32)
-    sum_ref[...] = total
-    square_ref[...] = jnp.sum(total * total, axis=1, keepdims=True)
+        total = total + jnp.dot(
+            refs[i][...], refs[parts + i][...], preferred_element_type=jnp.float32
+        )
+    refs[2 * parts][...] = total
+    refs[2 * parts + 1][...] = jnp.sum(total * total, axis=1, keepdims=True)
 
 
 def out_project(heads, weights):
     rows, inner = heads[0].shape
-    parts, _, cols = weights.shape
+    cols = weights[0].shape[1]
+    parts = len(heads)
     tile = 256
     return pl.pallas_call(
         functools.partial(out_kernel, parts),
         grid=(rows // tile,),
         in_specs=[pl.BlockSpec((tile, inner), lambda i: (i, 0))] * parts
-        + [pl.BlockSpec(weights.shape, lambda i: (0, 0, 0), pipeline_mode=pl.Buffered(1))],
+        + [pl.BlockSpec((inner, cols), lambda i: (0, 0), pipeline_mode=pl.Buffered(1))] * parts,
         out_specs=[
             pl.BlockSpec((tile, cols), lambda i: (i, 0)),
             pl.BlockSpec((tile, 1), lambda i: (i, 0)),
@@ -223,7 +218,7 @@
             flops=2 * rows * inner * parts * cols, bytes_accessed=6 * 10**6, transcendentals=0
         ),
         name="out_project",
-    )(*heads, weights)
+    )(*heads, *weights)
 
 
 def local(n_ctx, n_tp, tokens, norm_gain, q_weight, k_weight, v_weight, o_weight, post_gain, doc_ids, plan):
@@ -233,9 +228,6 @@
     shard = lax.axis_index("ctx")
     group = lax.axis_index("tp")
     cols = o_weight.shape[1] // n_tp
-    inner = o_weight.shape[0]
-    half = inner // 2
-    core = shard % 2
 
     def ctx_xor(a, m):
         return lax.ppermute(a, "ctx", [(i, i ^ m) for i in range(n_ctx)])
@@ -246,15 +238,7 @@
     def tp_xor(a, m):
         return lax.ppermute(a, "tp", [(i, i ^ m) for i in range(n_tp)])
 
-    gain = norm_gain.reshape(1, -1)
-    own_kv = project(tokens, gain, [k_weight, v_weight], None, "project_kv", 56)
-
-    own_weight = lax.dynamic_slice_in_dim(o_weight, group * cols, cols, axis=1)
-    slices = [
-        lax.dynamic_slice(o_weight, (core * half, (group ^ m) * cols), (half, cols))
-        for m in range(1, n_tp)
-    ]
-    own_kv, slices = lax.optimization_barrier((own_kv, slices))
+    own_kv = project(tokens, norm_gain, [k_weight, v_weight], None, "project_kv", 56)
 
     kvs = []
     near = own_kv
@@ -262,15 +246,7 @@
         near = near if back == 0 else ctx_z(near, 1)
         across = ctx_xor(near, 2)
         kvs.append([near, ctx_xor(near, 1), across, ctx_xor(across, 1)])
-    mine = jnp.stack([tp_xor(w, m + 1) for m, w in enumerate(slices)])
-    theirs = ctx_xor(mine, 1)
-    even = core == 0
-    out_weights = jnp.concatenate(
-        [jnp.where(even, mine, theirs), jnp.where(even, theirs, mine)], axis=1
-    )
-    out_weights = jnp.concatenate([own_weight[None], out_weights], axis=0)
-
-    queries = project(tokens, gain, [q_weight], query_scale, "project_q", 40)
+    queries = project(tokens, norm_gain, [q_weight], query_scale, "project_q", 40)
 
     first_block = jnp.sum((doc_ids[None, :] < doc_ids[:, None]).astype(jnp.int32), axis=1)
     own_first = lax.dynamic_slice_in_dim(first_block, shard * blocks, blocks, 0)
@@ -288,7 +264,14 @@
     carry = []
     for stage in range(BACK):
         carry = attend(stage, info, queries, kvs[stage], carry)
+
+    out_weights = [
+        lax.dynamic_slice_in_dim(o_weight, (group ^ m) * cols, cols, axis=1) for m in range(n_tp)
+    ]
     carry, out_weights, picker = lax.optimization_barrier((carry, out_weights, picker))
+    first, second = (1, 2, 3, 4), (5, 6, 7)
+    for m in first:
+        out_weights[m] = tp_xor(out_weights[m], m)
     natural = attend(BACK, info, queries, kvs[BACK], carry)
 
     width = natural.shape[1]
@@ -296,6 +279,9 @@
     striped = natural.reshape(blocks, n_ctx, piece, width).transpose(1, 0, 2, 3)
     striped = striped.reshape(n_ctx, blocks, piece * width)
     gathered = lax.all_to_all(striped, "ctx", 0, 0, tiled=True)
+    gathered, out_weights = lax.optimization_barrier((gathered, out_weights))
+    for m in second:
+        out_weights[m] = tp_xor(out_weights[m], m)
     ordered = jnp.dot(
         picker,
         gathered.reshape(total_blocks, piece * width),
@@ -304,6 +290,7 @@
     placed = lax.all_to_all(
         ordered.reshape(n_ctx, blocks, piece * width), "ctx", 0, 0, tiled=True
     )
+    placed, out_weights = lax.optimization_barrier((placed, out_weights))
     placed = (
         placed.reshape(n_ctx, blocks, piece, width).transpose(1, 0, 2, 3).reshape(rows, width)
     )

time: 164 us -> 160 us (0.976); the launches traced: 164 us -> 157 us
  blocking collectives: 39.8 us -> 0 us
  waiting for transfers between devices: 40 us -> 68.8 us
  starting transfers between devices: 36.7 us -> 53.5 us
  local copies, waits for them, and re-layouts: 22 us -> 10.7 us
    all_to_all x2 -> x0, blocking collectives: 39.8 us -> none  [the longest x1 24.4 us: local(): gathered = lax.all_to_all(striped, 'ctx', 0, 0, tiled=True)]
    ppermute x18, waiting for transfers between devices: 34.2 us -> 53.2 us  [tp_xor(): return lax.ppermute(a, 'tp', [(i, i ^ m) for i in range(n_tp)])]
    all_to_all x0 -> x2, starting transfers between devices: none -> 15.8 us  [the longest x1 8.27 us: local(): lax.all_to_all(ordered.reshape(n_ctx, blocks, piece * width), 'ctx', 0, 0...]
    ppermute x2, waiting for transfers between devices: 0.01 us -> 12.4 us  [ctx_z(): lax.ppermute(a, 'ctx', [(i, (i + d * PLANE) % n_ctx) for i in range(n_ctx)])]
    unnamed x32 -> x34, local copies, waits for them, and re-layouts: 9.22 us -> 2.69 us
    another operation x2 -> x0, local copies, waits for them, and re-layouts: 3.15 us -> none  [local(): mine = jnp.stack([tp_xor(w, m + 1) for m, w in enumerate(slices)])]
    ppermute x10 -> x9, waiting for transfers between devices: 5.82 us -> 3.2 us  [ctx_xor(): return lax.ppermute(a, 'ctx', [(i, i ^ m) for i in range(n_ctx)])]
    dynamic_slice x1, local copies, waits for them, and re-layouts: 2.24 us -> 4.65 us  [local(): lax.dynamic_slice_in_dim(o_weight, (group ^ m) * cols, cols, axis=1)]
  transfers between devices with their start and end apart: 30 -> 31, of which waited for: 18 -> 18; matrix products, arithmetic and copies ran while one was open for 8% -> 4% of each run, Pallas kernels for 6% -> 7%
where the time goes in v3:
time: 160 us; the launch traced here: 157 us
  waiting for transfers between devices  68.8 us (43%)
  starting transfers between devices  53.5 us (33%)
  Pallas kernels  20.7 us (13%)
  local copies, waits for them, and re-layouts  10.7 us (7%)
  other arithmetic  2.4 us (2%)
    ppermute x18, waiting for transfers between devices, tp_xor(): return lax.ppermute(a, 'tp', [(i, i ^ m) for i in range(n_tp)])  53.2 us
    ppermute x18, starting transfers between devices, tp_xor(): return lax.ppermute(a, 'tp', [(i, i ^ m) for i in range(n_tp)])  31.4 us
    pallas_call x2, Pallas kernels, project(): pl.pallas_call(functools.partial(project_kernel, scale, tile, count), in_...  12.5 us
    ppermute x2, waiting for transfers between devices, ctx_z(): lax.ppermute(a, 'ctx', [(i, (i + d * PLANE) % n_ctx) for i in range(n_ctx)])  12.4 us
    all_to_all x1, starting transfers between devices, local(): lax.all_to_all(ordered.reshape(n_ctx, blocks, piece * width), 'ctx', 0, 0...  8.27 us
    all_to_all x1, starting transfers between devices, local(): gathered = lax.all_to_all(striped, 'ctx', 0, 0, tiled=True)  7.54 us
    ppermute x9, starting transfers between devices, ctx_xor(): return lax.ppermute(a, 'ctx', [(i, i ^ m) for i in range(n_ctx)])  6.08 us
    pallas_call x3, Pallas kernels, attend(): pl.pallas_call(functools.partial(attend_kernel, rows, stage), in_specs=[p...  6.07 us
  transfers between devices with their start and end apart: 31, of which 18 were waited for; matrix products, arithmetic and copies ran while one was open for 4% of the time, Pallas kernels for 7%

profile of v3, /device:TPU:2, one launch (start us, length us, event | category | flops | bytes accessed | tf_op | source)
XLA Modules:
  0.0 157.5 jit_solution(17189822518063959620)
XLA Ops:
  0.0 7.2 %project_kv.1.refs_0_ = bf16[512,256]{1,0:T(8,128)(2,1)} custom-call(bf16[512,4608]{1,0:T(8,128)(2,1)} %x_hbm.3, f32[4608]{0:T(1024)} %g_ref.3, bf16[4608,128]{1,0:T(8,128)(2,1)} %refs_0_.3, bf16[4608,128]{1,0:T(8,128)(2,1)} %refs_1_.1), custom_call_target="tpu_custom_call" | custom-call | flops 1207959552 | bytes 7077888 | tf_op jit(solution)/shard_map/project_kv/pallas_call | solution.py:66
  7.3 2.3 %collective-permute-start.5 = (bf16[512,256]{1,0:T(8,128)(2,1)}, bf16[512,256]{1,0:T(8,128)(2,1)S(1)}, u32[]{:S(2)}, u32[]{:S(2)}) collective-permute-start(bf16[512,256]{1,0:T(8,128)(2,1)} %project_kv.1.refs_0_), channel_id=1, source_target_pairs={{0,16},{8,24},{16,0},{24,8},{32,48},{40,56},{48,32},{56,40},{64,80... | collective-permute-start | bytes 786440 | tf_op jit(solution)/shard_map/ppermute | solution.py:233
  10.6 10.3 %collective-permute-done.refs_0_ = bf16[512,256]{1,0:T(8,128)(2,1)S(1)} collective-permute-done((bf16[512,256]{1,0:T(8,128)(2,1)}, bf16[512,256]{1,0:T(8,128)(2,1)S(1)}, u32[]{:S(2)}, u32[]{:S(2)}) %collective-permute-start) | collective-permute-done | bytes 262176 | tf_op jit(solution)/shard_map/ppermute | solution.py:236
  21.0 5.3 %project_q.1.q_ref = bf16[512,256]{1,0:T(8,128)(2,1)S(1)} custom-call(bf16[512,4608]{1,0:T(8,128)(2,1)S(1)} %copy-done, f32[4608]{0:T(1024)S(1)} %copy-done.8, bf16[4608,256]{1,0:T(8,128)(2,1)S(1)} %copy-done.1), custom_call_target="tpu_custom_call" | custom-call | flops 1207959552 | bytes 7077888 | tf_op jit(solution)/shard_map/project_q/pallas_call | solution.py:66
  28.2 2.1 %collective-permute-done.7.refs_0_ = bf16[512,256]{1,0:T(8,128)(2,1)S(1)} collective-permute-done((bf16[512,256]{1,0:T(8,128)(2,1)S(1)}, bf16[512,256]{1,0:T(8,128)(2,1)S(1)}, u32[]{:S(2)}, u32[]{:S(2)}) %collective-permute-start.7) | collective-permute-done | bytes 262176 | tf_op jit(solution)/shard_map/ppermute | solution.py:236
  31.8 4.6 %constant_dynamic-slice_fusion = (bf16[256,576]{1,0:T(8,128)(2,1)}, bf16[256,576]{1,0:T(8,128)(2,1)}, bf16[256,576]{1,0:T(8,128)(2,1)}, bf16[256,576]{1,0:T(8,12...) fusion(bf16[256,4608]{1,0:T(8,128)(2,1)} %param.14, ...), kind=kLoop, calls=%fused_computation.9 | loop fusion | bytes 4718624 | tf_op jit(solution)/shard_map/dynamic_slice | solution.py:269
  37.1 3.2 %collective-permute-done.9.refs_2_ = bf16[512,256]{1,0:T(8,128)(2,1)S(1)} collective-permute-done((bf16[512,256]{1,0:T(8,128)(2,1)S(1)}, bf16[512,256]{1,0:T(8,128)(2,1)S(1)}, u32[]{:S(2)}, u32[]{:S(2)}) %collective-permute-start.9) | collective-permute-done | bytes 262176 | tf_op jit(solution)/shard_map/ppermute | solution.py:233
  40.3 4.4 %attend.3 = (f32[2,512,128]{2,1,0:T(8,128)S(1)}, f32[2,512,128]{2,1,0:T(8,128)S(1)}) custom-call(s32[5]{0:T(128)S(1)} %pad_add_fusion.info_ref, bf16[512,256]{1,0:T(8,128)(2,1)S(1)} %project_q.1.q_ref, bf16[512,256]{1,0:T(8,128)(2,1)S(1)} %copy-done.6, bf16[512,256]{1,0:T(8,128)(2,1)} %collective-permute-done.4.refs_1_, ...), custom_call_target="tpu_custom_call" | custom-call | flops 2000000000 | bytes 4000000 | tf_op jit(solution)/shard_map/attend/pallas_call | solution.py:168
  47.6 7.5 %all-to-all-start = ((bf16[32,4,1024]{2,1,0:T(4,128)(2,1)}), bf16[32,4,1024]{2,1,0:T(4,128)(2,1)S(1)}, u32[]{:S(2)}, u32[]{:S(2)}) async-start(bf16[32,4,1024]{2,1,0:T(4,128)(2,1)} %copy.18), calls=%async_computation | async-start | bytes 524288 | tf_op jit(solution)/shard_map/all_to_all | solution.py:281
  56.9 2.9 %collective-permute-start.12 = (bf16[256,576]{1,0:T(8,128)(2,1)S(1)}, bf16[256,576]{1,0:T(8,128)(2,1)S(1)}, u32[]{:S(2)}, u32[]{:S(2)}) collective-permute-start(bf16[256,576]{1,0:T(8,128)(2,1)S(1)} %copy-done.13), channel_id=1, source_target_pairs={{0,2},{1,3},{2,0},{3,1},{4,6},{5,7},{6,4},{7,5},{8,10},{9,11},{10,... | collective-permute-start | bytes 884744 | tf_op jit(solution)/shard_map/ppermute | solution.py:239
  60.0 2.4 %collective-permute-start.14 = (bf16[256,576]{1,0:T(8,128)(2,1)S(1)}, bf16[256,576]{1,0:T(8,128)(2,1)S(1)}, u32[]{:S(2)}, u32[]{:S(2)}) collective-permute-start(bf16[256,576]{1,0:T(8,128)(2,1)S(1)} %copy-done.11), channel_id=1, source_target_pairs={{0,4},{1,5},{2,6},{3,7},{4,0},{5,1},{6,2},{7,3},{8,12},{9,13},{10,... | collective-permute-start | bytes 884744 | tf_op jit(solution)/shard_map/ppermute | solution.py:239
  62.4 3.7 %collective-permute-done.11.refs_9_ = bf16[256,576]{1,0:T(8,128)(2,1)S(1)} collective-permute-done((bf16[256,576]{1,0:T(8,128)(2,1)}, bf16[256,576]{1,0:T(8,128)(2,1)S(1)}, u32[]{:S(2)}, u32[]{:S(2)}) %collective-permute-start.11) | collective-permute-done | bytes 294944 | tf_op jit(solution)/shard_map/ppermute | solution.py:239
  66.0 8.8 %collective-permute-done.12.refs_10_ = bf16[256,576]{1,0:T(8,128)(2,1)S(1)} collective-permute-done((bf16[256,576]{1,0:T(8,128)(2,1)S(1)}, bf16[256,576]{1,0:T(8,128)(2,1)S(1)}, u32[]{:S(2)}, u32[]{:S(2)}) %collective-permute-start.12) | collective-permute-done | bytes 294944 | tf_op jit(solution)/shard_map/ppermute | solution.py:239
  74.8 2.4 %collective-permute-done.13.refs_11_ = bf16[256,576]{1,0:T(8,128)(2,1)S(1)} collective-permute-done((bf16[256,576]{1,0:T(8,128)(2,1)S(1)}, bf16[256,576]{1,0:T(8,128)(2,1)S(1)}, u32[]{:S(2)}, u32[]{:S(2)}) %collective-permute-start.13) | collective-permute-done | bytes 294944 | tf_op jit(solution)/shard_map/ppermute | solution.py:239
  79.1 8.3 %all-to-all-start.1 = ((bf16[32,4,1024]{2,1,0:T(4,128)(2,1)}), bf16[32,4,1024]{2,1,0:T(4,128)(2,1)S(1)}, u32[]{:S(2)}, u32[]{:S(2)}) async-start(bf16[32,4,1024]{2,1,0:T(4,128)(2,1)} %reshape.35), calls=%async_computation.1 | async-start | bytes 524288 | tf_op jit(solution)/shard_map/all_to_all | solution.py:290
  88.2 3.4 %collective-permute-start.16 = (bf16[256,576]{1,0:T(8,128)(2,1)S(1)}, bf16[256,576]{1,0:T(8,128)(2,1)S(1)}, u32[]{:S(2)}, u32[]{:S(2)}) collective-permute-start(bf16[256,576]{1,0:T(8,128)(2,1)S(1)} %copy-done.10), channel_id=1, source_target_pairs={{0,6},{1,7},{2,4},{3,5},{4,2},{5,3},{6,0},{7,1},{8,14},{9,15},{10,... | collective-permute-start | bytes 884744 | tf_op jit(solution)/shard_map/ppermute | solution.py:239
  91.6 4.8 %collective-permute-start.17 = (bf16[256,576]{1,0:T(8,128)(2,1)S(1)}, bf16[256,576]{1,0:T(8,128)(2,1)S(1)}, u32[]{:S(2)}, u32[]{:S(2)}) collective-permute-start(bf16[256,576]{1,0:T(8,128)(2,1)S(1)} %copy-done.9), channel_id=1, source_target_pairs={{0,7},{1,6},{2,5},{3,4},{4,3},{5,2},{6,1},{7,0},{8,15},{9,14},{10,... | collective-permute-start | bytes 884744 | tf_op jit(solution)/shard_map/ppermute | solution.py:239
  96.3 5.7 %collective-permute-done.15.refs_13_ = bf16[256,576]{1,0:T(8,128)(2,1)S(1)} collective-permute-done((bf16[256,576]{1,0:T(8,128)(2,1)}, bf16[256,576]{1,0:T(8,128)(2,1)S(1)}, u32[]{:S(2)}, u32[]{:S(2)}) %collective-permute-start.15) | collective-permute-done | bytes 294944 | tf_op jit(solution)/shard_map/ppermute | solution.py:239
  102.0 8.2 %collective-permute-done.16.refs_14_ = bf16[256,576]{1,0:T(8,128)(2,1)S(1)} collective-permute-done((bf16[256,576]{1,0:T(8,128)(2,1)S(1)}, bf16[256,576]{1,0:T(8,128)(2,1)S(1)}, u32[]{:S(2)}, u32[]{:S(2)}) %collective-permute-start.16) | collective-permute-done | bytes 294944 | tf_op jit(solution)/shard_map/ppermute | solution.py:239
  110.2 5.5 %collective-permute-done.17.refs_15_ = bf16[256,576]{1,0:T(8,128)(2,1)S(1)} collective-permute-done((bf16[256,576]{1,0:T(8,128)(2,1)S(1)}, bf16[256,576]{1,0:T(8,128)(2,1)S(1)}, u32[]{:S(2)}, u32[]{:S(2)}) %collective-permute-start.17) | collective-permute-done | bytes 294944 | tf_op jit(solution)/shard_map/ppermute | solution.py:239
  116.0 1.9 %collective-permute-start.21 = (bf16[512,256]{1,0:T(8,128)(2,1)S(1)}, bf16[512,256]{1,0:T(8,128)(2,1)S(1)}, u32[]{:S(2)}, u32[]{:S(2)}) collective-permute-start(bf16[512,256]{1,0:T(8,128)(2,1)S(1)} %reshape.37.refs_0_), channel_id=1, source_target_pairs={{0,4},{1,5},{2,6},{3,7},{4,0},{5,1},{6,2},{7,3},{8,12},{9,13},{10,... | collective-permute-start | bytes 786440 | tf_op jit(solution)/shard_map/ppermute | solution.py:239
  117.9 2.0 %collective-permute-start.19 = (bf16[512,256]{1,0:T(8,128)(2,1)S(1)}, bf16[512,256]{1,0:T(8,128)(2,1)S(1)}, u32[]{:S(2)}, u32[]{:S(2)}) collective-permute-start(bf16[512,256]{1,0:T(8,128)(2,1)S(1)} %reshape.37.refs_0_), channel_id=1, source_target_pairs={{0,2},{1,3},{2,0},{3,1},{4,6},{5,7},{6,4},{7,5},{8,10},{9,11},{10,... | collective-permute-start | bytes 786440 | tf_op jit(solution)/shard_map/ppermute | solution.py:239
  121.4 3.8 %collective-permute-done.21.refs_4_ = bf16[512,256]{1,0:T(8,128)(2,1)S(1)} collective-permute-done((bf16[512,256]{1,0:T(8,128)(2,1)S(1)}, bf16[512,256]{1,0:T(8,128)(2,1)S(1)}, u32[]{:S(2)}, u32[]{:S(2)}) %collective-permute-start.21) | collective-permute-done | bytes 262176 | tf_op jit(solution)/shard_map/ppermute | solution.py:239
  125.2 2.7 %collective-permute-start.24 = (bf16[512,256]{1,0:T(8,128)(2,1)S(1)}, bf16[512,256]{1,0:T(8,128)(2,1)S(1)}, u32[]{:S(2)}, u32[]{:S(2)}) collective-permute-start(bf16[512,256]{1,0:T(8,128)(2,1)S(1)} %collective-permute-done.21.refs_4_), channel_id=1, source_target_pairs={{0,3},{1,2},{2,1},{3,0},{4,7},{5,6},{6,5},{7,4},{8,11},{9,10},{10,... | collective-permute-start | bytes 786440 | tf_op jit(solution)/shard_map/ppermute | solution.py:239
  128.7 1.7 %collective-permute-start.23 = (bf16[512,256]{1,0:T(8,128)(2,1)S(1)}, bf16[512,256]{1,0:T(8,128)(2,1)S(1)}, u32[]{:S(2)}, u32[]{:S(2)}) collective-permute-start(bf16[512,256]{1,0:T(8,128)(2,1)S(1)} %collective-permute-done.19.refs_2_), channel_id=1, source_target_pairs={{0,4},{1,5},{2,6},{3,7},{4,0},{5,1},{6,2},{7,3},{8,12},{9,13},{10,... | collective-permute-start | bytes 786440 | tf_op jit(solution)/shard_map/ppermute | solution.py:239
  130.4 2.0 %collective-permute-done.20.refs_3_ = bf16[512,256]{1,0:T(8,128)(2,1)S(1)} collective-permute-done((bf16[512,256]{1,0:T(8,128)(2,1)S(1)}, bf16[512,256]{1,0:T(8,128)(2,1)S(1)}, u32[]{:S(2)}, u32[]{:S(2)}) %collective-permute-start.20) | collective-permute-done | bytes 262176 | tf_op jit(solution)/shard_map/ppermute | solution.py:239
  132.4 1.8 %collective-permute-done.18.refs_1_ = bf16[512,256]{1,0:T(8,128)(2,1)S(1)} collective-permute-done((bf16[512,256]{1,0:T(8,128)(2,1)S(1)}, bf16[512,256]{1,0:T(8,128)(2,1)S(1)}, u32[]{:S(2)}, u32[]{:S(2)}) %collective-permute-start.18) | collective-permute-done | bytes 262176 | tf_op jit(solution)/shard_map/ppermute | solution.py:239
  134.2 3.8 %collective-permute-done.24.refs_7_ = bf16[512,256]{1,0:T(8,128)(2,1)S(1)} collective-permute-done((bf16[512,256]{1,0:T(8,128)(2,1)S(1)}, bf16[512,256]{1,0:T(8,128)(2,1)S(1)}, u32[]{:S(2)}, u32[]{:S(2)}) %collective-permute-start.24) | collective-permute-done | bytes 262176 | tf_op jit(solution)/shard_map/ppermute | solution.py:239
  139.9 2.1 %out_project.1 = (f32[512,576]{1,0:T(8,128)S(1)}, f32[512,1]{1,0:T(8,128)S(1)}) custom-call(bf16[512,256]{1,0:T(8,128)(2,1)S(1)} %reshape.37.refs_0_, bf16[512,256]{1,0:T(8,128)(2,1)S(1)} %collective-permute-done.18.refs_1_, bf16[512,256]{1,0:T(8,128)(2,1)S(1)} %collective-permute-done.19.refs_2_, bf16[512,256]{1,0:T(8,128)(2,1)S(1)} %collective-permute-done.20.refs_3_, ...), custom_call_target="tpu_custom_call" | custom-call | flops 1207959552 | bytes 6000000 | tf_op jit(solution)/shard_map/out_project/pallas_call | solution.py:203
  143.9 1.9 %collective-permute-start.25 = (f32[512]{0:T(512)S(1)}, f32[512]{0:T(512)S(1)}, u32[]{:S(2)}, u32[]{:S(2)}) collective-permute-start(f32[512]{0:T(512)S(1)} %reduce), channel_id=1, source_target_pairs={{0,4},{1,5},{2,6},{3,7},{4,0},{5,1},{6,2},{7,3},{8,12},{9,13},{10,... | collective-permute-start | bytes 6152 | tf_op jit(solution)/shard_map/ppermute | solution.py:239
  145.7 3.3 %collective-permute-done.25 = f32[512]{0:T(512)S(1)} collective-permute-done((f32[512]{0:T(512)S(1)}, f32[512]{0:T(512)S(1)}, u32[]{:S(2)}, u32[]{:S(2)}) %collective-permute-start.25) | collective-permute-done | bytes 2080 | tf_op jit(solution)/shard_map/ppermute | solution.py:239
  149.0 1.9 %collective-permute-start.28 = (f32[512]{0:T(512)S(1)}, f32[512]{0:T(512)S(1)}, u32[]{:S(2)}, u32[]{:S(2)}) collective-permute-start(f32[512]{0:T(512)S(1)} %add.65), channel_id=1, source_target_pairs={{0,2},{1,3},{2,0},{3,1},{4,6},{5,7},{6,4},{7,5},{8,10},{9,11},{10,... | collective-permute-start | bytes 6152 | tf_op jit(solution)/shard_map/ppermute | solution.py:239
  (91 shorter events, 25.3 us)
Async XLA Ops:
  7.3 20.9 %collective-permute-start.5 = (bf16[512,256]{1,0:T(8,128)(2,1)}, bf16[512,256]{1,0:T(8,128)(2,1)S(1)}, u32[]{:S(2)}, u32[]{:S(2)}) collective-permute-start(bf16[512,256]{1,0:T(8,128)(2,1)} %project_kv.1.refs_0_), channel_id=1, source_target_pairs={{0,16},{8,24},{16,0},{24,8},{32,48},{40,56},{48,32},{56,40},{64,80... | collective-permute-start | bytes 786440 | tf_op jit(solution)/shard_map/ppermute | solution.py:233
  9.6 27.4 %collective-permute-start.4 = (bf16[512,256]{1,0:T(8,128)(2,1)}, bf16[512,256]{1,0:T(8,128)(2,1)}, u32[]{:S(2)}, u32[]{:S(2)}) collective-permute-start(bf16[512,256]{1,0:T(8,128)(2,1)} %project_kv.1.refs_0_), channel_id=1, source_target_pairs={{0,8},{8,0},{16,24},{24,16},{32,40},{40,32},{48,56},{56,48},{64,72... | collective-permute-start | bytes 786440 | tf_op jit(solution)/shard_map/ppermute | solution.py:233
  9.6 11.3 %collective-permute-start = (bf16[512,256]{1,0:T(8,128)(2,1)}, bf16[512,256]{1,0:T(8,128)(2,1)S(1)}, u32[]{:S(2)}, u32[]{:S(2)}) collective-permute-start(bf16[512,256]{1,0:T(8,128)(2,1)} %project_kv.1.refs_0_), channel_id=1, source_target_pairs={{0,32},{8,40},{16,48},{24,56},{32,64},{40,72},{48,80},{56,88},{64,... | collective-permute-start | bytes 786440 | tf_op jit(solution)/shard_map/ppermute | solution.py:236
  20.9 9.3 %collective-permute-start.7 = (bf16[512,256]{1,0:T(8,128)(2,1)S(1)}, bf16[512,256]{1,0:T(8,128)(2,1)S(1)}, u32[]{:S(2)}, u32[]{:S(2)}) collective-permute-start(bf16[512,256]{1,0:T(8,128)(2,1)S(1)} %collective-permute-done.refs_0_), channel_id=1, source_target_pairs={{0,32},{8,40},{16,48},{24,56},{32,64},{40,72},{48,80},{56,88},{64,... | collective-permute-start | bytes 786440 | tf_op jit(solution)/shard_map/ppermute | solution.py:236
  26.5 9.9 %collective-permute-start.2 = (bf16[512,256]{1,0:T(8,128)(2,1)S(1)}, bf16[512,256]{1,0:T(8,128)(2,1)S(1)}, u32[]{:S(2)}, u32[]{:S(2)}) collective-permute-start(bf16[512,256]{1,0:T(8,128)(2,1)S(1)} %collective-permute-done.refs_0_), channel_id=1, source_target_pairs={{0,16},{8,24},{16,0},{24,8},{32,48},{40,56},{48,32},{56,40},{64,80... | collective-permute-start | bytes 786440 | tf_op jit(solution)/shard_map/ppermute | solution.py:233
  28.1 12.2 %collective-permute-start.6 = (bf16[512,256]{1,0:T(8,128)(2,1)S(1)}, bf16[512,256]{1,0:T(8,128)(2,1)S(1)}, u32[]{:S(2)}, u32[]{:S(2)}) collective-permute-start(bf16[512,256]{1,0:T(8,128)(2,1)S(1)} %collective-permute-done.5.refs_2_), channel_id=1, source_target_pairs={{0,8},{8,0},{16,24},{24,16},{32,40},{40,32},{48,56},{56,48},{64,72... | collective-permute-start | bytes 786440 | tf_op jit(solution)/shard_map/ppermute | solution.py:233
  30.3 10.0 %collective-permute-start.9 = (bf16[512,256]{1,0:T(8,128)(2,1)S(1)}, bf16[512,256]{1,0:T(8,128)(2,1)S(1)}, u32[]{:S(2)}, u32[]{:S(2)}) collective-permute-start(bf16[512,256]{1,0:T(8,128)(2,1)S(1)} %collective-permute-done.7.refs_0_), channel_id=1, source_target_pairs={{0,16},{8,24},{16,0},{24,8},{32,48},{40,56},{48,32},{56,40},{64,80... | collective-permute-start | bytes 786440 | tf_op jit(solution)/shard_map/ppermute | solution.py:233
  36.4 8.3 %collective-permute-start.1 = (bf16[512,256]{1,0:T(8,128)(2,1)S(1)}, bf16[512,256]{1,0:T(8,128)(2,1)S(1)}, u32[]{:S(2)}, u32[]{:S(2)}) collective-permute-start(bf16[512,256]{1,0:T(8,128)(2,1)S(1)} %collective-permute-done.refs_0_), channel_id=1, source_target_pairs={{0,8},{8,0},{16,24},{24,16},{32,40},{40,32},{48,56},{56,48},{64,72... | collective-permute-start | bytes 786440 | tf_op jit(solution)/shard_map/ppermute | solution.py:233
  36.4 8.3 %collective-permute-start.3 = (bf16[512,256]{1,0:T(8,128)(2,1)S(1)}, bf16[512,256]{1,0:T(8,128)(2,1)S(1)}, u32[]{:S(2)}, u32[]{:S(2)}) collective-permute-start(bf16[512,256]{1,0:T(8,128)(2,1)S(1)} %collective-permute-done.2.refs_2_), channel_id=1, source_target_pairs={{0,8},{8,0},{16,24},{24,16},{32,40},{40,32},{48,56},{56,48},{64,72... | collective-permute-start | bytes 786440 | tf_op jit(solution)/shard_map/ppermute | solution.py:233
  37.0 8.5 %collective-permute-start.8 = (bf16[512,256]{1,0:T(8,128)(2,1)S(1)}, bf16[512,256]{1,0:T(8,128)(2,1)S(1)}, u32[]{:S(2)}, u32[]{:S(2)}) collective-permute-start(bf16[512,256]{1,0:T(8,128)(2,1)S(1)} %collective-permute-done.7.refs_0_), channel_id=1, source_target_pairs={{0,8},{8,0},{16,24},{24,16},{32,40},{40,32},{48,56},{56,48},{64,72... | collective-permute-start | bytes 786440 | tf_op jit(solution)/shard_map/ppermute | solution.py:233
  40.3 5.2 %collective-permute-start.10 = (bf16[512,256]{1,0:T(8,128)(2,1)S(1)}, bf16[512,256]{1,0:T(8,128)(2,1)S(1)}, u32[]{:S(2)}, u32[]{:S(2)}) collective-permute-start(bf16[512,256]{1,0:T(8,128)(2,1)S(1)} %collective-permute-done.9.refs_2_), channel_id=1, source_target_pairs={{0,8},{8,0},{16,24},{24,16},{32,40},{40,32},{48,56},{56,48},{64,72... | collective-permute-start | bytes 786440 | tf_op jit(solution)/shard_map/ppermute | solution.py:233
  47.6 43.9 %copy-start.9 = (bf16[256,576]{1,0:T(8,128)(2,1)S(1)}, bf16[256,576]{1,0:T(8,128)(2,1)}, u32[]{:S(2)}) copy-start(bf16[256,576]{1,0:T(8,128)(2,1)} %get-tuple-element.63) | copy-start | bytes 884740
  47.6 29.6 %all-to-all-start = ((bf16[32,4,1024]{2,1,0:T(4,128)(2,1)}), bf16[32,4,1024]{2,1,0:T(4,128)(2,1)S(1)}, u32[]{:S(2)}, u32[]{:S(2)}) async-start(bf16[32,4,1024]{2,1,0:T(4,128)(2,1)} %copy.18), calls=%async_computation | async-start | bytes 524288 | tf_op jit(solution)/shard_map/all_to_all | solution.py:281
  55.2 10.9 %collective-permute-start.11 = (bf16[256,576]{1,0:T(8,128)(2,1)}, bf16[256,576]{1,0:T(8,128)(2,1)S(1)}, u32[]{:S(2)}, u32[]{:S(2)}) collective-permute-start(bf16[256,576]{1,0:T(8,128)(2,1)} %get-tuple-element.48), channel_id=1, source_target_pairs={{0,1},{1,0},{2,3},{3,2},{4,5},{5,4},{6,7},{7,6},{8,9},{9,8},{10,11... | collective-permute-start | bytes 884744 | tf_op jit(solution)/shard_map/ppermute | solution.py:239
  56.9 18.0 %collective-permute-start.12 = (bf16[256,576]{1,0:T(8,128)(2,1)S(1)}, bf16[256,576]{1,0:T(8,128)(2,1)S(1)}, u32[]{:S(2)}, u32[]{:S(2)}) collective-permute-start(bf16[256,576]{1,0:T(8,128)(2,1)S(1)} %copy-done.13), channel_id=1, source_target_pairs={{0,2},{1,3},{2,0},{3,1},{4,6},{5,7},{6,4},{7,5},{8,10},{9,11},{10,... | collective-permute-start | bytes 884744 | tf_op jit(solution)/shard_map/ppermute | solution.py:239
  59.8 17.4 %collective-permute-start.13 = (bf16[256,576]{1,0:T(8,128)(2,1)S(1)}, bf16[256,576]{1,0:T(8,128)(2,1)S(1)}, u32[]{:S(2)}, u32[]{:S(2)}) collective-permute-start(bf16[256,576]{1,0:T(8,128)(2,1)S(1)} %copy-done.12), channel_id=1, source_target_pairs={{0,3},{1,2},{2,1},{3,0},{4,7},{5,6},{6,5},{7,4},{8,11},{9,10},{10,... | collective-permute-start | bytes 884744 | tf_op jit(solution)/shard_map/ppermute | solution.py:239
  60.0 17.2 %collective-permute-start.14 = (bf16[256,576]{1,0:T(8,128)(2,1)S(1)}, bf16[256,576]{1,0:T(8,128)(2,1)S(1)}, u32[]{:S(2)}, u32[]{:S(2)}) collective-permute-start(bf16[256,576]{1,0:T(8,128)(2,1)S(1)} %copy-done.11), channel_id=1, source_target_pairs={{0,4},{1,5},{2,6},{3,7},{4,0},{5,1},{6,2},{7,3},{8,12},{9,13},{10,... | collective-permute-start | bytes 884744 | tf_op jit(solution)/shard_map/ppermute | solution.py:239
  79.1 36.7 %all-to-all-start.1 = ((bf16[32,4,1024]{2,1,0:T(4,128)(2,1)}), bf16[32,4,1024]{2,1,0:T(4,128)(2,1)S(1)}, u32[]{:S(2)}, u32[]{:S(2)}) async-start(bf16[32,4,1024]{2,1,0:T(4,128)(2,1)} %reshape.35), calls=%async_computation.1 | async-start | bytes 524288 | tf_op jit(solution)/shard_map/all_to_all | solution.py:290
  87.3 14.7 %collective-permute-start.15 = (bf16[256,576]{1,0:T(8,128)(2,1)}, bf16[256,576]{1,0:T(8,128)(2,1)S(1)}, u32[]{:S(2)}, u32[]{:S(2)}) collective-permute-start(bf16[256,576]{1,0:T(8,128)(2,1)} %get-tuple-element.61), channel_id=1, source_target_pairs={{0,5},{1,4},{2,7},{3,6},{4,1},{5,0},{6,3},{7,2},{8,13},{9,12},{10,... | collective-permute-start | bytes 884744 | tf_op jit(solution)/shard_map/ppermute | solution.py:239
  88.2 22.0 %collective-permute-start.16 = (bf16[256,576]{1,0:T(8,128)(2,1)S(1)}, bf16[256,576]{1,0:T(8,128)(2,1)S(1)}, u32[]{:S(2)}, u32[]{:S(2)}) collective-permute-start(bf16[256,576]{1,0:T(8,128)(2,1)S(1)} %copy-done.10), channel_id=1, source_target_pairs={{0,6},{1,7},{2,4},{3,5},{4,2},{5,3},{6,0},{7,1},{8,14},{9,15},{10,... | collective-permute-start | bytes 884744 | tf_op jit(solution)/shard_map/ppermute | solution.py:239
  91.6 24.1 %collective-permute-start.17 = (bf16[256,576]{1,0:T(8,128)(2,1)S(1)}, bf16[256,576]{1,0:T(8,128)(2,1)S(1)}, u32[]{:S(2)}, u32[]{:S(2)}) collective-permute-start(bf16[256,576]{1,0:T(8,128)(2,1)S(1)} %copy-done.9), channel_id=1, source_target_pairs={{0,7},{1,6},{2,5},{3,4},{4,3},{5,2},{6,1},{7,0},{8,15},{9,14},{10,... | collective-permute-start | bytes 884744 | tf_op jit(solution)/shard_map/ppermute | solution.py:239
  116.0 9.2 %collective-permute-start.21 = (bf16[512,256]{1,0:T(8,128)(2,1)S(1)}, bf16[512,256]{1,0:T(8,128)(2,1)S(1)}, u32[]{:S(2)}, u32[]{:S(2)}) collective-permute-start(bf16[512,256]{1,0:T(8,128)(2,1)S(1)} %reshape.37.refs_0_), channel_id=1, source_target_pairs={{0,4},{1,5},{2,6},{3,7},{4,0},{5,1},{6,2},{7,3},{8,12},{9,13},{10,... | collective-permute-start | bytes 786440 | tf_op jit(solution)/shard_map/ppermute | solution.py:239
  117.9 10.8 %collective-permute-start.19 = (bf16[512,256]{1,0:T(8,128)(2,1)S(1)}, bf16[512,256]{1,0:T(8,128)(2,1)S(1)}, u32[]{:S(2)}, u32[]{:S(2)}) collective-permute-start(bf16[512,256]{1,0:T(8,128)(2,1)S(1)} %reshape.37.refs_0_), channel_id=1, source_target_pairs={{0,2},{1,3},{2,0},{3,1},{4,6},{5,7},{6,4},{7,5},{8,10},{9,11},{10,... | collective-permute-start | bytes 786440 | tf_op jit(solution)/shard_map/ppermute | solution.py:239
  119.9 12.5 %collective-permute-start.20 = (bf16[512,256]{1,0:T(8,128)(2,1)S(1)}, bf16[512,256]{1,0:T(8,128)(2,1)S(1)}, u32[]{:S(2)}, u32[]{:S(2)}) collective-permute-start(bf16[512,256]{1,0:T(8,128)(2,1)S(1)} %reshape.37.refs_0_), channel_id=1, source_target_pairs={{0,3},{1,2},{2,1},{3,0},{4,7},{5,6},{6,5},{7,4},{8,11},{9,10},{10,... | collective-permute-start | bytes 786440 | tf_op jit(solution)/shard_map/ppermute | solution.py:239
  120.6 13.6 %collective-permute-start.18 = (bf16[512,256]{1,0:T(8,128)(2,1)S(1)}, bf16[512,256]{1,0:T(8,128)(2,1)S(1)}, u32[]{:S(2)}, u32[]{:S(2)}) collective-permute-start(bf16[512,256]{1,0:T(8,128)(2,1)S(1)} %reshape.37.refs_0_), channel_id=1, source_target_pairs={{0,1},{1,0},{2,3},{3,2},{4,5},{5,4},{6,7},{7,6},{8,9},{9,8},{10,11... | collective-permute-start | bytes 786440 | tf_op jit(solution)/shard_map/ppermute | solution.py:239
  125.2 12.8 %collective-permute-start.24 = (bf16[512,256]{1,0:T(8,128)(2,1)S(1)}, bf16[512,256]{1,0:T(8,128)(2,1)S(1)}, u32[]{:S(2)}, u32[]{:S(2)}) collective-permute-start(bf16[512,256]{1,0:T(8,128)(2,1)S(1)} %collective-permute-done.21.refs_4_), channel_id=1, source_target_pairs={{0,3},{1,2},{2,1},{3,0},{4,7},{5,6},{6,5},{7,4},{8,11},{9,10},{10,... | collective-permute-start | bytes 786440 | tf_op jit(solution)/shard_map/ppermute | solution.py:239
  127.9 10.1 %collective-permute-start.22 = (bf16[512,256]{1,0:T(8,128)(2,1)S(1)}, bf16[512,256]{1,0:T(8,128)(2,1)S(1)}, u32[]{:S(2)}, u32[]{:S(2)}) collective-permute-start(bf16[512,256]{1,0:T(8,128)(2,1)S(1)} %collective-permute-done.21.refs_4_), channel_id=1, source_target_pairs={{0,1},{1,0},{2,3},{3,2},{4,5},{5,4},{6,7},{7,6},{8,9},{9,8},{10,11... | collective-permute-start | bytes 786440 | tf_op jit(solution)/shard_map/ppermute | solution.py:239
  128.7 9.3 %collective-permute-start.23 = (bf16[512,256]{1,0:T(8,128)(2,1)S(1)}, bf16[512,256]{1,0:T(8,128)(2,1)S(1)}, u32[]{:S(2)}, u32[]{:S(2)}) collective-permute-start(bf16[512,256]{1,0:T(8,128)(2,1)S(1)} %collective-permute-done.19.refs_2_), channel_id=1, source_target_pairs={{0,4},{1,5},{2,6},{3,7},{4,0},{5,1},{6,2},{7,3},{8,12},{9,13},{10,... | collective-permute-start | bytes 786440 | tf_op jit(solution)/shard_map/ppermute | solution.py:239
  143.9 5.2 %collective-permute-start.25 = (f32[512]{0:T(512)S(1)}, f32[512]{0:T(512)S(1)}, u32[]{:S(2)}, u32[]{:S(2)}) collective-permute-start(f32[512]{0:T(512)S(1)} %reduce), channel_id=1, source_target_pairs={{0,4},{1,5},{2,6},{3,7},{4,0},{5,1},{6,2},{7,3},{8,12},{9,13},{10,... | collective-permute-start | bytes 6152 | tf_op jit(solution)/shard_map/ppermute | solution.py:239
  149.0 5.1 %collective-permute-start.28 = (f32[512]{0:T(512)S(1)}, f32[512]{0:T(512)S(1)}, u32[]{:S(2)}, u32[]{:S(2)}) collective-permute-start(f32[512]{0:T(512)S(1)} %add.65), channel_id=1, source_target_pairs={{0,2},{1,3},{2,0},{3,1},{4,6},{5,7},{6,4},{7,5},{8,10},{9,11},{10,... | collective-permute-start | bytes 6152 | tf_op jit(solution)/shard_map/ppermute | solution.py:239
  150.9 4.8 %collective-permute-start.27 = (f32[512]{0:T(512)S(1)}, f32[512]{0:T(512)S(1)}, u32[]{:S(2)}, u32[]{:S(2)}) collective-permute-start(f32[512]{0:T(512)S(1)} %add.65), channel_id=1, source_target_pairs={{0,3},{1,2},{2,1},{3,0},{4,7},{5,6},{6,5},{7,4},{8,11},{9,10},{10,... | collective-permute-start | bytes 6152 | tf_op jit(solution)/shard_map/ppermute | solution.py:239
  152.6 3.6 %collective-permute-start.26 = (f32[512]{0:T(512)S(1)}, f32[512]{0:T(512)S(1)}, u32[]{:S(2)}, u32[]{:S(2)}) collective-permute-start(f32[512]{0:T(512)S(1)} %add.65), channel_id=1, source_target_pairs={{0,1},{1,0},{2,3},{3,2},{4,5},{5,4},{6,7},{7,6},{8,9},{9,8},{10,11... | collective-permute-start | bytes 6152 | tf_op jit(solution)/shard_map/ppermute | solution.py:239
  (16 other events, 271.3 us)

commit v4 on v3

--- a/solution.py
+++ b/solution.py
@@ -19,9 +19,11 @@
 LOG2E = math.log2(math.e)
 
 
-def project_kernel(scale, tile, count, x_hbm, g_ref, *refs):
+def project_kernel(scale, tile, count, parts, core_ref, x_hbm, g_ref, *refs):
     w_hbms, refs = refs[:count], refs[count:]
-    out_ref, x_buf, normed_buf, w_buf, x_sems, w_sems = refs
+    o_hbm, refs = (refs[0], refs[1:]) if parts else (None, refs)
+    out_ref, cut_refs, refs = refs[0], refs[1 : 1 + parts // 2], refs[1 + parts // 2 :]
+    x_buf, normed_buf, w_buf, x_sems, w_sems, *cut_sems = refs
     tiles = x_buf.shape[0] // tile
 
     def span(i):
@@ -41,6 +43,24 @@
         x_copy(i).start()
     for copy in w_copies:
         copy.start()
+    cuts = []
+    if parts:
+        core, group = core_ref[0], core_ref[1]
+        half, wide = cut_refs[0].shape[1:]
+        cols = o_hbm.shape[1] // parts
+        for m in range(parts):
+            first = lax.div((group ^ m) * cols, HD) * HD
+            cuts.append(
+                pltpu.make_async_copy(
+                    o_hbm.at[
+                        pl.ds(pl.multiple_of(core * half, half), half),
+                        pl.ds(pl.multiple_of(first, HD), wide),
+                    ],
+                    cut_refs[m % (parts // 2)].at[m // (parts // 2)],
+                    cut_sems[0].at[m],
+                )
+            )
+            cuts[-1].start()
     gain = g_ref[...].reshape(1, -1)
 
     @pl.loop(0, tiles)
@@ -56,32 +76,47 @@
     if scale is not None:
         done = done * scale
     out_ref[...] = done.astype(jnp.bfloat16)
-
-
-def project(tokens, gain, weights, scale, name, vmem):
+    for copy in cuts:
+        copy.wait()
+
+
+def project(core, tokens, gain, weights, scale, name, o_weight=None, parts=0):
     rows, d = tokens.shape
     tile = 64
     count = len(weights)
     width = sum(w.shape[1] for w in weights)
+    anywhere = pl.BlockSpec(memory_space=pl.ANY)
+    whole = pl.BlockSpec(memory_space=pltpu.VMEM)
+    out_specs = [whole]
+    out_shape = [jax.ShapeDtypeStruct((rows, width), jnp.bfloat16)]
+    sems = [pltpu.SemaphoreType.DMA((rows // tile,)), pltpu.SemaphoreType.DMA((count,))]
+    operands = [core, tokens, gain, *weights]
+    if parts:
+        wide = -(-(o_weight.shape[1] // parts) // HD) * HD
+        out_specs += [whole] * (parts // 2)
+        out_shape += [
+            jax.ShapeDtypeStruct((2, o_weight.shape[0] // 2, wide), jnp.bfloat16)
+        ] * (parts // 2)
+        sems.append(pltpu.SemaphoreType.DMA((parts,)))
+        operands.append(o_weight)
     return pl.pallas_call(
-        functools.partial(project_kernel, scale, tile, count),
-        in_specs=[pl.BlockSpec(memory_space=pl.ANY), pl.BlockSpec(memory_space=pltpu.VMEM)]
-        + [pl.BlockSpec(memory_space=pl.ANY)] * count,
-        out_specs=pl.BlockSpec(memory_space=pltpu.VMEM),
-        out_shape=jax.ShapeDtypeStruct((rows, width), jnp.bfloat16),
+        functools.partial(project_kernel, scale, tile, count, parts),
+        in_specs=[pl.BlockSpec(memory_space=pltpu.SMEM), anywhere, whole]
+        + [anywhere] * (len(operands) - 3),
+        out_specs=out_specs,
+        out_shape=out_shape,
         scratch_shapes=[
             pltpu.VMEM((rows, d), jnp.bfloat16),
             pltpu.VMEM((rows, d), jnp.bfloat16),
             pltpu.VMEM((d, width), jnp.bfloat16),
-            pltpu.SemaphoreType.DMA((rows // tile,)),
-            pltpu.SemaphoreType.DMA((count,)),
-        ],
-        compiler_params=pltpu.CompilerParams(vmem_limit_bytes=vmem * 2**20),
+        ]
+        + sems,
+        compiler_params=pltpu.CompilerParams(vmem_limit_bytes=56 * 2**20),
         cost_estimate=pl.CostEstimate(
             flops=2 * rows * d * width, bytes_accessed=2 * d * (rows + width), transcendentals=0
         ),
         name=name,
-    )(tokens, gain, *weights)
+    )(*operands)
 
 
 def attend_kernel(rows, stage, info_ref, q_ref, *refs):
@@ -185,40 +220,63 @@
     )(info, q, *kvs, *carry)
 
 
-def out_kernel(parts, *refs):
-    total = jnp.dot(refs[0][...], refs[parts][...], preferred_element_type=jnp.float32)
-    for i in range(1, parts):
-        total = total + jnp.dot(
-            refs[i][...], refs[parts + i][...], preferred_element_type=jnp.float32
+def out_kernel(parts, cols, info_ref, *refs):
+    count = 4
+    w_refs, head_refs, (sum_ref, square_ref, lhs) = (
+        refs[:count],
+        refs[count : count + parts],
+        refs[count + parts :],
+    )
+    core, group = info_ref[0], info_ref[1]
+    groups, half, wide = w_refs[0].shape
+    for m in range(parts):
+        for i, side in enumerate((core, 1 - core)):
+            span = pl.ds(pl.multiple_of(side * half, half), half)
+            lhs[2 * i + m // groups, :, m % groups * half : (m % groups + 1) * half] = (
+                head_refs[m][:, span]
+            )
+    total = None
+    for i in range(count):
+        product = jnp.dot(
+            lhs[i],
+            w_refs[i][...].reshape(groups * half, wide),
+            preferred_element_type=jnp.float32,
         )
-    refs[2 * parts][...] = total
-    refs[2 * parts + 1][...] = jnp.sum(total * total, axis=1, keepdims=True)
-
-
-def out_project(heads, weights):
+        total = product if total is None else total + product
+    total = jnp.where(group % 2 == 1, total[:, wide - cols :], total[:, :cols])
+    sum_ref[...] = total
+    square = total * total
+    high = square.astype(jnp.bfloat16)
+    low = (square - high.astype(jnp.float32)).astype(jnp.bfloat16)
+    ones = jnp.ones((16, cols), jnp.bfloat16)
+    sums = None
+    for part in (high, low):
+        product = lax.dot_general(
+            ones, part, (((1,), (1,)), ((), ())), preferred_element_type=jnp.float32
+        )
+        sums = product if sums is None else sums + product
+    square_ref[...] = sums[:1]
+
+
+def out_project(info, heads, weights, cols):
     rows, inner = heads[0].shape
-    cols = weights[0].shape[1]
     parts = len(heads)
-    tile = 256
+    whole = pl.BlockSpec(memory_space=pltpu.VMEM)
     return pl.pallas_call(
-        functools.partial(out_kernel, parts),
-        grid=(rows // tile,),
-        in_specs=[pl.BlockSpec((tile, inner), lambda i: (i, 0))] * parts
-        + [pl.BlockSpec((inner, cols), lambda i: (0, 0), pipeline_mode=pl.Buffered(1))] * parts,
-        out_specs=[
-            pl.BlockSpec((tile, cols), lambda i: (i, 0)),
-            pl.BlockSpec((tile, 1), lambda i: (i, 0)),
-        ],
+        functools.partial(out_kernel, parts, cols),
+        in_specs=[pl.BlockSpec(memory_space=pltpu.SMEM)] + [whole] * (parts + len(weights)),
+        out_specs=[whole] * 2,
         out_shape=[
             jax.ShapeDtypeStruct((rows, cols), jnp.float32),
-            jax.ShapeDtypeStruct((rows, 1), jnp.float32),
+            jax.ShapeDtypeStruct((1, rows), jnp.float32),
         ],
+        scratch_shapes=[pltpu.VMEM((len(weights), rows, parts * inner // 4), jnp.bfloat16)],
         compiler_params=pltpu.CompilerParams(vmem_limit_bytes=32 * 2**20),
         cost_estimate=pl.CostEstimate(
             flops=2 * rows * inner * parts * cols, bytes_accessed=6 * 10**6, transcendentals=0
         ),
         name="out_project",
-    )(*heads, *weights)
+    )(info, *weights, *heads)
 
 
 def local(n_ctx, n_tp, tokens, norm_gain, q_weight, k_weight, v_weight, o_weight, post_gain, doc_ids, plan):
@@ -228,6 +286,7 @@
     shard = lax.axis_index("ctx")
     group = lax.axis_index("tp")
     cols = o_weight.shape[1] // n_tp
+    core = shard % 2
 
     def ctx_xor(a, m):
         return lax.ppermute(a, "ctx", [(i, i ^ m) for i in range(n_ctx)])
@@ -238,15 +297,14 @@
     def tp_xor(a, m):
         return lax.ppermute(a, "tp", [(i, i ^ m) for i in range(n_tp)])
 
-    own_kv = project(tokens, norm_gain, [k_weight, v_weight], None, "project_kv", 56)
-
-    kvs = []
-    near = own_kv
-    for back in range(BACK + 1):
-        near = near if back == 0 else ctx_z(near, 1)
-        across = ctx_xor(near, 2)
-        kvs.append([near, ctx_xor(near, 1), across, ctx_xor(across, 1)])
-    queries = project(tokens, norm_gain, [q_weight], query_scale, "project_q", 40)
+    which = jnp.stack([core, group]).astype(jnp.int32)
+    own_kv, *cuts = project(
+        which, tokens, norm_gain, [k_weight, v_weight], None, "project_kv", o_weight, n_tp
+    )
+    (queries,) = project(which, tokens, norm_gain, [q_weight], query_scale, "project_q")
+    cuts = [c if m == 0 else tp_xor(c, m) for m, c in enumerate(cuts)]
+    mine = jnp.stack([c[0] for c in cuts])
+    passed = jnp.stack([c[1] for c in cuts])
 
     first_block = jnp.sum((doc_ids[None, :] < doc_ids[:, None]).astype(jnp.int32), axis=1)
     own_first = lax.dynamic_slice_in_dim(first_block, shard * blocks, blocks, 0)
@@ -261,27 +319,27 @@
     target = plan * blocks + rank
     picker = (target[None, :] == block_ids[:, None]).astype(jnp.bfloat16)
 
+    back_one = ctx_z(own_kv, 1)
+    back_two = ctx_z(back_one, 1)
+    across = [ctx_xor(near, 2) for near in (own_kv, back_one, back_two)]
     carry = []
-    for stage in range(BACK):
-        carry = attend(stage, info, queries, kvs[stage], carry)
-
-    out_weights = [
-        lax.dynamic_slice_in_dim(o_weight, (group ^ m) * cols, cols, axis=1) for m in range(n_tp)
-    ]
-    carry, out_weights, picker = lax.optimization_barrier((carry, out_weights, picker))
-    first, second = (1, 2, 3, 4), (5, 6, 7)
-    for m in first:
-        out_weights[m] = tp_xor(out_weights[m], m)
-    natural = attend(BACK, info, queries, kvs[BACK], carry)
+    for stage, near in enumerate((own_kv, back_one)):
+        kvs = [near, ctx_xor(near, 1), across[stage], ctx_xor(across[stage], 1)]
+        carry = attend(stage, info, queries, kvs, carry)
+    far, carry, mine, passed, picker = lax.optimization_barrier(
+        (across[BACK], carry, mine, passed, picker)
+    )
+    passed = tp_xor(passed, n_tp // 2)
+    kvs = [back_two, ctx_xor(back_two, 1), far, ctx_xor(far, 1)]
+    natural = attend(BACK, info, queries, kvs, carry)
 
     width = natural.shape[1]
     piece = BLK // n_ctx
     striped = natural.reshape(blocks, n_ctx, piece, width).transpose(1, 0, 2, 3)
     striped = striped.reshape(n_ctx, blocks, piece * width)
     gathered = lax.all_to_all(striped, "ctx", 0, 0, tiled=True)
-    gathered, out_weights = lax.optimization_barrier((gathered, out_weights))
-    for m in second:
-        out_weights[m] = tp_xor(out_weights[m], m)
+    gathered, mine, passed = lax.optimization_barrier((gathered, mine, passed))
+    weights = [mine, passed, ctx_xor(mine, 1), ctx_xor(passed, 1)]
     ordered = jnp.dot(
         picker,
         gathered.reshape(total_blocks, piece * width),
@@ -290,7 +348,6 @@
     placed = lax.all_to_all(
         ordered.reshape(n_ctx, blocks, piece * width), "ctx", 0, 0, tiled=True
     )
-    placed, out_weights = lax.optimization_barrier((placed, out_weights))
     placed = (
         placed.reshape(n_ctx, blocks, piece, width).transpose(1, 0, 2, 3).reshape(rows, width)
     )
@@ -301,7 +358,7 @@
     heads[5] = tp_xor(heads[4], 1)
     heads[7] = tp_xor(heads[4], 3)
     heads[6] = tp_xor(heads[2], 4)
-    summed, squares = out_project(heads, out_weights)
+    summed, squares = out_project(which, heads, weights, cols)
     squares = squares.reshape(rows)
     squares = squares + tp_xor(squares, 4)
     squares = squares + tp_xor(squares, 1) + tp_xor(squares, 3) + tp_xor(squares, 2)

time: 160 us -> 132 us (0.82); the launches traced: 157 us -> 132 us
  starting transfers between devices: 53.5 us -> 43.6 us
  waiting for transfers between devices: 68.8 us -> 60 us
  local copies, waits for them, and re-layouts: 10.7 us -> 4.48 us
    ppermute x18 -> x15, waiting for transfers between devices: 53.2 us -> 34.4 us  [tp_xor(): return lax.ppermute(a, 'tp', [(i, i ^ m) for i in range(n_tp)])]
    all_to_all x1, waiting for transfers between devices: 0.01 us -> 11.5 us  [local(): lax.all_to_all(ordered.reshape(n_ctx, blocks, piece * width), 'ctx', 0, 0...]
    ppermute x18 -> x15, starting transfers between devices: 31.4 us -> 20.9 us  [tp_xor(): return lax.ppermute(a, 'tp', [(i, i ^ m) for i in range(n_tp)])]
    ppermute x2, waiting for transfers between devices: 12.4 us -> 3.56 us  [ctx_z(): lax.ppermute(a, 'ctx', [(i, (i + d * PLANE) % n_ctx) for i in range(n_ctx)])]
    all_to_all x1, waiting for transfers between devices: 0.01 us -> 7.5 us  [local(): gathered = lax.all_to_all(striped, 'ctx', 0, 0, tiled=True)]
    dynamic_slice x1 -> x0, local copies, waits for them, and re-layouts: 4.65 us -> none  [local(): lax.dynamic_slice_in_dim(o_weight, (group ^ m) * cols, cols, axis=1)]
    all_to_all x1, starting transfers between devices: 8.27 us -> 4.05 us  [local(): lax.all_to_all(ordered.reshape(n_ctx, blocks, piece * width), 'ctx', 0, 0...]
    pallas_call x3, Pallas kernels: 14.6 us -> 17.5 us  [the longest x2 13.9 us: project(): pl.pallas_call(functools.partial(project_kernel, scale, tile, count, part...]
  transfers between devices with their start and end apart: 31 -> 30, of which waited for: 18 -> 15; matrix products, arithmetic and copies ran while one was open for 4% -> 2% of each run, Pallas kernels for 7% -> 8%
where the time goes in v4:
time: 132 us
  waiting for transfers between devices  60 us (45%)
  starting transfers between devices  43.6 us (33%)
  Pallas kernels  21.9 us (17%)
  local copies, waits for them, and re-layouts  4.48 us (3%)
  other arithmetic  1.57 us (1%)
    ppermute x15, waiting for transfers between devices, tp_xor(): return lax.ppermute(a, 'tp', [(i, i ^ m) for i in range(n_tp)])  34.4 us
    ppermute x15, starting transfers between devices, tp_xor(): return lax.ppermute(a, 'tp', [(i, i ^ m) for i in range(n_tp)])  20.9 us
    pallas_call x2, Pallas kernels, project(): pl.pallas_call(functools.partial(project_kernel, scale, tile, count, part...  13.9 us
    all_to_all x1, waiting for transfers between devices, local(): lax.all_to_all(ordered.reshape(n_ctx, blocks, piece * width), 'ctx', 0, 0...  11.5 us
    all_to_all x1, starting transfers between devices, local(): gathered = lax.all_to_all(striped, 'ctx', 0, 0, tiled=True)  9.95 us
    all_to_all x1, waiting for transfers between devices, local(): gathered = lax.all_to_all(striped, 'ctx', 0, 0, tiled=True)  7.5 us
    ppermute x11, starting transfers between devices, ctx_xor(): return lax.ppermute(a, 'ctx', [(i, i ^ m) for i in range(n_ctx)])  6.54 us
    pallas_call x3, Pallas kernels, attend(): pl.pallas_call(functools.partial(attend_kernel, rows, stage), in_specs=[p...  4.45 us
  transfers between devices with their start and end apart: 30, of which 15 were waited for; matrix products, arithmetic and copies ran while one was open for 2% of the time, Pallas kernels for 8%

profile of v4, /device:TPU:2, one launch (start us, length us, event | category | flops | bytes accessed | tf_op | source)
XLA Modules:
  0.0 132.1 jit_solution(2155752155873989890)
XLA Ops:
  0.7 7.2 %project_kv.1 = (bf16[512,256]{1,0:T(8,128)(2,1)}, bf16[2,128,640]{2,1,0:T(8,128)(2,1)}, bf16[2,128,640]{2,1,0:T(8,128)(2,1)}, bf16[2,128,640]{2,1,0:T(8,128)(2,1)}, bf16[2,128,640]{2,1,0:T(8,128)(2,1)}) custom-call(s32[2]{0:T(128)} %pad_add_fusion.core_ref.info_ref, bf16[512,4608]{1,0:T(8,128)(2,1)} %x_hbm.3, f32[4608]{0:T(1024)} %g_ref.3, ...), custom_call_target="tpu_custom_call" | custom-call | flops 1207959552 | bytes 7077888 | tf_op jit(solution)/shard_map/project_kv/pallas_call | solution.py:102
  7.9 2.4 %collective-permute-start.8 = (bf16[512,256]{1,0:T(8,128)(2,1)}, bf16[512,256]{1,0:T(8,128)(2,1)S(1)}, u32[]{:S(2)}, u32[]{:S(2)}) collective-permute-start(bf16[512,256]{1,0:T(8,128)(2,1)} %get-tuple-element.25.refs_0_), channel_id=1, source_target_pairs={{0,16},{8,24},{16,0},{24,8},{32,48},{40,56},{48,32},{56,40},{64,80... | collective-permute-start | bytes 786440 | tf_op jit(solution)/shard_map/ppermute | solution.py:292
  10.4 1.6 %collective-permute-start.10 = (bf16[2,128,640]{2,1,0:T(8,128)(2,1)}, bf16[2,128,640]{2,1,0:T(8,128)(2,1)S(1)}, u32[]{:S(2)}, u32[]{:S(2)}) collective-permute-start(bf16[2,128,640]{2,1,0:T(8,128)(2,1)} %get-tuple-element.31), channel_id=1, source_target_pairs={{0,1},{1,0},{2,3},{3,2},{4,5},{5,4},{6,7},{7,6},{8,9},{9,8},{10,11... | collective-permute-start | bytes 983048 | tf_op jit(solution)/shard_map/ppermute | solution.py:298
  12.0 2.9 %collective-permute-start.11 = (bf16[2,128,640]{2,1,0:T(8,128)(2,1)}, bf16[2,128,640]{2,1,0:T(8,128)(2,1)S(1)}, u32[]{:S(2)}, u32[]{:S(2)}) collective-permute-start(bf16[2,128,640]{2,1,0:T(8,128)(2,1)} %get-tuple-element.32), channel_id=1, source_target_pairs={{0,2},{1,3},{2,0},{3,1},{4,6},{5,7},{6,4},{7,5},{8,10},{9,11},{10,... | collective-permute-start | bytes 983048 | tf_op jit(solution)/shard_map/ppermute | solution.py:298
  16.4 6.7 %project_q.1.q_ref = bf16[512,256]{1,0:T(8,128)(2,1)} custom-call(s32[2]{0:T(128)} %pad_add_fusion.core_ref.info_ref, bf16[512,4608]{1,0:T(8,128)(2,1)} %x_hbm.3, f32[4608]{0:T(1024)} %g_ref.3, bf16[4608,256]{1,0:T(8,128)(2,1)} %refs_0_.2), custom_call_target="tpu_custom_call" | custom-call | flops 1207959552 | bytes 7077888 | tf_op jit(solution)/shard_map/project_q/pallas_call | solution.py:102
  23.2 1.4 %collective-permute-start.12 = (bf16[2,128,640]{2,1,0:T(8,128)(2,1)S(1)}, bf16[2,128,640]{2,1,0:T(8,128)(2,1)S(1)}, u32[]{:S(2)}, u32[]{:S(2)}) collective-permute-start(bf16[2,128,640]{2,1,0:T(8,128)(2,1)S(1)} %copy-done.4), channel_id=1, source_target_pairs={{0,3},{1,2},{2,1},{3,0},{4,7},{5,6},{6,5},{7,4},{8,11},{9,10},{10,... | collective-permute-start | bytes 983048 | tf_op jit(solution)/shard_map/ppermute | solution.py:298
  24.6 1.5 %collective-permute-start.5 = (bf16[512,256]{1,0:T(8,128)(2,1)S(1)}, bf16[512,256]{1,0:T(8,128)(2,1)S(1)}, u32[]{:S(2)}, u32[]{:S(2)}) collective-permute-start(bf16[512,256]{1,0:T(8,128)(2,1)S(1)} %collective-permute-done.refs_0_), channel_id=1, source_target_pairs={{0,16},{8,24},{16,0},{24,8},{32,48},{40,56},{48,32},{56,40},{64,80... | collective-permute-start | bytes 786440 | tf_op jit(solution)/shard_map/ppermute | solution.py:292
  26.1 4.0 %collective-permute-done.11 = bf16[2,128,640]{2,1,0:T(8,128)(2,1)S(1)} collective-permute-done((bf16[2,128,640]{2,1,0:T(8,128)(2,1)}, bf16[2,128,640]{2,1,0:T(8,128)(2,1)S(1)}, u32[]{:S(2)}, u32[]{:S(2)}) %collective-permute-start.11) | collective-permute-done | bytes 327712 | tf_op jit(solution)/shard_map/ppermute | solution.py:298
  30.1 2.0 %collective-permute-start.1 = (bf16[512,256]{1,0:T(8,128)(2,1)S(1)}, bf16[512,256]{1,0:T(8,128)(2,1)S(1)}, u32[]{:S(2)}, u32[]{:S(2)}) collective-permute-start(bf16[512,256]{1,0:T(8,128)(2,1)S(1)} %collective-permute-done.refs_0_), channel_id=1, source_target_pairs={{0,32},{8,40},{16,48},{24,56},{32,64},{40,72},{48,80},{56,88},{64,... | collective-permute-start | bytes 786440 | tf_op jit(solution)/shard_map/ppermute | solution.py:295
  32.1 4.9 %collective-permute-done.12 = bf16[2,128,640]{2,1,0:T(8,128)(2,1)S(1)} collective-permute-done((bf16[2,128,640]{2,1,0:T(8,128)(2,1)S(1)}, bf16[2,128,640]{2,1,0:T(8,128)(2,1)S(1)}, u32[]{:S(2)}, u32[]{:S(2)}) %collective-permute-start.12) | collective-permute-done | bytes 327712 | tf_op jit(solution)/shard_map/ppermute | solution.py:298
  37.8 3.6 %collective-permute-done.1.refs_0_ = bf16[512,256]{1,0:T(8,128)(2,1)S(1)} collective-permute-done((bf16[512,256]{1,0:T(8,128)(2,1)S(1)}, bf16[512,256]{1,0:T(8,128)(2,1)S(1)}, u32[]{:S(2)}, u32[]{:S(2)}) %collective-permute-start.1) | collective-permute-done | bytes 262176 | tf_op jit(solution)/shard_map/ppermute | solution.py:295
  41.4 1.5 %collective-permute-start.3 = (bf16[512,256]{1,0:T(8,128)(2,1)S(1)}, bf16[512,256]{1,0:T(8,128)(2,1)S(1)}, u32[]{:S(2)}, u32[]{:S(2)}) collective-permute-start(bf16[512,256]{1,0:T(8,128)(2,1)S(1)} %collective-permute-done.1.refs_0_), channel_id=1, source_target_pairs={{0,16},{8,24},{16,0},{24,8},{32,48},{40,56},{48,32},{56,40},{64,80... | collective-permute-start | bytes 786440 | tf_op jit(solution)/shard_map/ppermute | solution.py:292
  42.9 2.7 %attend.3 = (f32[2,512,128]{2,1,0:T(8,128)S(1)}, f32[2,512,128]{2,1,0:T(8,128)S(1)}) custom-call(s32[5]{0:T(128)S(1)} %pad_add_fusion.1.info_ref, bf16[512,256]{1,0:T(8,128)(2,1)S(1)} %copy-done, bf16[512,256]{1,0:T(8,128)(2,1)S(1)} %copy-done.2, bf16[512,256]{1,0:T(8,128)(2,1)S(1)} %collective-permute-done.7.refs_1_, ...), custom_call_target="tpu_custom_call" | custom-call | flops 2000000000 | bytes 4000000 | tf_op jit(solution)/shard_map/attend/pallas_call | solution.py:203
  46.4 3.1 %collective-permute-done.3.refs_2_ = bf16[512,256]{1,0:T(8,128)(2,1)S(1)} collective-permute-done((bf16[512,256]{1,0:T(8,128)(2,1)S(1)}, bf16[512,256]{1,0:T(8,128)(2,1)S(1)}, u32[]{:S(2)}, u32[]{:S(2)}) %collective-permute-start.3) | collective-permute-done | bytes 262176 | tf_op jit(solution)/shard_map/ppermute | solution.py:292
  49.5 2.4 %collective-permute-start.14 = (bf16[4,128,640]{2,1,0:T(8,128)(2,1)S(1)}, bf16[4,128,640]{2,1,0:T(8,128)(2,1)S(1)}, u32[]{:S(2)}, u32[]{:S(2)}) collective-permute-start(bf16[4,128,640]{2,1,0:T(8,128)(2,1)S(1)} %get-tuple-element.38), channel_id=1, source_target_pairs={{0,4},{1,5},{2,6},{3,7},{4,0},{5,1},{6,2},{7,3},{8,12},{9,13},{10,... | collective-permute-start | bytes 1966088 | tf_op jit(solution)/shard_map/ppermute | solution.py:298
  54.1 10.0 %all-to-all-start = ((bf16[32,4,1024]{2,1,0:T(4,128)(2,1)}), bf16[32,4,1024]{2,1,0:T(4,128)(2,1)S(1)}, u32[]{:S(2)}, u32[]{:S(2)}) async-start(bf16[32,4,1024]{2,1,0:T(4,128)(2,1)} %copy.18), calls=%async_computation | async-start | bytes 524288 | tf_op jit(solution)/shard_map/all_to_all | solution.py:340
  64.0 4.6 %collective-permute-done.14.refs_1_ = bf16[4,128,640]{2,1,0:T(8,128)(2,1)S(1)} collective-permute-done((bf16[4,128,640]{2,1,0:T(8,128)(2,1)S(1)}, bf16[4,128,640]{2,1,0:T(8,128)(2,1)S(1)}, u32[]{:S(2)}, u32[]{:S(2)}) %collective-permute-start.14) | collective-permute-done | bytes 655392 | tf_op jit(solution)/shard_map/ppermute | solution.py:298
  68.6 7.5 %all-to-all-done = bf16[32,4,1024]{2,1,0:T(4,128)(2,1)S(1)} async-done(((bf16[32,4,1024]{2,1,0:T(4,128)(2,1)}), bf16[32,4,1024]{2,1,0:T(4,128)(2,1)S(1)}, u32[]{:S(2)}, u32[]{:S(2)}) %all-to-all-start) | async-done | bytes 262176 | tf_op jit(solution)/shard_map/all_to_all | solution.py:340
  77.2 4.1 %all-to-all-start.1 = ((bf16[32,4,1024]{2,1,0:T(4,128)(2,1)}), bf16[32,4,1024]{2,1,0:T(4,128)(2,1)S(1)}, u32[]{:S(2)}, u32[]{:S(2)}) async-start(bf16[32,4,1024]{2,1,0:T(4,128)(2,1)} %reshape.35), calls=%async_computation.1 | async-start | bytes 524288 | tf_op jit(solution)/shard_map/all_to_all | solution.py:348
  81.9 11.5 %all-to-all-done.1 = bf16[32,4,1024]{2,1,0:T(4,128)(2,1)S(1)} async-done(((bf16[32,4,1024]{2,1,0:T(4,128)(2,1)}), bf16[32,4,1024]{2,1,0:T(4,128)(2,1)S(1)}, u32[]{:S(2)}, u32[]{:S(2)}) %all-to-all-start.1) | async-done | bytes 262176 | tf_op jit(solution)/shard_map/all_to_all | solution.py:348
  93.7 2.2 %collective-permute-start.20 = (bf16[512,256]{1,0:T(8,128)(2,1)S(1)}, bf16[512,256]{1,0:T(8,128)(2,1)S(1)}, u32[]{:S(2)}, u32[]{:S(2)}) collective-permute-start(bf16[512,256]{1,0:T(8,128)(2,1)S(1)} %reshape.37.refs_4_), channel_id=1, source_target_pairs={{0,4},{1,5},{2,6},{3,7},{4,0},{5,1},{6,2},{7,3},{8,12},{9,13},{10,... | collective-permute-start | bytes 786440 | tf_op jit(solution)/shard_map/ppermute | solution.py:298
  96.5 2.2 %collective-permute-start.19 = (bf16[512,256]{1,0:T(8,128)(2,1)S(1)}, bf16[512,256]{1,0:T(8,128)(2,1)S(1)}, u32[]{:S(2)}, u32[]{:S(2)}) collective-permute-start(bf16[512,256]{1,0:T(8,128)(2,1)S(1)} %reshape.37.refs_4_), channel_id=1, source_target_pairs={{0,3},{1,2},{2,1},{3,0},{4,7},{5,6},{6,5},{7,4},{8,11},{9,10},{10,... | collective-permute-start | bytes 786440 | tf_op jit(solution)/shard_map/ppermute | solution.py:298
  99.4 3.4 %collective-permute-done.20.refs_8_ = bf16[512,256]{1,0:T(8,128)(2,1)S(1)} collective-permute-done((bf16[512,256]{1,0:T(8,128)(2,1)S(1)}, bf16[512,256]{1,0:T(8,128)(2,1)S(1)}, u32[]{:S(2)}, u32[]{:S(2)}) %collective-permute-start.20) | collective-permute-done | bytes 262176 | tf_op jit(solution)/shard_map/ppermute | solution.py:298
  103.4 3.3 %collective-permute-done.18.refs_6_ = bf16[512,256]{1,0:T(8,128)(2,1)S(1)} collective-permute-done((bf16[512,256]{1,0:T(8,128)(2,1)S(1)}, bf16[512,256]{1,0:T(8,128)(2,1)S(1)}, u32[]{:S(2)}, u32[]{:S(2)}) %collective-permute-start.18) | collective-permute-done | bytes 262176 | tf_op jit(solution)/shard_map/ppermute | solution.py:298
  106.6 1.4 %collective-permute-start.22 = (bf16[512,256]{1,0:T(8,128)(2,1)S(1)}, bf16[512,256]{1,0:T(8,128)(2,1)S(1)}, u32[]{:S(2)}, u32[]{:S(2)}) collective-permute-start(bf16[512,256]{1,0:T(8,128)(2,1)S(1)} %collective-permute-done.18.refs_6_), channel_id=1, source_target_pairs={{0,4},{1,5},{2,6},{3,7},{4,0},{5,1},{6,2},{7,3},{8,12},{9,13},{10,... | collective-permute-start | bytes 786440 | tf_op jit(solution)/shard_map/ppermute | solution.py:298
  108.0 2.3 %collective-permute-done.19.refs_7_ = bf16[512,256]{1,0:T(8,128)(2,1)S(1)} collective-permute-done((bf16[512,256]{1,0:T(8,128)(2,1)S(1)}, bf16[512,256]{1,0:T(8,128)(2,1)S(1)}, u32[]{:S(2)}, u32[]{:S(2)}) %collective-permute-start.19) | collective-permute-done | bytes 262176 | tf_op jit(solution)/shard_map/ppermute | solution.py:298
  110.4 5.5 %collective-permute-done.23.refs_11_ = bf16[512,256]{1,0:T(8,128)(2,1)S(1)} collective-permute-done((bf16[512,256]{1,0:T(8,128)(2,1)S(1)}, bf16[512,256]{1,0:T(8,128)(2,1)S(1)}, u32[]{:S(2)}, u32[]{:S(2)}) %collective-permute-start.23) | collective-permute-done | bytes 262176 | tf_op jit(solution)/shard_map/ppermute | solution.py:298
  115.9 3.5 %out_project.1 = (f32[512,576]{1,0:T(8,128)S(1)}, f32[1,512]{1,0:T(1,128)S(1)}) custom-call(s32[2]{0:T(128)S(1)} %copy-done.1, bf16[4,128,640]{2,1,0:T(8,128)(2,1)S(1)} %get-tuple-element.39.refs_0_, bf16[4,128,640]{2,1,0:T(8,128)(2,1)S(1)} %collective-permute-done.14.refs_1_, bf16[4,128,640]{2,1,0:T(8,128)(2,1)S(1)} %collective-permute-done.15.refs_2_, ...), custom_call_target="tpu_custom_call" | custom-call | flops 1207959552 | bytes 6000000 | tf_op jit(solution)/shard_map/out_project/pallas_call | solution.py:265
  119.4 1.5 %collective-permute-start.24 = (f32[512]{0:T(512)S(1)}, f32[512]{0:T(512)S(1)}, u32[]{:S(2)}, u32[]{:S(2)}) collective-permute-start(f32[512]{0:T(512)S(1)} %bitcast.12), channel_id=1, source_target_pairs={{0,4},{1,5},{2,6},{3,7},{4,0},{5,1},{6,2},{7,3},{8,12},{9,13},{10,... | collective-permute-start | bytes 6152 | tf_op jit(solution)/shard_map/ppermute | solution.py:298
  120.9 3.7 %collective-permute-done.24 = f32[512]{0:T(512)S(1)} collective-permute-done((f32[512]{0:T(512)S(1)}, f32[512]{0:T(512)S(1)}, u32[]{:S(2)}, u32[]{:S(2)}) %collective-permute-start.24) | collective-permute-done | bytes 2080 | tf_op jit(solution)/shard_map/ppermute | solution.py:298
  125.4 1.9 %collective-permute-start.26 = (f32[512]{0:T(512)S(1)}, f32[512]{0:T(512)S(1)}, u32[]{:S(2)}, u32[]{:S(2)}) collective-permute-start(f32[512]{0:T(512)S(1)} %add.37), channel_id=1, source_target_pairs={{0,3},{1,2},{2,1},{3,0},{4,7},{5,6},{6,5},{7,4},{8,11},{9,10},{10,... | collective-permute-start | bytes 6152 | tf_op jit(solution)/shard_map/ppermute | solution.py:298
  128.1 1.6 %collective-permute-done.27 = f32[512]{0:T(512)S(1)} collective-permute-done((f32[512]{0:T(512)S(1)}, f32[512]{0:T(512)S(1)}, u32[]{:S(2)}, u32[]{:S(2)}) %collective-permute-start.27) | collective-permute-done | bytes 2080 | tf_op jit(solution)/shard_map/ppermute | solution.py:298
  (73 shorter events, 14.0 us)
Async XLA Ops:
  7.9 22.2 %collective-permute-start.8 = (bf16[512,256]{1,0:T(8,128)(2,1)}, bf16[512,256]{1,0:T(8,128)(2,1)S(1)}, u32[]{:S(2)}, u32[]{:S(2)}) collective-permute-start(bf16[512,256]{1,0:T(8,128)(2,1)} %get-tuple-element.25.refs_0_), channel_id=1, source_target_pairs={{0,16},{8,24},{16,0},{24,8},{32,48},{40,56},{48,32},{56,40},{64,80... | collective-permute-start | bytes 786440 | tf_op jit(solution)/shard_map/ppermute | solution.py:292
  10.2 32.6 %collective-permute-start.7 = (bf16[512,256]{1,0:T(8,128)(2,1)}, bf16[512,256]{1,0:T(8,128)(2,1)S(1)}, u32[]{:S(2)}, u32[]{:S(2)}) collective-permute-start(bf16[512,256]{1,0:T(8,128)(2,1)} %get-tuple-element.25.refs_0_), channel_id=1, source_target_pairs={{0,8},{8,0},{16,24},{24,16},{32,40},{40,32},{48,56},{56,48},{64,72... | collective-permute-start | bytes 786440 | tf_op jit(solution)/shard_map/ppermute | solution.py:292
  10.2 13.0 %collective-permute-start = (bf16[512,256]{1,0:T(8,128)(2,1)}, bf16[512,256]{1,0:T(8,128)(2,1)S(1)}, u32[]{:S(2)}, u32[]{:S(2)}) collective-permute-start(bf16[512,256]{1,0:T(8,128)(2,1)} %get-tuple-element.25.refs_0_), channel_id=1, source_target_pairs={{0,32},{8,40},{16,48},{24,56},{32,64},{40,72},{48,80},{56,88},{64,... | collective-permute-start | bytes 786440 | tf_op jit(solution)/shard_map/ppermute | solution.py:295
  10.4 14.1 %collective-permute-start.10 = (bf16[2,128,640]{2,1,0:T(8,128)(2,1)}, bf16[2,128,640]{2,1,0:T(8,128)(2,1)S(1)}, u32[]{:S(2)}, u32[]{:S(2)}) collective-permute-start(bf16[2,128,640]{2,1,0:T(8,128)(2,1)} %get-tuple-element.31), channel_id=1, source_target_pairs={{0,1},{1,0},{2,3},{3,2},{4,5},{5,4},{6,7},{7,6},{8,9},{9,8},{10,11... | collective-permute-start | bytes 983048 | tf_op jit(solution)/shard_map/ppermute | solution.py:298
  12.0 18.1 %collective-permute-start.11 = (bf16[2,128,640]{2,1,0:T(8,128)(2,1)}, bf16[2,128,640]{2,1,0:T(8,128)(2,1)S(1)}, u32[]{:S(2)}, u32[]{:S(2)}) collective-permute-start(bf16[2,128,640]{2,1,0:T(8,128)(2,1)} %get-tuple-element.32), channel_id=1, source_target_pairs={{0,2},{1,3},{2,0},{3,1},{4,6},{5,7},{6,4},{7,5},{8,10},{9,11},{10,... | collective-permute-start | bytes 983048 | tf_op jit(solution)/shard_map/ppermute | solution.py:298
  23.2 13.8 %collective-permute-start.12 = (bf16[2,128,640]{2,1,0:T(8,128)(2,1)S(1)}, bf16[2,128,640]{2,1,0:T(8,128)(2,1)S(1)}, u32[]{:S(2)}, u32[]{:S(2)}) collective-permute-start(bf16[2,128,640]{2,1,0:T(8,128)(2,1)S(1)} %copy-done.4), channel_id=1, source_target_pairs={{0,3},{1,2},{2,1},{3,0},{4,7},{5,6},{6,5},{7,4},{8,11},{9,10},{10,... | collective-permute-start | bytes 983048 | tf_op jit(solution)/shard_map/ppermute | solution.py:298
  24.6 12.5 %collective-permute-start.5 = (bf16[512,256]{1,0:T(8,128)(2,1)S(1)}, bf16[512,256]{1,0:T(8,128)(2,1)S(1)}, u32[]{:S(2)}, u32[]{:S(2)}) collective-permute-start(bf16[512,256]{1,0:T(8,128)(2,1)S(1)} %collective-permute-done.refs_0_), channel_id=1, source_target_pairs={{0,16},{8,24},{16,0},{24,8},{32,48},{40,56},{48,32},{56,40},{64,80... | collective-permute-start | bytes 786440 | tf_op jit(solution)/shard_map/ppermute | solution.py:292
  30.1 15.6 %collective-permute-start.4 = (bf16[512,256]{1,0:T(8,128)(2,1)S(1)}, bf16[512,256]{1,0:T(8,128)(2,1)S(1)}, u32[]{:S(2)}, u32[]{:S(2)}) collective-permute-start(bf16[512,256]{1,0:T(8,128)(2,1)S(1)} %collective-permute-done.refs_0_), channel_id=1, source_target_pairs={{0,8},{8,0},{16,24},{24,16},{32,40},{40,32},{48,56},{56,48},{64,72... | collective-permute-start | bytes 786440 | tf_op jit(solution)/shard_map/ppermute | solution.py:292
  30.1 11.3 %collective-permute-start.1 = (bf16[512,256]{1,0:T(8,128)(2,1)S(1)}, bf16[512,256]{1,0:T(8,128)(2,1)S(1)}, u32[]{:S(2)}, u32[]{:S(2)}) collective-permute-start(bf16[512,256]{1,0:T(8,128)(2,1)S(1)} %collective-permute-done.refs_0_), channel_id=1, source_target_pairs={{0,32},{8,40},{16,48},{24,56},{32,64},{40,72},{48,80},{56,88},{64,... | collective-permute-start | bytes 786440 | tf_op jit(solution)/shard_map/ppermute | solution.py:295
  37.0 5.9 %collective-permute-start.9 = (bf16[512,256]{1,0:T(8,128)(2,1)S(1)}, bf16[512,256]{1,0:T(8,128)(2,1)S(1)}, u32[]{:S(2)}, u32[]{:S(2)}) collective-permute-start(bf16[512,256]{1,0:T(8,128)(2,1)S(1)} %collective-permute-done.8.refs_2_), channel_id=1, source_target_pairs={{0,8},{8,0},{16,24},{24,16},{32,40},{40,32},{48,56},{56,48},{64,72... | collective-permute-start | bytes 786440 | tf_op jit(solution)/shard_map/ppermute | solution.py:292
  37.0 8.6 %collective-permute-start.6 = (bf16[512,256]{1,0:T(8,128)(2,1)S(1)}, bf16[512,256]{1,0:T(8,128)(2,1)S(1)}, u32[]{:S(2)}, u32[]{:S(2)}) collective-permute-start(bf16[512,256]{1,0:T(8,128)(2,1)S(1)} %collective-permute-done.5.refs_2_), channel_id=1, source_target_pairs={{0,8},{8,0},{16,24},{24,16},{32,40},{40,32},{48,56},{56,48},{64,72... | collective-permute-start | bytes 786440 | tf_op jit(solution)/shard_map/ppermute | solution.py:292
  41.4 8.1 %collective-permute-start.3 = (bf16[512,256]{1,0:T(8,128)(2,1)S(1)}, bf16[512,256]{1,0:T(8,128)(2,1)S(1)}, u32[]{:S(2)}, u32[]{:S(2)}) collective-permute-start(bf16[512,256]{1,0:T(8,128)(2,1)S(1)} %collective-permute-done.1.refs_0_), channel_id=1, source_target_pairs={{0,16},{8,24},{16,0},{24,8},{32,48},{40,56},{48,32},{56,40},{64,80... | collective-permute-start | bytes 786440 | tf_op jit(solution)/shard_map/ppermute | solution.py:292
  42.9 9.1 %collective-permute-start.2 = (bf16[512,256]{1,0:T(8,128)(2,1)S(1)}, bf16[512,256]{1,0:T(8,128)(2,1)S(1)}, u32[]{:S(2)}, u32[]{:S(2)}) collective-permute-start(bf16[512,256]{1,0:T(8,128)(2,1)S(1)} %collective-permute-done.1.refs_0_), channel_id=1, source_target_pairs={{0,8},{8,0},{16,24},{24,16},{32,40},{40,32},{48,56},{56,48},{64,72... | collective-permute-start | bytes 786440 | tf_op jit(solution)/shard_map/ppermute | solution.py:292
  49.5 2.4 %collective-permute-start.13 = (bf16[512,256]{1,0:T(8,128)(2,1)S(1)}, bf16[512,256]{1,0:T(8,128)(2,1)S(1)}, u32[]{:S(2)}, u32[]{:S(2)}) collective-permute-start(bf16[512,256]{1,0:T(8,128)(2,1)S(1)} %collective-permute-done.3.refs_2_), channel_id=1, source_target_pairs={{0,8},{8,0},{16,24},{24,16},{32,40},{40,32},{48,56},{56,48},{64,72... | collective-permute-start | bytes 786440 | tf_op jit(solution)/shard_map/ppermute | solution.py:292
  49.5 19.1 %collective-permute-start.14 = (bf16[4,128,640]{2,1,0:T(8,128)(2,1)S(1)}, bf16[4,128,640]{2,1,0:T(8,128)(2,1)S(1)}, u32[]{:S(2)}, u32[]{:S(2)}) collective-permute-start(bf16[4,128,640]{2,1,0:T(8,128)(2,1)S(1)} %get-tuple-element.38), channel_id=1, source_target_pairs={{0,4},{1,5},{2,6},{3,7},{4,0},{5,1},{6,2},{7,3},{8,12},{9,13},{10,... | collective-permute-start | bytes 1966088 | tf_op jit(solution)/shard_map/ppermute | solution.py:298
  54.1 22.0 %all-to-all-start = ((bf16[32,4,1024]{2,1,0:T(4,128)(2,1)}), bf16[32,4,1024]{2,1,0:T(4,128)(2,1)S(1)}, u32[]{:S(2)}, u32[]{:S(2)}) async-start(bf16[32,4,1024]{2,1,0:T(4,128)(2,1)} %copy.18), calls=%async_computation | async-start | bytes 524288 | tf_op jit(solution)/shard_map/all_to_all | solution.py:340
  76.4 39.5 %copy-start.1 = (s32[2]{0:T(128)S(1)}, s32[2]{0:T(128)}, u32[]{:S(2)}) copy-start(s32[2]{0:T(128)} %pad_add_fusion.core_ref.info_ref) | copy-start | bytes 28
  77.2 16.1 %all-to-all-start.1 = ((bf16[32,4,1024]{2,1,0:T(4,128)(2,1)}), bf16[32,4,1024]{2,1,0:T(4,128)(2,1)S(1)}, u32[]{:S(2)}, u32[]{:S(2)}) async-start(bf16[32,4,1024]{2,1,0:T(4,128)(2,1)} %reshape.35), calls=%async_computation.1 | async-start | bytes 524288 | tf_op jit(solution)/shard_map/all_to_all | solution.py:348
  81.3 17.4 %collective-permute-start.15 = (bf16[4,128,640]{2,1,0:T(8,128)(2,1)S(1)}, bf16[4,128,640]{2,1,0:T(8,128)(2,1)S(1)}, u32[]{:S(2)}, u32[]{:S(2)}) collective-permute-start(bf16[4,128,640]{2,1,0:T(8,128)(2,1)S(1)} %get-tuple-element.39.refs_0_), channel_id=1, source_target_pairs={{0,8},{8,0},{16,24},{24,16},{32,40},{40,32},{48,56},{56,48},{64,72... | collective-permute-start | bytes 1966088 | tf_op jit(solution)/shard_map/ppermute | solution.py:292
  81.5 21.5 %collective-permute-start.16 = (bf16[4,128,640]{2,1,0:T(8,128)(2,1)S(1)}, bf16[4,128,640]{2,1,0:T(8,128)(2,1)S(1)}, u32[]{:S(2)}, u32[]{:S(2)}) collective-permute-start(bf16[4,128,640]{2,1,0:T(8,128)(2,1)S(1)} %collective-permute-done.14.refs_1_), channel_id=1, source_target_pairs={{0,8},{8,0},{16,24},{24,16},{32,40},{40,32},{48,56},{56,48},{64,72... | collective-permute-start | bytes 1966088 | tf_op jit(solution)/shard_map/ppermute | solution.py:292
  93.7 37.2 %copy-start.3 = (f32[576]{0:T(1024)S(1)}, f32[576]{0:T(1024)}, u32[]{:S(2)}) copy-start(f32[576]{0:T(1024)} %param.15) | copy-start | bytes 6916
  93.7 9.1 %collective-permute-start.20 = (bf16[512,256]{1,0:T(8,128)(2,1)S(1)}, bf16[512,256]{1,0:T(8,128)(2,1)S(1)}, u32[]{:S(2)}, u32[]{:S(2)}) collective-permute-start(bf16[512,256]{1,0:T(8,128)(2,1)S(1)} %reshape.37.refs_4_), channel_id=1, source_target_pairs={{0,4},{1,5},{2,6},{3,7},{4,0},{5,1},{6,2},{7,3},{8,12},{9,13},{10,... | collective-permute-start | bytes 786440 | tf_op jit(solution)/shard_map/ppermute | solution.py:298
  95.9 10.8 %collective-permute-start.18 = (bf16[512,256]{1,0:T(8,128)(2,1)S(1)}, bf16[512,256]{1,0:T(8,128)(2,1)S(1)}, u32[]{:S(2)}, u32[]{:S(2)}) collective-permute-start(bf16[512,256]{1,0:T(8,128)(2,1)S(1)} %reshape.37.refs_4_), channel_id=1, source_target_pairs={{0,2},{1,3},{2,0},{3,1},{4,6},{5,7},{6,4},{7,5},{8,10},{9,11},{10,... | collective-permute-start | bytes 786440 | tf_op jit(solution)/shard_map/ppermute | solution.py:298
  96.5 13.8 %collective-permute-start.19 = (bf16[512,256]{1,0:T(8,128)(2,1)S(1)}, bf16[512,256]{1,0:T(8,128)(2,1)S(1)}, u32[]{:S(2)}, u32[]{:S(2)}) collective-permute-start(bf16[512,256]{1,0:T(8,128)(2,1)S(1)} %reshape.37.refs_4_), channel_id=1, source_target_pairs={{0,3},{1,2},{2,1},{3,0},{4,7},{5,6},{6,5},{7,4},{8,11},{9,10},{10,... | collective-permute-start | bytes 786440 | tf_op jit(solution)/shard_map/ppermute | solution.py:298
  98.7 11.7 %collective-permute-start.17 = (bf16[512,256]{1,0:T(8,128)(2,1)S(1)}, bf16[512,256]{1,0:T(8,128)(2,1)S(1)}, u32[]{:S(2)}, u32[]{:S(2)}) collective-permute-start(bf16[512,256]{1,0:T(8,128)(2,1)S(1)} %reshape.37.refs_4_), channel_id=1, source_target_pairs={{0,1},{1,0},{2,3},{3,2},{4,5},{5,4},{6,7},{7,6},{8,9},{9,8},{10,11... | collective-permute-start | bytes 786440 | tf_op jit(solution)/shard_map/ppermute | solution.py:298
  102.8 13.1 %collective-permute-start.23 = (bf16[512,256]{1,0:T(8,128)(2,1)S(1)}, bf16[512,256]{1,0:T(8,128)(2,1)S(1)}, u32[]{:S(2)}, u32[]{:S(2)}) collective-permute-start(bf16[512,256]{1,0:T(8,128)(2,1)S(1)} %collective-permute-done.20.refs_8_), channel_id=1, source_target_pairs={{0,3},{1,2},{2,1},{3,0},{4,7},{5,6},{6,5},{7,4},{8,11},{9,10},{10,... | collective-permute-start | bytes 786440 | tf_op jit(solution)/shard_map/ppermute | solution.py:298
  103.0 12.9 %collective-permute-start.21 = (bf16[512,256]{1,0:T(8,128)(2,1)S(1)}, bf16[512,256]{1,0:T(8,128)(2,1)S(1)}, u32[]{:S(2)}, u32[]{:S(2)}) collective-permute-start(bf16[512,256]{1,0:T(8,128)(2,1)S(1)} %collective-permute-done.20.refs_8_), channel_id=1, source_target_pairs={{0,1},{1,0},{2,3},{3,2},{4,5},{5,4},{6,7},{7,6},{8,9},{9,8},{10,11... | collective-permute-start | bytes 786440 | tf_op jit(solution)/shard_map/ppermute | solution.py:298
  106.6 9.2 %collective-permute-start.22 = (bf16[512,256]{1,0:T(8,128)(2,1)S(1)}, bf16[512,256]{1,0:T(8,128)(2,1)S(1)}, u32[]{:S(2)}, u32[]{:S(2)}) collective-permute-start(bf16[512,256]{1,0:T(8,128)(2,1)S(1)} %collective-permute-done.18.refs_6_), channel_id=1, source_target_pairs={{0,4},{1,5},{2,6},{3,7},{4,0},{5,1},{6,2},{7,3},{8,12},{9,13},{10,... | collective-permute-start | bytes 786440 | tf_op jit(solution)/shard_map/ppermute | solution.py:298
  119.4 5.2 %collective-permute-start.24 = (f32[512]{0:T(512)S(1)}, f32[512]{0:T(512)S(1)}, u32[]{:S(2)}, u32[]{:S(2)}) collective-permute-start(f32[512]{0:T(512)S(1)} %bitcast.12), channel_id=1, source_target_pairs={{0,4},{1,5},{2,6},{3,7},{4,0},{5,1},{6,2},{7,3},{8,12},{9,13},{10,... | collective-permute-start | bytes 6152 | tf_op jit(solution)/shard_map/ppermute | solution.py:298
  124.6 5.1 %collective-permute-start.27 = (f32[512]{0:T(512)S(1)}, f32[512]{0:T(512)S(1)}, u32[]{:S(2)}, u32[]{:S(2)}) collective-permute-start(f32[512]{0:T(512)S(1)} %add.37), channel_id=1, source_target_pairs={{0,2},{1,3},{2,0},{3,1},{4,6},{5,7},{6,4},{7,5},{8,10},{9,11},{10,... | collective-permute-start | bytes 6152 | tf_op jit(solution)/shard_map/ppermute | solution.py:298
  125.4 4.8 %collective-permute-start.26 = (f32[512]{0:T(512)S(1)}, f32[512]{0:T(512)S(1)}, u32[]{:S(2)}, u32[]{:S(2)}) collective-permute-start(f32[512]{0:T(512)S(1)} %add.37), channel_id=1, source_target_pairs={{0,3},{1,2},{2,1},{3,0},{4,7},{5,6},{6,5},{7,4},{8,11},{9,10},{10,... | collective-permute-start | bytes 6152 | tf_op jit(solution)/shard_map/ppermute | solution.py:298
  127.2 3.6 %collective-permute-start.25 = (f32[512]{0:T(512)S(1)}, f32[512]{0:T(512)S(1)}, u32[]{:S(2)}, u32[]{:S(2)}) collective-permute-start(f32[512]{0:T(512)S(1)} %add.37), channel_id=1, source_target_pairs={{0,1},{1,0},{2,3},{3,2},{4,5},{5,4},{6,7},{7,6},{8,9},{9,8},{10,11... | collective-permute-start | bytes 6152 | tf_op jit(solution)/shard_map/ppermute | solution.py:298
  (5 other events, 46.0 us)

commit v5 on v4

--- a/solution.py
+++ b/solution.py
@@ -220,26 +220,26 @@
     )(info, q, *kvs, *carry)
 
 
-def out_kernel(parts, cols, info_ref, *refs):
-    count = 4
+def out_kernel(parts, cols, places, info_ref, *refs):
+    count = len(places)
     w_refs, head_refs, (sum_ref, square_ref, lhs) = (
         refs[:count],
         refs[count : count + parts],
         refs[count + parts :],
     )
     core, group = info_ref[0], info_ref[1]
-    groups, half, wide = w_refs[0].shape
-    for m in range(parts):
-        for i, side in enumerate((core, 1 - core)):
-            span = pl.ds(pl.multiple_of(side * half, half), half)
-            lhs[2 * i + m // groups, :, m % groups * half : (m % groups + 1) * half] = (
-                head_refs[m][:, span]
-            )
-    total = None
-    for i in range(count):
+    half, wide = w_refs[0].shape[1:]
+    total, at = None, 0
+    for w_ref, (side, members) in zip(w_refs, places):
+        side = core if side == 0 else 1 - core
+        span = pl.ds(pl.multiple_of(side * half, half), half)
+        first = at
+        for m in members:
+            lhs[:, at : at + half] = head_refs[m][:, span]
+            at += half
         product = jnp.dot(
-            lhs[i],
-            w_refs[i][...].reshape(groups * half, wide),
+            lhs[:, first:at],
+            w_ref[...].reshape(at - first, wide),
             preferred_element_type=jnp.float32,
         )
         total = product if total is None else total + product
@@ -258,19 +258,19 @@
     square_ref[...] = sums[:1]
 
 
-def out_project(info, heads, weights, cols):
+def out_project(info, heads, weights, places, cols):
     rows, inner = heads[0].shape
     parts = len(heads)
     whole = pl.BlockSpec(memory_space=pltpu.VMEM)
     return pl.pallas_call(
-        functools.partial(out_kernel, parts, cols),
+        functools.partial(out_kernel, parts, cols, places),
         in_specs=[pl.BlockSpec(memory_space=pltpu.SMEM)] + [whole] * (parts + len(weights)),
         out_specs=[whole] * 2,
         out_shape=[
             jax.ShapeDtypeStruct((rows, cols), jnp.float32),
             jax.ShapeDtypeStruct((1, rows), jnp.float32),
         ],
-        scratch_shapes=[pltpu.VMEM((len(weights), rows, parts * inner // 4), jnp.bfloat16)],
+        scratch_shapes=[pltpu.VMEM((rows, parts * inner), jnp.bfloat16)],
         compiler_params=pltpu.CompilerParams(vmem_limit_bytes=32 * 2**20),
         cost_estimate=pl.CostEstimate(
             flops=2 * rows * inner * parts * cols, bytes_accessed=6 * 10**6, transcendentals=0
@@ -302,10 +302,6 @@
         which, tokens, norm_gain, [k_weight, v_weight], None, "project_kv", o_weight, n_tp
     )
     (queries,) = project(which, tokens, norm_gain, [q_weight], query_scale, "project_q")
-    cuts = [c if m == 0 else tp_xor(c, m) for m, c in enumerate(cuts)]
-    mine = jnp.stack([c[0] for c in cuts])
-    passed = jnp.stack([c[1] for c in cuts])
-
     first_block = jnp.sum((doc_ids[None, :] < doc_ids[:, None]).astype(jnp.int32), axis=1)
     own_first = lax.dynamic_slice_in_dim(first_block, shard * blocks, blocks, 0)
     plane_first = (shard // PLANE - BACK) * PLANE * blocks
@@ -319,18 +315,25 @@
     target = plan * blocks + rank
     picker = (target[None, :] == block_ids[:, None]).astype(jnp.bfloat16)
 
-    back_one = ctx_z(own_kv, 1)
-    back_two = ctx_z(back_one, 1)
-    across = [ctx_xor(near, 2) for near in (own_kv, back_one, back_two)]
+    planes = [own_kv, ctx_z(own_kv, 1)]
+    across = [ctx_xor(own_kv, 2)]
+    cuts = [tp_xor(c, m) if m % 2 else c for m, c in enumerate(cuts)]
+    planes, queries, cuts[2] = lax.optimization_barrier((planes, queries, cuts[2]))
+    planes.append(ctx_z(planes[1], 1))
+    across += [ctx_xor(near, 2) for near in planes[1:]]
+    cuts[2] = tp_xor(cuts[2], 2)
     carry = []
-    for stage, near in enumerate((own_kv, back_one)):
+    for stage in range(BACK):
+        near = planes[stage]
         kvs = [near, ctx_xor(near, 1), across[stage], ctx_xor(across[stage], 1)]
         carry = attend(stage, info, queries, kvs, carry)
+    mine = jnp.stack([c[0] for c in cuts])
+    passed = jnp.stack([c[1] for c in cuts])
     far, carry, mine, passed, picker = lax.optimization_barrier(
         (across[BACK], carry, mine, passed, picker)
     )
     passed = tp_xor(passed, n_tp // 2)
-    kvs = [back_two, ctx_xor(back_two, 1), far, ctx_xor(far, 1)]
+    kvs = [planes[BACK], ctx_xor(planes[BACK], 1), far, ctx_xor(far, 1)]
     natural = attend(BACK, info, queries, kvs, carry)
 
     width = natural.shape[1]
@@ -340,6 +343,8 @@
     gathered = lax.all_to_all(striped, "ctx", 0, 0, tiled=True)
     gathered, mine, passed = lax.optimization_barrier((gathered, mine, passed))
     weights = [mine, passed, ctx_xor(mine, 1), ctx_xor(passed, 1)]
+    kept, crossed = tuple(range(n_tp // 2)), tuple(range(n_tp // 2, n_tp))
+    places = ((0, kept), (0, crossed), (1, kept), (1, crossed))
     ordered = jnp.dot(
         picker,
         gathered.reshape(total_blocks, piece * width),
@@ -358,7 +363,7 @@
     heads[5] = tp_xor(heads[4], 1)
     heads[7] = tp_xor(heads[4], 3)
     heads[6] = tp_xor(heads[2], 4)
-    summed, squares = out_project(which, heads, weights, cols)
+    summed, squares = out_project(which, heads, weights, places, cols)
     squares = squares.reshape(rows)
     squares = squares + tp_xor(squares, 4)
     squares = squares + tp_xor(squares, 1) + tp_xor(squares, 3) + tp_xor(squares, 2)

time: 132 us -> 123 us (0.932)
  waiting for transfers between devices: 60 us -> 51.1 us
    ppermute x15, waiting for transfers between devices: 34.4 us -> 23.7 us  [tp_xor(): return lax.ppermute(a, 'tp', [(i, i ^ m) for i in range(n_tp)])]
    all_to_all x1, waiting for transfers between devices: 7.5 us -> 9.58 us  [local(): gathered = lax.all_to_all(striped, 'ctx', 0, 0, tiled=True)]
    all_to_all x1, starting transfers between devices: 9.95 us -> 11.9 us  [local(): gathered = lax.all_to_all(striped, 'ctx', 0, 0, tiled=True)]
    ppermute x11, waiting for transfers between devices: 3.12 us -> 1.21 us  [ctx_xor(): return lax.ppermute(a, 'ctx', [(i, i ^ m) for i in range(n_ctx)])]
    ppermute x2, waiting for transfers between devices: 3.56 us -> 5.15 us  [ctx_z(): lax.ppermute(a, 'ctx', [(i, (i + d * PLANE) % n_ctx) for i in range(n_ctx)])]
  transfers between devices with their start and end apart: 30 -> 30, of which waited for: 15 -> 16; matrix products, arithmetic and copies ran while one was open for 2% -> 3% of each run, Pallas kernels for 8% -> 9%
where the time goes in v5:
time: 123 us; the launch traced here: 124 us
  waiting for transfers between devices  51.1 us (42%)
  starting transfers between devices  44.1 us (36%)
  Pallas kernels  21.9 us (18%)
  local copies, waits for them, and re-layouts  4.48 us (4%)
  other arithmetic  1.57 us (1%)
    ppermute x15, waiting for transfers between devices, tp_xor(): return lax.ppermute(a, 'tp', [(i, i ^ m) for i in range(n_tp)])  23.7 us
    ppermute x15, starting transfers between devices, tp_xor(): return lax.ppermute(a, 'tp', [(i, i ^ m) for i in range(n_tp)])  20 us
    pallas_call x2, Pallas kernels, project(): pl.pallas_call(functools.partial(project_kernel, scale, tile, count, part...  13.9 us
    all_to_all x1, starting transfers between devices, local(): gathered = lax.all_to_all(striped, 'ctx', 0, 0, tiled=True)  11.9 us
    all_to_all x1, waiting for transfers between devices, local(): lax.all_to_all(ordered.reshape(n_ctx, blocks, piece * width), 'ctx', 0, 0...  11.5 us
    all_to_all x1, waiting for transfers between devices, local(): gathered = lax.all_to_all(striped, 'ctx', 0, 0, tiled=True)  9.58 us
    ppermute x11, starting transfers between devices, ctx_xor(): return lax.ppermute(a, 'ctx', [(i, i ^ m) for i in range(n_ctx)])  6.16 us
    ppermute x2, waiting for transfers between devices, ctx_z(): lax.ppermute(a, 'ctx', [(i, (i + d * PLANE) % n_ctx) for i in range(n_ctx)])  5.15 us
  transfers between devices with their start and end apart: 30, of which 16 were waited for; matrix products, arithmetic and copies ran while one was open for 3% of the time, Pallas kernels for 9%

profile of v5, /device:TPU:2, one launch (start us, length us, event | category | flops | bytes accessed | tf_op | source)
XLA Modules:
  0.0 123.6 jit_solution(58464843935678860)
XLA Ops:
  0.7 7.2 %project_kv.1 = (bf16[512,256]{1,0:T(8,128)(2,1)}, bf16[2,128,640]{2,1,0:T(8,128)(2,1)}, bf16[2,128,640]{2,1,0:T(8,128)(2,1)}, bf16[2,128,640]{2,1,0:T(8,128)(2,1)}, bf16[2,128,640]{2,1,0:T(8,128)(2,1)}) custom-call(s32[2]{0:T(128)} %pad_add_fusion.core_ref.info_ref, bf16[512,4608]{1,0:T(8,128)(2,1)} %x_hbm.3, f32[4608]{0:T(1024)} %g_ref.3, ...), custom_call_target="tpu_custom_call" | custom-call | flops 1207959552 | bytes 7077888 | tf_op jit(solution)/shard_map/project_kv/pallas_call | solution.py:102
  7.9 2.4 %collective-permute-start.8 = (bf16[512,256]{1,0:T(8,128)(2,1)}, bf16[512,256]{1,0:T(8,128)(2,1)S(1)}, u32[]{:S(2)}, u32[]{:S(2)}) collective-permute-start(bf16[512,256]{1,0:T(8,128)(2,1)} %get-tuple-element.33.refs_0_), channel_id=1, source_target_pairs={{0,16},{8,24},{16,0},{24,8},{32,48},{40,56},{48,32},{56,40},{64,80... | collective-permute-start | bytes 786440 | tf_op jit(solution)/shard_map/ppermute | solution.py:292
  10.4 1.6 %collective-permute-start.10 = (bf16[2,128,640]{2,1,0:T(8,128)(2,1)}, bf16[2,128,640]{2,1,0:T(8,128)(2,1)S(1)}, u32[]{:S(2)}, u32[]{:S(2)}) collective-permute-start(bf16[2,128,640]{2,1,0:T(8,128)(2,1)} %get-tuple-element.39), channel_id=1, source_target_pairs={{0,1},{1,0},{2,3},{3,2},{4,5},{5,4},{6,7},{7,6},{8,9},{9,8},{10,11... | collective-permute-start | bytes 983048 | tf_op jit(solution)/shard_map/ppermute | solution.py:298
  12.0 2.2 %collective-permute-start.12 = (bf16[2,128,640]{2,1,0:T(8,128)(2,1)}, bf16[2,128,640]{2,1,0:T(8,128)(2,1)S(1)}, u32[]{:S(2)}, u32[]{:S(2)}) collective-permute-start(bf16[2,128,640]{2,1,0:T(8,128)(2,1)} %get-tuple-element.41), channel_id=1, source_target_pairs={{0,3},{1,2},{2,1},{3,0},{4,7},{5,6},{6,5},{7,4},{8,11},{9,10},{10,... | collective-permute-start | bytes 983048 | tf_op jit(solution)/shard_map/ppermute | solution.py:298
  14.6 1.0 fusion.1
  15.7 6.7 %project_q.1.q_ref = bf16[512,256]{1,0:T(8,128)(2,1)} custom-call(s32[2]{0:T(128)} %pad_add_fusion.core_ref.info_ref, bf16[512,4608]{1,0:T(8,128)(2,1)} %x_hbm.3, f32[4608]{0:T(1024)} %g_ref.3, bf16[4608,256]{1,0:T(8,128)(2,1)} %refs_0_.3), custom_call_target="tpu_custom_call" | custom-call | flops 1207959552 | bytes 7077888 | tf_op jit(solution)/shard_map/project_q/pallas_call | solution.py:102
  22.5 1.5 %collective-permute-start.5 = (bf16[512,256]{1,0:T(8,128)(2,1)S(1)}, bf16[512,256]{1,0:T(8,128)(2,1)S(1)}, u32[]{:S(2)}, u32[]{:S(2)}) collective-permute-start(bf16[512,256]{1,0:T(8,128)(2,1)S(1)} %collective-permute-done.refs_0_), channel_id=1, source_target_pairs={{0,16},{8,24},{16,0},{24,8},{32,48},{40,56},{48,32},{56,40},{64,80... | collective-permute-start | bytes 786440 | tf_op jit(solution)/shard_map/ppermute | solution.py:292
  24.0 1.9 %collective-permute-start.1 = (bf16[512,256]{1,0:T(8,128)(2,1)S(1)}, bf16[512,256]{1,0:T(8,128)(2,1)S(1)}, u32[]{:S(2)}, u32[]{:S(2)}) collective-permute-start(bf16[512,256]{1,0:T(8,128)(2,1)S(1)} %collective-permute-done.refs_0_), channel_id=1, source_target_pairs={{0,32},{8,40},{16,48},{24,56},{32,64},{40,72},{48,80},{56,88},{64,... | collective-permute-start | bytes 786440 | tf_op jit(solution)/shard_map/ppermute | solution.py:295
  28.0 5.1 %collective-permute-done.1.refs_0_ = bf16[512,256]{1,0:T(8,128)(2,1)S(1)} collective-permute-done((bf16[512,256]{1,0:T(8,128)(2,1)S(1)}, bf16[512,256]{1,0:T(8,128)(2,1)S(1)}, u32[]{:S(2)}, u32[]{:S(2)}) %collective-permute-start.1) | collective-permute-done | bytes 262176 | tf_op jit(solution)/shard_map/ppermute | solution.py:295
  34.2 2.7 %attend.3 = (f32[2,512,128]{2,1,0:T(8,128)S(1)}, f32[2,512,128]{2,1,0:T(8,128)S(1)}) custom-call(s32[5]{0:T(128)S(1)} %pad_add_fusion.1.info_ref, bf16[512,256]{1,0:T(8,128)(2,1)S(1)} %copy-done, bf16[512,256]{1,0:T(8,128)(2,1)S(1)} %copy-done.2, bf16[512,256]{1,0:T(8,128)(2,1)S(1)} %collective-permute-done.7.refs_1_, ...), custom_call_target="tpu_custom_call" | custom-call | flops 2000000000 | bytes 4000000 | tf_op jit(solution)/shard_map/attend/pallas_call | solution.py:203
  39.5 2.1 %collective-permute-start.14 = (bf16[4,128,640]{2,1,0:T(8,128)(2,1)S(1)}, bf16[4,128,640]{2,1,0:T(8,128)(2,1)S(1)}, u32[]{:S(2)}, u32[]{:S(2)}) collective-permute-start(bf16[4,128,640]{2,1,0:T(8,128)(2,1)S(1)} %get-tuple-element.46), channel_id=1, source_target_pairs={{0,4},{1,5},{2,6},{3,7},{4,0},{5,1},{6,2},{7,3},{8,12},{9,13},{10,... | collective-permute-start | bytes 1966088 | tf_op jit(solution)/shard_map/ppermute | solution.py:298
  43.8 11.9 %all-to-all-start = ((bf16[32,4,1024]{2,1,0:T(4,128)(2,1)}), bf16[32,4,1024]{2,1,0:T(4,128)(2,1)S(1)}, u32[]{:S(2)}, u32[]{:S(2)}) async-start(bf16[32,4,1024]{2,1,0:T(4,128)(2,1)} %copy.18), calls=%async_computation | async-start | bytes 524288 | tf_op jit(solution)/shard_map/all_to_all | solution.py:343
  55.7 2.5 %collective-permute-done.14.refs_1_ = bf16[4,128,640]{2,1,0:T(8,128)(2,1)S(1)} collective-permute-done((bf16[4,128,640]{2,1,0:T(8,128)(2,1)S(1)}, bf16[4,128,640]{2,1,0:T(8,128)(2,1)S(1)}, u32[]{:S(2)}, u32[]{:S(2)}) %collective-permute-start.14) | collective-permute-done | bytes 655392 | tf_op jit(solution)/shard_map/ppermute | solution.py:298
  58.2 9.6 %all-to-all-done = bf16[32,4,1024]{2,1,0:T(4,128)(2,1)S(1)} async-done(((bf16[32,4,1024]{2,1,0:T(4,128)(2,1)}), bf16[32,4,1024]{2,1,0:T(4,128)(2,1)S(1)}, u32[]{:S(2)}, u32[]{:S(2)}) %all-to-all-start) | async-done | bytes 262176 | tf_op jit(solution)/shard_map/all_to_all | solution.py:343
  68.9 4.0 %all-to-all-start.1 = ((bf16[32,4,1024]{2,1,0:T(4,128)(2,1)}), bf16[32,4,1024]{2,1,0:T(4,128)(2,1)S(1)}, u32[]{:S(2)}, u32[]{:S(2)}) async-start(bf16[32,4,1024]{2,1,0:T(4,128)(2,1)} %reshape.35), calls=%async_computation.1 | async-start | bytes 524288 | tf_op jit(solution)/shard_map/all_to_all | solution.py:353
  73.5 11.5 %all-to-all-done.1 = bf16[32,4,1024]{2,1,0:T(4,128)(2,1)S(1)} async-done(((bf16[32,4,1024]{2,1,0:T(4,128)(2,1)}), bf16[32,4,1024]{2,1,0:T(4,128)(2,1)S(1)}, u32[]{:S(2)}, u32[]{:S(2)}) %all-to-all-start.1) | async-done | bytes 262176 | tf_op jit(solution)/shard_map/all_to_all | solution.py:353
  85.2 2.1 %collective-permute-start.20 = (bf16[512,256]{1,0:T(8,128)(2,1)S(1)}, bf16[512,256]{1,0:T(8,128)(2,1)S(1)}, u32[]{:S(2)}, u32[]{:S(2)}) collective-permute-start(bf16[512,256]{1,0:T(8,128)(2,1)S(1)} %reshape.37.refs_4_), channel_id=1, source_target_pairs={{0,4},{1,5},{2,6},{3,7},{4,0},{5,1},{6,2},{7,3},{8,12},{9,13},{10,... | collective-permute-start | bytes 786440 | tf_op jit(solution)/shard_map/ppermute | solution.py:298
  88.0 2.6 %collective-permute-start.19 = (bf16[512,256]{1,0:T(8,128)(2,1)S(1)}, bf16[512,256]{1,0:T(8,128)(2,1)S(1)}, u32[]{:S(2)}, u32[]{:S(2)}) collective-permute-start(bf16[512,256]{1,0:T(8,128)(2,1)S(1)} %reshape.37.refs_4_), channel_id=1, source_target_pairs={{0,3},{1,2},{2,1},{3,0},{4,7},{5,6},{6,5},{7,4},{8,11},{9,10},{10,... | collective-permute-start | bytes 786440 | tf_op jit(solution)/shard_map/ppermute | solution.py:298
  90.8 3.6 %collective-permute-done.20.refs_8_ = bf16[512,256]{1,0:T(8,128)(2,1)S(1)} collective-permute-done((bf16[512,256]{1,0:T(8,128)(2,1)S(1)}, bf16[512,256]{1,0:T(8,128)(2,1)S(1)}, u32[]{:S(2)}, u32[]{:S(2)}) %collective-permute-start.20) | collective-permute-done | bytes 262176 | tf_op jit(solution)/shard_map/ppermute | solution.py:298
  94.4 1.1 collective-permute-start.23
  95.4 2.6 %collective-permute-done.18.refs_6_ = bf16[512,256]{1,0:T(8,128)(2,1)S(1)} collective-permute-done((bf16[512,256]{1,0:T(8,128)(2,1)S(1)}, bf16[512,256]{1,0:T(8,128)(2,1)S(1)}, u32[]{:S(2)}, u32[]{:S(2)}) %collective-permute-start.18) | collective-permute-done | bytes 262176 | tf_op jit(solution)/shard_map/ppermute | solution.py:298
  98.1 1.6 %collective-permute-start.22 = (bf16[512,256]{1,0:T(8,128)(2,1)S(1)}, bf16[512,256]{1,0:T(8,128)(2,1)S(1)}, u32[]{:S(2)}, u32[]{:S(2)}) collective-permute-start(bf16[512,256]{1,0:T(8,128)(2,1)S(1)} %collective-permute-done.18.refs_6_), channel_id=1, source_target_pairs={{0,4},{1,5},{2,6},{3,7},{4,0},{5,1},{6,2},{7,3},{8,12},{9,13},{10,... | collective-permute-start | bytes 786440 | tf_op jit(solution)/shard_map/ppermute | solution.py:298
  99.6 2.1 %collective-permute-done.19.refs_7_ = bf16[512,256]{1,0:T(8,128)(2,1)S(1)} collective-permute-done((bf16[512,256]{1,0:T(8,128)(2,1)S(1)}, bf16[512,256]{1,0:T(8,128)(2,1)S(1)}, u32[]{:S(2)}, u32[]{:S(2)}) %collective-permute-start.19) | collective-permute-done | bytes 262176 | tf_op jit(solution)/shard_map/ppermute | solution.py:298
  102.1 5.2 %collective-permute-done.23.refs_11_ = bf16[512,256]{1,0:T(8,128)(2,1)S(1)} collective-permute-done((bf16[512,256]{1,0:T(8,128)(2,1)S(1)}, bf16[512,256]{1,0:T(8,128)(2,1)S(1)}, u32[]{:S(2)}, u32[]{:S(2)}) %collective-permute-start.23) | collective-permute-done | bytes 262176 | tf_op jit(solution)/shard_map/ppermute | solution.py:298
  107.3 3.5 %out_project.1 = (f32[512,576]{1,0:T(8,128)S(1)}, f32[1,512]{1,0:T(1,128)S(1)}) custom-call(s32[2]{0:T(128)S(1)} %copy-done.1, bf16[4,128,640]{2,1,0:T(8,128)(2,1)S(1)} %get-tuple-element.47.refs_0_, bf16[4,128,640]{2,1,0:T(8,128)(2,1)S(1)} %collective-permute-done.14.refs_1_, bf16[4,128,640]{2,1,0:T(8,128)(2,1)S(1)} %collective-permute-done.15.refs_2_, ...), custom_call_target="tpu_custom_call" | custom-call | flops 1207959552 | bytes 6000000 | tf_op jit(solution)/shard_map/out_project/pallas_call | solution.py:265
  110.8 1.6 %collective-permute-start.24 = (f32[512]{0:T(512)S(1)}, f32[512]{0:T(512)S(1)}, u32[]{:S(2)}, u32[]{:S(2)}) collective-permute-start(f32[512]{0:T(512)S(1)} %bitcast.12), channel_id=1, source_target_pairs={{0,4},{1,5},{2,6},{3,7},{4,0},{5,1},{6,2},{7,3},{8,12},{9,13},{10,... | collective-permute-start | bytes 6152 | tf_op jit(solution)/shard_map/ppermute | solution.py:298
  112.5 3.5 %collective-permute-done.24 = f32[512]{0:T(512)S(1)} collective-permute-done((f32[512]{0:T(512)S(1)}, f32[512]{0:T(512)S(1)}, u32[]{:S(2)}, u32[]{:S(2)}) %collective-permute-start.24) | collective-permute-done | bytes 2080 | tf_op jit(solution)/shard_map/ppermute | solution.py:298
  116.0 1.3 %collective-permute-start.27 = (f32[512]{0:T(512)S(1)}, f32[512]{0:T(512)S(1)}, u32[]{:S(2)}, u32[]{:S(2)}) collective-permute-start(f32[512]{0:T(512)S(1)} %add.37), channel_id=1, source_target_pairs={{0,2},{1,3},{2,0},{3,1},{4,6},{5,7},{6,4},{7,5},{8,10},{9,11},{10,... | collective-permute-start | bytes 6152 | tf_op jit(solution)/shard_map/ppermute | solution.py:298
  117.3 1.5 %collective-permute-start.26 = (f32[512]{0:T(512)S(1)}, f32[512]{0:T(512)S(1)}, u32[]{:S(2)}, u32[]{:S(2)}) collective-permute-start(f32[512]{0:T(512)S(1)} %add.37), channel_id=1, source_target_pairs={{0,3},{1,2},{2,1},{3,0},{4,7},{5,6},{6,5},{7,4},{8,11},{9,10},{10,... | collective-permute-start | bytes 6152 | tf_op jit(solution)/shard_map/ppermute | solution.py:298
  119.5 1.6 %collective-permute-done.27 = f32[512]{0:T(512)S(1)} collective-permute-done((f32[512]{0:T(512)S(1)}, f32[512]{0:T(512)S(1)}, u32[]{:S(2)}, u32[]{:S(2)}) %collective-permute-start.27) | collective-permute-done | bytes 2080 | tf_op jit(solution)/shard_map/ppermute | solution.py:298
  121.1 1.0 collective-permute-done.26
  122.6 1.1 copy.17
  (73 shorter events, 13.4 us)
Async XLA Ops:
  7.9 18.1 %collective-permute-start.8 = (bf16[512,256]{1,0:T(8,128)(2,1)}, bf16[512,256]{1,0:T(8,128)(2,1)S(1)}, u32[]{:S(2)}, u32[]{:S(2)}) collective-permute-start(bf16[512,256]{1,0:T(8,128)(2,1)} %get-tuple-element.33.refs_0_), channel_id=1, source_target_pairs={{0,16},{8,24},{16,0},{24,8},{32,48},{40,56},{48,32},{56,40},{64,80... | collective-permute-start | bytes 786440 | tf_op jit(solution)/shard_map/ppermute | solution.py:292
  10.2 12.3 %collective-permute-start = (bf16[512,256]{1,0:T(8,128)(2,1)}, bf16[512,256]{1,0:T(8,128)(2,1)S(1)}, u32[]{:S(2)}, u32[]{:S(2)}) collective-permute-start(bf16[512,256]{1,0:T(8,128)(2,1)} %get-tuple-element.33.refs_0_), channel_id=1, source_target_pairs={{0,32},{8,40},{16,48},{24,56},{32,64},{40,72},{48,80},{56,88},{64,... | collective-permute-start | bytes 786440 | tf_op jit(solution)/shard_map/ppermute | solution.py:295
  10.4 15.5 %collective-permute-start.10 = (bf16[2,128,640]{2,1,0:T(8,128)(2,1)}, bf16[2,128,640]{2,1,0:T(8,128)(2,1)S(1)}, u32[]{:S(2)}, u32[]{:S(2)}) collective-permute-start(bf16[2,128,640]{2,1,0:T(8,128)(2,1)} %get-tuple-element.39), channel_id=1, source_target_pairs={{0,1},{1,0},{2,3},{3,2},{4,5},{5,4},{6,7},{7,6},{8,9},{9,8},{10,11... | collective-permute-start | bytes 983048 | tf_op jit(solution)/shard_map/ppermute | solution.py:298
  12.0 14.5 %collective-permute-start.12 = (bf16[2,128,640]{2,1,0:T(8,128)(2,1)}, bf16[2,128,640]{2,1,0:T(8,128)(2,1)S(1)}, u32[]{:S(2)}, u32[]{:S(2)}) collective-permute-start(bf16[2,128,640]{2,1,0:T(8,128)(2,1)} %get-tuple-element.41), channel_id=1, source_target_pairs={{0,3},{1,2},{2,1},{3,0},{4,7},{5,6},{6,5},{7,4},{8,11},{9,10},{10,... | collective-permute-start | bytes 983048 | tf_op jit(solution)/shard_map/ppermute | solution.py:298
  22.5 11.2 %collective-permute-start.5 = (bf16[512,256]{1,0:T(8,128)(2,1)S(1)}, bf16[512,256]{1,0:T(8,128)(2,1)S(1)}, u32[]{:S(2)}, u32[]{:S(2)}) collective-permute-start(bf16[512,256]{1,0:T(8,128)(2,1)S(1)} %collective-permute-done.refs_0_), channel_id=1, source_target_pairs={{0,16},{8,24},{16,0},{24,8},{32,48},{40,56},{48,32},{56,40},{64,80... | collective-permute-start | bytes 786440 | tf_op jit(solution)/shard_map/ppermute | solution.py:292
  24.0 9.1 %collective-permute-start.1 = (bf16[512,256]{1,0:T(8,128)(2,1)S(1)}, bf16[512,256]{1,0:T(8,128)(2,1)S(1)}, u32[]{:S(2)}, u32[]{:S(2)}) collective-permute-start(bf16[512,256]{1,0:T(8,128)(2,1)S(1)} %collective-permute-done.refs_0_), channel_id=1, source_target_pairs={{0,32},{8,40},{16,48},{24,56},{32,64},{40,72},{48,80},{56,88},{64,... | collective-permute-start | bytes 786440 | tf_op jit(solution)/shard_map/ppermute | solution.py:295
  26.0 7.7 %collective-permute-start.7 = (bf16[512,256]{1,0:T(8,128)(2,1)S(1)}, bf16[512,256]{1,0:T(8,128)(2,1)S(1)}, u32[]{:S(2)}, u32[]{:S(2)}) collective-permute-start(bf16[512,256]{1,0:T(8,128)(2,1)S(1)} %copy-done.2), channel_id=1, source_target_pairs={{0,8},{8,0},{16,24},{24,16},{32,40},{40,32},{48,56},{56,48},{64,72... | collective-permute-start | bytes 786440 | tf_op jit(solution)/shard_map/ppermute | solution.py:292
  26.0 1.9 %collective-permute-start.9 = (bf16[512,256]{1,0:T(8,128)(2,1)S(1)}, bf16[512,256]{1,0:T(8,128)(2,1)S(1)}, u32[]{:S(2)}, u32[]{:S(2)}) collective-permute-start(bf16[512,256]{1,0:T(8,128)(2,1)S(1)} %collective-permute-done.8.refs_2_), channel_id=1, source_target_pairs={{0,8},{8,0},{16,24},{24,16},{32,40},{40,32},{48,56},{56,48},{64,72... | collective-permute-start | bytes 786440 | tf_op jit(solution)/shard_map/ppermute | solution.py:292
  26.5 11.3 %collective-permute-start.11 = (bf16[2,128,640]{2,1,0:T(8,128)(2,1)S(1)}, bf16[2,128,640]{2,1,0:T(8,128)(2,1)S(1)}, u32[]{:S(2)}, u32[]{:S(2)}) collective-permute-start(bf16[2,128,640]{2,1,0:T(8,128)(2,1)S(1)} %copy-done.4), channel_id=1, source_target_pairs={{0,2},{1,3},{2,0},{3,1},{4,6},{5,7},{6,4},{7,5},{8,10},{9,11},{10,... | collective-permute-start | bytes 983048 | tf_op jit(solution)/shard_map/ppermute | solution.py:298
  27.9 10.2 %collective-permute-start.4 = (bf16[512,256]{1,0:T(8,128)(2,1)S(1)}, bf16[512,256]{1,0:T(8,128)(2,1)S(1)}, u32[]{:S(2)}, u32[]{:S(2)}) collective-permute-start(bf16[512,256]{1,0:T(8,128)(2,1)S(1)} %collective-permute-done.refs_0_), channel_id=1, source_target_pairs={{0,8},{8,0},{16,24},{24,16},{32,40},{40,32},{48,56},{56,48},{64,72... | collective-permute-start | bytes 786440 | tf_op jit(solution)/shard_map/ppermute | solution.py:292
  33.2 6.4 %collective-permute-start.3 = (bf16[512,256]{1,0:T(8,128)(2,1)S(1)}, bf16[512,256]{1,0:T(8,128)(2,1)S(1)}, u32[]{:S(2)}, u32[]{:S(2)}) collective-permute-start(bf16[512,256]{1,0:T(8,128)(2,1)S(1)} %collective-permute-done.1.refs_0_), channel_id=1, source_target_pairs={{0,16},{8,24},{16,0},{24,8},{32,48},{40,56},{48,32},{56,40},{64,80... | collective-permute-start | bytes 786440 | tf_op jit(solution)/shard_map/ppermute | solution.py:292
  33.7 8.0 %collective-permute-start.2 = (bf16[512,256]{1,0:T(8,128)(2,1)S(1)}, bf16[512,256]{1,0:T(8,128)(2,1)S(1)}, u32[]{:S(2)}, u32[]{:S(2)}) collective-permute-start(bf16[512,256]{1,0:T(8,128)(2,1)S(1)} %collective-permute-done.1.refs_0_), channel_id=1, source_target_pairs={{0,8},{8,0},{16,24},{24,16},{32,40},{40,32},{48,56},{56,48},{64,72... | collective-permute-start | bytes 786440 | tf_op jit(solution)/shard_map/ppermute | solution.py:292
  33.7 4.4 %collective-permute-start.6 = (bf16[512,256]{1,0:T(8,128)(2,1)S(1)}, bf16[512,256]{1,0:T(8,128)(2,1)S(1)}, u32[]{:S(2)}, u32[]{:S(2)}) collective-permute-start(bf16[512,256]{1,0:T(8,128)(2,1)S(1)} %collective-permute-done.5.refs_2_), channel_id=1, source_target_pairs={{0,8},{8,0},{16,24},{24,16},{32,40},{40,32},{48,56},{56,48},{64,72... | collective-permute-start | bytes 786440 | tf_op jit(solution)/shard_map/ppermute | solution.py:292
  39.5 2.1 %collective-permute-start.13 = (bf16[512,256]{1,0:T(8,128)(2,1)S(1)}, bf16[512,256]{1,0:T(8,128)(2,1)S(1)}, u32[]{:S(2)}, u32[]{:S(2)}) collective-permute-start(bf16[512,256]{1,0:T(8,128)(2,1)S(1)} %collective-permute-done.3.refs_2_), channel_id=1, source_target_pairs={{0,8},{8,0},{16,24},{24,16},{32,40},{40,32},{48,56},{56,48},{64,72... | collective-permute-start | bytes 786440 | tf_op jit(solution)/shard_map/ppermute | solution.py:292
  39.5 18.6 %collective-permute-start.14 = (bf16[4,128,640]{2,1,0:T(8,128)(2,1)S(1)}, bf16[4,128,640]{2,1,0:T(8,128)(2,1)S(1)}, u32[]{:S(2)}, u32[]{:S(2)}) collective-permute-start(bf16[4,128,640]{2,1,0:T(8,128)(2,1)S(1)} %get-tuple-element.46), channel_id=1, source_target_pairs={{0,4},{1,5},{2,6},{3,7},{4,0},{5,1},{6,2},{7,3},{8,12},{9,13},{10,... | collective-permute-start | bytes 1966088 | tf_op jit(solution)/shard_map/ppermute | solution.py:298
  43.8 24.0 %all-to-all-start = ((bf16[32,4,1024]{2,1,0:T(4,128)(2,1)}), bf16[32,4,1024]{2,1,0:T(4,128)(2,1)S(1)}, u32[]{:S(2)}, u32[]{:S(2)}) async-start(bf16[32,4,1024]{2,1,0:T(4,128)(2,1)} %copy.18), calls=%async_computation | async-start | bytes 524288 | tf_op jit(solution)/shard_map/all_to_all | solution.py:343
  68.0 39.2 %copy-start.1 = (s32[2]{0:T(128)S(1)}, s32[2]{0:T(128)}, u32[]{:S(2)}) copy-start(s32[2]{0:T(128)} %pad_add_fusion.core_ref.info_ref) | copy-start | bytes 28
  68.9 16.1 %all-to-all-start.1 = ((bf16[32,4,1024]{2,1,0:T(4,128)(2,1)}), bf16[32,4,1024]{2,1,0:T(4,128)(2,1)S(1)}, u32[]{:S(2)}, u32[]{:S(2)}) async-start(bf16[32,4,1024]{2,1,0:T(4,128)(2,1)} %reshape.35), calls=%async_computation.1 | async-start | bytes 524288 | tf_op jit(solution)/shard_map/all_to_all | solution.py:353
  72.9 17.8 %collective-permute-start.15 = (bf16[4,128,640]{2,1,0:T(8,128)(2,1)S(1)}, bf16[4,128,640]{2,1,0:T(8,128)(2,1)S(1)}, u32[]{:S(2)}, u32[]{:S(2)}) collective-permute-start(bf16[4,128,640]{2,1,0:T(8,128)(2,1)S(1)} %get-tuple-element.47.refs_0_), channel_id=1, source_target_pairs={{0,8},{8,0},{16,24},{24,16},{32,40},{40,32},{48,56},{56,48},{64,72... | collective-permute-start | bytes 1966088 | tf_op jit(solution)/shard_map/ppermute | solution.py:292
  73.1 22.3 %collective-permute-start.16 = (bf16[4,128,640]{2,1,0:T(8,128)(2,1)S(1)}, bf16[4,128,640]{2,1,0:T(8,128)(2,1)S(1)}, u32[]{:S(2)}, u32[]{:S(2)}) collective-permute-start(bf16[4,128,640]{2,1,0:T(8,128)(2,1)S(1)} %collective-permute-done.14.refs_1_), channel_id=1, source_target_pairs={{0,8},{8,0},{16,24},{24,16},{32,40},{40,32},{48,56},{56,48},{64,72... | collective-permute-start | bytes 1966088 | tf_op jit(solution)/shard_map/ppermute | solution.py:292
  85.2 37.2 %copy-start.3 = (f32[576]{0:T(1024)S(1)}, f32[576]{0:T(1024)}, u32[]{:S(2)}) copy-start(f32[576]{0:T(1024)} %param.15) | copy-start | bytes 6916
  85.2 9.1 %collective-permute-start.20 = (bf16[512,256]{1,0:T(8,128)(2,1)S(1)}, bf16[512,256]{1,0:T(8,128)(2,1)S(1)}, u32[]{:S(2)}, u32[]{:S(2)}) collective-permute-start(bf16[512,256]{1,0:T(8,128)(2,1)S(1)} %reshape.37.refs_4_), channel_id=1, source_target_pairs={{0,4},{1,5},{2,6},{3,7},{4,0},{5,1},{6,2},{7,3},{8,12},{9,13},{10,... | collective-permute-start | bytes 786440 | tf_op jit(solution)/shard_map/ppermute | solution.py:298
  87.3 10.8 %collective-permute-start.18 = (bf16[512,256]{1,0:T(8,128)(2,1)S(1)}, bf16[512,256]{1,0:T(8,128)(2,1)S(1)}, u32[]{:S(2)}, u32[]{:S(2)}) collective-permute-start(bf16[512,256]{1,0:T(8,128)(2,1)S(1)} %reshape.37.refs_4_), channel_id=1, source_target_pairs={{0,2},{1,3},{2,0},{3,1},{4,6},{5,7},{6,4},{7,5},{8,10},{9,11},{10,... | collective-permute-start | bytes 786440 | tf_op jit(solution)/shard_map/ppermute | solution.py:298
  88.0 13.7 %collective-permute-start.19 = (bf16[512,256]{1,0:T(8,128)(2,1)S(1)}, bf16[512,256]{1,0:T(8,128)(2,1)S(1)}, u32[]{:S(2)}, u32[]{:S(2)}) collective-permute-start(bf16[512,256]{1,0:T(8,128)(2,1)S(1)} %reshape.37.refs_4_), channel_id=1, source_target_pairs={{0,3},{1,2},{2,1},{3,0},{4,7},{5,6},{6,5},{7,4},{8,11},{9,10},{10,... | collective-permute-start | bytes 786440 | tf_op jit(solution)/shard_map/ppermute | solution.py:298
  90.7 11.4 %collective-permute-start.17 = (bf16[512,256]{1,0:T(8,128)(2,1)S(1)}, bf16[512,256]{1,0:T(8,128)(2,1)S(1)}, u32[]{:S(2)}, u32[]{:S(2)}) collective-permute-start(bf16[512,256]{1,0:T(8,128)(2,1)S(1)} %reshape.37.refs_4_), channel_id=1, source_target_pairs={{0,1},{1,0},{2,3},{3,2},{4,5},{5,4},{6,7},{7,6},{8,9},{9,8},{10,11... | collective-permute-start | bytes 786440 | tf_op jit(solution)/shard_map/ppermute | solution.py:298
  94.4 12.9 %collective-permute-start.23 = (bf16[512,256]{1,0:T(8,128)(2,1)S(1)}, bf16[512,256]{1,0:T(8,128)(2,1)S(1)}, u32[]{:S(2)}, u32[]{:S(2)}) collective-permute-start(bf16[512,256]{1,0:T(8,128)(2,1)S(1)} %collective-permute-done.20.refs_8_), channel_id=1, source_target_pairs={{0,3},{1,2},{2,1},{3,0},{4,7},{5,6},{6,5},{7,4},{8,11},{9,10},{10,... | collective-permute-start | bytes 786440 | tf_op jit(solution)/shard_map/ppermute | solution.py:298
  95.4 11.9 %collective-permute-start.21 = (bf16[512,256]{1,0:T(8,128)(2,1)S(1)}, bf16[512,256]{1,0:T(8,128)(2,1)S(1)}, u32[]{:S(2)}, u32[]{:S(2)}) collective-permute-start(bf16[512,256]{1,0:T(8,128)(2,1)S(1)} %collective-permute-done.20.refs_8_), channel_id=1, source_target_pairs={{0,1},{1,0},{2,3},{3,2},{4,5},{5,4},{6,7},{7,6},{8,9},{9,8},{10,11... | collective-permute-start | bytes 786440 | tf_op jit(solution)/shard_map/ppermute | solution.py:298
  98.1 9.2 %collective-permute-start.22 = (bf16[512,256]{1,0:T(8,128)(2,1)S(1)}, bf16[512,256]{1,0:T(8,128)(2,1)S(1)}, u32[]{:S(2)}, u32[]{:S(2)}) collective-permute-start(bf16[512,256]{1,0:T(8,128)(2,1)S(1)} %collective-permute-done.18.refs_6_), channel_id=1, source_target_pairs={{0,4},{1,5},{2,6},{3,7},{4,0},{5,1},{6,2},{7,3},{8,12},{9,13},{10,... | collective-permute-start | bytes 786440 | tf_op jit(solution)/shard_map/ppermute | solution.py:298
  110.8 5.2 %collective-permute-start.24 = (f32[512]{0:T(512)S(1)}, f32[512]{0:T(512)S(1)}, u32[]{:S(2)}, u32[]{:S(2)}) collective-permute-start(f32[512]{0:T(512)S(1)} %bitcast.12), channel_id=1, source_target_pairs={{0,4},{1,5},{2,6},{3,7},{4,0},{5,1},{6,2},{7,3},{8,12},{9,13},{10,... | collective-permute-start | bytes 6152 | tf_op jit(solution)/shard_map/ppermute | solution.py:298
  116.0 5.1 %collective-permute-start.27 = (f32[512]{0:T(512)S(1)}, f32[512]{0:T(512)S(1)}, u32[]{:S(2)}, u32[]{:S(2)}) collective-permute-start(f32[512]{0:T(512)S(1)} %add.37), channel_id=1, source_target_pairs={{0,2},{1,3},{2,0},{3,1},{4,6},{5,7},{6,4},{7,5},{8,10},{9,11},{10,... | collective-permute-start | bytes 6152 | tf_op jit(solution)/shard_map/ppermute | solution.py:298
  117.3 4.8 %collective-permute-start.26 = (f32[512]{0:T(512)S(1)}, f32[512]{0:T(512)S(1)}, u32[]{:S(2)}, u32[]{:S(2)}) collective-permute-start(f32[512]{0:T(512)S(1)} %add.37), channel_id=1, source_target_pairs={{0,3},{1,2},{2,1},{3,0},{4,7},{5,6},{6,5},{7,4},{8,11},{9,10},{10,... | collective-permute-start | bytes 6152 | tf_op jit(solution)/shard_map/ppermute | solution.py:298
  118.8 3.6 %collective-permute-start.25 = (f32[512]{0:T(512)S(1)}, f32[512]{0:T(512)S(1)}, u32[]{:S(2)}, u32[]{:S(2)}) collective-permute-start(f32[512]{0:T(512)S(1)} %add.37), channel_id=1, source_target_pairs={{0,1},{1,0},{2,3},{3,2},{4,5},{5,4},{6,7},{7,6},{8,9},{9,8},{10,11... | collective-permute-start | bytes 6152 | tf_op jit(solution)/shard_map/ppermute | solution.py:298
  (5 other events, 60.1 us)

commit v6 on v5

--- a/solution.py
+++ b/solution.py
@@ -19,7 +19,7 @@
 LOG2E = math.log2(math.e)
 
 
-def project_kernel(scale, tile, count, parts, core_ref, x_hbm, g_ref, *refs):
+def project_kernel(scale, tile, count, parts, x_hbm, g_ref, *refs):
     w_hbms, refs = refs[:count], refs[count:]
     o_hbm, refs = (refs[0], refs[1:]) if parts else (None, refs)
     out_ref, cut_refs, refs = refs[0], refs[1 : 1 + parts // 2], refs[1 + parts // 2 :]
@@ -45,7 +45,7 @@
         copy.start()
     cuts = []
     if parts:
-        core, group = core_ref[0], core_ref[1]
+        core, group = lax.rem(lax.axis_index("ctx"), 2), lax.axis_index("tp")
         half, wide = cut_refs[0].shape[1:]
         cols = o_hbm.shape[1] // parts
         for m in range(parts):
@@ -80,7 +80,7 @@
         copy.wait()
 
 
-def project(core, tokens, gain, weights, scale, name, o_weight=None, parts=0):
+def project(tokens, gain, weights, scale, name, o_weight=None, parts=0):
     rows, d = tokens.shape
     tile = 64
     count = len(weights)
@@ -90,7 +90,7 @@
     out_specs = [whole]
     out_shape = [jax.ShapeDtypeStruct((rows, width), jnp.bfloat16)]
     sems = [pltpu.SemaphoreType.DMA((rows // tile,)), pltpu.SemaphoreType.DMA((count,))]
-    operands = [core, tokens, gain, *weights]
+    operands = [tokens, gain, *weights]
     if parts:
         wide = -(-(o_weight.shape[1] // parts) // HD) * HD
         out_specs += [whole] * (parts // 2)
@@ -101,8 +101,7 @@
         operands.append(o_weight)
     return pl.pallas_call(
         functools.partial(project_kernel, scale, tile, count, parts),
-        in_specs=[pl.BlockSpec(memory_space=pltpu.SMEM), anywhere, whole]
-        + [anywhere] * (len(operands) - 3),
+        in_specs=[anywhere, whole] + [anywhere] * (len(operands) - 2),
         out_specs=out_specs,
         out_shape=out_shape,
         scratch_shapes=[
@@ -220,17 +219,20 @@
     )(info, q, *kvs, *carry)
 
 
-def out_kernel(parts, cols, places, info_ref, *refs):
+def out_kernel(heads, cols, places, *refs):
     count = len(places)
-    w_refs, head_refs, (sum_ref, square_ref, lhs) = (
-        refs[:count],
-        refs[count : count + parts],
-        refs[count + parts :],
-    )
-    core, group = info_ref[0], info_ref[1]
+    w_refs, refs = refs[:count], refs[count:]
+    head_refs, refs = refs[:heads], refs[heads:]
+    total = None
+    if cols:
+        before_ref, sum_ref, square_ref, lhs = refs
+        total = before_ref[...]
+    else:
+        sum_ref, lhs = refs
+    core, group = lax.rem(lax.axis_index("ctx"), 2), lax.axis_index("tp")
     half, wide = w_refs[0].shape[1:]
-    total, at = None, 0
-    for w_ref, (side, members) in zip(w_refs, places):
+    at = 0
+    for w_ref, (side, first_group, members) in zip(w_refs, places):
         side = core if side == 0 else 1 - core
         span = pl.ds(pl.multiple_of(side * half, half), half)
         first = at
@@ -239,10 +241,13 @@
             at += half
         product = jnp.dot(
             lhs[:, first:at],
-            w_ref[...].reshape(at - first, wide),
+            w_ref[first_group : first_group + len(members)].reshape(at - first, wide),
             preferred_element_type=jnp.float32,
         )
         total = product if total is None else total + product
+    if not cols:
+        sum_ref[...] = total
+        return
     total = jnp.where(group % 2 == 1, total[:, wide - cols :], total[:, :cols])
     sum_ref[...] = total
     square = total * total
@@ -258,25 +263,31 @@
     square_ref[...] = sums[:1]
 
 
-def out_project(info, heads, weights, places, cols):
+def out_project(heads, weights, places, before=None, cols=0):
     rows, inner = heads[0].shape
-    parts = len(heads)
+    wide = weights[0].shape[2]
     whole = pl.BlockSpec(memory_space=pltpu.VMEM)
-    return pl.pallas_call(
-        functools.partial(out_kernel, parts, cols, places),
-        in_specs=[pl.BlockSpec(memory_space=pltpu.SMEM)] + [whole] * (parts + len(weights)),
-        out_specs=[whole] * 2,
-        out_shape=[
+    if cols:
+        out_shape = [
             jax.ShapeDtypeStruct((rows, cols), jnp.float32),
             jax.ShapeDtypeStruct((1, rows), jnp.float32),
-        ],
-        scratch_shapes=[pltpu.VMEM((rows, parts * inner), jnp.bfloat16)],
+        ]
+        extra = [before]
+    else:
+        out_shape = [jax.ShapeDtypeStruct((rows, wide), jnp.float32)]
+        extra = []
+    return pl.pallas_call(
+        functools.partial(out_kernel, len(heads), cols, places),
+        in_specs=[whole] * (len(heads) + len(weights) + len(extra)),
+        out_specs=[whole] * len(out_shape),
+        out_shape=out_shape,
+        scratch_shapes=[pltpu.VMEM((rows, len(heads) * inner), jnp.bfloat16)],
         compiler_params=pltpu.CompilerParams(vmem_limit_bytes=32 * 2**20),
         cost_estimate=pl.CostEstimate(
-            flops=2 * rows * inner * parts * cols, bytes_accessed=6 * 10**6, transcendentals=0
+            flops=2 * rows * inner * len(heads) * wide, bytes_accessed=6 * 10**6, transcendentals=0
         ),
         name="out_project",
-    )(info, *weights, *heads)
+    )(*weights, *heads, *extra)
 
 
 def local(n_ctx, n_tp, tokens, norm_gain, q_weight, k_weight, v_weight, o_weight, post_gain, doc_ids, plan):
@@ -284,9 +295,7 @@
     blocks = rows // BLK
     total_blocks = doc_ids.shape[0]
     shard = lax.axis_index("ctx")
-    group = lax.axis_index("tp")
     cols = o_weight.shape[1] // n_tp
-    core = shard % 2
 
     def ctx_xor(a, m):
         return lax.ppermute(a, "ctx", [(i, i ^ m) for i in range(n_ctx)])
@@ -297,11 +306,11 @@
     def tp_xor(a, m):
         return lax.ppermute(a, "tp", [(i, i ^ m) for i in range(n_tp)])
 
-    which = jnp.stack([core, group]).astype(jnp.int32)
     own_kv, *cuts = project(
-        which, tokens, norm_gain, [k_weight, v_weight], None, "project_kv", o_weight, n_tp
-    )
-    (queries,) = project(which, tokens, norm_gain, [q_weight], query_scale, "project_q")
+        tokens, norm_gain, [k_weight, v_weight], None, "project_kv", o_weight, n_tp
+    )
+    (queries,) = project(tokens, norm_gain, [q_weight], query_scale, "project_q")
+
     first_block = jnp.sum((doc_ids[None, :] < doc_ids[:, None]).astype(jnp.int32), axis=1)
     own_first = lax.dynamic_slice_in_dim(first_block, shard * blocks, blocks, 0)
     plane_first = (shard // PLANE - BACK) * PLANE * blocks
@@ -309,24 +318,28 @@
         [(shard % PLANE).reshape(1), (own_first - plane_first) * BLK]
     ).astype(jnp.int32)
 
+    planes = [own_kv, ctx_z(own_kv, 1)]
+    across = [ctx_xor(own_kv, 2)]
+    cuts = [tp_xor(c, m) if m % 2 else c for m, c in enumerate(cuts)]
+    planes, queries, cuts[2], plan = lax.optimization_barrier((planes, queries, cuts[2], plan))
+    planes.append(ctx_z(planes[1], 1))
+    across.append(ctx_xor(planes[1], 2))
+    cuts[2] = tp_xor(cuts[2], 2)
+
     same = (plan[None, :] == plan[:, None]).astype(jnp.int32)
     block_ids = jnp.arange(total_blocks, dtype=jnp.int32)
     rank = jnp.sum(same * (block_ids[None, :] < block_ids[:, None]), axis=1)
     target = plan * blocks + rank
     picker = (target[None, :] == block_ids[:, None]).astype(jnp.bfloat16)
 
-    planes = [own_kv, ctx_z(own_kv, 1)]
-    across = [ctx_xor(own_kv, 2)]
-    cuts = [tp_xor(c, m) if m % 2 else c for m, c in enumerate(cuts)]
-    planes, queries, cuts[2] = lax.optimization_barrier((planes, queries, cuts[2]))
-    planes.append(ctx_z(planes[1], 1))
-    across += [ctx_xor(near, 2) for near in planes[1:]]
-    cuts[2] = tp_xor(cuts[2], 2)
     carry = []
     for stage in range(BACK):
         near = planes[stage]
         kvs = [near, ctx_xor(near, 1), across[stage], ctx_xor(across[stage], 1)]
         carry = attend(stage, info, queries, kvs, carry)
+        if stage == 0:
+            planes[BACK], carry = lax.optimization_barrier((planes[BACK], carry))
+            across.append(ctx_xor(planes[BACK], 2))
     mine = jnp.stack([c[0] for c in cuts])
     passed = jnp.stack([c[1] for c in cuts])
     far, carry, mine, passed, picker = lax.optimization_barrier(
@@ -343,8 +356,6 @@
     gathered = lax.all_to_all(striped, "ctx", 0, 0, tiled=True)
     gathered, mine, passed = lax.optimization_barrier((gathered, mine, passed))
     weights = [mine, passed, ctx_xor(mine, 1), ctx_xor(passed, 1)]
-    kept, crossed = tuple(range(n_tp // 2)), tuple(range(n_tp // 2, n_tp))
-    places = ((0, kept), (0, crossed), (1, kept), (1, crossed))
     ordered = jnp.dot(
         picker,
         gathered.reshape(total_blocks, piece * width),
@@ -363,10 +374,18 @@
     heads[5] = tp_xor(heads[4], 1)
     heads[7] = tp_xor(heads[4], 3)
     heads[6] = tp_xor(heads[2], 4)
-    summed, squares = out_project(which, heads, weights, places, cols)
+    half_tp = n_tp // 2
+    near = tuple(range(half_tp))
+    places = ((0, 0, near), (0, 0, (half_tp,)), (1, 0, near), (1, 0, (half_tp,)))
+    (summed,) = out_project(heads[: half_tp + 1], weights, places)
+    rest = tuple(range(half_tp - 1))
+    places = ((0, 1, rest), (1, 1, rest))
+    summed, squares = out_project(
+        heads[half_tp + 1 :], weights[1::2], places, summed, cols
+    )
     squares = squares.reshape(rows)
     squares = squares + tp_xor(squares, 4)
-    squares = squares + tp_xor(squares, 1) + tp_xor(squares, 3) + tp_xor(squares, 2)
+    squares = squares + tp_xor(squares, 2) + tp_xor(squares, 1) + tp_xor(squares, 3)
     scale = lax.rsqrt(squares / features + norm_eps)
     return (summed * scale[:, None] * post_gain).astype(jnp.bfloat16)
 

time: 123 us -> 122 us (level); the launches traced: 124 us -> 121 us
  starting transfers between devices: 44.1 us -> 48.1 us
  waiting for transfers between devices: 51.1 us -> 47.4 us
  Pallas kernels: 21.9 us -> 20.2 us
    ppermute x2, waiting for transfers between devices: 5.15 us -> 2.29 us  [ctx_z(): lax.ppermute(a, 'ctx', [(i, (i + d * PLANE) % n_ctx) for i in range(n_ctx)])]
    ppermute x15, starting transfers between devices: 20 us -> 22.3 us  [tp_xor(): return lax.ppermute(a, 'tp', [(i, i ^ m) for i in range(n_tp)])]
    ppermute x2, starting transfers between devices: 2.1 us -> 3.99 us  [ctx_z(): lax.ppermute(a, 'ctx', [(i, (i + d * PLANE) % n_ctx) for i in range(n_ctx)])]
    pallas_call x1 -> x2, Pallas kernels: 3.52 us -> 3.13 us  [out_project(): pl.pallas_call(functools.partial(out_kernel, len(heads), cols, places), i...]
  transfers between devices with their start and end apart: 30 -> 30, of which waited for: 16 -> 16; matrix products, arithmetic and copies ran while one was open for 3% -> 2% of each run, Pallas kernels for 9% -> 9%
where the time goes in v6:
time: 122 us; the launch traced here: 121 us
  starting transfers between devices  48.1 us (39%)
  waiting for transfers between devices  47.4 us (39%)
  Pallas kernels  20.2 us (17%)
  local copies, waits for them, and re-layouts  3.49 us (3%)
    ppermute x15, waiting for transfers between devices, tp_xor(): return lax.ppermute(a, 'tp', [(i, i ^ m) for i in range(n_tp)])  23.1 us
    ppermute x15, starting transfers between devices, tp_xor(): return lax.ppermute(a, 'tp', [(i, i ^ m) for i in range(n_tp)])  22.3 us
    pallas_call x2, Pallas kernels, project(): pl.pallas_call(functools.partial(project_kernel, scale, tile, count, part...  13.8 us
    all_to_all x1, starting transfers between devices, local(): gathered = lax.all_to_all(striped, 'ctx', 0, 0, tiled=True)  12.4 us
    all_to_all x1, waiting for transfers between devices, local(): lax.all_to_all(ordered.reshape(n_ctx, blocks, piece * width), 'ctx', 0, 0...  11.5 us
    all_to_all x1, waiting for transfers between devices, local(): gathered = lax.all_to_all(striped, 'ctx', 0, 0, tiled=True)  10.1 us
    ppermute x11, starting transfers between devices, ctx_xor(): return lax.ppermute(a, 'ctx', [(i, i ^ m) for i in range(n_ctx)])  5.44 us
    ppermute x2, starting transfers between devices, ctx_z(): lax.ppermute(a, 'ctx', [(i, (i + d * PLANE) % n_ctx) for i in range(n_ctx)])  3.99 us
  transfers between devices with their start and end apart: 30, of which 16 were waited for; matrix products, arithmetic and copies ran while one was open for 2% of the time, Pallas kernels for 9%

profile of v6, /device:TPU:2, one launch (start us, length us, event | category | flops | bytes accessed | tf_op | source)
XLA Modules:
  0.0 120.7 jit_solution(17133177093891141922)
XLA Ops:
  0.0 7.2 %project_kv.1 = (bf16[512,256]{1,0:T(8,128)(2,1)}, bf16[2,128,640]{2,1,0:T(8,128)(2,1)}, bf16[2,128,640]{2,1,0:T(8,128)(2,1)}, bf16[2,128,640]{2,1,0:T(8,128)(2,1)}, bf16[2,128,640]{2,1,0:T(8,128)(2,1)}) custom-call(bf16[512,4608]{1,0:T(8,128)(2,1)} %x_hbm.3, f32[4608]{0:T(1024)} %g_ref.3, bf16[4608,128]{1,0:T(8,128)(2,1)} %refs_0_.2, ...), custom_call_target="tpu_custom_call" | custom-call | flops 1207959552 | bytes 7077888 | tf_op jit(solution)/shard_map/project_kv/pallas_call | solution.py:102
  7.2 2.0 %collective-permute-start = (bf16[512,256]{1,0:T(8,128)(2,1)}, bf16[512,256]{1,0:T(8,128)(2,1)S(1)}, u32[]{:S(2)}, u32[]{:S(2)}) collective-permute-start(bf16[512,256]{1,0:T(8,128)(2,1)} %get-tuple-element.37.refs_0_), channel_id=1, source_target_pairs={{0,32},{8,40},{16,48},{24,56},{32,64},{40,72},{48,80},{56,88},{64,... | collective-permute-start | bytes 786440 | tf_op jit(solution)/shard_map/ppermute | solution.py:304
  9.7 1.6 %collective-permute-start.10 = (bf16[2,128,640]{2,1,0:T(8,128)(2,1)}, bf16[2,128,640]{2,1,0:T(8,128)(2,1)S(1)}, u32[]{:S(2)}, u32[]{:S(2)}) collective-permute-start(bf16[2,128,640]{2,1,0:T(8,128)(2,1)} %get-tuple-element.46), channel_id=1, source_target_pairs={{0,1},{1,0},{2,3},{3,2},{4,5},{5,4},{6,7},{7,6},{8,9},{9,8},{10,11... | collective-permute-start | bytes 983048 | tf_op jit(solution)/shard_map/ppermute | solution.py:307
  11.3 2.2 %collective-permute-start.12 = (bf16[2,128,640]{2,1,0:T(8,128)(2,1)}, bf16[2,128,640]{2,1,0:T(8,128)(2,1)S(1)}, u32[]{:S(2)}, u32[]{:S(2)}) collective-permute-start(bf16[2,128,640]{2,1,0:T(8,128)(2,1)} %get-tuple-element.48), channel_id=1, source_target_pairs={{0,3},{1,2},{2,1},{3,0},{4,7},{5,6},{6,5},{7,4},{8,11},{9,10},{10,... | collective-permute-start | bytes 983048 | tf_op jit(solution)/shard_map/ppermute | solution.py:307
  13.7 6.7 %project_q.1.q_ref = bf16[512,256]{1,0:T(8,128)(2,1)} custom-call(bf16[512,4608]{1,0:T(8,128)(2,1)} %x_hbm.3, f32[4608]{0:T(1024)} %g_ref.3, bf16[4608,256]{1,0:T(8,128)(2,1)} %refs_0_.3), custom_call_target="tpu_custom_call" | custom-call | flops 1207959552 | bytes 7077888 | tf_op jit(solution)/shard_map/project_q/pallas_call | solution.py:102
  20.6 2.0 %collective-permute-start.1 = (bf16[512,256]{1,0:T(8,128)(2,1)S(1)}, bf16[512,256]{1,0:T(8,128)(2,1)S(1)}, u32[]{:S(2)}, u32[]{:S(2)}) collective-permute-start(bf16[512,256]{1,0:T(8,128)(2,1)S(1)} %collective-permute-done.refs_0_), channel_id=1, source_target_pairs={{0,32},{8,40},{16,48},{24,56},{32,64},{40,72},{48,80},{56,88},{64,... | collective-permute-start | bytes 786440 | tf_op jit(solution)/shard_map/ppermute | solution.py:304
  22.6 1.5 %collective-permute-start.8 = (bf16[512,256]{1,0:T(8,128)(2,1)S(1)}, bf16[512,256]{1,0:T(8,128)(2,1)S(1)}, u32[]{:S(2)}, u32[]{:S(2)}) collective-permute-start(bf16[512,256]{1,0:T(8,128)(2,1)S(1)} %collective-permute-done.refs_0_), channel_id=1, source_target_pairs={{0,16},{8,24},{16,0},{24,8},{32,48},{40,56},{48,32},{56,40},{64,80... | collective-permute-start | bytes 786440 | tf_op jit(solution)/shard_map/ppermute | solution.py:301
  26.3 1.6 %attend.3 = (f32[2,512,128]{2,1,0:T(8,128)S(1)}, f32[2,512,128]{2,1,0:T(8,128)S(1)}) custom-call(s32[5]{0:T(128)S(1)} %pad_add_fusion.info_ref, bf16[512,256]{1,0:T(8,128)(2,1)S(1)} %copy-done, bf16[512,256]{1,0:T(8,128)(2,1)S(1)} %copy-done.1, bf16[512,256]{1,0:T(8,128)(2,1)S(1)} %collective-permute-done.2.refs_1_, ...), custom_call_target="tpu_custom_call" | custom-call | flops 2000000000 | bytes 4000000 | tf_op jit(solution)/shard_map/attend/pallas_call | solution.py:202
  27.9 2.3 %collective-permute-done.1.refs_0_ = bf16[512,256]{1,0:T(8,128)(2,1)S(1)} collective-permute-done((bf16[512,256]{1,0:T(8,128)(2,1)S(1)}, bf16[512,256]{1,0:T(8,128)(2,1)S(1)}, u32[]{:S(2)}, u32[]{:S(2)}) %collective-permute-start.1) | collective-permute-done | bytes 262176 | tf_op jit(solution)/shard_map/ppermute | solution.py:304
  30.2 1.5 %collective-permute-start.6 = (bf16[512,256]{1,0:T(8,128)(2,1)S(1)}, bf16[512,256]{1,0:T(8,128)(2,1)S(1)}, u32[]{:S(2)}, u32[]{:S(2)}) collective-permute-start(bf16[512,256]{1,0:T(8,128)(2,1)S(1)} %collective-permute-done.1.refs_0_), channel_id=1, source_target_pairs={{0,16},{8,24},{16,0},{24,8},{32,48},{40,56},{48,32},{56,40},{64,80... | collective-permute-start | bytes 786440 | tf_op jit(solution)/shard_map/ppermute | solution.py:301
  32.2 4.1 %collective-permute-done.11 = bf16[2,128,640]{2,1,0:T(8,128)(2,1)S(1)} collective-permute-done((bf16[2,128,640]{2,1,0:T(8,128)(2,1)S(1)}, bf16[2,128,640]{2,1,0:T(8,128)(2,1)S(1)}, u32[]{:S(2)}, u32[]{:S(2)}) %collective-permute-start.11) | collective-permute-done | bytes 327712 | tf_op jit(solution)/shard_map/ppermute | solution.py:307
  37.4 2.2 %collective-permute-start.14 = (bf16[4,128,640]{2,1,0:T(8,128)(2,1)S(1)}, bf16[4,128,640]{2,1,0:T(8,128)(2,1)S(1)}, u32[]{:S(2)}, u32[]{:S(2)}) collective-permute-start(bf16[4,128,640]{2,1,0:T(8,128)(2,1)S(1)} %get-tuple-element.54), channel_id=1, source_target_pairs={{0,4},{1,5},{2,6},{3,7},{4,0},{5,1},{6,2},{7,3},{8,12},{9,13},{10,... | collective-permute-start | bytes 1966088 | tf_op jit(solution)/shard_map/ppermute | solution.py:307
  41.7 12.4 %all-to-all-start = ((bf16[32,4,1024]{2,1,0:T(4,128)(2,1)}), bf16[32,4,1024]{2,1,0:T(4,128)(2,1)S(1)}, u32[]{:S(2)}, u32[]{:S(2)}) async-start(bf16[32,4,1024]{2,1,0:T(4,128)(2,1)} %copy.18), calls=%async_computation | async-start | bytes 524288 | tf_op jit(solution)/shard_map/all_to_all | solution.py:356
  54.1 1.9 %collective-permute-done.14.refs_1_.refs_0_ = bf16[4,128,640]{2,1,0:T(8,128)(2,1)S(1)} collective-permute-done((bf16[4,128,640]{2,1,0:T(8,128)(2,1)S(1)}, bf16[4,128,640]{2,1,0:T(8,128)(2,1)S(1)}, u32[]{:S(2)}, u32[]{:S(2)}) %collective-permute-start.14) | collective-permute-done | bytes 655392 | tf_op jit(solution)/shard_map/ppermute | solution.py:307
  56.1 10.1 %all-to-all-done = bf16[32,4,1024]{2,1,0:T(4,128)(2,1)S(1)} async-done(((bf16[32,4,1024]{2,1,0:T(4,128)(2,1)}), bf16[32,4,1024]{2,1,0:T(4,128)(2,1)S(1)}, u32[]{:S(2)}, u32[]{:S(2)}) %all-to-all-start) | async-done | bytes 262176 | tf_op jit(solution)/shard_map/all_to_all | solution.py:356
  67.3 4.0 %all-to-all-start.1 = ((bf16[32,4,1024]{2,1,0:T(4,128)(2,1)}), bf16[32,4,1024]{2,1,0:T(4,128)(2,1)S(1)}, u32[]{:S(2)}, u32[]{:S(2)}) async-start(bf16[32,4,1024]{2,1,0:T(4,128)(2,1)} %reshape.35), calls=%async_computation.1 | async-start | bytes 524288 | tf_op jit(solution)/shard_map/all_to_all | solution.py:364
  71.9 11.5 %all-to-all-done.1 = bf16[32,4,1024]{2,1,0:T(4,128)(2,1)S(1)} async-done(((bf16[32,4,1024]{2,1,0:T(4,128)(2,1)}), bf16[32,4,1024]{2,1,0:T(4,128)(2,1)S(1)}, u32[]{:S(2)}, u32[]{:S(2)}) %all-to-all-start.1) | async-done | bytes 262176 | tf_op jit(solution)/shard_map/all_to_all | solution.py:364
  83.7 2.1 %collective-permute-start.16 = (bf16[512,256]{1,0:T(8,128)(2,1)S(1)}, bf16[512,256]{1,0:T(8,128)(2,1)S(1)}, u32[]{:S(2)}, u32[]{:S(2)}) collective-permute-start(bf16[512,256]{1,0:T(8,128)(2,1)S(1)} %reshape.37.refs_4_), channel_id=1, source_target_pairs={{0,4},{1,5},{2,6},{3,7},{4,0},{5,1},{6,2},{7,3},{8,12},{9,13},{10,... | collective-permute-start | bytes 786440 | tf_op jit(solution)/shard_map/ppermute | solution.py:307
  87.7 2.2 %collective-permute-start.23 = (bf16[512,256]{1,0:T(8,128)(2,1)S(1)}, bf16[512,256]{1,0:T(8,128)(2,1)S(1)}, u32[]{:S(2)}, u32[]{:S(2)}) collective-permute-start(bf16[512,256]{1,0:T(8,128)(2,1)S(1)} %reshape.37.refs_4_), channel_id=1, source_target_pairs={{0,3},{1,2},{2,1},{3,0},{4,7},{5,6},{6,5},{7,4},{8,11},{9,10},{10,... | collective-permute-start | bytes 786440 | tf_op jit(solution)/shard_map/ppermute | solution.py:307
  89.8 3.0 %collective-permute-done.16.refs_8_ = bf16[512,256]{1,0:T(8,128)(2,1)S(1)} collective-permute-done((bf16[512,256]{1,0:T(8,128)(2,1)S(1)}, bf16[512,256]{1,0:T(8,128)(2,1)S(1)}, u32[]{:S(2)}, u32[]{:S(2)}) %collective-permute-start.16) | collective-permute-done | bytes 262176 | tf_op jit(solution)/shard_map/ppermute | solution.py:307
  93.5 3.1 %collective-permute-done.18.refs_6_ = bf16[512,256]{1,0:T(8,128)(2,1)S(1)} collective-permute-done((bf16[512,256]{1,0:T(8,128)(2,1)S(1)}, bf16[512,256]{1,0:T(8,128)(2,1)S(1)}, u32[]{:S(2)}, u32[]{:S(2)}) %collective-permute-start.18) | collective-permute-done | bytes 262176 | tf_op jit(solution)/shard_map/ppermute | solution.py:307
  96.5 1.6 %collective-permute-start.19 = (bf16[512,256]{1,0:T(8,128)(2,1)S(1)}, bf16[512,256]{1,0:T(8,128)(2,1)S(1)}, u32[]{:S(2)}, u32[]{:S(2)}) collective-permute-start(bf16[512,256]{1,0:T(8,128)(2,1)S(1)} %collective-permute-done.18.refs_6_), channel_id=1, source_target_pairs={{0,4},{1,5},{2,6},{3,7},{4,0},{5,1},{6,2},{7,3},{8,12},{9,13},{10,... | collective-permute-start | bytes 786440 | tf_op jit(solution)/shard_map/ppermute | solution.py:307
  99.1 1.4 %collective-permute-done.22.refs_5_ = bf16[512,256]{1,0:T(8,128)(2,1)S(1)} collective-permute-done((bf16[512,256]{1,0:T(8,128)(2,1)S(1)}, bf16[512,256]{1,0:T(8,128)(2,1)S(1)}, u32[]{:S(2)}, u32[]{:S(2)}) %collective-permute-start.22) | collective-permute-done | bytes 262176 | tf_op jit(solution)/shard_map/ppermute | solution.py:307
  100.5 1.3 %out_project.2.refs_5_ = f32[512,640]{1,0:T(8,128)S(1)} custom-call(bf16[4,128,640]{2,1,0:T(8,128)(2,1)S(1)} %get-tuple-element.58.refs_0_, bf16[4,128,640]{2,1,0:T(8,128)(2,1)S(1)} %collective-permute-done.14.refs_1_.refs_0_, bf16[4,128,640]{2,1,0:T(8,128)(2,1)S(1)} %collective-permute-done.21.refs_2_, ...), custom_call_target="tpu_custom_call" | custom-call | flops 838860800 | bytes 6000000 | tf_op jit(solution)/shard_map/out_project/pallas_call | solution.py:279
  101.8 2.3 %collective-permute-done.17.refs_2_ = bf16[512,256]{1,0:T(8,128)(2,1)S(1)} collective-permute-done((bf16[512,256]{1,0:T(8,128)(2,1)S(1)}, bf16[512,256]{1,0:T(8,128)(2,1)S(1)}, u32[]{:S(2)}, u32[]{:S(2)}) %collective-permute-start.17) | collective-permute-done | bytes 262176 | tf_op jit(solution)/shard_map/ppermute | solution.py:307
  104.4 1.3 %collective-permute-done.20.refs_4_ = bf16[512,256]{1,0:T(8,128)(2,1)S(1)} collective-permute-done((bf16[512,256]{1,0:T(8,128)(2,1)S(1)}, bf16[512,256]{1,0:T(8,128)(2,1)S(1)}, u32[]{:S(2)}, u32[]{:S(2)}) %collective-permute-start.20) | collective-permute-done | bytes 262176 | tf_op jit(solution)/shard_map/ppermute | solution.py:307
  105.7 1.8 %out_project.3 = (f32[512,576]{1,0:T(8,128)S(1)}, f32[1,512]{1,0:T(1,128)S(1)}) custom-call(bf16[4,128,640]{2,1,0:T(8,128)(2,1)S(1)} %collective-permute-done.14.refs_1_.refs_0_, bf16[4,128,640]{2,1,0:T(8,128)(2,1)S(1)} %collective-permute-done.15.refs_3_.refs_1_, bf16[512,256]{1,0:T(8,128)(2,1)S(1)} %collective-permute-done.17.refs_2_, ...), custom_call_target="tpu_custom_call" | custom-call | flops 503316480 | bytes 6000000 | tf_op jit(solution)/shard_map/out_project/pallas_call | solution.py:279
  107.5 2.0 %collective-permute-start.24 = (f32[512]{0:T(512)S(1)}, f32[512]{0:T(512)S(1)}, u32[]{:S(2)}, u32[]{:S(2)}) collective-permute-start(f32[512]{0:T(512)S(1)} %bitcast.10), channel_id=1, source_target_pairs={{0,4},{1,5},{2,6},{3,7},{4,0},{5,1},{6,2},{7,3},{8,12},{9,13},{10,... | collective-permute-start | bytes 6152 | tf_op jit(solution)/shard_map/ppermute | solution.py:307
  109.5 3.2 %collective-permute-done.24 = f32[512]{0:T(512)S(1)} collective-permute-done((f32[512]{0:T(512)S(1)}, f32[512]{0:T(512)S(1)}, u32[]{:S(2)}, u32[]{:S(2)}) %collective-permute-start.24) | collective-permute-done | bytes 2080 | tf_op jit(solution)/shard_map/ppermute | solution.py:307
  112.7 1.3 %collective-permute-start.25 = (f32[512]{0:T(512)S(1)}, f32[512]{0:T(512)S(1)}, u32[]{:S(2)}, u32[]{:S(2)}) collective-permute-start(f32[512]{0:T(512)S(1)} %add.33), channel_id=1, source_target_pairs={{0,2},{1,3},{2,0},{3,1},{4,6},{5,7},{6,4},{7,5},{8,10},{9,11},{10,... | collective-permute-start | bytes 6152 | tf_op jit(solution)/shard_map/ppermute | solution.py:307
  114.6 2.2 %collective-permute-start.27 = (f32[512]{0:T(512)S(1)}, f32[512]{0:T(512)S(1)}, u32[]{:S(2)}, u32[]{:S(2)}) collective-permute-start(f32[512]{0:T(512)S(1)} %add.33), channel_id=1, source_target_pairs={{0,3},{1,2},{2,1},{3,0},{4,7},{5,6},{6,5},{7,4},{8,11},{9,10},{10,... | collective-permute-start | bytes 6152 | tf_op jit(solution)/shard_map/ppermute | solution.py:307
  117.8 1.6 %collective-permute-done.27 = f32[512]{0:T(512)S(1)} collective-permute-done((f32[512]{0:T(512)S(1)}, f32[512]{0:T(512)S(1)}, u32[]{:S(2)}, u32[]{:S(2)}) %collective-permute-start.27) | collective-permute-done | bytes 2080 | tf_op jit(solution)/shard_map/ppermute | solution.py:307
  (73 shorter events, 15.5 us)
Async XLA Ops:
  0.0 13.5 %copy-start.5 = (s32[128]{0:T(128)S(1)}, s32[128]{0:T(128)}, u32[]{:S(2)}) copy-start(s32[128]{0:T(128)} %param.16) | copy-start | bytes 1540
  7.2 13.4 %collective-permute-start = (bf16[512,256]{1,0:T(8,128)(2,1)}, bf16[512,256]{1,0:T(8,128)(2,1)S(1)}, u32[]{:S(2)}, u32[]{:S(2)}) collective-permute-start(bf16[512,256]{1,0:T(8,128)(2,1)} %get-tuple-element.37.refs_0_), channel_id=1, source_target_pairs={{0,32},{8,40},{16,48},{24,56},{32,64},{40,72},{48,80},{56,88},{64,... | collective-permute-start | bytes 786440 | tf_op jit(solution)/shard_map/ppermute | solution.py:304
  9.2 15.1 %collective-permute-start.3 = (bf16[512,256]{1,0:T(8,128)(2,1)}, bf16[512,256]{1,0:T(8,128)(2,1)S(1)}, u32[]{:S(2)}, u32[]{:S(2)}) collective-permute-start(bf16[512,256]{1,0:T(8,128)(2,1)} %get-tuple-element.37.refs_0_), channel_id=1, source_target_pairs={{0,16},{8,24},{16,0},{24,8},{32,48},{40,56},{48,32},{56,40},{64,80... | collective-permute-start | bytes 786440 | tf_op jit(solution)/shard_map/ppermute | solution.py:301
  9.7 14.7 %collective-permute-start.10 = (bf16[2,128,640]{2,1,0:T(8,128)(2,1)}, bf16[2,128,640]{2,1,0:T(8,128)(2,1)S(1)}, u32[]{:S(2)}, u32[]{:S(2)}) collective-permute-start(bf16[2,128,640]{2,1,0:T(8,128)(2,1)} %get-tuple-element.46), channel_id=1, source_target_pairs={{0,1},{1,0},{2,3},{3,2},{4,5},{5,4},{6,7},{7,6},{8,9},{9,8},{10,11... | collective-permute-start | bytes 983048 | tf_op jit(solution)/shard_map/ppermute | solution.py:307
  11.3 13.7 %collective-permute-start.12 = (bf16[2,128,640]{2,1,0:T(8,128)(2,1)}, bf16[2,128,640]{2,1,0:T(8,128)(2,1)S(1)}, u32[]{:S(2)}, u32[]{:S(2)}) collective-permute-start(bf16[2,128,640]{2,1,0:T(8,128)(2,1)} %get-tuple-element.48), channel_id=1, source_target_pairs={{0,3},{1,2},{2,1},{3,0},{4,7},{5,6},{6,5},{7,4},{8,11},{9,10},{10,... | collective-permute-start | bytes 983048 | tf_op jit(solution)/shard_map/ppermute | solution.py:307
  20.6 9.6 %collective-permute-start.1 = (bf16[512,256]{1,0:T(8,128)(2,1)S(1)}, bf16[512,256]{1,0:T(8,128)(2,1)S(1)}, u32[]{:S(2)}, u32[]{:S(2)}) collective-permute-start(bf16[512,256]{1,0:T(8,128)(2,1)S(1)} %collective-permute-done.refs_0_), channel_id=1, source_target_pairs={{0,32},{8,40},{16,48},{24,56},{32,64},{40,72},{48,80},{56,88},{64,... | collective-permute-start | bytes 786440 | tf_op jit(solution)/shard_map/ppermute | solution.py:304
  22.6 9.1 %collective-permute-start.8 = (bf16[512,256]{1,0:T(8,128)(2,1)S(1)}, bf16[512,256]{1,0:T(8,128)(2,1)S(1)}, u32[]{:S(2)}, u32[]{:S(2)}) collective-permute-start(bf16[512,256]{1,0:T(8,128)(2,1)S(1)} %collective-permute-done.refs_0_), channel_id=1, source_target_pairs={{0,16},{8,24},{16,0},{24,8},{32,48},{40,56},{48,32},{56,40},{64,80... | collective-permute-start | bytes 786440 | tf_op jit(solution)/shard_map/ppermute | solution.py:301
  24.3 1.6 %collective-permute-start.2 = (bf16[512,256]{1,0:T(8,128)(2,1)S(1)}, bf16[512,256]{1,0:T(8,128)(2,1)S(1)}, u32[]{:S(2)}, u32[]{:S(2)}) collective-permute-start(bf16[512,256]{1,0:T(8,128)(2,1)S(1)} %copy-done.1), channel_id=1, source_target_pairs={{0,8},{8,0},{16,24},{24,16},{32,40},{40,32},{48,56},{56,48},{64,72... | collective-permute-start | bytes 786440 | tf_op jit(solution)/shard_map/ppermute | solution.py:301
  24.4 1.9 %collective-permute-start.4 = (bf16[512,256]{1,0:T(8,128)(2,1)S(1)}, bf16[512,256]{1,0:T(8,128)(2,1)S(1)}, u32[]{:S(2)}, u32[]{:S(2)}) collective-permute-start(bf16[512,256]{1,0:T(8,128)(2,1)S(1)} %collective-permute-done.3.refs_2_), channel_id=1, source_target_pairs={{0,8},{8,0},{16,24},{24,16},{32,40},{40,32},{48,56},{56,48},{64,72... | collective-permute-start | bytes 786440 | tf_op jit(solution)/shard_map/ppermute | solution.py:301
  25.0 11.3 %collective-permute-start.11 = (bf16[2,128,640]{2,1,0:T(8,128)(2,1)S(1)}, bf16[2,128,640]{2,1,0:T(8,128)(2,1)S(1)}, u32[]{:S(2)}, u32[]{:S(2)}) collective-permute-start(bf16[2,128,640]{2,1,0:T(8,128)(2,1)S(1)} %copy-done.4), channel_id=1, source_target_pairs={{0,2},{1,3},{2,0},{3,1},{4,6},{5,7},{6,4},{7,5},{8,10},{9,11},{10,... | collective-permute-start | bytes 983048 | tf_op jit(solution)/shard_map/ppermute | solution.py:307
  25.9 10.6 %collective-permute-start.7 = (bf16[512,256]{1,0:T(8,128)(2,1)S(1)}, bf16[512,256]{1,0:T(8,128)(2,1)S(1)}, u32[]{:S(2)}, u32[]{:S(2)}) collective-permute-start(bf16[512,256]{1,0:T(8,128)(2,1)S(1)} %collective-permute-done.refs_0_), channel_id=1, source_target_pairs={{0,8},{8,0},{16,24},{24,16},{32,40},{40,32},{48,56},{56,48},{64,72... | collective-permute-start | bytes 786440 | tf_op jit(solution)/shard_map/ppermute | solution.py:301
  30.2 7.1 %collective-permute-start.6 = (bf16[512,256]{1,0:T(8,128)(2,1)S(1)}, bf16[512,256]{1,0:T(8,128)(2,1)S(1)}, u32[]{:S(2)}, u32[]{:S(2)}) collective-permute-start(bf16[512,256]{1,0:T(8,128)(2,1)S(1)} %collective-permute-done.1.refs_0_), channel_id=1, source_target_pairs={{0,16},{8,24},{16,0},{24,8},{32,48},{40,56},{48,32},{56,40},{64,80... | collective-permute-start | bytes 786440 | tf_op jit(solution)/shard_map/ppermute | solution.py:301
  31.7 8.0 %collective-permute-start.5 = (bf16[512,256]{1,0:T(8,128)(2,1)S(1)}, bf16[512,256]{1,0:T(8,128)(2,1)S(1)}, u32[]{:S(2)}, u32[]{:S(2)}) collective-permute-start(bf16[512,256]{1,0:T(8,128)(2,1)S(1)} %collective-permute-done.1.refs_0_), channel_id=1, source_target_pairs={{0,8},{8,0},{16,24},{24,16},{32,40},{40,32},{48,56},{56,48},{64,72... | collective-permute-start | bytes 786440 | tf_op jit(solution)/shard_map/ppermute | solution.py:301
  31.7 4.9 %collective-permute-start.9 = (bf16[512,256]{1,0:T(8,128)(2,1)S(1)}, bf16[512,256]{1,0:T(8,128)(2,1)S(1)}, u32[]{:S(2)}, u32[]{:S(2)}) collective-permute-start(bf16[512,256]{1,0:T(8,128)(2,1)S(1)} %collective-permute-done.8.refs_2_), channel_id=1, source_target_pairs={{0,8},{8,0},{16,24},{24,16},{32,40},{40,32},{48,56},{56,48},{64,72... | collective-permute-start | bytes 786440 | tf_op jit(solution)/shard_map/ppermute | solution.py:301
  37.3 2.3 %collective-permute-start.13 = (bf16[512,256]{1,0:T(8,128)(2,1)S(1)}, bf16[512,256]{1,0:T(8,128)(2,1)S(1)}, u32[]{:S(2)}, u32[]{:S(2)}) collective-permute-start(bf16[512,256]{1,0:T(8,128)(2,1)S(1)} %collective-permute-done.6.refs_2_), channel_id=1, source_target_pairs={{0,8},{8,0},{16,24},{24,16},{32,40},{40,32},{48,56},{56,48},{64,72... | collective-permute-start | bytes 786440 | tf_op jit(solution)/shard_map/ppermute | solution.py:301
  37.4 18.7 %collective-permute-start.14 = (bf16[4,128,640]{2,1,0:T(8,128)(2,1)S(1)}, bf16[4,128,640]{2,1,0:T(8,128)(2,1)S(1)}, u32[]{:S(2)}, u32[]{:S(2)}) collective-permute-start(bf16[4,128,640]{2,1,0:T(8,128)(2,1)S(1)} %get-tuple-element.54), channel_id=1, source_target_pairs={{0,4},{1,5},{2,6},{3,7},{4,0},{5,1},{6,2},{7,3},{8,12},{9,13},{10,... | collective-permute-start | bytes 1966088 | tf_op jit(solution)/shard_map/ppermute | solution.py:307
  41.7 24.5 %all-to-all-start = ((bf16[32,4,1024]{2,1,0:T(4,128)(2,1)}), bf16[32,4,1024]{2,1,0:T(4,128)(2,1)S(1)}, u32[]{:S(2)}, u32[]{:S(2)}) async-start(bf16[32,4,1024]{2,1,0:T(4,128)(2,1)} %copy.18), calls=%async_computation | async-start | bytes 524288 | tf_op jit(solution)/shard_map/all_to_all | solution.py:356
  67.3 16.1 %all-to-all-start.1 = ((bf16[32,4,1024]{2,1,0:T(4,128)(2,1)}), bf16[32,4,1024]{2,1,0:T(4,128)(2,1)S(1)}, u32[]{:S(2)}, u32[]{:S(2)}) async-start(bf16[32,4,1024]{2,1,0:T(4,128)(2,1)} %reshape.35), calls=%async_computation.1 | async-start | bytes 524288 | tf_op jit(solution)/shard_map/all_to_all | solution.py:364
  71.3 16.3 %collective-permute-start.15 = (bf16[4,128,640]{2,1,0:T(8,128)(2,1)S(1)}, bf16[4,128,640]{2,1,0:T(8,128)(2,1)S(1)}, u32[]{:S(2)}, u32[]{:S(2)}) collective-permute-start(bf16[4,128,640]{2,1,0:T(8,128)(2,1)S(1)} %collective-permute-done.14.refs_1_.refs_0_), channel_id=1, source_target_pairs={{0,8},{8,0},{16,24},{24,16},{32,40},{40,32},{48,56},{56,48},{64,72... | collective-permute-start | bytes 1966088 | tf_op jit(solution)/shard_map/ppermute | solution.py:301
  71.5 26.5 %collective-permute-start.21 = (bf16[4,128,640]{2,1,0:T(8,128)(2,1)S(1)}, bf16[4,128,640]{2,1,0:T(8,128)(2,1)S(1)}, u32[]{:S(2)}, u32[]{:S(2)}) collective-permute-start(bf16[4,128,640]{2,1,0:T(8,128)(2,1)S(1)} %get-tuple-element.58.refs_0_), channel_id=1, source_target_pairs={{0,8},{8,0},{16,24},{24,16},{32,40},{40,32},{48,56},{56,48},{64,72... | collective-permute-start | bytes 1966088 | tf_op jit(solution)/shard_map/ppermute | solution.py:301
  83.7 9.1 %collective-permute-start.16 = (bf16[512,256]{1,0:T(8,128)(2,1)S(1)}, bf16[512,256]{1,0:T(8,128)(2,1)S(1)}, u32[]{:S(2)}, u32[]{:S(2)}) collective-permute-start(bf16[512,256]{1,0:T(8,128)(2,1)S(1)} %reshape.37.refs_4_), channel_id=1, source_target_pairs={{0,4},{1,5},{2,6},{3,7},{4,0},{5,1},{6,2},{7,3},{8,12},{9,13},{10,... | collective-permute-start | bytes 786440 | tf_op jit(solution)/shard_map/ppermute | solution.py:307
  85.7 10.8 %collective-permute-start.18 = (bf16[512,256]{1,0:T(8,128)(2,1)S(1)}, bf16[512,256]{1,0:T(8,128)(2,1)S(1)}, u32[]{:S(2)}, u32[]{:S(2)}) collective-permute-start(bf16[512,256]{1,0:T(8,128)(2,1)S(1)} %reshape.37.refs_4_), channel_id=1, source_target_pairs={{0,2},{1,3},{2,0},{3,1},{4,6},{5,7},{6,4},{7,5},{8,10},{9,11},{10,... | collective-permute-start | bytes 786440 | tf_op jit(solution)/shard_map/ppermute | solution.py:307
  86.4 14.0 %collective-permute-start.22 = (bf16[512,256]{1,0:T(8,128)(2,1)S(1)}, bf16[512,256]{1,0:T(8,128)(2,1)S(1)}, u32[]{:S(2)}, u32[]{:S(2)}) collective-permute-start(bf16[512,256]{1,0:T(8,128)(2,1)S(1)} %reshape.37.refs_4_), channel_id=1, source_target_pairs={{0,1},{1,0},{2,3},{3,2},{4,5},{5,4},{6,7},{7,6},{8,9},{9,8},{10,11... | collective-permute-start | bytes 786440 | tf_op jit(solution)/shard_map/ppermute | solution.py:307
  87.7 12.8 %collective-permute-start.23 = (bf16[512,256]{1,0:T(8,128)(2,1)S(1)}, bf16[512,256]{1,0:T(8,128)(2,1)S(1)}, u32[]{:S(2)}, u32[]{:S(2)}) collective-permute-start(bf16[512,256]{1,0:T(8,128)(2,1)S(1)} %reshape.37.refs_4_), channel_id=1, source_target_pairs={{0,3},{1,2},{2,1},{3,0},{4,7},{5,6},{6,5},{7,4},{8,11},{9,10},{10,... | collective-permute-start | bytes 786440 | tf_op jit(solution)/shard_map/ppermute | solution.py:307
  92.8 11.3 %collective-permute-start.17 = (bf16[512,256]{1,0:T(8,128)(2,1)S(1)}, bf16[512,256]{1,0:T(8,128)(2,1)S(1)}, u32[]{:S(2)}, u32[]{:S(2)}) collective-permute-start(bf16[512,256]{1,0:T(8,128)(2,1)S(1)} %collective-permute-done.16.refs_8_), channel_id=1, source_target_pairs={{0,1},{1,0},{2,3},{3,2},{4,5},{5,4},{6,7},{7,6},{8,9},{9,8},{10,11... | collective-permute-start | bytes 786440 | tf_op jit(solution)/shard_map/ppermute | solution.py:307
  96.5 7.9 %collective-permute-start.19 = (bf16[512,256]{1,0:T(8,128)(2,1)S(1)}, bf16[512,256]{1,0:T(8,128)(2,1)S(1)}, u32[]{:S(2)}, u32[]{:S(2)}) collective-permute-start(bf16[512,256]{1,0:T(8,128)(2,1)S(1)} %collective-permute-done.18.refs_6_), channel_id=1, source_target_pairs={{0,4},{1,5},{2,6},{3,7},{4,0},{5,1},{6,2},{7,3},{8,12},{9,13},{10,... | collective-permute-start | bytes 786440 | tf_op jit(solution)/shard_map/ppermute | solution.py:307
  98.1 7.6 %collective-permute-start.20 = (bf16[512,256]{1,0:T(8,128)(2,1)S(1)}, bf16[512,256]{1,0:T(8,128)(2,1)S(1)}, u32[]{:S(2)}, u32[]{:S(2)}) collective-permute-start(bf16[512,256]{1,0:T(8,128)(2,1)S(1)} %collective-permute-done.16.refs_8_), channel_id=1, source_target_pairs={{0,3},{1,2},{2,1},{3,0},{4,7},{5,6},{6,5},{7,4},{8,11},{9,10},{10,... | collective-permute-start | bytes 786440 | tf_op jit(solution)/shard_map/ppermute | solution.py:307
  101.8 17.6 %copy-start.3 = (f32[576]{0:T(1024)S(1)}, f32[576]{0:T(1024)}, u32[]{:S(2)}) copy-start(f32[576]{0:T(1024)} %param.15) | copy-start | bytes 6916
  107.5 5.2 %collective-permute-start.24 = (f32[512]{0:T(512)S(1)}, f32[512]{0:T(512)S(1)}, u32[]{:S(2)}, u32[]{:S(2)}) collective-permute-start(f32[512]{0:T(512)S(1)} %bitcast.10), channel_id=1, source_target_pairs={{0,4},{1,5},{2,6},{3,7},{4,0},{5,1},{6,2},{7,3},{8,12},{9,13},{10,... | collective-permute-start | bytes 6152 | tf_op jit(solution)/shard_map/ppermute | solution.py:307
  112.7 5.1 %collective-permute-start.25 = (f32[512]{0:T(512)S(1)}, f32[512]{0:T(512)S(1)}, u32[]{:S(2)}, u32[]{:S(2)}) collective-permute-start(f32[512]{0:T(512)S(1)} %add.33), channel_id=1, source_target_pairs={{0,2},{1,3},{2,0},{3,1},{4,6},{5,7},{6,4},{7,5},{8,10},{9,11},{10,... | collective-permute-start | bytes 6152 | tf_op jit(solution)/shard_map/ppermute | solution.py:307
  114.0 3.8 %collective-permute-start.26 = (f32[512]{0:T(512)S(1)}, f32[512]{0:T(512)S(1)}, u32[]{:S(2)}, u32[]{:S(2)}) collective-permute-start(f32[512]{0:T(512)S(1)} %add.33), channel_id=1, source_target_pairs={{0,1},{1,0},{2,3},{3,2},{4,5},{5,4},{6,7},{7,6},{8,9},{9,8},{10,11... | collective-permute-start | bytes 6152 | tf_op jit(solution)/shard_map/ppermute | solution.py:307
  114.6 4.8 %collective-permute-start.27 = (f32[512]{0:T(512)S(1)}, f32[512]{0:T(512)S(1)}, u32[]{:S(2)}, u32[]{:S(2)}) collective-permute-start(f32[512]{0:T(512)S(1)} %add.33), channel_id=1, source_target_pairs={{0,3},{1,2},{2,1},{3,0},{4,7},{5,6},{6,5},{7,4},{8,11},{9,10},{10,... | collective-permute-start | bytes 6152 | tf_op jit(solution)/shard_map/ppermute | solution.py:307
  (5 other events, 38.6 us)

commit v7 on v6

--- a/solution.py
+++ b/solution.py
@@ -62,13 +62,23 @@
             )
             cuts[-1].start()
     gain = g_ref[...].reshape(1, -1)
+    depth = x_buf.shape[1]
+    chunk = math.gcd(depth, 512)
 
     @pl.loop(0, tiles)
     def _(i):
         x_copy(i).wait()
-        x = x_buf[span(i)].astype(jnp.float32)
-        r = lax.rsqrt(jnp.mean(x * x, axis=1, keepdims=True) + norm_eps)
-        normed_buf[span(i)] = (x * r * gain).astype(jnp.bfloat16)
+        squares = None
+        for at in range(0, depth, chunk):
+            x = x_buf[span(i), at : at + chunk].astype(jnp.float32)
+            squares = x * x if squares is None else squares + x * x
+        r = lax.rsqrt(jnp.sum(squares, axis=1, keepdims=True) / depth + norm_eps)
+        r = jnp.broadcast_to(r, (tile, chunk))
+        for at in range(0, depth, chunk):
+            x = x_buf[span(i), at : at + chunk].astype(jnp.float32)
+            normed_buf[span(i), at : at + chunk] = (x * r * gain[:, at : at + chunk]).astype(
+                jnp.bfloat16
+            )
 
     for copy in w_copies:
         copy.wait()
@@ -330,7 +340,10 @@
     block_ids = jnp.arange(total_blocks, dtype=jnp.int32)
     rank = jnp.sum(same * (block_ids[None, :] < block_ids[:, None]), axis=1)
     target = plan * blocks + rank
-    picker = (target[None, :] == block_ids[:, None]).astype(jnp.bfloat16)
+    lines = BLK // n_ctx // 2
+    line_ids = jnp.arange(total_blocks * lines, dtype=jnp.int32)
+    line_target = (target[:, None] * lines + jnp.arange(lines, dtype=jnp.int32)).reshape(-1)
+    picker = (line_target[None, :] == line_ids[:, None]).astype(jnp.bfloat16)
 
     carry = []
     for stage in range(BACK):
@@ -350,20 +363,19 @@
     natural = attend(BACK, info, queries, kvs, carry)
 
     width = natural.shape[1]
-    piece = BLK // n_ctx
+    piece, fold = BLK // n_ctx, 2
     striped = natural.reshape(blocks, n_ctx, piece, width).transpose(1, 0, 2, 3)
-    striped = striped.reshape(n_ctx, blocks, piece * width)
+    striped = striped.reshape(n_ctx, blocks * piece // fold, fold * width)
     gathered = lax.all_to_all(striped, "ctx", 0, 0, tiled=True)
     gathered, mine, passed = lax.optimization_barrier((gathered, mine, passed))
     weights = [mine, passed, ctx_xor(mine, 1), ctx_xor(passed, 1)]
     ordered = jnp.dot(
         picker,
-        gathered.reshape(total_blocks, piece * width),
+        gathered.reshape(total_blocks * piece // fold, fold * width),
         preferred_element_type=jnp.float32,
     ).astype(jnp.bfloat16)
-    placed = lax.all_to_all(
-        ordered.reshape(n_ctx, blocks, piece * width), "ctx", 0, 0, tiled=True
-    )
+    placed = lax.all_to_all(ordered.reshape(striped.shape), "ctx", 0, 0, tiled=True)
+    placed, weights = lax.optimization_barrier((placed, weights))
     placed = (
         placed.reshape(n_ctx, blocks, piece, width).transpose(1, 0, 2, 3).reshape(rows, width)
     )

time: 122 us -> 120 us (0.984); the launches traced: 121 us -> 122 us
  blocking collectives: 0 us -> 15.4 us
  waiting for transfers between devices: 47.4 us -> 34.1 us
    all_to_all x0 -> x1, blocking collectives: none -> 15.4 us  [local(): lax.all_to_all(ordered.reshape(striped.shape), 'ctx', 0, 0, tiled=True)]
    all_to_all x1 -> x0, waiting for transfers between devices: 11.5 us -> none  [local(): lax.all_to_all(ordered.reshape(n_ctx, blocks, piece * width), 'ctx', 0, 0...]
    all_to_all x1 -> x0, starting transfers between devices: 3.99 us -> none  [local(): lax.all_to_all(ordered.reshape(n_ctx, blocks, piece * width), 'ctx', 0, 0...]
    all_to_all x1, starting transfers between devices: 12.4 us -> 15.8 us  [local(): gathered = lax.all_to_all(striped, 'ctx', 0, 0, tiled=True)]
    ppermute x2, waiting for transfers between devices: 2.29 us -> 0.04 us  [ctx_z(): lax.ppermute(a, 'ctx', [(i, (i + d * PLANE) % n_ctx) for i in range(n_ctx)])]
    pallas_call x3, Pallas kernels: 3.27 us -> 5.27 us  [attend(): pl.pallas_call(functools.partial(attend_kernel, rows, stage), in_specs=[p...]
    all_to_all x1, waiting for transfers between devices: 10.1 us -> 12.1 us  [local(): gathered = lax.all_to_all(striped, 'ctx', 0, 0, tiled=True)]
    ppermute x15, waiting for transfers between devices: 23.1 us -> 21.6 us  [tp_xor(): return lax.ppermute(a, 'tp', [(i, i ^ m) for i in range(n_tp)])]
  transfers between devices with their start and end apart: 30 -> 29, of which waited for: 16 -> 13; matrix products, arithmetic and copies ran while one was open for 2% -> 2% of each run, Pallas kernels for 9% -> 10%
where the time goes in v7:
time: 120 us; the launch traced here: 122 us
  starting transfers between devices  47.1 us (39%)
  waiting for transfers between devices  34.1 us (28%)
  Pallas kernels  21.3 us (18%)
  blocking collectives  15.4 us (13%)
  local copies, waits for them, and re-layouts  2.7 us (2%)
    ppermute x15, starting transfers between devices, tp_xor(): return lax.ppermute(a, 'tp', [(i, i ^ m) for i in range(n_tp)])  22 us
    ppermute x15, waiting for transfers between devices, tp_xor(): return lax.ppermute(a, 'tp', [(i, i ^ m) for i in range(n_tp)])  21.6 us
    all_to_all x1, starting transfers between devices, local(): gathered = lax.all_to_all(striped, 'ctx', 0, 0, tiled=True)  15.8 us
    all_to_all x1, blocking collectives, local(): lax.all_to_all(ordered.reshape(striped.shape), 'ctx', 0, 0, tiled=True)  15.4 us
    pallas_call x2, Pallas kernels, project(): pl.pallas_call(functools.partial(project_kernel, scale, tile, count, part...  12.9 us
    all_to_all x1, waiting for transfers between devices, local(): gathered = lax.all_to_all(striped, 'ctx', 0, 0, tiled=True)  12.1 us
    ppermute x11, starting transfers between devices, ctx_xor(): return lax.ppermute(a, 'ctx', [(i, i ^ m) for i in range(n_ctx)])  5.35 us
    pallas_call x3, Pallas kernels, attend(): pl.pallas_call(functools.partial(attend_kernel, rows, stage), in_specs=[p...  5.27 us
  transfers between devices with their start and end apart: 29, of which 13 were waited for; matrix products, arithmetic and copies ran while one was open for 2% of the time, Pallas kernels for 10%

profile of v7, /device:TPU:2, one launch (start us, length us, event | category | flops | bytes accessed | tf_op | source)
XLA Modules:
  0.0 122.2 jit_solution(5860662772580880576)
XLA Ops:
  0.0 6.8 %project_kv.1 = (bf16[512,256]{1,0:T(8,128)(2,1)}, bf16[2,128,640]{2,1,0:T(8,128)(2,1)}, bf16[2,128,640]{2,1,0:T(8,128)(2,1)}, bf16[2,128,640]{2,1,0:T(8,128)(2,1)}, bf16[2,128,640]{2,1,0:T(8,128)(2,1)}) custom-call(bf16[512,4608]{1,0:T(8,128)(2,1)} %x_hbm.3, f32[4608]{0:T(1024)} %g_ref.3, bf16[4608,128]{1,0:T(8,128)(2,1)} %refs_0_.2, ...), custom_call_target="tpu_custom_call" | custom-call | flops 1207959552 | bytes 7077888 | tf_op jit(solution)/shard_map/project_kv/pallas_call | solution.py:112
  6.8 2.0 %collective-permute-start = (bf16[512,256]{1,0:T(8,128)(2,1)}, bf16[512,256]{1,0:T(8,128)(2,1)S(1)}, u32[]{:S(2)}, u32[]{:S(2)}) collective-permute-start(bf16[512,256]{1,0:T(8,128)(2,1)} %get-tuple-element.42.refs_0_), channel_id=1, source_target_pairs={{0,32},{8,40},{16,48},{24,56},{32,64},{40,72},{48,80},{56,88},{64,... | collective-permute-start | bytes 786440 | tf_op jit(solution)/shard_map/ppermute | solution.py:314
  9.4 1.6 %collective-permute-start.9 = (bf16[2,128,640]{2,1,0:T(8,128)(2,1)}, bf16[2,128,640]{2,1,0:T(8,128)(2,1)S(1)}, u32[]{:S(2)}, u32[]{:S(2)}) collective-permute-start(bf16[2,128,640]{2,1,0:T(8,128)(2,1)} %get-tuple-element.51), channel_id=1, source_target_pairs={{0,1},{1,0},{2,3},{3,2},{4,5},{5,4},{6,7},{7,6},{8,9},{9,8},{10,11... | collective-permute-start | bytes 983048 | tf_op jit(solution)/shard_map/ppermute | solution.py:317
  10.9 2.2 %collective-permute-start.11 = (bf16[2,128,640]{2,1,0:T(8,128)(2,1)}, bf16[2,128,640]{2,1,0:T(8,128)(2,1)S(1)}, u32[]{:S(2)}, u32[]{:S(2)}) collective-permute-start(bf16[2,128,640]{2,1,0:T(8,128)(2,1)} %get-tuple-element.53), channel_id=1, source_target_pairs={{0,3},{1,2},{2,1},{3,0},{4,7},{5,6},{6,5},{7,4},{8,11},{9,10},{10,... | collective-permute-start | bytes 983048 | tf_op jit(solution)/shard_map/ppermute | solution.py:317
  13.3 6.1 %project_q.1.q_ref = bf16[512,256]{1,0:T(8,128)(2,1)} custom-call(bf16[512,4608]{1,0:T(8,128)(2,1)} %x_hbm.3, f32[4608]{0:T(1024)} %g_ref.3, bf16[4608,256]{1,0:T(8,128)(2,1)} %refs_0_.3), custom_call_target="tpu_custom_call" | custom-call | flops 1207959552 | bytes 7077888 | tf_op jit(solution)/shard_map/project_q/pallas_call | solution.py:112
  19.7 2.0 %collective-permute-start.1 = (bf16[512,256]{1,0:T(8,128)(2,1)S(1)}, bf16[512,256]{1,0:T(8,128)(2,1)S(1)}, u32[]{:S(2)}, u32[]{:S(2)}) collective-permute-start(bf16[512,256]{1,0:T(8,128)(2,1)S(1)} %collective-permute-done.refs_0_), channel_id=1, source_target_pairs={{0,32},{8,40},{16,48},{24,56},{32,64},{40,72},{48,80},{56,88},{64,... | collective-permute-start | bytes 786440 | tf_op jit(solution)/shard_map/ppermute | solution.py:314
  21.7 1.5 %collective-permute-start.7 = (bf16[512,256]{1,0:T(8,128)(2,1)S(1)}, bf16[512,256]{1,0:T(8,128)(2,1)S(1)}, u32[]{:S(2)}, u32[]{:S(2)}) collective-permute-start(bf16[512,256]{1,0:T(8,128)(2,1)S(1)} %collective-permute-done.refs_0_), channel_id=1, source_target_pairs={{0,16},{8,24},{16,0},{24,8},{32,48},{40,56},{48,32},{56,40},{64,80... | collective-permute-start | bytes 786440 | tf_op jit(solution)/shard_map/ppermute | solution.py:311
  25.6 3.6 %attend.3 = (f32[2,512,128]{2,1,0:T(8,128)S(1)}, f32[2,512,128]{2,1,0:T(8,128)S(1)}) custom-call(s32[5]{0:T(128)S(1)} %pad_add_fusion.info_ref, bf16[512,256]{1,0:T(8,128)(2,1)S(1)} %copy-done, bf16[512,256]{1,0:T(8,128)(2,1)S(1)} %copy-done.1, bf16[512,256]{1,0:T(8,128)(2,1)S(1)} %collective-permute-done.2.refs_1_, ...), custom_call_target="tpu_custom_call" | custom-call | flops 2000000000 | bytes 4000000 | tf_op jit(solution)/shard_map/attend/pallas_call | solution.py:212
  29.2 1.5 %collective-permute-start.5 = (bf16[512,256]{1,0:T(8,128)(2,1)S(1)}, bf16[512,256]{1,0:T(8,128)(2,1)S(1)}, u32[]{:S(2)}, u32[]{:S(2)}) collective-permute-start(bf16[512,256]{1,0:T(8,128)(2,1)S(1)} %collective-permute-done.1.refs_0_), channel_id=1, source_target_pairs={{0,16},{8,24},{16,0},{24,8},{32,48},{40,56},{48,32},{56,40},{64,80... | collective-permute-start | bytes 786440 | tf_op jit(solution)/shard_map/ppermute | solution.py:311
  31.2 4.4 %collective-permute-done.10 = bf16[2,128,640]{2,1,0:T(8,128)(2,1)S(1)} collective-permute-done((bf16[2,128,640]{2,1,0:T(8,128)(2,1)S(1)}, bf16[2,128,640]{2,1,0:T(8,128)(2,1)S(1)}, u32[]{:S(2)}, u32[]{:S(2)}) %collective-permute-start.10) | collective-permute-done | bytes 327712 | tf_op jit(solution)/shard_map/ppermute | solution.py:317
  36.7 2.2 %collective-permute-start.14 = (bf16[4,128,640]{2,1,0:T(8,128)(2,1)S(1)}, bf16[4,128,640]{2,1,0:T(8,128)(2,1)S(1)}, u32[]{:S(2)}, u32[]{:S(2)}) collective-permute-start(bf16[4,128,640]{2,1,0:T(8,128)(2,1)S(1)} %get-tuple-element.60), channel_id=1, source_target_pairs={{0,4},{1,5},{2,6},{3,7},{4,0},{5,1},{6,2},{7,3},{8,12},{9,13},{10,... | collective-permute-start | bytes 1966088 | tf_op jit(solution)/shard_map/ppermute | solution.py:317
  38.9 1.0 attend.5
  41.0 15.8 %all-to-all-start = ((bf16[32,8,512]{2,1,0:T(8,128)(2,1)}), bf16[32,8,512]{2,1,0:T(8,128)(2,1)S(1)}, u32[]{:S(2)}, u32[]{:S(2)}) async-start(bf16[32,8,512]{2,1,0:T(8,128)(2,1)} %reshape.48), calls=%async_computation | async-start | bytes 524288 | tf_op jit(solution)/shard_map/all_to_all | solution.py:369
  56.8 12.1 %all-to-all-done = bf16[32,8,512]{2,1,0:T(8,128)(2,1)S(1)} async-done(((bf16[32,8,512]{2,1,0:T(8,128)(2,1)}), bf16[32,8,512]{2,1,0:T(8,128)(2,1)S(1)}, u32[]{:S(2)}, u32[]{:S(2)}) %all-to-all-start) | async-done | bytes 262176 | tf_op jit(solution)/shard_map/all_to_all | solution.py:369
  69.6 15.4 %all_to_all.10 = bf16[32,8,512]{2,1,0:T(8,128)(2,1)S(1)} all-to-all(bf16[32,8,512]{2,1,0:T(8,128)(2,1)S(1)} %fusion), channel_id=1, replica_groups=mesh['ctx'=32,'tp'=8] {'ctx'}, dimensions={0} | all-to-all | bytes 524288 | tf_op jit(solution)/shard_map/all_to_all | solution.py:377
  87.0 1.2 collective-permute-start.22
  88.2 2.2 %collective-permute-start.23 = (bf16[512,256]{1,0:T(8,128)(2,1)S(1)}, bf16[512,256]{1,0:T(8,128)(2,1)S(1)}, u32[]{:S(2)}, u32[]{:S(2)}) collective-permute-start(bf16[512,256]{1,0:T(8,128)(2,1)S(1)} %reshape.52.refs_4_), channel_id=1, source_target_pairs={{0,3},{1,2},{2,1},{3,0},{4,7},{5,6},{6,5},{7,4},{8,11},{9,10},{10,... | collective-permute-start | bytes 786440 | tf_op jit(solution)/shard_map/ppermute | solution.py:317
  90.3 4.1 %collective-permute-done.17.refs_8_ = bf16[512,256]{1,0:T(8,128)(2,1)S(1)} collective-permute-done((bf16[512,256]{1,0:T(8,128)(2,1)S(1)}, bf16[512,256]{1,0:T(8,128)(2,1)S(1)}, u32[]{:S(2)}, u32[]{:S(2)}) %collective-permute-start.17) | collective-permute-done | bytes 262176 | tf_op jit(solution)/shard_map/ppermute | solution.py:317
  95.1 1.9 %collective-permute-done.19.refs_6_ = bf16[512,256]{1,0:T(8,128)(2,1)S(1)} collective-permute-done((bf16[512,256]{1,0:T(8,128)(2,1)S(1)}, bf16[512,256]{1,0:T(8,128)(2,1)S(1)}, u32[]{:S(2)}, u32[]{:S(2)}) %collective-permute-start.19) | collective-permute-done | bytes 262176 | tf_op jit(solution)/shard_map/ppermute | solution.py:317
  97.0 2.7 %collective-permute-start.20 = (bf16[512,256]{1,0:T(8,128)(2,1)S(1)}, bf16[512,256]{1,0:T(8,128)(2,1)S(1)}, u32[]{:S(2)}, u32[]{:S(2)}) collective-permute-start(bf16[512,256]{1,0:T(8,128)(2,1)S(1)} %collective-permute-done.19.refs_6_), channel_id=1, source_target_pairs={{0,4},{1,5},{2,6},{3,7},{4,0},{5,1},{6,2},{7,3},{8,12},{9,13},{10,... | collective-permute-start | bytes 786440 | tf_op jit(solution)/shard_map/ppermute | solution.py:317
  99.8 1.0 collective-permute-start.21
  101.0 1.3 %out_project.2.refs_5_ = f32[512,640]{1,0:T(8,128)S(1)} custom-call(bf16[4,128,640]{2,1,0:T(8,128)(2,1)S(1)} %get-tuple-element.67.refs_0_, bf16[4,128,640]{2,1,0:T(8,128)(2,1)S(1)} %collective-permute-done.14.refs_1_.refs_0_, bf16[4,128,640]{2,1,0:T(8,128)(2,1)S(1)} %collective-permute-done.15.refs_2_, ...), custom_call_target="tpu_custom_call" | custom-call | flops 838860800 | bytes 6000000 | tf_op jit(solution)/shard_map/out_project/pallas_call | solution.py:289
  102.4 2.3 %collective-permute-done.18.refs_2_ = bf16[512,256]{1,0:T(8,128)(2,1)S(1)} collective-permute-done((bf16[512,256]{1,0:T(8,128)(2,1)S(1)}, bf16[512,256]{1,0:T(8,128)(2,1)S(1)}, u32[]{:S(2)}, u32[]{:S(2)}) %collective-permute-start.18) | collective-permute-done | bytes 262176 | tf_op jit(solution)/shard_map/ppermute | solution.py:317
  104.9 2.4 %collective-permute-done.21.refs_4_ = bf16[512,256]{1,0:T(8,128)(2,1)S(1)} collective-permute-done((bf16[512,256]{1,0:T(8,128)(2,1)S(1)}, bf16[512,256]{1,0:T(8,128)(2,1)S(1)}, u32[]{:S(2)}, u32[]{:S(2)}) %collective-permute-start.21) | collective-permute-done | bytes 262176 | tf_op jit(solution)/shard_map/ppermute | solution.py:317
  107.3 1.8 %out_project.3 = (f32[512,576]{1,0:T(8,128)S(1)}, f32[1,512]{1,0:T(1,128)S(1)}) custom-call(bf16[4,128,640]{2,1,0:T(8,128)(2,1)S(1)} %collective-permute-done.14.refs_1_.refs_0_, bf16[4,128,640]{2,1,0:T(8,128)(2,1)S(1)} %collective-permute-done.16.refs_3_.refs_1_, bf16[512,256]{1,0:T(8,128)(2,1)S(1)} %collective-permute-done.18.refs_2_, ...), custom_call_target="tpu_custom_call" | custom-call | flops 503316480 | bytes 6000000 | tf_op jit(solution)/shard_map/out_project/pallas_call | solution.py:289
  109.1 1.7 %collective-permute-start.24 = (f32[512]{0:T(512)S(1)}, f32[512]{0:T(512)S(1)}, u32[]{:S(2)}, u32[]{:S(2)}) collective-permute-start(f32[512]{0:T(512)S(1)} %bitcast.12), channel_id=1, source_target_pairs={{0,4},{1,5},{2,6},{3,7},{4,0},{5,1},{6,2},{7,3},{8,12},{9,13},{10,... | collective-permute-start | bytes 6152 | tf_op jit(solution)/shard_map/ppermute | solution.py:317
  110.8 3.5 %collective-permute-done.24 = f32[512]{0:T(512)S(1)} collective-permute-done((f32[512]{0:T(512)S(1)}, f32[512]{0:T(512)S(1)}, u32[]{:S(2)}, u32[]{:S(2)}) %collective-permute-start.24) | collective-permute-done | bytes 2080 | tf_op jit(solution)/shard_map/ppermute | solution.py:317
  114.6 1.6 %collective-permute-start.26 = (f32[512]{0:T(512)S(1)}, f32[512]{0:T(512)S(1)}, u32[]{:S(2)}, u32[]{:S(2)}) collective-permute-start(f32[512]{0:T(512)S(1)} %add.57), channel_id=1, source_target_pairs={{0,1},{1,0},{2,3},{3,2},{4,5},{5,4},{6,7},{7,6},{8,9},{9,8},{10,11... | collective-permute-start | bytes 6152 | tf_op jit(solution)/shard_map/ppermute | solution.py:317
  116.2 2.2 %collective-permute-start.27 = (f32[512]{0:T(512)S(1)}, f32[512]{0:T(512)S(1)}, u32[]{:S(2)}, u32[]{:S(2)}) collective-permute-start(f32[512]{0:T(512)S(1)} %add.57), channel_id=1, source_target_pairs={{0,3},{1,2},{2,1},{3,0},{4,7},{5,6},{6,5},{7,4},{8,11},{9,10},{10,... | collective-permute-start | bytes 6152 | tf_op jit(solution)/shard_map/ppermute | solution.py:317
  118.4 1.0 collective-permute-done.25
  119.4 1.6 %collective-permute-done.27 = f32[512]{0:T(512)S(1)} collective-permute-done((f32[512]{0:T(512)S(1)}, f32[512]{0:T(512)S(1)}, u32[]{:S(2)}, u32[]{:S(2)}) %collective-permute-start.27) | collective-permute-done | bytes 2080 | tf_op jit(solution)/shard_map/ppermute | solution.py:317
  121.2 1.1 copy.16
  (72 shorter events, 10.3 us)
Async XLA Ops:
  0.0 13.1 %copy-start.5 = (s32[128]{0:T(128)S(1)}, s32[128]{0:T(128)}, u32[]{:S(2)}) copy-start(s32[128]{0:T(128)} %param.16) | copy-start | bytes 1540
  6.8 12.8 %collective-permute-start = (bf16[512,256]{1,0:T(8,128)(2,1)}, bf16[512,256]{1,0:T(8,128)(2,1)S(1)}, u32[]{:S(2)}, u32[]{:S(2)}) collective-permute-start(bf16[512,256]{1,0:T(8,128)(2,1)} %get-tuple-element.42.refs_0_), channel_id=1, source_target_pairs={{0,32},{8,40},{16,48},{24,56},{32,64},{40,72},{48,80},{56,88},{64,... | collective-permute-start | bytes 786440 | tf_op jit(solution)/shard_map/ppermute | solution.py:314
  8.8 14.8 %collective-permute-start.3 = (bf16[512,256]{1,0:T(8,128)(2,1)}, bf16[512,256]{1,0:T(8,128)(2,1)S(1)}, u32[]{:S(2)}, u32[]{:S(2)}) collective-permute-start(bf16[512,256]{1,0:T(8,128)(2,1)} %get-tuple-element.42.refs_0_), channel_id=1, source_target_pairs={{0,16},{8,24},{16,0},{24,8},{32,48},{40,56},{48,32},{56,40},{64,80... | collective-permute-start | bytes 786440 | tf_op jit(solution)/shard_map/ppermute | solution.py:311
  9.4 14.4 %collective-permute-start.9 = (bf16[2,128,640]{2,1,0:T(8,128)(2,1)}, bf16[2,128,640]{2,1,0:T(8,128)(2,1)S(1)}, u32[]{:S(2)}, u32[]{:S(2)}) collective-permute-start(bf16[2,128,640]{2,1,0:T(8,128)(2,1)} %get-tuple-element.51), channel_id=1, source_target_pairs={{0,1},{1,0},{2,3},{3,2},{4,5},{5,4},{6,7},{7,6},{8,9},{9,8},{10,11... | collective-permute-start | bytes 983048 | tf_op jit(solution)/shard_map/ppermute | solution.py:317
  10.9 13.3 %collective-permute-start.11 = (bf16[2,128,640]{2,1,0:T(8,128)(2,1)}, bf16[2,128,640]{2,1,0:T(8,128)(2,1)S(1)}, u32[]{:S(2)}, u32[]{:S(2)}) collective-permute-start(bf16[2,128,640]{2,1,0:T(8,128)(2,1)} %get-tuple-element.53), channel_id=1, source_target_pairs={{0,3},{1,2},{2,1},{3,0},{4,7},{5,6},{6,5},{7,4},{8,11},{9,10},{10,... | collective-permute-start | bytes 983048 | tf_op jit(solution)/shard_map/ppermute | solution.py:317
  13.3 10.3 %copy-start.1 = (bf16[512,256]{1,0:T(8,128)(2,1)S(1)}, bf16[512,256]{1,0:T(8,128)(2,1)}, u32[]{:S(2)}) copy-start(bf16[512,256]{1,0:T(8,128)(2,1)} %get-tuple-element.42.refs_0_) | copy-start | bytes 786436
  19.7 9.6 %collective-permute-start.1 = (bf16[512,256]{1,0:T(8,128)(2,1)S(1)}, bf16[512,256]{1,0:T(8,128)(2,1)S(1)}, u32[]{:S(2)}, u32[]{:S(2)}) collective-permute-start(bf16[512,256]{1,0:T(8,128)(2,1)S(1)} %collective-permute-done.refs_0_), channel_id=1, source_target_pairs={{0,32},{8,40},{16,48},{24,56},{32,64},{40,72},{48,80},{56,88},{64,... | collective-permute-start | bytes 786440 | tf_op jit(solution)/shard_map/ppermute | solution.py:314
  21.7 9.1 %collective-permute-start.7 = (bf16[512,256]{1,0:T(8,128)(2,1)S(1)}, bf16[512,256]{1,0:T(8,128)(2,1)S(1)}, u32[]{:S(2)}, u32[]{:S(2)}) collective-permute-start(bf16[512,256]{1,0:T(8,128)(2,1)S(1)} %collective-permute-done.refs_0_), channel_id=1, source_target_pairs={{0,16},{8,24},{16,0},{24,8},{32,48},{40,56},{48,32},{56,40},{64,80... | collective-permute-start | bytes 786440 | tf_op jit(solution)/shard_map/ppermute | solution.py:311
  23.6 1.6 %collective-permute-start.2 = (bf16[512,256]{1,0:T(8,128)(2,1)S(1)}, bf16[512,256]{1,0:T(8,128)(2,1)S(1)}, u32[]{:S(2)}, u32[]{:S(2)}) collective-permute-start(bf16[512,256]{1,0:T(8,128)(2,1)S(1)} %copy-done.1), channel_id=1, source_target_pairs={{0,8},{8,0},{16,24},{24,16},{32,40},{40,32},{48,56},{56,48},{64,72... | collective-permute-start | bytes 786440 | tf_op jit(solution)/shard_map/ppermute | solution.py:311
  23.7 1.9 %collective-permute-start.4 = (bf16[512,256]{1,0:T(8,128)(2,1)S(1)}, bf16[512,256]{1,0:T(8,128)(2,1)S(1)}, u32[]{:S(2)}, u32[]{:S(2)}) collective-permute-start(bf16[512,256]{1,0:T(8,128)(2,1)S(1)} %collective-permute-done.3.refs_2_), channel_id=1, source_target_pairs={{0,8},{8,0},{16,24},{24,16},{32,40},{40,32},{48,56},{56,48},{64,72... | collective-permute-start | bytes 786440 | tf_op jit(solution)/shard_map/ppermute | solution.py:311
  24.3 11.3 %collective-permute-start.10 = (bf16[2,128,640]{2,1,0:T(8,128)(2,1)S(1)}, bf16[2,128,640]{2,1,0:T(8,128)(2,1)S(1)}, u32[]{:S(2)}, u32[]{:S(2)}) collective-permute-start(bf16[2,128,640]{2,1,0:T(8,128)(2,1)S(1)} %copy-done.4), channel_id=1, source_target_pairs={{0,2},{1,3},{2,0},{3,1},{4,6},{5,7},{6,4},{7,5},{8,10},{9,11},{10,... | collective-permute-start | bytes 983048 | tf_op jit(solution)/shard_map/ppermute | solution.py:317
  25.3 10.6 %collective-permute-start.6 = (bf16[512,256]{1,0:T(8,128)(2,1)S(1)}, bf16[512,256]{1,0:T(8,128)(2,1)S(1)}, u32[]{:S(2)}, u32[]{:S(2)}) collective-permute-start(bf16[512,256]{1,0:T(8,128)(2,1)S(1)} %collective-permute-done.refs_0_), channel_id=1, source_target_pairs={{0,8},{8,0},{16,24},{24,16},{32,40},{40,32},{48,56},{56,48},{64,72... | collective-permute-start | bytes 786440 | tf_op jit(solution)/shard_map/ppermute | solution.py:311
  29.2 7.4 %collective-permute-start.5 = (bf16[512,256]{1,0:T(8,128)(2,1)S(1)}, bf16[512,256]{1,0:T(8,128)(2,1)S(1)}, u32[]{:S(2)}, u32[]{:S(2)}) collective-permute-start(bf16[512,256]{1,0:T(8,128)(2,1)S(1)} %collective-permute-done.1.refs_0_), channel_id=1, source_target_pairs={{0,16},{8,24},{16,0},{24,8},{32,48},{40,56},{48,32},{56,40},{64,80... | collective-permute-start | bytes 786440 | tf_op jit(solution)/shard_map/ppermute | solution.py:311
  30.7 8.2 %collective-permute-start.12 = (bf16[512,256]{1,0:T(8,128)(2,1)S(1)}, bf16[512,256]{1,0:T(8,128)(2,1)S(1)}, u32[]{:S(2)}, u32[]{:S(2)}) collective-permute-start(bf16[512,256]{1,0:T(8,128)(2,1)S(1)} %collective-permute-done.1.refs_0_), channel_id=1, source_target_pairs={{0,8},{8,0},{16,24},{24,16},{32,40},{40,32},{48,56},{56,48},{64,72... | collective-permute-start | bytes 786440 | tf_op jit(solution)/shard_map/ppermute | solution.py:311
  30.7 5.1 %collective-permute-start.8 = (bf16[512,256]{1,0:T(8,128)(2,1)S(1)}, bf16[512,256]{1,0:T(8,128)(2,1)S(1)}, u32[]{:S(2)}, u32[]{:S(2)}) collective-permute-start(bf16[512,256]{1,0:T(8,128)(2,1)S(1)} %collective-permute-done.7.refs_2_), channel_id=1, source_target_pairs={{0,8},{8,0},{16,24},{24,16},{32,40},{40,32},{48,56},{56,48},{64,72... | collective-permute-start | bytes 786440 | tf_op jit(solution)/shard_map/ppermute | solution.py:311
  36.6 2.3 %collective-permute-start.13 = (bf16[512,256]{1,0:T(8,128)(2,1)S(1)}, bf16[512,256]{1,0:T(8,128)(2,1)S(1)}, u32[]{:S(2)}, u32[]{:S(2)}) collective-permute-start(bf16[512,256]{1,0:T(8,128)(2,1)S(1)} %collective-permute-done.5.refs_2_), channel_id=1, source_target_pairs={{0,8},{8,0},{16,24},{24,16},{32,40},{40,32},{48,56},{56,48},{64,72... | collective-permute-start | bytes 786440 | tf_op jit(solution)/shard_map/ppermute | solution.py:311
  36.7 20.1 %collective-permute-start.14 = (bf16[4,128,640]{2,1,0:T(8,128)(2,1)S(1)}, bf16[4,128,640]{2,1,0:T(8,128)(2,1)S(1)}, u32[]{:S(2)}, u32[]{:S(2)}) collective-permute-start(bf16[4,128,640]{2,1,0:T(8,128)(2,1)S(1)} %get-tuple-element.60), channel_id=1, source_target_pairs={{0,4},{1,5},{2,6},{3,7},{4,0},{5,1},{6,2},{7,3},{8,12},{9,13},{10,... | collective-permute-start | bytes 1966088 | tf_op jit(solution)/shard_map/ppermute | solution.py:317
  41.0 27.9 %all-to-all-start = ((bf16[32,8,512]{2,1,0:T(8,128)(2,1)}), bf16[32,8,512]{2,1,0:T(8,128)(2,1)S(1)}, u32[]{:S(2)}, u32[]{:S(2)}) async-start(bf16[32,8,512]{2,1,0:T(8,128)(2,1)} %reshape.48), calls=%async_computation | async-start | bytes 524288 | tf_op jit(solution)/shard_map/all_to_all | solution.py:369
  68.9 16.1 %collective-permute-start.15 = (bf16[4,128,640]{2,1,0:T(8,128)(2,1)S(1)}, bf16[4,128,640]{2,1,0:T(8,128)(2,1)S(1)}, u32[]{:S(2)}, u32[]{:S(2)}) collective-permute-start(bf16[4,128,640]{2,1,0:T(8,128)(2,1)S(1)} %get-tuple-element.67.refs_0_), channel_id=1, source_target_pairs={{0,8},{8,0},{16,24},{24,16},{32,40},{40,32},{48,56},{56,48},{64,72... | collective-permute-start | bytes 1966088 | tf_op jit(solution)/shard_map/ppermute | solution.py:311
  68.9 16.1 %collective-permute-start.16 = (bf16[4,128,640]{2,1,0:T(8,128)(2,1)S(1)}, bf16[4,128,640]{2,1,0:T(8,128)(2,1)S(1)}, u32[]{:S(2)}, u32[]{:S(2)}) collective-permute-start(bf16[4,128,640]{2,1,0:T(8,128)(2,1)S(1)} %collective-permute-done.14.refs_1_.refs_0_), channel_id=1, source_target_pairs={{0,8},{8,0},{16,24},{24,16},{32,40},{40,32},{48,56},{56,48},{64,72... | collective-permute-start | bytes 1966088 | tf_op jit(solution)/shard_map/ppermute | solution.py:311
  85.4 9.1 %collective-permute-start.17 = (bf16[512,256]{1,0:T(8,128)(2,1)S(1)}, bf16[512,256]{1,0:T(8,128)(2,1)S(1)}, u32[]{:S(2)}, u32[]{:S(2)}) collective-permute-start(bf16[512,256]{1,0:T(8,128)(2,1)S(1)} %reshape.52.refs_4_), channel_id=1, source_target_pairs={{0,4},{1,5},{2,6},{3,7},{4,0},{5,1},{6,2},{7,3},{8,12},{9,13},{10,... | collective-permute-start | bytes 786440 | tf_op jit(solution)/shard_map/ppermute | solution.py:317
  86.3 10.8 %collective-permute-start.19 = (bf16[512,256]{1,0:T(8,128)(2,1)S(1)}, bf16[512,256]{1,0:T(8,128)(2,1)S(1)}, u32[]{:S(2)}, u32[]{:S(2)}) collective-permute-start(bf16[512,256]{1,0:T(8,128)(2,1)S(1)} %reshape.52.refs_4_), channel_id=1, source_target_pairs={{0,2},{1,3},{2,0},{3,1},{4,6},{5,7},{6,4},{7,5},{8,10},{9,11},{10,... | collective-permute-start | bytes 786440 | tf_op jit(solution)/shard_map/ppermute | solution.py:317
  87.0 14.0 %collective-permute-start.22 = (bf16[512,256]{1,0:T(8,128)(2,1)S(1)}, bf16[512,256]{1,0:T(8,128)(2,1)S(1)}, u32[]{:S(2)}, u32[]{:S(2)}) collective-permute-start(bf16[512,256]{1,0:T(8,128)(2,1)S(1)} %reshape.52.refs_4_), channel_id=1, source_target_pairs={{0,1},{1,0},{2,3},{3,2},{4,5},{5,4},{6,7},{7,6},{8,9},{9,8},{10,11... | collective-permute-start | bytes 786440 | tf_op jit(solution)/shard_map/ppermute | solution.py:317
  88.2 12.8 %collective-permute-start.23 = (bf16[512,256]{1,0:T(8,128)(2,1)S(1)}, bf16[512,256]{1,0:T(8,128)(2,1)S(1)}, u32[]{:S(2)}, u32[]{:S(2)}) collective-permute-start(bf16[512,256]{1,0:T(8,128)(2,1)S(1)} %reshape.52.refs_4_), channel_id=1, source_target_pairs={{0,3},{1,2},{2,1},{3,0},{4,7},{5,6},{6,5},{7,4},{8,11},{9,10},{10,... | collective-permute-start | bytes 786440 | tf_op jit(solution)/shard_map/ppermute | solution.py:317
  94.5 10.2 %collective-permute-start.18 = (bf16[512,256]{1,0:T(8,128)(2,1)S(1)}, bf16[512,256]{1,0:T(8,128)(2,1)S(1)}, u32[]{:S(2)}, u32[]{:S(2)}) collective-permute-start(bf16[512,256]{1,0:T(8,128)(2,1)S(1)} %collective-permute-done.17.refs_8_), channel_id=1, source_target_pairs={{0,1},{1,0},{2,3},{3,2},{4,5},{5,4},{6,7},{7,6},{8,9},{9,8},{10,11... | collective-permute-start | bytes 786440 | tf_op jit(solution)/shard_map/ppermute | solution.py:317
  97.0 7.9 %collective-permute-start.20 = (bf16[512,256]{1,0:T(8,128)(2,1)S(1)}, bf16[512,256]{1,0:T(8,128)(2,1)S(1)}, u32[]{:S(2)}, u32[]{:S(2)}) collective-permute-start(bf16[512,256]{1,0:T(8,128)(2,1)S(1)} %collective-permute-done.19.refs_6_), channel_id=1, source_target_pairs={{0,4},{1,5},{2,6},{3,7},{4,0},{5,1},{6,2},{7,3},{8,12},{9,13},{10,... | collective-permute-start | bytes 786440 | tf_op jit(solution)/shard_map/ppermute | solution.py:317
  99.8 7.6 %collective-permute-start.21 = (bf16[512,256]{1,0:T(8,128)(2,1)S(1)}, bf16[512,256]{1,0:T(8,128)(2,1)S(1)}, u32[]{:S(2)}, u32[]{:S(2)}) collective-permute-start(bf16[512,256]{1,0:T(8,128)(2,1)S(1)} %collective-permute-done.17.refs_8_), channel_id=1, source_target_pairs={{0,3},{1,2},{2,1},{3,0},{4,7},{5,6},{6,5},{7,4},{8,11},{9,10},{10,... | collective-permute-start | bytes 786440 | tf_op jit(solution)/shard_map/ppermute | solution.py:317
  102.4 18.6 %copy-start.3 = (f32[576]{0:T(1024)S(1)}, f32[576]{0:T(1024)}, u32[]{:S(2)}) copy-start(f32[576]{0:T(1024)} %param.15) | copy-start | bytes 6916
  109.1 5.2 %collective-permute-start.24 = (f32[512]{0:T(512)S(1)}, f32[512]{0:T(512)S(1)}, u32[]{:S(2)}, u32[]{:S(2)}) collective-permute-start(f32[512]{0:T(512)S(1)} %bitcast.12), channel_id=1, source_target_pairs={{0,4},{1,5},{2,6},{3,7},{4,0},{5,1},{6,2},{7,3},{8,12},{9,13},{10,... | collective-permute-start | bytes 6152 | tf_op jit(solution)/shard_map/ppermute | solution.py:317
  114.3 5.1 %collective-permute-start.25 = (f32[512]{0:T(512)S(1)}, f32[512]{0:T(512)S(1)}, u32[]{:S(2)}, u32[]{:S(2)}) collective-permute-start(f32[512]{0:T(512)S(1)} %add.57), channel_id=1, source_target_pairs={{0,2},{1,3},{2,0},{3,1},{4,6},{5,7},{6,4},{7,5},{8,10},{9,11},{10,... | collective-permute-start | bytes 6152 | tf_op jit(solution)/shard_map/ppermute | solution.py:317
  114.6 4.9 %collective-permute-start.26 = (f32[512]{0:T(512)S(1)}, f32[512]{0:T(512)S(1)}, u32[]{:S(2)}, u32[]{:S(2)}) collective-permute-start(f32[512]{0:T(512)S(1)} %add.57), channel_id=1, source_target_pairs={{0,1},{1,0},{2,3},{3,2},{4,5},{5,4},{6,7},{7,6},{8,9},{9,8},{10,11... | collective-permute-start | bytes 6152 | tf_op jit(solution)/shard_map/ppermute | solution.py:317
  116.2 4.8 %collective-permute-start.27 = (f32[512]{0:T(512)S(1)}, f32[512]{0:T(512)S(1)}, u32[]{:S(2)}, u32[]{:S(2)}) collective-permute-start(f32[512]{0:T(512)S(1)} %add.57), channel_id=1, source_target_pairs={{0,3},{1,2},{2,1},{3,0},{4,7},{5,6},{6,5},{7,4},{8,11},{9,10},{10,... | collective-permute-start | bytes 6152 | tf_op jit(solution)/shard_map/ppermute | solution.py:317
  (4 other events, 27.2 us)

commit v8 on v7

--- a/solution.py
+++ b/solution.py
@@ -184,7 +184,10 @@
     end = place if stage == 0 else PLANE
     lo = jnp.clip(lax.div(jnp.maximum(starts[0], 0), rows), 0, end)
     clear = jnp.clip(lax.div(jnp.maximum(starts[-1], 0) + rows - 1, rows), lo, end)
-    for copy in copies:
+    copies[0].wait()
+    if stage == 0:
+        tile(place, True, True)
+    for copy in copies[1:]:
         copy.wait()
 
     @pl.loop(lo, clear)
@@ -195,8 +198,6 @@
     def _(s):
         tile(s, False, False)
 
-    if stage == 0:
-        tile(place, True, True)
     if stage == BACK:
         for h in range(heads):
             total = jnp.sum(den_ref[h], axis=1, keepdims=True)

time: 120 us -> 121 us (level); the launches traced: 122 us -> 118 us
  starting transfers between devices: 47.1 us -> 39.9 us
  waiting for transfers between devices: 34.1 us -> 36 us
  blocking collectives: 15.4 us -> 17 us
    ppermute x15, waiting for transfers between devices: 21.6 us -> 29.5 us  [tp_xor(): return lax.ppermute(a, 'tp', [(i, i ^ m) for i in range(n_tp)])]
    all_to_all x1, waiting for transfers between devices: 12.1 us -> 4.35 us  [local(): gathered = lax.all_to_all(striped, 'ctx', 0, 0, tiled=True)]
    all_to_all x1, starting transfers between devices: 15.8 us -> 8.38 us  [local(): gathered = lax.all_to_all(striped, 'ctx', 0, 0, tiled=True)]
    ppermute x11, waiting for transfers between devices: 0.39 us -> 2.08 us  [ctx_xor(): return lax.ppermute(a, 'ctx', [(i, i ^ m) for i in range(n_ctx)])]
    all_to_all x1, blocking collectives: 15.4 us -> 17 us  [local(): lax.all_to_all(ordered.reshape(striped.shape), 'ctx', 0, 0, tiled=True)]
  transfers between devices with their start and end apart: 29 -> 29, of which waited for: 13 -> 14; matrix products, arithmetic and copies ran while one was open for 2% -> 2% of each run, Pallas kernels for 10% -> 11%
where the time goes in v8:
time: 121 us; the launch traced here: 118 us
  starting transfers between devices  39.9 us (33%)
  waiting for transfers between devices  36 us (30%)
  Pallas kernels  21.3 us (18%)
  blocking collectives  17 us (14%)
  local copies, waits for them, and re-layouts  2.7 us (2%)
    ppermute x15, waiting for transfers between devices, tp_xor(): return lax.ppermute(a, 'tp', [(i, i ^ m) for i in range(n_tp)])  29.5 us
    ppermute x15, starting transfers between devices, tp_xor(): return lax.ppermute(a, 'tp', [(i, i ^ m) for i in range(n_tp)])  22.2 us
    all_to_all x1, blocking collectives, local(): lax.all_to_all(ordered.reshape(striped.shape), 'ctx', 0, 0, tiled=True)  17 us
    pallas_call x2, Pallas kernels, project(): pl.pallas_call(functools.partial(project_kernel, scale, tile, count, part...  12.9 us
    all_to_all x1, starting transfers between devices, local(): gathered = lax.all_to_all(striped, 'ctx', 0, 0, tiled=True)  8.38 us
    ppermute x11, starting transfers between devices, ctx_xor(): return lax.ppermute(a, 'ctx', [(i, i ^ m) for i in range(n_ctx)])  5.37 us
    pallas_call x3, Pallas kernels, attend(): pl.pallas_call(functools.partial(attend_kernel, rows, stage), in_specs=[p...  5.27 us
    all_to_all x1, waiting for transfers between devices, local(): gathered = lax.all_to_all(striped, 'ctx', 0, 0, tiled=True)  4.35 us
  transfers between devices with their start and end apart: 29, of which 14 were waited for; matrix products, arithmetic and copies ran while one was open for 2% of the time, Pallas kernels for 11%

profile of v8, /device:TPU:2, one launch (start us, length us, event | category | flops | bytes accessed | tf_op | source)
XLA Modules:
  0.0 118.5 jit_solution(16006474327489228966)
XLA Ops:
  0.0 6.8 %project_kv.1 = (bf16[512,256]{1,0:T(8,128)(2,1)}, bf16[2,128,640]{2,1,0:T(8,128)(2,1)}, bf16[2,128,640]{2,1,0:T(8,128)(2,1)}, bf16[2,128,640]{2,1,0:T(8,128)(2,1)}, bf16[2,128,640]{2,1,0:T(8,128)(2,1)}) custom-call(bf16[512,4608]{1,0:T(8,128)(2,1)} %x_hbm.3, f32[4608]{0:T(1024)} %g_ref.3, bf16[4608,128]{1,0:T(8,128)(2,1)} %refs_0_.2, ...), custom_call_target="tpu_custom_call" | custom-call | flops 1207959552 | bytes 7077888 | tf_op jit(solution)/shard_map/project_kv/pallas_call | solution.py:112
  6.8 2.0 %collective-permute-start = (bf16[512,256]{1,0:T(8,128)(2,1)}, bf16[512,256]{1,0:T(8,128)(2,1)S(1)}, u32[]{:S(2)}, u32[]{:S(2)}) collective-permute-start(bf16[512,256]{1,0:T(8,128)(2,1)} %get-tuple-element.42.refs_0_), channel_id=1, source_target_pairs={{0,32},{8,40},{16,48},{24,56},{32,64},{40,72},{48,80},{56,88},{64,... | collective-permute-start | bytes 786440 | tf_op jit(solution)/shard_map/ppermute | solution.py:315
  9.4 1.6 %collective-permute-start.9 = (bf16[2,128,640]{2,1,0:T(8,128)(2,1)}, bf16[2,128,640]{2,1,0:T(8,128)(2,1)S(1)}, u32[]{:S(2)}, u32[]{:S(2)}) collective-permute-start(bf16[2,128,640]{2,1,0:T(8,128)(2,1)} %get-tuple-element.51), channel_id=1, source_target_pairs={{0,1},{1,0},{2,3},{3,2},{4,5},{5,4},{6,7},{7,6},{8,9},{9,8},{10,11... | collective-permute-start | bytes 983048 | tf_op jit(solution)/shard_map/ppermute | solution.py:318
  10.9 2.2 %collective-permute-start.11 = (bf16[2,128,640]{2,1,0:T(8,128)(2,1)}, bf16[2,128,640]{2,1,0:T(8,128)(2,1)S(1)}, u32[]{:S(2)}, u32[]{:S(2)}) collective-permute-start(bf16[2,128,640]{2,1,0:T(8,128)(2,1)} %get-tuple-element.53), channel_id=1, source_target_pairs={{0,3},{1,2},{2,1},{3,0},{4,7},{5,6},{6,5},{7,4},{8,11},{9,10},{10,... | collective-permute-start | bytes 983048 | tf_op jit(solution)/shard_map/ppermute | solution.py:318
  13.3 6.1 %project_q.1.q_ref = bf16[512,256]{1,0:T(8,128)(2,1)} custom-call(bf16[512,4608]{1,0:T(8,128)(2,1)} %x_hbm.3, f32[4608]{0:T(1024)} %g_ref.3, bf16[4608,256]{1,0:T(8,128)(2,1)} %refs_0_.3), custom_call_target="tpu_custom_call" | custom-call | flops 1207959552 | bytes 7077888 | tf_op jit(solution)/shard_map/project_q/pallas_call | solution.py:112
  19.7 2.0 %collective-permute-start.1 = (bf16[512,256]{1,0:T(8,128)(2,1)S(1)}, bf16[512,256]{1,0:T(8,128)(2,1)S(1)}, u32[]{:S(2)}, u32[]{:S(2)}) collective-permute-start(bf16[512,256]{1,0:T(8,128)(2,1)S(1)} %collective-permute-done.refs_0_), channel_id=1, source_target_pairs={{0,32},{8,40},{16,48},{24,56},{32,64},{40,72},{48,80},{56,88},{64,... | collective-permute-start | bytes 786440 | tf_op jit(solution)/shard_map/ppermute | solution.py:315
  21.7 1.5 %collective-permute-start.7 = (bf16[512,256]{1,0:T(8,128)(2,1)S(1)}, bf16[512,256]{1,0:T(8,128)(2,1)S(1)}, u32[]{:S(2)}, u32[]{:S(2)}) collective-permute-start(bf16[512,256]{1,0:T(8,128)(2,1)S(1)} %collective-permute-done.refs_0_), channel_id=1, source_target_pairs={{0,16},{8,24},{16,0},{24,8},{32,48},{40,56},{48,32},{56,40},{64,80... | collective-permute-start | bytes 786440 | tf_op jit(solution)/shard_map/ppermute | solution.py:312
  25.6 3.6 %attend.3 = (f32[2,512,128]{2,1,0:T(8,128)S(1)}, f32[2,512,128]{2,1,0:T(8,128)S(1)}) custom-call(s32[5]{0:T(128)S(1)} %pad_add_fusion.info_ref, bf16[512,256]{1,0:T(8,128)(2,1)S(1)} %copy-done, bf16[512,256]{1,0:T(8,128)(2,1)S(1)} %copy-done.1, bf16[512,256]{1,0:T(8,128)(2,1)S(1)} %collective-permute-done.2.refs_1_, ...), custom_call_target="tpu_custom_call" | custom-call | flops 2000000000 | bytes 4000000 | tf_op jit(solution)/shard_map/attend/pallas_call | solution.py:213
  29.2 1.5 %collective-permute-start.5 = (bf16[512,256]{1,0:T(8,128)(2,1)S(1)}, bf16[512,256]{1,0:T(8,128)(2,1)S(1)}, u32[]{:S(2)}, u32[]{:S(2)}) collective-permute-start(bf16[512,256]{1,0:T(8,128)(2,1)S(1)} %collective-permute-done.1.refs_0_), channel_id=1, source_target_pairs={{0,16},{8,24},{16,0},{24,8},{32,48},{40,56},{48,32},{56,40},{64,80... | collective-permute-start | bytes 786440 | tf_op jit(solution)/shard_map/ppermute | solution.py:312
  31.2 4.4 %collective-permute-done.10 = bf16[2,128,640]{2,1,0:T(8,128)(2,1)S(1)} collective-permute-done((bf16[2,128,640]{2,1,0:T(8,128)(2,1)S(1)}, bf16[2,128,640]{2,1,0:T(8,128)(2,1)S(1)}, u32[]{:S(2)}, u32[]{:S(2)}) %collective-permute-start.10) | collective-permute-done | bytes 327712 | tf_op jit(solution)/shard_map/ppermute | solution.py:318
  36.6 1.7 %collective-permute-done.5.refs_2_ = bf16[512,256]{1,0:T(8,128)(2,1)S(1)} collective-permute-done((bf16[512,256]{1,0:T(8,128)(2,1)S(1)}, bf16[512,256]{1,0:T(8,128)(2,1)S(1)}, u32[]{:S(2)}, u32[]{:S(2)}) %collective-permute-start.5) | collective-permute-done | bytes 262176 | tf_op jit(solution)/shard_map/ppermute | solution.py:312
  38.4 2.4 %collective-permute-start.14 = (bf16[4,128,640]{2,1,0:T(8,128)(2,1)S(1)}, bf16[4,128,640]{2,1,0:T(8,128)(2,1)S(1)}, u32[]{:S(2)}, u32[]{:S(2)}) collective-permute-start(bf16[4,128,640]{2,1,0:T(8,128)(2,1)S(1)} %get-tuple-element.60), channel_id=1, source_target_pairs={{0,4},{1,5},{2,6},{3,7},{4,0},{5,1},{6,2},{7,3},{8,12},{9,13},{10,... | collective-permute-start | bytes 1966088 | tf_op jit(solution)/shard_map/ppermute | solution.py:318
  42.8 8.4 %all-to-all-start = ((bf16[32,8,512]{2,1,0:T(8,128)(2,1)}), bf16[32,8,512]{2,1,0:T(8,128)(2,1)S(1)}, u32[]{:S(2)}, u32[]{:S(2)}) async-start(bf16[32,8,512]{2,1,0:T(8,128)(2,1)} %reshape.48), calls=%async_computation | async-start | bytes 524288 | tf_op jit(solution)/shard_map/all_to_all | solution.py:370
  51.2 7.7 %collective-permute-done.14.refs_1_.refs_0_ = bf16[4,128,640]{2,1,0:T(8,128)(2,1)S(1)} collective-permute-done((bf16[4,128,640]{2,1,0:T(8,128)(2,1)S(1)}, bf16[4,128,640]{2,1,0:T(8,128)(2,1)S(1)}, u32[]{:S(2)}, u32[]{:S(2)}) %collective-permute-start.14) | collective-permute-done | bytes 655392 | tf_op jit(solution)/shard_map/ppermute | solution.py:318
  59.0 4.4 %all-to-all-done = bf16[32,8,512]{2,1,0:T(8,128)(2,1)S(1)} async-done(((bf16[32,8,512]{2,1,0:T(8,128)(2,1)}), bf16[32,8,512]{2,1,0:T(8,128)(2,1)S(1)}, u32[]{:S(2)}, u32[]{:S(2)}) %all-to-all-start) | async-done | bytes 262176 | tf_op jit(solution)/shard_map/all_to_all | solution.py:370
  64.1 17.0 %all_to_all.10 = bf16[32,8,512]{2,1,0:T(8,128)(2,1)S(1)} all-to-all(bf16[32,8,512]{2,1,0:T(8,128)(2,1)S(1)} %fusion), channel_id=1, replica_groups=mesh['ctx'=32,'tp'=8] {'ctx'}, dimensions={0} | all-to-all | bytes 524288 | tf_op jit(solution)/shard_map/all_to_all | solution.py:378
  81.4 1.5 %collective-permute-start.17 = (bf16[512,256]{1,0:T(8,128)(2,1)S(1)}, bf16[512,256]{1,0:T(8,128)(2,1)S(1)}, u32[]{:S(2)}, u32[]{:S(2)}) collective-permute-start(bf16[512,256]{1,0:T(8,128)(2,1)S(1)} %reshape.52.refs_4_), channel_id=1, source_target_pairs={{0,4},{1,5},{2,6},{3,7},{4,0},{5,1},{6,2},{7,3},{8,12},{9,13},{10,... | collective-permute-start | bytes 786440 | tf_op jit(solution)/shard_map/ppermute | solution.py:318
  82.9 1.9 %collective-permute-start.19 = (bf16[512,256]{1,0:T(8,128)(2,1)S(1)}, bf16[512,256]{1,0:T(8,128)(2,1)S(1)}, u32[]{:S(2)}, u32[]{:S(2)}) collective-permute-start(bf16[512,256]{1,0:T(8,128)(2,1)S(1)} %reshape.52.refs_4_), channel_id=1, source_target_pairs={{0,2},{1,3},{2,0},{3,1},{4,6},{5,7},{6,4},{7,5},{8,10},{9,11},{10,... | collective-permute-start | bytes 786440 | tf_op jit(solution)/shard_map/ppermute | solution.py:318
  85.5 1.5 %collective-permute-start.23 = (bf16[512,256]{1,0:T(8,128)(2,1)S(1)}, bf16[512,256]{1,0:T(8,128)(2,1)S(1)}, u32[]{:S(2)}, u32[]{:S(2)}) collective-permute-start(bf16[512,256]{1,0:T(8,128)(2,1)S(1)} %reshape.52.refs_4_), channel_id=1, source_target_pairs={{0,3},{1,2},{2,1},{3,0},{4,7},{5,6},{6,5},{7,4},{8,11},{9,10},{10,... | collective-permute-start | bytes 786440 | tf_op jit(solution)/shard_map/ppermute | solution.py:318
  87.0 3.6 %collective-permute-done.17.refs_8_ = bf16[512,256]{1,0:T(8,128)(2,1)S(1)} collective-permute-done((bf16[512,256]{1,0:T(8,128)(2,1)S(1)}, bf16[512,256]{1,0:T(8,128)(2,1)S(1)}, u32[]{:S(2)}, u32[]{:S(2)}) %collective-permute-start.17) | collective-permute-done | bytes 262176 | tf_op jit(solution)/shard_map/ppermute | solution.py:318
  91.2 2.5 %collective-permute-done.19.refs_6_ = bf16[512,256]{1,0:T(8,128)(2,1)S(1)} collective-permute-done((bf16[512,256]{1,0:T(8,128)(2,1)S(1)}, bf16[512,256]{1,0:T(8,128)(2,1)S(1)}, u32[]{:S(2)}, u32[]{:S(2)}) %collective-permute-start.19) | collective-permute-done | bytes 262176 | tf_op jit(solution)/shard_map/ppermute | solution.py:318
  93.7 2.2 %collective-permute-start.20 = (bf16[512,256]{1,0:T(8,128)(2,1)S(1)}, bf16[512,256]{1,0:T(8,128)(2,1)S(1)}, u32[]{:S(2)}, u32[]{:S(2)}) collective-permute-start(bf16[512,256]{1,0:T(8,128)(2,1)S(1)} %collective-permute-done.19.refs_6_), channel_id=1, source_target_pairs={{0,4},{1,5},{2,6},{3,7},{4,0},{5,1},{6,2},{7,3},{8,12},{9,13},{10,... | collective-permute-start | bytes 786440 | tf_op jit(solution)/shard_map/ppermute | solution.py:318
  96.8 1.5 %collective-permute-done.22.refs_5_ = bf16[512,256]{1,0:T(8,128)(2,1)S(1)} collective-permute-done((bf16[512,256]{1,0:T(8,128)(2,1)S(1)}, bf16[512,256]{1,0:T(8,128)(2,1)S(1)}, u32[]{:S(2)}, u32[]{:S(2)}) %collective-permute-start.22) | collective-permute-done | bytes 262176 | tf_op jit(solution)/shard_map/ppermute | solution.py:318
  98.3 1.3 %out_project.2.refs_5_ = f32[512,640]{1,0:T(8,128)S(1)} custom-call(bf16[4,128,640]{2,1,0:T(8,128)(2,1)S(1)} %get-tuple-element.67.refs_0_, bf16[4,128,640]{2,1,0:T(8,128)(2,1)S(1)} %collective-permute-done.14.refs_1_.refs_0_, bf16[4,128,640]{2,1,0:T(8,128)(2,1)S(1)} %collective-permute-done.15.refs_2_, ...), custom_call_target="tpu_custom_call" | custom-call | flops 838860800 | bytes 6000000 | tf_op jit(solution)/shard_map/out_project/pallas_call | solution.py:290
  99.7 2.3 %collective-permute-done.18.refs_2_ = bf16[512,256]{1,0:T(8,128)(2,1)S(1)} collective-permute-done((bf16[512,256]{1,0:T(8,128)(2,1)S(1)}, bf16[512,256]{1,0:T(8,128)(2,1)S(1)}, u32[]{:S(2)}, u32[]{:S(2)}) %collective-permute-start.18) | collective-permute-done | bytes 262176 | tf_op jit(solution)/shard_map/ppermute | solution.py:318
  102.0 1.4 %collective-permute-done.21.refs_4_ = bf16[512,256]{1,0:T(8,128)(2,1)S(1)} collective-permute-done((bf16[512,256]{1,0:T(8,128)(2,1)S(1)}, bf16[512,256]{1,0:T(8,128)(2,1)S(1)}, u32[]{:S(2)}, u32[]{:S(2)}) %collective-permute-start.21) | collective-permute-done | bytes 262176 | tf_op jit(solution)/shard_map/ppermute | solution.py:318
  103.4 1.8 %out_project.3 = (f32[512,576]{1,0:T(8,128)S(1)}, f32[1,512]{1,0:T(1,128)S(1)}) custom-call(bf16[4,128,640]{2,1,0:T(8,128)(2,1)S(1)} %collective-permute-done.14.refs_1_.refs_0_, bf16[4,128,640]{2,1,0:T(8,128)(2,1)S(1)} %collective-permute-done.16.refs_3_.refs_1_, bf16[512,256]{1,0:T(8,128)(2,1)S(1)} %collective-permute-done.18.refs_2_, ...), custom_call_target="tpu_custom_call" | custom-call | flops 503316480 | bytes 6000000 | tf_op jit(solution)/shard_map/out_project/pallas_call | solution.py:290
  105.2 1.7 %collective-permute-start.24 = (f32[512]{0:T(512)S(1)}, f32[512]{0:T(512)S(1)}, u32[]{:S(2)}, u32[]{:S(2)}) collective-permute-start(f32[512]{0:T(512)S(1)} %bitcast.12), channel_id=1, source_target_pairs={{0,4},{1,5},{2,6},{3,7},{4,0},{5,1},{6,2},{7,3},{8,12},{9,13},{10,... | collective-permute-start | bytes 6152 | tf_op jit(solution)/shard_map/ppermute | solution.py:318
  106.9 3.5 %collective-permute-done.24 = f32[512]{0:T(512)S(1)} collective-permute-done((f32[512]{0:T(512)S(1)}, f32[512]{0:T(512)S(1)}, u32[]{:S(2)}, u32[]{:S(2)}) %collective-permute-start.24) | collective-permute-done | bytes 2080 | tf_op jit(solution)/shard_map/ppermute | solution.py:318
  110.4 1.4 %collective-permute-start.25 = (f32[512]{0:T(512)S(1)}, f32[512]{0:T(512)S(1)}, u32[]{:S(2)}, u32[]{:S(2)}) collective-permute-start(f32[512]{0:T(512)S(1)} %add.57), channel_id=1, source_target_pairs={{0,2},{1,3},{2,0},{3,1},{4,6},{5,7},{6,4},{7,5},{8,10},{9,11},{10,... | collective-permute-start | bytes 6152 | tf_op jit(solution)/shard_map/ppermute | solution.py:318
  112.4 2.0 %collective-permute-start.27 = (f32[512]{0:T(512)S(1)}, f32[512]{0:T(512)S(1)}, u32[]{:S(2)}, u32[]{:S(2)}) collective-permute-start(f32[512]{0:T(512)S(1)} %add.57), channel_id=1, source_target_pairs={{0,3},{1,2},{2,1},{3,0},{4,7},{5,6},{6,5},{7,4},{8,11},{9,10},{10,... | collective-permute-start | bytes 6152 | tf_op jit(solution)/shard_map/ppermute | solution.py:318
  115.5 1.8 %collective-permute-done.27 = f32[512]{0:T(512)S(1)} collective-permute-done((f32[512]{0:T(512)S(1)}, f32[512]{0:T(512)S(1)}, u32[]{:S(2)}, u32[]{:S(2)}) %collective-permute-start.27) | collective-permute-done | bytes 2080 | tf_op jit(solution)/shard_map/ppermute | solution.py:318
  (72 shorter events, 13.3 us)
Async XLA Ops:
  0.0 13.1 %copy-start.5 = (s32[128]{0:T(128)S(1)}, s32[128]{0:T(128)}, u32[]{:S(2)}) copy-start(s32[128]{0:T(128)} %param.16) | copy-start | bytes 1540
  6.8 12.8 %collective-permute-start = (bf16[512,256]{1,0:T(8,128)(2,1)}, bf16[512,256]{1,0:T(8,128)(2,1)S(1)}, u32[]{:S(2)}, u32[]{:S(2)}) collective-permute-start(bf16[512,256]{1,0:T(8,128)(2,1)} %get-tuple-element.42.refs_0_), channel_id=1, source_target_pairs={{0,32},{8,40},{16,48},{24,56},{32,64},{40,72},{48,80},{56,88},{64,... | collective-permute-start | bytes 786440 | tf_op jit(solution)/shard_map/ppermute | solution.py:315
  8.8 14.8 %collective-permute-start.3 = (bf16[512,256]{1,0:T(8,128)(2,1)}, bf16[512,256]{1,0:T(8,128)(2,1)S(1)}, u32[]{:S(2)}, u32[]{:S(2)}) collective-permute-start(bf16[512,256]{1,0:T(8,128)(2,1)} %get-tuple-element.42.refs_0_), channel_id=1, source_target_pairs={{0,16},{8,24},{16,0},{24,8},{32,48},{40,56},{48,32},{56,40},{64,80... | collective-permute-start | bytes 786440 | tf_op jit(solution)/shard_map/ppermute | solution.py:312
  9.4 14.4 %collective-permute-start.9 = (bf16[2,128,640]{2,1,0:T(8,128)(2,1)}, bf16[2,128,640]{2,1,0:T(8,128)(2,1)S(1)}, u32[]{:S(2)}, u32[]{:S(2)}) collective-permute-start(bf16[2,128,640]{2,1,0:T(8,128)(2,1)} %get-tuple-element.51), channel_id=1, source_target_pairs={{0,1},{1,0},{2,3},{3,2},{4,5},{5,4},{6,7},{7,6},{8,9},{9,8},{10,11... | collective-permute-start | bytes 983048 | tf_op jit(solution)/shard_map/ppermute | solution.py:318
  10.9 13.3 %collective-permute-start.11 = (bf16[2,128,640]{2,1,0:T(8,128)(2,1)}, bf16[2,128,640]{2,1,0:T(8,128)(2,1)S(1)}, u32[]{:S(2)}, u32[]{:S(2)}) collective-permute-start(bf16[2,128,640]{2,1,0:T(8,128)(2,1)} %get-tuple-element.53), channel_id=1, source_target_pairs={{0,3},{1,2},{2,1},{3,0},{4,7},{5,6},{6,5},{7,4},{8,11},{9,10},{10,... | collective-permute-start | bytes 983048 | tf_op jit(solution)/shard_map/ppermute | solution.py:318
  13.3 10.3 %copy-start.1 = (bf16[512,256]{1,0:T(8,128)(2,1)S(1)}, bf16[512,256]{1,0:T(8,128)(2,1)}, u32[]{:S(2)}) copy-start(bf16[512,256]{1,0:T(8,128)(2,1)} %get-tuple-element.42.refs_0_) | copy-start | bytes 786436
  19.7 9.6 %collective-permute-start.1 = (bf16[512,256]{1,0:T(8,128)(2,1)S(1)}, bf16[512,256]{1,0:T(8,128)(2,1)S(1)}, u32[]{:S(2)}, u32[]{:S(2)}) collective-permute-start(bf16[512,256]{1,0:T(8,128)(2,1)S(1)} %collective-permute-done.refs_0_), channel_id=1, source_target_pairs={{0,32},{8,40},{16,48},{24,56},{32,64},{40,72},{48,80},{56,88},{64,... | collective-permute-start | bytes 786440 | tf_op jit(solution)/shard_map/ppermute | solution.py:315
  21.7 9.1 %collective-permute-start.7 = (bf16[512,256]{1,0:T(8,128)(2,1)S(1)}, bf16[512,256]{1,0:T(8,128)(2,1)S(1)}, u32[]{:S(2)}, u32[]{:S(2)}) collective-permute-start(bf16[512,256]{1,0:T(8,128)(2,1)S(1)} %collective-permute-done.refs_0_), channel_id=1, source_target_pairs={{0,16},{8,24},{16,0},{24,8},{32,48},{40,56},{48,32},{56,40},{64,80... | collective-permute-start | bytes 786440 | tf_op jit(solution)/shard_map/ppermute | solution.py:312
  23.6 1.6 %collective-permute-start.2 = (bf16[512,256]{1,0:T(8,128)(2,1)S(1)}, bf16[512,256]{1,0:T(8,128)(2,1)S(1)}, u32[]{:S(2)}, u32[]{:S(2)}) collective-permute-start(bf16[512,256]{1,0:T(8,128)(2,1)S(1)} %copy-done.1), channel_id=1, source_target_pairs={{0,8},{8,0},{16,24},{24,16},{32,40},{40,32},{48,56},{56,48},{64,72... | collective-permute-start | bytes 786440 | tf_op jit(solution)/shard_map/ppermute | solution.py:312
  23.7 1.9 %collective-permute-start.4 = (bf16[512,256]{1,0:T(8,128)(2,1)S(1)}, bf16[512,256]{1,0:T(8,128)(2,1)S(1)}, u32[]{:S(2)}, u32[]{:S(2)}) collective-permute-start(bf16[512,256]{1,0:T(8,128)(2,1)S(1)} %collective-permute-done.3.refs_2_), channel_id=1, source_target_pairs={{0,8},{8,0},{16,24},{24,16},{32,40},{40,32},{48,56},{56,48},{64,72... | collective-permute-start | bytes 786440 | tf_op jit(solution)/shard_map/ppermute | solution.py:312
  24.3 11.3 %collective-permute-start.10 = (bf16[2,128,640]{2,1,0:T(8,128)(2,1)S(1)}, bf16[2,128,640]{2,1,0:T(8,128)(2,1)S(1)}, u32[]{:S(2)}, u32[]{:S(2)}) collective-permute-start(bf16[2,128,640]{2,1,0:T(8,128)(2,1)S(1)} %copy-done.4), channel_id=1, source_target_pairs={{0,2},{1,3},{2,0},{3,1},{4,6},{5,7},{6,4},{7,5},{8,10},{9,11},{10,... | collective-permute-start | bytes 983048 | tf_op jit(solution)/shard_map/ppermute | solution.py:318
  25.3 10.6 %collective-permute-start.6 = (bf16[512,256]{1,0:T(8,128)(2,1)S(1)}, bf16[512,256]{1,0:T(8,128)(2,1)S(1)}, u32[]{:S(2)}, u32[]{:S(2)}) collective-permute-start(bf16[512,256]{1,0:T(8,128)(2,1)S(1)} %collective-permute-done.refs_0_), channel_id=1, source_target_pairs={{0,8},{8,0},{16,24},{24,16},{32,40},{40,32},{48,56},{56,48},{64,72... | collective-permute-start | bytes 786440 | tf_op jit(solution)/shard_map/ppermute | solution.py:312
  29.2 9.1 %collective-permute-start.5 = (bf16[512,256]{1,0:T(8,128)(2,1)S(1)}, bf16[512,256]{1,0:T(8,128)(2,1)S(1)}, u32[]{:S(2)}, u32[]{:S(2)}) collective-permute-start(bf16[512,256]{1,0:T(8,128)(2,1)S(1)} %collective-permute-done.1.refs_0_), channel_id=1, source_target_pairs={{0,16},{8,24},{16,0},{24,8},{32,48},{40,56},{48,32},{56,40},{64,80... | collective-permute-start | bytes 786440 | tf_op jit(solution)/shard_map/ppermute | solution.py:312
  30.7 10.1 %collective-permute-start.12 = (bf16[512,256]{1,0:T(8,128)(2,1)S(1)}, bf16[512,256]{1,0:T(8,128)(2,1)S(1)}, u32[]{:S(2)}, u32[]{:S(2)}) collective-permute-start(bf16[512,256]{1,0:T(8,128)(2,1)S(1)} %collective-permute-done.1.refs_0_), channel_id=1, source_target_pairs={{0,8},{8,0},{16,24},{24,16},{32,40},{40,32},{48,56},{56,48},{64,72... | collective-permute-start | bytes 786440 | tf_op jit(solution)/shard_map/ppermute | solution.py:312
  30.7 5.1 %collective-permute-start.8 = (bf16[512,256]{1,0:T(8,128)(2,1)S(1)}, bf16[512,256]{1,0:T(8,128)(2,1)S(1)}, u32[]{:S(2)}, u32[]{:S(2)}) collective-permute-start(bf16[512,256]{1,0:T(8,128)(2,1)S(1)} %collective-permute-done.7.refs_2_), channel_id=1, source_target_pairs={{0,8},{8,0},{16,24},{24,16},{32,40},{40,32},{48,56},{56,48},{64,72... | collective-permute-start | bytes 786440 | tf_op jit(solution)/shard_map/ppermute | solution.py:312
  38.3 2.5 %collective-permute-start.13 = (bf16[512,256]{1,0:T(8,128)(2,1)S(1)}, bf16[512,256]{1,0:T(8,128)(2,1)S(1)}, u32[]{:S(2)}, u32[]{:S(2)}) collective-permute-start(bf16[512,256]{1,0:T(8,128)(2,1)S(1)} %collective-permute-done.5.refs_2_), channel_id=1, source_target_pairs={{0,8},{8,0},{16,24},{24,16},{32,40},{40,32},{48,56},{56,48},{64,72... | collective-permute-start | bytes 786440 | tf_op jit(solution)/shard_map/ppermute | solution.py:312
  38.4 20.5 %collective-permute-start.14 = (bf16[4,128,640]{2,1,0:T(8,128)(2,1)S(1)}, bf16[4,128,640]{2,1,0:T(8,128)(2,1)S(1)}, u32[]{:S(2)}, u32[]{:S(2)}) collective-permute-start(bf16[4,128,640]{2,1,0:T(8,128)(2,1)S(1)} %get-tuple-element.60), channel_id=1, source_target_pairs={{0,4},{1,5},{2,6},{3,7},{4,0},{5,1},{6,2},{7,3},{8,12},{9,13},{10,... | collective-permute-start | bytes 1966088 | tf_op jit(solution)/shard_map/ppermute | solution.py:318
  42.8 20.5 %all-to-all-start = ((bf16[32,8,512]{2,1,0:T(8,128)(2,1)}), bf16[32,8,512]{2,1,0:T(8,128)(2,1)S(1)}, u32[]{:S(2)}, u32[]{:S(2)}) async-start(bf16[32,8,512]{2,1,0:T(8,128)(2,1)} %reshape.48), calls=%async_computation | async-start | bytes 524288 | tf_op jit(solution)/shard_map/all_to_all | solution.py:370
  63.3 17.7 %collective-permute-start.15 = (bf16[4,128,640]{2,1,0:T(8,128)(2,1)S(1)}, bf16[4,128,640]{2,1,0:T(8,128)(2,1)S(1)}, u32[]{:S(2)}, u32[]{:S(2)}) collective-permute-start(bf16[4,128,640]{2,1,0:T(8,128)(2,1)S(1)} %get-tuple-element.67.refs_0_), channel_id=1, source_target_pairs={{0,8},{8,0},{16,24},{24,16},{32,40},{40,32},{48,56},{56,48},{64,72... | collective-permute-start | bytes 1966088 | tf_op jit(solution)/shard_map/ppermute | solution.py:312
  63.3 17.7 %collective-permute-start.16 = (bf16[4,128,640]{2,1,0:T(8,128)(2,1)S(1)}, bf16[4,128,640]{2,1,0:T(8,128)(2,1)S(1)}, u32[]{:S(2)}, u32[]{:S(2)}) collective-permute-start(bf16[4,128,640]{2,1,0:T(8,128)(2,1)S(1)} %collective-permute-done.14.refs_1_.refs_0_), channel_id=1, source_target_pairs={{0,8},{8,0},{16,24},{24,16},{32,40},{40,32},{48,56},{56,48},{64,72... | collective-permute-start | bytes 1966088 | tf_op jit(solution)/shard_map/ppermute | solution.py:312
  81.4 9.1 %collective-permute-start.17 = (bf16[512,256]{1,0:T(8,128)(2,1)S(1)}, bf16[512,256]{1,0:T(8,128)(2,1)S(1)}, u32[]{:S(2)}, u32[]{:S(2)}) collective-permute-start(bf16[512,256]{1,0:T(8,128)(2,1)S(1)} %reshape.52.refs_4_), channel_id=1, source_target_pairs={{0,4},{1,5},{2,6},{3,7},{4,0},{5,1},{6,2},{7,3},{8,12},{9,13},{10,... | collective-permute-start | bytes 786440 | tf_op jit(solution)/shard_map/ppermute | solution.py:318
  82.9 10.8 %collective-permute-start.19 = (bf16[512,256]{1,0:T(8,128)(2,1)S(1)}, bf16[512,256]{1,0:T(8,128)(2,1)S(1)}, u32[]{:S(2)}, u32[]{:S(2)}) collective-permute-start(bf16[512,256]{1,0:T(8,128)(2,1)S(1)} %reshape.52.refs_4_), channel_id=1, source_target_pairs={{0,2},{1,3},{2,0},{3,1},{4,6},{5,7},{6,4},{7,5},{8,10},{9,11},{10,... | collective-permute-start | bytes 786440 | tf_op jit(solution)/shard_map/ppermute | solution.py:318
  84.8 13.6 %collective-permute-start.22 = (bf16[512,256]{1,0:T(8,128)(2,1)S(1)}, bf16[512,256]{1,0:T(8,128)(2,1)S(1)}, u32[]{:S(2)}, u32[]{:S(2)}) collective-permute-start(bf16[512,256]{1,0:T(8,128)(2,1)S(1)} %reshape.52.refs_4_), channel_id=1, source_target_pairs={{0,1},{1,0},{2,3},{3,2},{4,5},{5,4},{6,7},{7,6},{8,9},{9,8},{10,11... | collective-permute-start | bytes 786440 | tf_op jit(solution)/shard_map/ppermute | solution.py:318
  85.5 12.9 %collective-permute-start.23 = (bf16[512,256]{1,0:T(8,128)(2,1)S(1)}, bf16[512,256]{1,0:T(8,128)(2,1)S(1)}, u32[]{:S(2)}, u32[]{:S(2)}) collective-permute-start(bf16[512,256]{1,0:T(8,128)(2,1)S(1)} %reshape.52.refs_4_), channel_id=1, source_target_pairs={{0,3},{1,2},{2,1},{3,0},{4,7},{5,6},{6,5},{7,4},{8,11},{9,10},{10,... | collective-permute-start | bytes 786440 | tf_op jit(solution)/shard_map/ppermute | solution.py:318
  90.5 11.4 %collective-permute-start.18 = (bf16[512,256]{1,0:T(8,128)(2,1)S(1)}, bf16[512,256]{1,0:T(8,128)(2,1)S(1)}, u32[]{:S(2)}, u32[]{:S(2)}) collective-permute-start(bf16[512,256]{1,0:T(8,128)(2,1)S(1)} %collective-permute-done.17.refs_8_), channel_id=1, source_target_pairs={{0,1},{1,0},{2,3},{3,2},{4,5},{5,4},{6,7},{7,6},{8,9},{9,8},{10,11... | collective-permute-start | bytes 786440 | tf_op jit(solution)/shard_map/ppermute | solution.py:318
  93.7 8.3 %collective-permute-start.20 = (bf16[512,256]{1,0:T(8,128)(2,1)S(1)}, bf16[512,256]{1,0:T(8,128)(2,1)S(1)}, u32[]{:S(2)}, u32[]{:S(2)}) collective-permute-start(bf16[512,256]{1,0:T(8,128)(2,1)S(1)} %collective-permute-done.19.refs_6_), channel_id=1, source_target_pairs={{0,4},{1,5},{2,6},{3,7},{4,0},{5,1},{6,2},{7,3},{8,12},{9,13},{10,... | collective-permute-start | bytes 786440 | tf_op jit(solution)/shard_map/ppermute | solution.py:318
  95.8 7.6 %collective-permute-start.21 = (bf16[512,256]{1,0:T(8,128)(2,1)S(1)}, bf16[512,256]{1,0:T(8,128)(2,1)S(1)}, u32[]{:S(2)}, u32[]{:S(2)}) collective-permute-start(bf16[512,256]{1,0:T(8,128)(2,1)S(1)} %collective-permute-done.17.refs_8_), channel_id=1, source_target_pairs={{0,3},{1,2},{2,1},{3,0},{4,7},{5,6},{6,5},{7,4},{8,11},{9,10},{10,... | collective-permute-start | bytes 786440 | tf_op jit(solution)/shard_map/ppermute | solution.py:318
  99.7 17.5 %copy-start.3 = (f32[576]{0:T(1024)S(1)}, f32[576]{0:T(1024)}, u32[]{:S(2)}) copy-start(f32[576]{0:T(1024)} %param.15) | copy-start | bytes 6916
  105.2 5.2 %collective-permute-start.24 = (f32[512]{0:T(512)S(1)}, f32[512]{0:T(512)S(1)}, u32[]{:S(2)}, u32[]{:S(2)}) collective-permute-start(f32[512]{0:T(512)S(1)} %bitcast.12), channel_id=1, source_target_pairs={{0,4},{1,5},{2,6},{3,7},{4,0},{5,1},{6,2},{7,3},{8,12},{9,13},{10,... | collective-permute-start | bytes 6152 | tf_op jit(solution)/shard_map/ppermute | solution.py:318
  110.4 5.1 %collective-permute-start.25 = (f32[512]{0:T(512)S(1)}, f32[512]{0:T(512)S(1)}, u32[]{:S(2)}, u32[]{:S(2)}) collective-permute-start(f32[512]{0:T(512)S(1)} %add.57), channel_id=1, source_target_pairs={{0,2},{1,3},{2,0},{3,1},{4,6},{5,7},{6,4},{7,5},{8,10},{9,11},{10,... | collective-permute-start | bytes 6152 | tf_op jit(solution)/shard_map/ppermute | solution.py:318
  111.7 3.7 %collective-permute-start.26 = (f32[512]{0:T(512)S(1)}, f32[512]{0:T(512)S(1)}, u32[]{:S(2)}, u32[]{:S(2)}) collective-permute-start(f32[512]{0:T(512)S(1)} %add.57), channel_id=1, source_target_pairs={{0,1},{1,0},{2,3},{3,2},{4,5},{5,4},{6,7},{7,6},{8,9},{9,8},{10,11... | collective-permute-start | bytes 6152 | tf_op jit(solution)/shard_map/ppermute | solution.py:318
  112.4 4.8 %collective-permute-start.27 = (f32[512]{0:T(512)S(1)}, f32[512]{0:T(512)S(1)}, u32[]{:S(2)}, u32[]{:S(2)}) collective-permute-start(f32[512]{0:T(512)S(1)} %add.57), channel_id=1, source_target_pairs={{0,3},{1,2},{2,1},{3,0},{4,7},{5,6},{6,5},{7,4},{8,11},{9,10},{10,... | collective-permute-start | bytes 6152 | tf_op jit(solution)/shard_map/ppermute | solution.py:318
  (4 other events, 27.2 us)
